TPU v7x, 32 devices: a whole 2x2x4 slice. The times are simulated.
32 devices in a mesh: row: 16 (over z, y, x), col: 2 (over core).
Axes of the slice: x: 2, y: 2, z: 4, core: 2. Of those that a mesh axis runs over, the one named last changes fastest.
Arguments:
- points: float32 [2048, 384], P(('row', 'col')), may hold values from -0.3 to 0.3
- coeffs: float32 [2048, 2], P(('row', 'col')), may hold values from -6 to 6
- metric: float32 [384, 384], replicated, may hold values from -1 to 5, as said below
Outputs:
- metric_next: float32 [384, 384], replicated
- transformed: float32 [2048, 384], P(('row', 'col'))
Inputs may be any that keep to these rules, and one draw needn't show every extreme that they name: `metric`: symmetric and positive definite.
All inputs are finite; a program needn't handle non-finite values.
Results may differ from a plain program's by a relative error of at most 0.0003.
The roundings to bfloat16 on the way count: a program that leaves them out, or rounds other values in their place, can miss the bound.
Values sent between devices are 32-bit elements; how exact they have to be, the bound alone decides.
No kernel may reach another device: no remote copies, remote signals or barrier semaphores. Data moves between devices by JAX's collectives and lax.ppermute only.
A program may use at most 64 MiB of HBM per device.

v0:
```python
import math

import jax
import jax.numpy as jnp
from jax import lax
from jax.sharding import PartitionSpec as P

HIGH = lax.Precision.HIGHEST


def tile_terms(query_y, query_norm, centers, center_coef, center_norm):
    cross_term = jnp.dot(query_y, centers.T, precision=HIGH, preferred_element_type=jnp.float32)
    dist_sq = query_norm[:, None] + center_norm[None, :] - 2.0 * cross_term
    distance = jnp.sqrt(jnp.maximum(dist_sq, 0.0))
    weights = jnp.exp(-distance) / jnp.maximum(distance, 0.5)
    coef_sums = jnp.dot(weights, center_coef, precision=HIGH, preferred_element_type=jnp.float32)
    mixed = (weights[:, None, :] * center_coef.T[None, :, :]).astype(jnp.bfloat16)
    rows_all = mixed.shape[0] * mixed.shape[1]
    center_sums = jnp.dot(
        mixed.reshape(rows_all, mixed.shape[2]),
        centers.astype(jnp.bfloat16),
        preferred_element_type=jnp.float32,
    )
    return (coef_sums, center_sums.reshape(mixed.shape[0], mixed.shape[1], centers.shape[1]))


def block_terms(query_y, query_norm, centers, center_coef, center_norm):
    count_all = centers.shape[0]
    step_rows = math.gcd(count_all, 512)
    coef_total = None
    center_total = None
    for begin in range(0, count_all, step_rows):
        coef_sums, center_sums = tile_terms(
            query_y,
            query_norm,
            centers[begin : begin + step_rows],
            center_coef[begin : begin + step_rows],
            center_norm[begin : begin + step_rows],
        )
        if coef_total is None:
            coef_total, center_total = (coef_sums, center_sums)
        else:
            coef_total, center_total = (coef_total + coef_sums, center_total + center_sums)
    return (coef_total, center_total)


def local(points, coeffs, metric):
    rows_own = points.shape[0]
    width = points.shape[1]
    outs_n = coeffs.shape[1]
    query_x = lax.all_gather(points, "col", axis=0, tiled=True)
    query_y = jnp.dot(query_x, metric, precision=HIGH, preferred_element_type=jnp.float32)
    query_n = jnp.sum(query_x * query_y, axis=1)
    offset = lax.axis_index("col") * rows_own
    own_norm = lax.dynamic_slice_in_dim(query_n, offset, rows_own, 0)
    coef_sums, center_sums = block_terms(
        query_y,
        query_n,
        lax.all_gather(points, "row", axis=0, tiled=True),
        lax.all_gather(coeffs, "row", axis=0, tiled=True),
        lax.all_gather(own_norm, "row", axis=0, tiled=True),
    )
    coef_sums, center_sums = (coef_sums, center_sums)
    partial_value = coef_sums[:, :, None] * query_x[:, None, :] - center_sums
    own_part = lax.psum_scatter(partial_value, "col", scatter_dimension=0, tiled=True)
    grads = -jnp.dot(
        own_part.reshape(rows_own * outs_n, width),
        metric,
        precision=HIGH,
        preferred_element_type=jnp.float32,
    )
    outer_local = lax.dot_general(
        grads, grads, (((0,), (0,)), ((), ())), precision=HIGH, preferred_element_type=jnp.float32
    )
    outer = lax.psum(outer_local, ("row", "col"))
    metric_next = outer * (width / jnp.trace(outer))
    transformed = jnp.dot(points, metric_next, precision=HIGH, preferred_element_type=jnp.float32)
    return (metric_next, transformed)


def solution(mesh):
    return jax.shard_map(
        local,
        mesh=mesh,
        in_specs=(P(("row", "col"), None), P(("row", "col"), None), P()),
        out_specs=(P(), P(("row", "col"), None)),
        check_vma=False,
    )
```

profile of v0, /device:TPU:0, one launch (start us, length us, event | category | flops | bytes accessed | tf_op | source)
XLA Modules:
  0.0 249.8 jit_solution(2894906630994143601)
XLA Ops:
  7.2 0.0 copy-start
  7.2 0.0 all-gather.3.cloned.1.call-start
  7.2 0.7 all-gather.3.cloned.1.call-update
  7.9 0.0 reduce-scatter.2.cloned.1.call-start
  8.0 42.7 %all-gather = f32[16,64,2]{1,2,0:T(2,128)S(1)} all-gather(f32[1,64,2]{1,2,0:T(2,128)} %bitcast.32), channel_id=1, replica_groups=mesh['row'=16,'col'=2] {'row'}, dimensions={0}, use_global_device_ids=true | all-gather | bytes 8704 | tf_op jit(solution)/shard_map/all_gather | solution.py:60
  50.6 0.1 reshape.35
  50.7 0.1 reshape.34
  50.8 1.2 dynamic-slice
  52.7 2.2 all_gather.12
  54.8 0.0 copy-done
  54.8 0.7 multiply_reduce_fusion
  55.5 0.2 dynamic-slice_dynamic-update-slice_fusion
  55.7 36.6 %all-reduce = f32[1024]{0:T(1024)S(1)} all-reduce(f32[1024]{0:T(1024)S(1)} %dynamic-slice_dynamic-update-slice_fusion), channel_id=1, replica_groups=mesh['row'=16,'col'=2] {'row'}, use_global_device_ids=true, to_apply=%add | all-reduce | flops 1024 | bytes 8192
  92.3 0.0 all-gather.3.cloned.1.call-done
  92.4 0.0 copy-start.2
  92.4 2.3 maximum_divide_fusion.1
  94.7 0.3 fusion.24
  94.9 0.0 copy-done.2
  94.9 1.1 maximum_divide_fusion
  96.1 0.3 convolution_add_fusion.1
  96.3 0.4 fusion.10
  96.7 1.0 fusion
  97.7 0.0 reduce-scatter.2.cloned.1.call-update
  97.8 0.0 all-reduce.3.cloned.1.call-start
  97.8 5.7 %reduce-scatter.2.cloned.1.call-done = f32[64,2,384]{2,0,1:T(8,128)} async-done(((f32[128,2,384]{2,0,1:T(8,128)}), f32[64,2,384]{2,0,1:T(8,128)}) %reduce-scatter.2.cloned.1.call-update) | async-done | bytes 196624 | tf_op jit(solution)/shard_map/reduce_scatter | solution.py:65
  103.5 1.1 copy.10
  104.6 0.1 reshape.26
  104.7 0.6 convolution_negate_fusion
  105.3 0.0 copy-start.3
  105.3 1.5 fusion.25
  106.8 0.0 all-reduce.3.cloned.1.call-update
  106.8 131.8 %all-reduce.3.cloned.1.call-done = f32[384,384]{1,0:T(8,128)} async-done(((f32[384,384]{1,0:T(8,128)}), f32[384,384]{1,0:T(8,128)}) %all-reduce.3.cloned.1.call-update) | async-done | bytes 589840 | tf_op jit(solution)/shard_map/psum | solution.py:75
  238.6 1.7 select_reduce_fusion
  241.0 1.1 broadcast_multiply_fusion
  242.1 0.0 copy-done.3
  242.1 0.0 copy-start.1
  242.1 1.1 convolution_bitcast_fusion
  243.3 0.0 copy-done.1
  (5 shorter events, 0.0 us)
Async XLA Ops:
  7.2 47.7 %copy-start = (f32[384,384]{1,0:T(8,128)S(1)}, f32[384,384]{1,0:T(8,128)}, u32[]{:S(2)}) copy-start(f32[384,384]{1,0:T(8,128)} %param.5) | copy-start | bytes 1769476
  7.2 85.2 %all-gather.3.cloned.1.call-start = ((), (), s32[]{:S(2)}) async-start(), calls=%async_computation.1 | async-start | bytes 1671168 | tf_op jit(solution)/shard_map/all_gather | solution.py:59
  7.9 95.6 %reduce-scatter.2.cloned.1.call-start = ((), (), s32[]{:S(2)}) async-start(), calls=%async_computation.2 | async-start | bytes 589824 | tf_op jit(solution)/shard_map/reduce_scatter | solution.py:65
  92.4 2.6 %copy-start.2 = (f32[1024,384]{1,0:T(8,128)S(1)}, f32[1024,384]{1,0:T(8,128)}, u32[]{:S(2)}) copy-start(f32[1024,384]{1,0:T(8,128)} %all-gather.3.cloned.1.call-done) | copy-start | bytes 4718596
  97.8 140.8 %all-reduce.3.cloned.1.call-start = ((), (), s32[]{:S(2)}) async-start(), calls=%async_computation.3 | async-start | bytes 1179648 | tf_op jit(solution)/shard_map/psum | solution.py:75
  105.3 136.8 %copy-start.3 = (f32[64,384]{1,0:T(8,128)S(1)}, f32[64,384]{1,0:T(8,128)}, u32[]{:S(2)}) copy-start(f32[64,384]{1,0:T(8,128)} %param.3) | copy-start | bytes 294916
  242.1 1.1 copy-start.1
Sparse Core Ops, SparseCore 0:
  10.8 60.5 all-gather.2
  97.9 5.5 reduce-scatter.1
  110.2 128.3 all-reduce.2
where the time goes:
time: 250 us
  waiting for transfers between devices  138 us (55%)
  blocking collectives  81.4 us (33%)
  between operations  15.2 us (6%)
  matrix products  9.19 us (4%)
  local copies, waits for them, and re-layouts  2.84 us (1%)
  other arithmetic  2.83 us (1%)
    psum x1, waiting for transfers between devices, local(): outer = lax.psum(outer_local, ('row', 'col'))  132 us
    all_gather x1, blocking collectives, local(): lax.all_gather(coeffs, 'row', axis=0, tiled=True)  42.7 us
    unnamed x1, blocking collectives  36.6 us
    reduce_scatter x1, waiting for transfers between devices, local(): lax.psum_scatter(partial_value, 'col', scatter_dimension=0, tiled=True)  5.7 us
  transfers between devices with their start and end apart: 3, of which 2 were waited for; matrix products, arithmetic and copies ran while one was open for 1% of the time, Pallas kernels for 0%

commit v1 on v0

v1 whole, which is shorter than its diff:
```python
import jax
import jax.numpy as jnp
from jax import lax
from jax.sharding import PartitionSpec as P

HIGH = lax.Precision.HIGHEST
AXES = ("row", "col")


def dot(a, b, dims=(((1,), (0,)), ((), ()))):
    return lax.dot_general(a, b, dims, precision=HIGH, preferred_element_type=jnp.float32)


def bits_of(count):
    assert count & (count - 1) == 0
    return [1 << b for b in range(count.bit_length() - 1)]


class Hops:
    def __init__(self, rows, cols):
        self.rows, self.cols = rows, cols

    def __call__(self, value, even, odd=None):
        odd = even if odd is None else odd
        pairs = []
        for r in range(self.rows):
            for c in range(self.cols):
                dr, dc = odd if c & 1 else even
                pairs.append((r * self.cols + c, (r ^ dr) * self.cols + (c ^ dc)))
        return lax.ppermute(value, AXES, pairs)


def pack_own(points, coeffs, metric):
    rows, width = points.shape
    norm = jnp.sum(points * dot(points, metric), axis=1)
    vals = jnp.concatenate([coeffs.T, norm[None, :]], axis=0)
    aux = jnp.pad(vals, ((0, 8 - vals.shape[0]), (0, width - rows)))
    return jnp.concatenate([points, aux], axis=0)


def tile_terms(query_x, metric, centers, coef, norm):
    query_y = dot(query_x, metric)
    query_n = jnp.sum(query_x * query_y, axis=1)
    cross = dot(query_y, centers, (((1,), (1,)), ((), ())))
    dist_sq = query_n[:, None] + norm[None, :] - 2.0 * cross
    distance = jnp.sqrt(jnp.maximum(dist_sq, 0.0))
    weights = jnp.exp(-distance) / jnp.maximum(distance, 0.5)
    low = centers.astype(jnp.bfloat16)
    parts = []
    for c in range(coef.shape[0]):
        scaled = weights * coef[c][None, :]
        sums = jnp.sum(scaled, axis=1)
        center_sums = jnp.dot(scaled.astype(jnp.bfloat16), low, preferred_element_type=jnp.float32)
        parts.append(sums[:, None] * query_x - center_sums)
    return jnp.concatenate(parts, axis=0)


def make_local(rows_all, cols_all):
    hop = Hops(rows_all, cols_all)
    row_bits = bits_of(rows_all)
    col_bits = bits_of(cols_all)
    bit_a, bit_b = row_bits[0], row_bits[1]
    line_bits = row_bits[2:]

    def gather_centers(block):
        have = [block]
        for bit in reversed(line_bits):
            have = have + [hop(piece, (bit, 0)) for piece in have]
        both = jnp.stack(have)
        for bit in col_bits:
            both = jnp.concatenate([both, hop(both, (0, bit))], axis=0)
        return both

    def local(points, coeffs, metric):
        own, width = points.shape
        outs_n = coeffs.shape[1]
        block = pack_own(points, coeffs, metric)
        got_a = hop(points, (bit_a, 0), (bit_b, 0))
        got_b = hop(jnp.concatenate([points, got_a], axis=0), (bit_b, 0), (bit_a, 0))
        held = gather_centers(block)
        count = held.shape[0]
        centers = held[:, :own].reshape(count * own, width)
        aux = held[:, own : own + outs_n + 1, :own].transpose(1, 0, 2).reshape(outs_n + 1, count * own)
        coef, norm = aux[:outs_n], aux[outs_n]

        away = jnp.concatenate([got_a, got_b[own:]], axis=0)
        home = jnp.concatenate([points, got_b[:own]], axis=0)
        sent = hop(tile_terms(away, metric, centers, coef, norm), (bit_a, 0), (bit_b, 0))
        total = (tile_terms(home, metric, centers, coef, norm) + sent).reshape(outs_n, 2, own, width)
        part = total[:, 0] + hop(total[:, 1], (bit_b, 0), (bit_a, 0))

        grads = dot(part.reshape(outs_n * own, width), metric)
        outer = dot(grads, grads, (((0,), (0,)), ((), ())))

        tile = 128 if width % 128 == 0 else width
        span = width // tile
        upper = [(i, j) for i in range(span) for j in range(i, span)]
        blocks = [outer[i * tile : (i + 1) * tile, j * tile : (j + 1) * tile] for i, j in upper]
        if len(blocks) % 2:
            blocks.append(jnp.zeros((tile, tile), jnp.float32))
        half = len(blocks) // 2
        first, second = jnp.stack(blocks[:half]), jnp.stack(blocks[half:])
        odd = (lax.axis_index("col") & 1) == 1
        keep = jnp.where(odd, second, first) + hop(jnp.where(odd, first, second), (0, 1))
        rest = [(bit, 0) for bit in row_bits]
        turn = len(rest) // 2
        for even_hop, odd_hop in zip(rest, rest[turn:] + rest[:turn]):
            keep = keep + hop(keep, even_hop, odd_hop)
        for bit in col_bits[1:]:
            keep = keep + hop(keep, (0, bit))
        other = hop(keep, (0, 1))
        first, second = jnp.where(odd, other, keep), jnp.where(odd, keep, other)
        final = dict(zip(upper, [first[k] for k in range(half)] + [second[k] for k in range(half)]))
        outer = jnp.concatenate(
            [
                jnp.concatenate([final[i, j] if i <= j else final[j, i].T for j in range(span)], axis=1)
                for i in range(span)
            ],
            axis=0,
        )
        metric_next = outer * (width / jnp.trace(outer))
        transformed = dot(points, metric_next)
        return (metric_next, transformed)

    return local


def solution(mesh):
    return jax.shard_map(
        make_local(mesh.shape["row"], mesh.shape["col"]),
        mesh=mesh,
        in_specs=(P(AXES, None), P(AXES, None), P()),
        out_specs=(P(), P(AXES, None)),
        check_vma=False,
    )
```

time: 250 us -> 75 us (0.30)
  waiting for transfers between devices: 138 us -> 44.2 us
  blocking collectives: 81.4 us -> 0 us
  starting transfers between devices: 0.12 us -> 14.6 us
  between operations: 15.2 us -> 1.71 us
    psum x1 -> x0, waiting for transfers between devices: 132 us -> none  [local(): outer = lax.psum(outer_local, ('row', 'col'))]
    all_gather x2 -> x0, blocking collectives: 44.8 us -> none  [the longest x1 42.7 us: local(): lax.all_gather(coeffs, 'row', axis=0, tiled=True)]
    ppermute x0 -> x14, waiting for transfers between devices: none -> 44.2 us  [__call__(): return lax.ppermute(value, AXES, pairs)]
    unnamed x1 -> x0, blocking collectives: 36.6 us -> none
    ppermute x0 -> x14, starting transfers between devices: none -> 14.6 us  [__call__(): return lax.ppermute(value, AXES, pairs)]
    reduce_scatter x1 -> x0, waiting for transfers between devices: 5.7 us -> none  [local(): lax.psum_scatter(partial_value, 'col', scatter_dimension=0, tiled=True)]
    dot_general x10 -> x12, matrix products: 9.19 us -> 8.68 us  [the longest x8 7.72 us: dot(): lax.dot_general(a, b, dims, precision=HIGH, preferred_element_type=jnp.fl...]
  transfers between devices with their start and end apart: 3 -> 14, of which waited for: 2 -> 11; matrix products, arithmetic and copies ran while one was open for 1% -> 3% of each run, Pallas kernels for 0% -> 0%
where the time goes in v1:
time: 75 us; the launch traced here: 74.8 us
  waiting for transfers between devices  44.2 us (59%)
  starting transfers between devices  14.6 us (19%)
  matrix products  8.68 us (12%)
  local copies, waits for them, and re-layouts  4.4 us (6%)
  between operations  1.71 us (2%)
  other arithmetic  1.2 us (2%)
    ppermute x14, waiting for transfers between devices, __call__(): return lax.ppermute(value, AXES, pairs)  44.2 us
    ppermute x14, starting transfers between devices, __call__(): return lax.ppermute(value, AXES, pairs)  14.6 us
    dot_general x8, matrix products, dot(): lax.dot_general(a, b, dims, precision=HIGH, preferred_element_type=jnp.fl...  7.72 us
    unnamed x13, local copies, waits for them, and re-layouts  3.09 us
  transfers between devices with their start and end apart: 14, of which 11 were waited for; matrix products, arithmetic and copies ran while one was open for 3% of the time, Pallas kernels for 0%

profile of v1, /device:TPU:0, one launch (start us, length us, event | category | flops | bytes accessed | tf_op | source)
XLA Modules:
  0.0 74.8 jit_solution(4477582970794495001)
XLA Ops:
  0.6 0.0 copy-start
  0.6 0.0 copy-start.1
  0.7 1.0 %copy-done = f32[384,384]{1,0:T(8,128)S(1)} copy-done((f32[384,384]{1,0:T(8,128)S(1)}, f32[384,384]{1,0:T(8,128)}, u32[]{:S(2)}) %copy-start) | copy-done | bytes 589848
  1.7 1.5 %fusion.6 = f32[64]{0:T(128)S(1)} fusion(f32[64,384]{1,0:T(8,128)} %param.3, f32[384,384]{1,0:T(8,128)S(1)} %copy-done), kind=kOutput, calls=%fused_computation.10 | convolution fusion | flops 113295296 | bytes 688384 | tf_op jit(solution)/shard_map/dot_general | solution.py:11
  3.2 0.0 copy-start.2
  3.2 0.7 copy-done.2
  3.9 0.0 copy-done.1
  4.0 4.1 %collective-permute-start.2 = (f32[72,384]{1,0:T(8,128)S(1)}, f32[72,384]{1,0:T(8,128)S(1)}, u32[]{:S(2)}, u32[]{:S(2)}) collective-permute-start(f32[72,384]{1,0:T(8,128)S(1)} %get-tuple-element.33), channel_id=1, source_target_pairs={{0,16},{1,17},{2,18},{3,19},{4,20},{5,21},{6,22},{7,23},{8,24},{9,... | collective-permute-start | bytes 331784 | tf_op jit(solution)/shard_map/ppermute | solution.py:30
  8.1 1.6 %collective-permute-start.3 = (f32[72,384]{1,0:T(8,128)S(1)}, f32[72,384]{1,0:T(8,128)S(1)}, u32[]{:S(2)}, u32[]{:S(2)}) collective-permute-start(f32[72,384]{1,0:T(8,128)S(1)} %get-tuple-element.33), channel_id=1, source_target_pairs={{0,8},{1,9},{2,10},{3,11},{4,12},{5,13},{6,14},{7,15},{8,0},{9,1},... | collective-permute-start | bytes 331784 | tf_op jit(solution)/shard_map/ppermute | solution.py:30
  9.6 1.5 %collective-permute-start = (f32[64,384]{1,0:T(8,128)S(1)}, f32[64,384]{1,0:T(8,128)S(1)}, u32[]{:S(2)}, u32[]{:S(2)}) collective-permute-start(f32[64,384]{1,0:T(8,128)S(1)} %copy-done.1), channel_id=1, source_target_pairs={{0,2},{1,5},{2,0},{3,7},{4,6},{5,1},{6,4},{7,3},{8,10},{9,13},{10,... | collective-permute-start | bytes 294920 | tf_op jit(solution)/shard_map/ppermute | solution.py:30
  11.1 3.1 %collective-permute-done = f32[64,384]{1,0:T(8,128)S(1)} collective-permute-done((f32[64,384]{1,0:T(8,128)S(1)}, f32[64,384]{1,0:T(8,128)S(1)}, u32[]{:S(2)}, u32[]{:S(2)}) %collective-permute-start) | collective-permute-done | bytes 98336 | tf_op jit(solution)/shard_map/ppermute | solution.py:30
  14.3 1.6 %collective-permute-start.1 = (f32[128,384]{1,0:T(8,128)S(1)}, f32[128,384]{1,0:T(8,128)S(1)}, u32[]{:S(2)}, u32[]{:S(2)}) collective-permute-start(f32[128,384]{1,0:T(8,128)S(1)} %pad_maximum_fusion.2), channel_id=1, source_target_pairs={{0,4},{1,3},{2,6},{3,1},{4,0},{5,7},{6,2},{7,5},{8,12},{9,11},{10,... | collective-permute-start | bytes 589832 | tf_op jit(solution)/shard_map/ppermute | solution.py:30
  15.9 0.0 collective-permute-done.2
  15.9 0.4 collective-permute-start.4
  16.3 0.0 collective-permute-done.3
  16.4 4.3 %collective-permute-done.4 = f32[72,384]{1,0:T(8,128)S(1)} collective-permute-done((f32[72,384]{1,0:T(8,128)S(1)}, f32[72,384]{1,0:T(8,128)S(1)}, u32[]{:S(2)}, u32[]{:S(2)}) %collective-permute-start.4) | collective-permute-done | bytes 110624 | tf_op jit(solution)/shard_map/ppermute | solution.py:30
  20.7 0.1 collective-permute-start.5
  20.8 0.0 collective-permute-done.1
  20.8 0.7 multiply_reduce_fusion.5
  21.4 0.7 multiply_reduce_fusion.4
  22.1 0.4 collective-permute-done.5
  22.5 0.1 slice.96
  22.7 0.1 mul.88
  22.8 0.1 mul.93
  22.9 0.1 add.50
  22.9 1.0 %maximum_divide_fusion.1 = f32[128,512]{1,0:T(8,128)S(1)} fusion(f32[128,384]{1,0:T(8,128)S(1)} %get-tuple-element.37, f32[512,384]{1,0:T(8,128)S(1)} %bitcast.75, f32[512]{0:T(512)S(1)} %add.50, f32[128]{0:T(128)S(1)} %get-tuple-element.36), kind=kOutput, calls=%fused_computation.19 | convolution fusion | flops 302448640 | bytes 1247744 | tf_op jit(solution)/shard_map/dot_general | solution.py:11
  24.0 1.2 %multiply_reduce_fusion.1 = (f32[128]{0:T(128)S(1)}, f32[128]{0:T(128)S(1)}, f32[128]{0:T(128)S(1)}, f32[128]{0:T(128)S(1)}, f32[128,512]{1,0:T(8,128)S(1)}) fusion(f32[512]{0:T(512)S(1)} %mul.88, f32[512]{0:T(512)S(1)} %mul.93, f32[128,512]{1,0:T(8,128)S(1)} %maximum_divide_fusion.1, f32[128,384]{1,0:T(8,128)S(1)} %get-tuple-element.35, ...), kind=kOutput, calls=%fused_computation.23 | convolution fusion | flops 302972416 | bytes 1516032 | tf_op jit(solution)/shard_map/dot_general | solution.py:11
  25.2 0.2 multiply_subtract_fusion
  25.5 0.2 multiply_subtract_fusion.1
  25.7 1.6 %collective-permute-start.6 = (f32[256,384]{1,0:T(8,128)S(1)}, f32[256,384]{1,0:T(8,128)S(1)}, u32[]{:S(2)}, u32[]{:S(2)}) collective-permute-start(f32[256,384]{1,0:T(8,128)S(1)} %pad_maximum_fusion.1), channel_id=1, source_target_pairs={{0,2},{1,5},{2,0},{3,7},{4,6},{5,1},{6,4},{7,3},{8,10},{9,13},{10,... | collective-permute-start | bytes 1179656 | tf_op jit(solution)/shard_map/ppermute | solution.py:30
  27.3 0.2 multiply_subtract_fusion.2
  27.5 0.2 multiply_subtract_fusion.3
  27.8 5.8 %collective-permute-done.6 = f32[256,384]{1,0:T(8,128)S(1)} collective-permute-done((f32[256,384]{1,0:T(8,128)S(1)}, f32[256,384]{1,0:T(8,128)S(1)}, u32[]{:S(2)}, u32[]{:S(2)}) %collective-permute-start.6) | collective-permute-done | bytes 393248 | tf_op jit(solution)/shard_map/ppermute | solution.py:30
  33.7 0.6 collective-permute-start.7
  34.2 5.2 %collective-permute-done.7 = f32[2,64,384]{2,1,0:T(8,128)S(1)} collective-permute-done((f32[2,64,384]{2,1,0:T(8,128)S(1)}, f32[2,64,384]{2,1,0:T(8,128)S(1)}, u32[]{:S(2)}, u32[]{:S(2)}) %collective-permute-start.7) | collective-permute-done | bytes 196640 | tf_op jit(solution)/shard_map/ppermute | solution.py:30
  39.4 0.6 fusion.23
  40.0 0.7 fusion.24
  40.7 0.1 copy.23
  40.8 0.1 copy.22
  40.9 0.1 copy.21
  41.0 0.1 copy.11
  41.2 0.1 copy.9
  41.3 0.1 collective-permute-start.8
  41.4 0.1 copy.12
  41.6 1.3 %collective-permute-done.8 = f32[3,128,128]{1,2,0:T(8,128)S(1)} collective-permute-done((f32[3,128,128]{1,2,0:T(8,128)S(1)}, f32[3,128,128]{1,2,0:T(8,128)S(1)}, u32[]{:S(2)}, u32[]{:S(2)}) %collective-permute-start.8) | collective-permute-done | bytes 196640 | tf_op jit(solution)/shard_map/ppermute | solution.py:30
  42.9 1.6 %collective-permute-start.9 = (f32[3,128,128]{1,2,0:T(8,128)S(1)}, f32[3,128,128]{1,2,0:T(8,128)S(1)}, u32[]{:S(2)}, u32[]{:S(2)}) collective-permute-start(f32[3,128,128]{1,2,0:T(8,128)S(1)} %add.57), channel_id=1, source_target_pairs={{0,2},{1,9},{2,0},{3,11},{4,6},{5,13},{6,4},{7,15},{8,10},{9,1},{1... | collective-permute-start | bytes 589832 | tf_op jit(solution)/shard_map/ppermute | solution.py:30
  44.4 4.2 %collective-permute-done.9 = f32[3,128,128]{1,2,0:T(8,128)S(1)} collective-permute-done((f32[3,128,128]{1,2,0:T(8,128)S(1)}, f32[3,128,128]{1,2,0:T(8,128)S(1)}, u32[]{:S(2)}, u32[]{:S(2)}) %collective-permute-start.9) | collective-permute-done | bytes 196640 | tf_op jit(solution)/shard_map/ppermute | solution.py:30
  48.6 0.6 collective-permute-start.10
  49.2 5.2 %collective-permute-done.10 = f32[3,128,128]{1,2,0:T(8,128)S(1)} collective-permute-done((f32[3,128,128]{1,2,0:T(8,128)S(1)}, f32[3,128,128]{1,2,0:T(8,128)S(1)}, u32[]{:S(2)}, u32[]{:S(2)}) %collective-permute-start.10) | collective-permute-done | bytes 196640 | tf_op jit(solution)/shard_map/ppermute | solution.py:30
  54.4 0.5 collective-permute-start.11
  54.9 5.2 %collective-permute-done.11 = f32[3,128,128]{1,2,0:T(8,128)S(1)} collective-permute-done((f32[3,128,128]{1,2,0:T(8,128)S(1)}, f32[3,128,128]{1,2,0:T(8,128)S(1)}, u32[]{:S(2)}, u32[]{:S(2)}) %collective-permute-start.11) | collective-permute-done | bytes 196640 | tf_op jit(solution)/shard_map/ppermute | solution.py:30
  60.1 0.4 collective-permute-start.12
  60.5 8.2 %collective-permute-done.12 = f32[3,128,128]{1,2,0:T(8,128)S(1)} collective-permute-done((f32[3,128,128]{1,2,0:T(8,128)S(1)}, f32[3,128,128]{1,2,0:T(8,128)S(1)}, u32[]{:S(2)}, u32[]{:S(2)}) %collective-permute-start.12) | collective-permute-done | bytes 196640 | tf_op jit(solution)/shard_map/ppermute | solution.py:30
  68.8 0.1 copy.13
  68.9 0.1 collective-permute-start.13
  69.0 1.4 %collective-permute-done.13 = f32[3,128,128]{2,1,0:T(8,128)S(1)} collective-permute-done((f32[3,128,128]{2,1,0:T(8,128)S(1)}, f32[3,128,128]{2,1,0:T(8,128)S(1)}, u32[]{:S(2)}, u32[]{:S(2)}) %collective-permute-start.13) | collective-permute-done | bytes 196640 | tf_op jit(solution)/shard_map/ppermute | solution.py:30
  70.4 0.1 copy.16
  70.6 0.1 copy.17
  70.8 0.1 copy.18
  70.9 0.7 select_reduce_fusion
  72.3 1.1 %copy.19 = f32[384,384]{1,0:T(8,128)} copy(f32[384,384]{0,1:T(8,128)S(1)} %broadcast_multiply_fusion) | data formatting | bytes 1179648
  73.4 1.4 %convolution_bitcast_fusion = f32[64,384]{1,0:T(8,128)} fusion(f32[384,384]{0,1:T(8,128)S(1)} %broadcast_multiply_fusion, f32[64,384]{1,0:T(8,128)S(1)} %copy-done.1), kind=kOutput, calls=%fused_computation.9 | convolution fusion | flops 113246208 | bytes 786432 | tf_op jit(solution)/shard_map/dot_general | solution.py:11
  (32 shorter events, 0.7 us)
Async XLA Ops:
  0.6 1.1 %copy-start = (f32[384,384]{1,0:T(8,128)S(1)}, f32[384,384]{1,0:T(8,128)}, u32[]{:S(2)}) copy-start(f32[384,384]{1,0:T(8,128)} %param.5) | copy-start | bytes 1769476
  0.6 3.3 %copy-start.1 = (f32[64,384]{1,0:T(8,128)S(1)}, f32[64,384]{1,0:T(8,128)}, u32[]{:S(2)}) copy-start(f32[64,384]{1,0:T(8,128)} %param.3) | copy-start | bytes 294916
  3.2 0.7 copy-start.2
  4.0 11.9 %collective-permute-start.2 = (f32[72,384]{1,0:T(8,128)S(1)}, f32[72,384]{1,0:T(8,128)S(1)}, u32[]{:S(2)}, u32[]{:S(2)}) collective-permute-start(f32[72,384]{1,0:T(8,128)S(1)} %get-tuple-element.33), channel_id=1, source_target_pairs={{0,16},{1,17},{2,18},{3,19},{4,20},{5,21},{6,22},{7,23},{8,24},{9,... | collective-permute-start | bytes 331784 | tf_op jit(solution)/shard_map/ppermute | solution.py:30
  8.1 8.3 %collective-permute-start.3 = (f32[72,384]{1,0:T(8,128)S(1)}, f32[72,384]{1,0:T(8,128)S(1)}, u32[]{:S(2)}, u32[]{:S(2)}) collective-permute-start(f32[72,384]{1,0:T(8,128)S(1)} %get-tuple-element.33), channel_id=1, source_target_pairs={{0,8},{1,9},{2,10},{3,11},{4,12},{5,13},{6,14},{7,15},{8,0},{9,1},... | collective-permute-start | bytes 331784 | tf_op jit(solution)/shard_map/ppermute | solution.py:30
  9.6 4.6 %collective-permute-start = (f32[64,384]{1,0:T(8,128)S(1)}, f32[64,384]{1,0:T(8,128)S(1)}, u32[]{:S(2)}, u32[]{:S(2)}) collective-permute-start(f32[64,384]{1,0:T(8,128)S(1)} %copy-done.1), channel_id=1, source_target_pairs={{0,2},{1,5},{2,0},{3,7},{4,6},{5,1},{6,4},{7,3},{8,10},{9,13},{10,... | collective-permute-start | bytes 294920 | tf_op jit(solution)/shard_map/ppermute | solution.py:30
  14.3 6.5 %collective-permute-start.1 = (f32[128,384]{1,0:T(8,128)S(1)}, f32[128,384]{1,0:T(8,128)S(1)}, u32[]{:S(2)}, u32[]{:S(2)}) collective-permute-start(f32[128,384]{1,0:T(8,128)S(1)} %pad_maximum_fusion.2), channel_id=1, source_target_pairs={{0,4},{1,3},{2,6},{3,1},{4,0},{5,7},{6,2},{7,5},{8,12},{9,11},{10,... | collective-permute-start | bytes 589832 | tf_op jit(solution)/shard_map/ppermute | solution.py:30
  15.9 4.7 %collective-permute-start.4 = (f32[72,384]{1,0:T(8,128)S(1)}, f32[72,384]{1,0:T(8,128)S(1)}, u32[]{:S(2)}, u32[]{:S(2)}) collective-permute-start(f32[72,384]{1,0:T(8,128)S(1)} %collective-permute-done.2), channel_id=1, source_target_pairs={{0,8},{1,9},{2,10},{3,11},{4,12},{5,13},{6,14},{7,15},{8,0},{9,1},... | collective-permute-start | bytes 331784 | tf_op jit(solution)/shard_map/ppermute | solution.py:30
  20.7 1.9 %collective-permute-start.5 = (f32[4,72,384]{2,1,0:T(8,128)S(1)}, f32[4,72,384]{2,1,0:T(8,128)S(1)}, u32[]{:S(2)}, u32[]{:S(2)}) collective-permute-start(f32[4,72,384]{2,1,0:T(8,128)S(1)} %pad_maximum_fusion), channel_id=1, source_target_pairs={{0,1},{1,0},{2,3},{3,2},{4,5},{5,4},{6,7},{7,6},{8,9},{9,8},{10,11... | collective-permute-start | bytes 1327112 | tf_op jit(solution)/shard_map/ppermute | solution.py:30
  25.7 7.8 %collective-permute-start.6 = (f32[256,384]{1,0:T(8,128)S(1)}, f32[256,384]{1,0:T(8,128)S(1)}, u32[]{:S(2)}, u32[]{:S(2)}) collective-permute-start(f32[256,384]{1,0:T(8,128)S(1)} %pad_maximum_fusion.1), channel_id=1, source_target_pairs={{0,2},{1,5},{2,0},{3,7},{4,6},{5,1},{6,4},{7,3},{8,10},{9,13},{10,... | collective-permute-start | bytes 1179656 | tf_op jit(solution)/shard_map/ppermute | solution.py:30
  33.7 5.7 %collective-permute-start.7 = (f32[2,64,384]{2,1,0:T(8,128)S(1)}, f32[2,64,384]{2,1,0:T(8,128)S(1)}, u32[]{:S(2)}, u32[]{:S(2)}) collective-permute-start(f32[2,64,384]{2,1,0:T(8,128)S(1)} %slice_bitcast_fusion), channel_id=1, source_target_pairs={{0,4},{1,3},{2,6},{3,1},{4,0},{5,7},{6,2},{7,5},{8,12},{9,11},{10,... | collective-permute-start | bytes 589832 | tf_op jit(solution)/shard_map/ppermute | solution.py:30
  41.3 1.5 %collective-permute-start.8 = (f32[3,128,128]{1,2,0:T(8,128)S(1)}, f32[3,128,128]{1,2,0:T(8,128)S(1)}, u32[]{:S(2)}, u32[]{:S(2)}) collective-permute-start(f32[3,128,128]{1,2,0:T(8,128)S(1)} %get-tuple-element.28), channel_id=1, source_target_pairs={{0,1},{1,0},{2,3},{3,2},{4,5},{5,4},{6,7},{7,6},{8,9},{9,8},{10,11... | collective-permute-start | bytes 589832 | tf_op jit(solution)/shard_map/ppermute | solution.py:30
  42.9 5.7 %collective-permute-start.9 = (f32[3,128,128]{1,2,0:T(8,128)S(1)}, f32[3,128,128]{1,2,0:T(8,128)S(1)}, u32[]{:S(2)}, u32[]{:S(2)}) collective-permute-start(f32[3,128,128]{1,2,0:T(8,128)S(1)} %add.57), channel_id=1, source_target_pairs={{0,2},{1,9},{2,0},{3,11},{4,6},{5,13},{6,4},{7,15},{8,10},{9,1},{1... | collective-permute-start | bytes 589832 | tf_op jit(solution)/shard_map/ppermute | solution.py:30
  48.6 5.7 %collective-permute-start.10 = (f32[3,128,128]{1,2,0:T(8,128)S(1)}, f32[3,128,128]{1,2,0:T(8,128)S(1)}, u32[]{:S(2)}, u32[]{:S(2)}) collective-permute-start(f32[3,128,128]{1,2,0:T(8,128)S(1)} %add.58), channel_id=1, source_target_pairs={{0,4},{1,17},{2,6},{3,19},{4,0},{5,21},{6,2},{7,23},{8,12},{9,25},... | collective-permute-start | bytes 589832 | tf_op jit(solution)/shard_map/ppermute | solution.py:30
  54.4 5.7 %collective-permute-start.11 = (f32[3,128,128]{1,2,0:T(8,128)S(1)}, f32[3,128,128]{1,2,0:T(8,128)S(1)}, u32[]{:S(2)}, u32[]{:S(2)}) collective-permute-start(f32[3,128,128]{1,2,0:T(8,128)S(1)} %add.59), channel_id=1, source_target_pairs={{0,8},{1,3},{2,10},{3,1},{4,12},{5,7},{6,14},{7,5},{8,0},{9,11},{1... | collective-permute-start | bytes 589832 | tf_op jit(solution)/shard_map/ppermute | solution.py:30
  60.1 8.6 %collective-permute-start.12 = (f32[3,128,128]{1,2,0:T(8,128)S(1)}, f32[3,128,128]{1,2,0:T(8,128)S(1)}, u32[]{:S(2)}, u32[]{:S(2)}) collective-permute-start(f32[3,128,128]{1,2,0:T(8,128)S(1)} %add.60), channel_id=1, source_target_pairs={{0,16},{1,5},{2,18},{3,7},{4,20},{5,1},{6,22},{7,3},{8,24},{9,13},... | collective-permute-start | bytes 589832 | tf_op jit(solution)/shard_map/ppermute | solution.py:30
  68.9 1.5 %collective-permute-start.13 = (f32[3,128,128]{2,1,0:T(8,128)S(1)}, f32[3,128,128]{2,1,0:T(8,128)S(1)}, u32[]{:S(2)}, u32[]{:S(2)}) collective-permute-start(f32[3,128,128]{2,1,0:T(8,128)S(1)} %copy.13), channel_id=1, source_target_pairs={{0,1},{1,0},{2,3},{3,2},{4,5},{5,4},{6,7},{7,6},{8,9},{9,8},{10,11... | collective-permute-start | bytes 589832 | tf_op jit(solution)/shard_map/ppermute | solution.py:30

commit v2 on v1

v2 whole, which is shorter than its diff:
```python
import jax
import jax.numpy as jnp
from jax import lax
from jax.experimental import pallas as pl
from jax.experimental.pallas import tpu as pltpu
from jax.sharding import PartitionSpec as P

HIGH = lax.Precision.HIGHEST
AXES = ("row", "col")
EXTRA = 8


def dot(a, b, dims=(((1,), (0,)), ((), ()))):
    return lax.dot_general(a, b, dims, precision=HIGH, preferred_element_type=jnp.float32)


def bits_of(count):
    assert count & (count - 1) == 0
    return [1 << b for b in range(count.bit_length() - 1)]


def make_hop(rows, cols):
    def hop(value, even, odd=None):
        odd = even if odd is None else odd
        pairs = []
        for r in range(rows):
            for c in range(cols):
                dr, dc = odd if c & 1 else even
                pairs.append((r * cols + c, (r ^ dr) * cols + (c ^ dc)))
        return lax.ppermute(value, AXES, pairs)

    return hop


def call(body, out_shape, args, flops):
    moved = sum(4 * a.size for a in args) + sum(4 * s.size for s in jax.tree.leaves(out_shape))
    return pl.pallas_call(
        body,
        out_shape=out_shape,
        in_specs=[pl.BlockSpec(memory_space=pltpu.VMEM)] * len(args),
        out_specs=jax.tree.map(lambda _: pl.BlockSpec(memory_space=pltpu.VMEM), out_shape),
        compiler_params=pltpu.CompilerParams(vmem_limit_bytes=40 * 1024 * 1024),
        cost_estimate=pl.CostEstimate(flops=flops, bytes_accessed=moved, transcendentals=0),
    )(*args)


def shape(*dims):
    return jax.ShapeDtypeStruct(dims, jnp.float32)


def pack_own(points, coeffs):
    rows, width = points.shape
    cols = coeffs.T
    aux = jnp.concatenate([cols, cols], axis=1)
    aux = jnp.pad(aux, ((0, EXTRA - cols.shape[0]), (0, width - 2 * rows)))
    return jnp.concatenate([points, aux], axis=0)


def center_terms(refs, metric, own, outs_n):
    pieces, coefs = [], []
    for ref in refs:
        for k in range(ref.shape[0] // (own + EXTRA)):
            first = k * (own + EXTRA)
            pieces.append(ref[first : first + own, :])
            coefs.append(ref[first + own : first + own + EXTRA, 0 : 2 * own])
    centers = jnp.concatenate(pieces, axis=0)
    ones = jnp.ones((8, centers.shape[1]), jnp.float32)
    norm = dot(ones, centers * dot(centers, metric), (((1,), (1,)), ((), ())))[0:1]
    lane = lax.broadcasted_iota(jnp.int32, coefs[0].shape, 1)
    merged = [jnp.where(lane < own, coefs[k], coefs[k + 1]) for k in range(0, len(coefs), 2)]
    coef = jnp.concatenate(merged, axis=1)
    return centers, norm, [coef[c : c + 1] for c in range(outs_n)]


def query_sums(query_x, query_y, centers, norm, coefs):
    query_n = jnp.sum(query_x * query_y, axis=1, keepdims=True)
    cross = dot(query_y, centers, (((1,), (1,)), ((), ())))
    distance = jnp.sqrt(jnp.maximum(query_n + norm - 2.0 * cross, 0.0))
    weights = jnp.exp(-distance) / jnp.maximum(distance, 0.5)
    low = centers.astype(jnp.bfloat16)
    parts = []
    for coef in coefs:
        scaled = weights * coef
        sums = jnp.sum(scaled, axis=1, keepdims=True)
        center_sums = jnp.dot(scaled.astype(jnp.bfloat16), low, preferred_element_type=jnp.float32)
        parts.append(sums * query_x - center_sums)
    return parts


def early_sums(queries, blocks, metric, outs_n):
    own, width = queries[0].shape
    count = len(queries)

    def body(*refs):
        query_refs, block_refs = refs[:count], refs[count : count + len(blocks)]
        metric_ref, total_ref, mapped_ref = refs[count + len(blocks) :]
        query_x = jnp.concatenate([ref[...] for ref in query_refs], axis=0)
        query_y = dot(query_x, metric_ref[...])
        mapped_ref[...] = query_y
        for k in range(0, len(blocks), 2):
            parts = query_sums(query_x, query_y, *center_terms(block_refs[k : k + 2], metric_ref[...], own, outs_n))
            for c in range(outs_n):
                if k == 0:
                    total_ref[c] = parts[c]
                else:
                    total_ref[c] = total_ref[c] + parts[c]

    args = list(queries) + list(blocks) + [metric]
    centers = sum(b.shape[0] for b in blocks)
    flops = 12 * (count * own + centers) * width * width + 12 * count * own * centers * width
    return call(body, (shape(outs_n, count * own, width), shape(count * own, width)), args, flops)


def late_sums(queries, first, total, mapped, blocks, metric, outs_n):
    own, width = queries[0].shape
    count = len(queries)

    def body(*refs):
        query_refs, block_refs = refs[:count], refs[count : count + len(blocks)]
        metric_ref, total_ref, mapped_ref = refs[count + len(blocks) : count + len(blocks) + 3]
        out_refs = refs[count + len(blocks) + 3 :]
        rows = slice(first * own, (first + count) * own)
        query_x = jnp.concatenate([ref[...] for ref in query_refs], axis=0)
        query_y = mapped_ref[rows, :]
        sums = [total_ref[c, rows, :] for c in range(outs_n)]
        for k in range(0, len(blocks), 2):
            parts = query_sums(query_x, query_y, *center_terms(block_refs[k : k + 2], metric_ref[...], own, outs_n))
            sums = [a + b for a, b in zip(sums, parts)]
        for q in range(count):
            for c in range(outs_n):
                out_refs[q][c * own : (c + 1) * own, :] = sums[c][q * own : (q + 1) * own, :]

    args = list(queries) + list(blocks) + [metric, total, mapped]
    centers = sum(b.shape[0] for b in blocks)
    flops = 12 * centers * width * width + 12 * count * own * centers * width
    return call(body, tuple(shape(outs_n * own, width) for _ in queries), args, flops)


def upper_tiles(width):
    tile = 128 if width % 128 == 0 else width
    span = width // tile
    return tile, span, [(i, j) for i in range(span) for j in range(i, span)]


def outer_halves(part, arrived, metric):
    width = part.shape[1]
    tile, span, upper = upper_tiles(width)
    half = (len(upper) + 1) // 2

    def body(part_ref, arrived_ref, metric_ref, keep_ref, send_ref):
        odd = (lax.axis_index("col") & 1) == 1
        grads = dot(part_ref[...] + arrived_ref[...], metric_ref[...])
        tiles = [[] for _ in upper]
        for i in range(span):
            slab = dot(grads[:, i * tile : (i + 1) * tile], grads[:, i * tile :], (((0,), (0,)), ((), ())))
            for j in range(i, span):
                tiles[upper.index((i, j))] = slab[:, (j - i) * tile : (j - i + 1) * tile]
        while len(tiles) < 2 * half:
            tiles.append(jnp.zeros((tile, tile), jnp.float32))
        for k in range(half):
            keep_ref[k * tile : (k + 1) * tile, :] = jnp.where(odd, tiles[half + k], tiles[k])
            send_ref[k * tile : (k + 1) * tile, :] = jnp.where(odd, tiles[k], tiles[half + k])

    out = shape(half * tile, tile)
    return call(body, (out, out), [part, arrived, metric], 24 * part.shape[0] * width * width)


def finish(keep, other, points):
    rows, width = points.shape
    tile, span, upper = upper_tiles(width)
    half = (len(upper) + 1) // 2

    def body(keep_ref, other_ref, points_ref, next_ref, mapped_ref):
        odd = (lax.axis_index("col") & 1) == 1
        kept = [keep_ref[k * tile : (k + 1) * tile, :] for k in range(half)]
        came = [other_ref[k * tile : (k + 1) * tile, :] for k in range(half)]
        tiles = [jnp.where(odd, b, a) for a, b in zip(kept, came)]
        tiles += [jnp.where(odd, a, b) for a, b in zip(kept, came)]
        final = dict(zip(upper, tiles))
        diag = final[0, 0]
        for i in range(1, span):
            diag = diag + final[i, i]
        eye = lax.broadcasted_iota(jnp.int32, diag.shape, 0) == lax.broadcasted_iota(jnp.int32, diag.shape, 1)
        trace = jnp.sum(jnp.where(eye, diag, 0.0), keepdims=True)
        scale = width / trace
        for i, j in upper:
            value = final[i, j] * scale
            next_ref[i * tile : (i + 1) * tile, j * tile : (j + 1) * tile] = value
            if i != j:
                next_ref[j * tile : (j + 1) * tile, i * tile : (i + 1) * tile] = value.T
        mapped_ref[...] = dot(points_ref[...], next_ref[...])

    return call(body, (shape(width, width), shape(rows, width)), [keep, other, points], 12 * rows * width * width)


def make_local(rows_all, cols_all):
    hop = make_hop(rows_all, cols_all)
    row_bits = bits_of(rows_all)
    col_bits = bits_of(cols_all)
    bit_a, bit_b = row_bits[0], row_bits[1]
    line_bits = row_bits[2:]

    def to_a(value):
        return hop(value, (bit_a, 0), (bit_b, 0))

    def to_b(value):
        return hop(value, (bit_b, 0), (bit_a, 0))

    def over_cols(block):
        have = [block]
        for bit in col_bits:
            have = have + [hop(piece, (0, bit)) for piece in have]
        return have

    def local(points, coeffs, metric):
        own, width = points.shape
        outs_n = coeffs.shape[1]
        have = [pack_own(points, coeffs)]
        for bit in reversed(line_bits):
            have = have + [hop(piece, (bit, 0)) for piece in have]
        from_a = to_a(points)
        from_b = to_b(points)
        from_ab = to_b(from_a)
        early = over_cols(jnp.concatenate(have[:-1], axis=0))
        late = over_cols(have[-1])

        queries = [from_ab, from_a, from_b, points]
        total, mapped = early_sums(queries, early, metric, outs_n)
        part_ab, part_a = late_sums(queries[:2], 0, total, mapped, late, metric, outs_n)
        sent_ab, sent_a = to_a(part_ab), to_a(part_a)
        part_b, part_own = late_sums(queries[2:], 2, total, mapped, late, metric, outs_n)
        sent_b = to_b(part_b + sent_ab)

        keep, send = outer_halves(part_own + sent_a, sent_b, metric)
        keep = keep + hop(send, (0, 1))
        rest = [(bit, 0) for bit in row_bits]
        turn = len(rest) // 2
        for even_hop, odd_hop in zip(rest, rest[turn:] + rest[:turn]):
            keep = keep + hop(keep, even_hop, odd_hop)
        for bit in col_bits[1:]:
            keep = keep + hop(keep, (0, bit))
        return finish(keep, hop(keep, (0, 1)), points)

    return local


def solution(mesh):
    return jax.shard_map(
        make_local(mesh.shape["row"], mesh.shape["col"]),
        mesh=mesh,
        in_specs=(P(AXES, None), P(AXES, None), P()),
        out_specs=(P(), P(AXES, None)),
        check_vma=False,
    )
```

time: 75 us -> 72.1 us (0.961)
  starting transfers between devices: 14.6 us -> 25 us
  waiting for transfers between devices: 44.2 us -> 34.2 us
  Pallas kernels: 0 us -> 9.26 us
  matrix products: 8.68 us -> 0 us
  local copies, waits for them, and re-layouts: 4.4 us -> 0.67 us
  between operations: 1.71 us -> 0.76 us
  other arithmetic: 1.2 us -> 2.06 us
    ppermute x14 -> x17, starting transfers between devices: 14.6 us -> 25 us  [hop(): return lax.ppermute(value, AXES, pairs)]
    ppermute x14 -> x17, waiting for transfers between devices: 44.2 us -> 34.2 us  [hop(): return lax.ppermute(value, AXES, pairs)]
    pallas_call x0 -> x5, Pallas kernels: none -> 9.26 us  [call(): pl.pallas_call(body, out_shape=out_shape, in_specs=[pl.BlockSpec(memory_s...]
    dot_general x12 -> x0, matrix products: 8.68 us -> none  [the longest x8 7.72 us: dot(): lax.dot_general(a, b, dims, precision=HIGH, preferred_element_type=jnp.fl...]
    unnamed x13 -> x6, local copies, waits for them, and re-layouts: 3.09 us -> 0.67 us
    concatenate x4 -> x3, other arithmetic: 0.07 us -> 1.89 us  [the longest x1 0.92 us: local(): early = over_cols(jnp.concatenate(have[:-1], axis=0))]
  transfers between devices with their start and end apart: 14 -> 17, of which waited for: 11 -> 15; matrix products, arithmetic and copies ran while one was open for 3% -> 0% of each run, Pallas kernels for 0% -> 7%
where the time goes in v2:
time: 72.1 us; the launch traced here: 72 us
  waiting for transfers between devices  34.2 us (47%)
  starting transfers between devices  25 us (35%)
  Pallas kernels  9.26 us (13%)
  other arithmetic  2.06 us (3%)
  between operations  0.76 us (1%)
    ppermute x17, waiting for transfers between devices, hop(): return lax.ppermute(value, AXES, pairs)  34.2 us
    ppermute x17, starting transfers between devices, hop(): return lax.ppermute(value, AXES, pairs)  25 us
    pallas_call x5, Pallas kernels, call(): pl.pallas_call(body, out_shape=out_shape, in_specs=[pl.BlockSpec(memory_s...  9.26 us
  transfers between devices with their start and end apart: 17, of which 15 were waited for; matrix products, arithmetic and copies ran while one was open for 0% of the time, Pallas kernels for 7%

profile of v2, /device:TPU:0, one launch (start us, length us, event | category | flops | bytes accessed | tf_op | source)
XLA Modules:
  0.0 72.0 jit_solution(14115580392132256209)
XLA Ops:
  0.6 0.0 copy-start.2
  0.6 0.0 copy-start
  0.6 0.7 copy-done.2
  1.3 0.1 select_maximum_fusion
  1.4 0.9 %pad_maximum_fusion.1 = f32[72,384]{1,0:T(8,128)S(1)} fusion(f32[8,384]{1,0:T(8,128)S(1)} %select_maximum_fusion, f32[64,384]{1,0:T(8,128)} %points_ref.1), kind=kLoop, calls=%fused_computation.1 | loop fusion | flops 27648 | bytes 221184 | tf_op jit(solution)/shard_map/concatenate | solution.py:56
  2.3 0.0 copy-start.1
  2.3 4.1 %collective-permute-start.1 = (f32[72,384]{1,0:T(8,128)S(1)}, f32[72,384]{1,0:T(8,128)S(1)}, u32[]{:S(2)}, u32[]{:S(2)}) collective-permute-start(f32[72,384]{1,0:T(8,128)S(1)} %pad_maximum_fusion.1), channel_id=1, source_target_pairs={{0,16},{1,17},{2,18},{3,19},{4,20},{5,21},{6,22},{7,23},{8,24},{9,... | collective-permute-start | bytes 331784 | tf_op jit(solution)/shard_map/ppermute | solution.py:30
  6.4 1.6 %collective-permute-start.6 = (f32[72,384]{1,0:T(8,128)S(1)}, f32[72,384]{1,0:T(8,128)S(1)}, u32[]{:S(2)}, u32[]{:S(2)}) collective-permute-start(f32[72,384]{1,0:T(8,128)S(1)} %pad_maximum_fusion.1), channel_id=1, source_target_pairs={{0,8},{1,9},{2,10},{3,11},{4,12},{5,13},{6,14},{7,15},{8,0},{9,1},... | collective-permute-start | bytes 331784 | tf_op jit(solution)/shard_map/ppermute | solution.py:30
  8.0 4.0 %collective-permute-done.1 = f32[72,384]{1,0:T(8,128)S(1)} collective-permute-done((f32[72,384]{1,0:T(8,128)S(1)}, f32[72,384]{1,0:T(8,128)S(1)}, u32[]{:S(2)}, u32[]{:S(2)}) %collective-permute-start.1) | collective-permute-done | bytes 110624 | tf_op jit(solution)/shard_map/ppermute | solution.py:30
  11.9 0.2 collective-permute-done.6
  12.2 0.9 %pad_maximum_fusion.refs_4_ = f32[216,384]{1,0:T(8,128)S(1)} fusion(f32[72,384]{1,0:T(8,128)S(1)} %collective-permute-done.6, f32[72,384]{1,0:T(8,128)S(1)} %collective-permute-done.1, f32[8,384]{1,0:T(8,128)S(1)} %select_maximum_fusion, f32[64,384]{1,0:T(8,128)} %points_ref.1), kind=kLoop, calls=%fused_computation | loop fusion | flops 248832 | bytes 663552 | tf_op jit(solution)/shard_map/concatenate | solution.py:224
  13.1 0.1 collective-permute-start.7
  13.2 0.0 copy-done.1
  13.2 1.6 %collective-permute-start.4 = (f32[64,384]{1,0:T(8,128)S(1)}, f32[64,384]{1,0:T(8,128)S(1)}, u32[]{:S(2)}, u32[]{:S(2)}) collective-permute-start(f32[64,384]{1,0:T(8,128)S(1)} %copy-done.1), channel_id=1, source_target_pairs={{0,2},{1,5},{2,0},{3,7},{4,6},{5,1},{6,4},{7,3},{8,10},{9,13},{10,... | collective-permute-start | bytes 294920 | tf_op jit(solution)/shard_map/ppermute | solution.py:30
  14.8 1.4 %collective-permute-start.2 = (f32[72,384]{1,0:T(8,128)S(1)}, f32[72,384]{1,0:T(8,128)S(1)}, u32[]{:S(2)}, u32[]{:S(2)}) collective-permute-start(f32[72,384]{1,0:T(8,128)S(1)} %collective-permute-done.1), channel_id=1, source_target_pairs={{0,8},{1,9},{2,10},{3,11},{4,12},{5,13},{6,14},{7,15},{8,0},{9,1},... | collective-permute-start | bytes 331784 | tf_op jit(solution)/shard_map/ppermute | solution.py:30
  16.1 1.5 %collective-permute-start = (f32[64,384]{1,0:T(8,128)S(1)}, f32[64,384]{1,0:T(8,128)S(1)}, u32[]{:S(2)}, u32[]{:S(2)}) collective-permute-start(f32[64,384]{1,0:T(8,128)S(1)} %copy-done.1), channel_id=1, source_target_pairs={{0,4},{1,3},{2,6},{3,1},{4,0},{5,7},{6,2},{7,5},{8,12},{9,11},{10,... | collective-permute-start | bytes 294920 | tf_op jit(solution)/shard_map/ppermute | solution.py:30
  17.6 0.2 collective-permute-done.4.refs_1_
  17.8 1.9 %collective-permute-start.5 = (f32[64,384]{1,0:T(8,128)S(1)}, f32[64,384]{1,0:T(8,128)S(1)}, u32[]{:S(2)}, u32[]{:S(2)}) collective-permute-start(f32[64,384]{1,0:T(8,128)S(1)} %collective-permute-done.4.refs_1_), channel_id=1, source_target_pairs={{0,4},{1,3},{2,6},{3,1},{4,0},{5,7},{6,2},{7,5},{8,12},{9,11},{10,... | collective-permute-start | bytes 294920 | tf_op jit(solution)/shard_map/ppermute | solution.py:30
  19.7 0.2 collective-permute-done.2.refs_2_
  19.9 0.0 collective-permute-start.3
  19.9 0.8 %collective-permute-done.refs_2_.refs_0_ = f32[64,384]{1,0:T(8,128)S(1)} collective-permute-done((f32[64,384]{1,0:T(8,128)S(1)}, f32[64,384]{1,0:T(8,128)S(1)}, u32[]{:S(2)}, u32[]{:S(2)}) %collective-permute-start) | collective-permute-done | bytes 98336 | tf_op jit(solution)/shard_map/ppermute | solution.py:30
  20.7 1.7 %collective-permute-done.5.refs_0_ = f32[64,384]{1,0:T(8,128)S(1)} collective-permute-done((f32[64,384]{1,0:T(8,128)S(1)}, f32[64,384]{1,0:T(8,128)S(1)}, u32[]{:S(2)}, u32[]{:S(2)}) %collective-permute-start.5) | collective-permute-done | bytes 98336 | tf_op jit(solution)/shard_map/ppermute | solution.py:30
  22.5 0.0 collective-permute-done.7.refs_5_
  22.5 0.0 copy-done
  22.5 4.0 %shard_map.50 = (f32[2,256,384]{2,1,0:T(8,128)S(1)}, f32[256,384]{1,0:T(8,128)S(1)}) custom-call(f32[64,384]{1,0:T(8,128)S(1)} %collective-permute-done.5.refs_0_, f32[64,384]{1,0:T(8,128)S(1)} %collective-permute-done.4.refs_1_, f32[64,384]{1,0:T(8,128)S(1)} %collective-permute-done.refs_2_.refs_0_, f32[64,384]{1,0:T(8,128)S(1)} %copy-done.1, ...), custom_call_target="tpu_custom_call" | custom-call | flops 1727004672 | bytes 2826240 | tf_op jit(solution)/shard_map/pallas_call | solution.py:37
  26.5 0.0 collective-permute-done.3.refs_3_
  26.5 1.4 %shard_map.52 = (f32[128,384]{1,0:T(8,128)S(1)}, f32[128,384]{1,0:T(8,128)S(1)}) custom-call(f32[64,384]{1,0:T(8,128)S(1)} %collective-permute-done.5.refs_0_, f32[64,384]{1,0:T(8,128)S(1)} %collective-permute-done.4.refs_1_, f32[72,384]{1,0:T(8,128)S(1)} %collective-permute-done.2.refs_2_, f32[72,384]{1,0:T(8,128)S(1)} %collective-permute-done.3.refs_3_, ...), custom_call_target="tpu_custom_call" | custom-call | flops 339738624 | bytes 2580480 | tf_op jit(solution)/shard_map/pallas_call | solution.py:37
  27.9 1.6 %collective-permute-start.9 = (f32[128,384]{1,0:T(8,128)S(1)}, f32[128,384]{1,0:T(8,128)S(1)}, u32[]{:S(2)}, u32[]{:S(2)}) collective-permute-start(f32[128,384]{1,0:T(8,128)S(1)} %get-tuple-element.15), channel_id=1, source_target_pairs={{0,2},{1,5},{2,0},{3,7},{4,6},{5,1},{6,4},{7,3},{8,10},{9,13},{10,... | collective-permute-start | bytes 589832 | tf_op jit(solution)/shard_map/ppermute | solution.py:30
  29.5 0.5 collective-permute-start.8
  30.0 1.4 %shard_map.51 = (f32[128,384]{1,0:T(8,128)S(1)}, f32[128,384]{1,0:T(8,128)S(1)}) custom-call(f32[64,384]{1,0:T(8,128)S(1)} %collective-permute-done.refs_2_.refs_0_, f32[64,384]{1,0:T(8,128)S(1)} %copy-done.1, f32[72,384]{1,0:T(8,128)S(1)} %collective-permute-done.2.refs_2_, f32[72,384]{1,0:T(8,128)S(1)} %collective-permute-done.3.refs_3_, ...), custom_call_target="tpu_custom_call" | custom-call | flops 339738624 | bytes 2580480 | tf_op jit(solution)/shard_map/pallas_call | solution.py:37
  31.4 2.2 %collective-permute-done.9 = f32[128,384]{1,0:T(8,128)S(1)} collective-permute-done((f32[128,384]{1,0:T(8,128)S(1)}, f32[128,384]{1,0:T(8,128)S(1)}, u32[]{:S(2)}, u32[]{:S(2)}) %collective-permute-start.9) | collective-permute-done | bytes 196640 | tf_op jit(solution)/shard_map/ppermute | solution.py:30
  33.6 2.3 %collective-permute-start.10 = (f32[128,384]{1,0:T(8,128)S(1)}, f32[128,384]{1,0:T(8,128)S(1)}, u32[]{:S(2)}, u32[]{:S(2)}) collective-permute-start(f32[128,384]{1,0:T(8,128)S(1)} %add.24), channel_id=1, source_target_pairs={{0,4},{1,3},{2,6},{3,1},{4,0},{5,7},{6,2},{7,5},{8,12},{9,11},{10,... | collective-permute-start | bytes 589832 | tf_op jit(solution)/shard_map/ppermute | solution.py:30
  35.9 1.9 %collective-permute-done.8 = f32[128,384]{1,0:T(8,128)S(1)} collective-permute-done((f32[128,384]{1,0:T(8,128)S(1)}, f32[128,384]{1,0:T(8,128)S(1)}, u32[]{:S(2)}, u32[]{:S(2)}) %collective-permute-start.8) | collective-permute-done | bytes 196640 | tf_op jit(solution)/shard_map/ppermute | solution.py:30
  37.8 1.7 %collective-permute-done.10.arrived_ref = f32[128,384]{1,0:T(8,128)S(1)} collective-permute-done((f32[128,384]{1,0:T(8,128)S(1)}, f32[128,384]{1,0:T(8,128)S(1)}, u32[]{:S(2)}, u32[]{:S(2)}) %collective-permute-start.10) | collective-permute-done | bytes 196640 | tf_op jit(solution)/shard_map/ppermute | solution.py:30
  39.6 1.2 %shard_map.53 = (f32[384,128]{1,0:T(8,128)S(1)}, f32[384,128]{1,0:T(8,128)S(1)}) custom-call(f32[128,384]{1,0:T(8,128)S(1)} %add.23.part_ref, f32[128,384]{1,0:T(8,128)S(1)} %collective-permute-done.10.arrived_ref, f32[384,384]{1,0:T(8,128)S(1)} %copy-done), custom_call_target="tpu_custom_call" | custom-call | flops 452984832 | bytes 1376256 | tf_op jit(solution)/shard_map/pallas_call | solution.py:37
  40.7 0.1 collective-permute-start.11
  40.8 1.4 %collective-permute-done.11 = f32[384,128]{1,0:T(8,128)S(1)} collective-permute-done((f32[384,128]{1,0:T(8,128)S(1)}, f32[384,128]{1,0:T(8,128)S(1)}, u32[]{:S(2)}, u32[]{:S(2)}) %collective-permute-start.11) | collective-permute-done | bytes 196640 | tf_op jit(solution)/shard_map/ppermute | solution.py:30
  42.3 1.6 %collective-permute-start.12 = (f32[384,128]{1,0:T(8,128)S(1)}, f32[384,128]{1,0:T(8,128)S(1)}, u32[]{:S(2)}, u32[]{:S(2)}) collective-permute-start(f32[384,128]{1,0:T(8,128)S(1)} %add.25), channel_id=1, source_target_pairs={{0,2},{1,9},{2,0},{3,11},{4,6},{5,13},{6,4},{7,15},{8,10},{9,1},{1... | collective-permute-start | bytes 589832 | tf_op jit(solution)/shard_map/ppermute | solution.py:30
  43.8 4.2 %collective-permute-done.12 = f32[384,128]{1,0:T(8,128)S(1)} collective-permute-done((f32[384,128]{1,0:T(8,128)S(1)}, f32[384,128]{1,0:T(8,128)S(1)}, u32[]{:S(2)}, u32[]{:S(2)}) %collective-permute-start.12) | collective-permute-done | bytes 196640 | tf_op jit(solution)/shard_map/ppermute | solution.py:30
  48.0 2.1 %collective-permute-start.13 = (f32[384,128]{1,0:T(8,128)S(1)}, f32[384,128]{1,0:T(8,128)S(1)}, u32[]{:S(2)}, u32[]{:S(2)}) collective-permute-start(f32[384,128]{1,0:T(8,128)S(1)} %add.26), channel_id=1, source_target_pairs={{0,4},{1,17},{2,6},{3,19},{4,0},{5,21},{6,2},{7,23},{8,12},{9,25},... | collective-permute-start | bytes 589832 | tf_op jit(solution)/shard_map/ppermute | solution.py:30
  50.1 3.6 %collective-permute-done.13 = f32[384,128]{1,0:T(8,128)S(1)} collective-permute-done((f32[384,128]{1,0:T(8,128)S(1)}, f32[384,128]{1,0:T(8,128)S(1)}, u32[]{:S(2)}, u32[]{:S(2)}) %collective-permute-start.13) | collective-permute-done | bytes 196640 | tf_op jit(solution)/shard_map/ppermute | solution.py:30
  53.8 2.9 %collective-permute-start.14 = (f32[384,128]{1,0:T(8,128)S(1)}, f32[384,128]{1,0:T(8,128)S(1)}, u32[]{:S(2)}, u32[]{:S(2)}) collective-permute-start(f32[384,128]{1,0:T(8,128)S(1)} %add.27), channel_id=1, source_target_pairs={{0,8},{1,3},{2,10},{3,1},{4,12},{5,7},{6,14},{7,5},{8,0},{9,11},{1... | collective-permute-start | bytes 589832 | tf_op jit(solution)/shard_map/ppermute | solution.py:30
  56.7 3.6 %collective-permute-done.14 = f32[384,128]{1,0:T(8,128)S(1)} collective-permute-done((f32[384,128]{1,0:T(8,128)S(1)}, f32[384,128]{1,0:T(8,128)S(1)}, u32[]{:S(2)}, u32[]{:S(2)}) %collective-permute-start.14) | collective-permute-done | bytes 196640 | tf_op jit(solution)/shard_map/ppermute | solution.py:30
  60.4 1.8 %collective-permute-start.15 = (f32[384,128]{1,0:T(8,128)S(1)}, f32[384,128]{1,0:T(8,128)S(1)}, u32[]{:S(2)}, u32[]{:S(2)}) collective-permute-start(f32[384,128]{1,0:T(8,128)S(1)} %add.28), channel_id=1, source_target_pairs={{0,16},{1,5},{2,18},{3,7},{4,20},{5,1},{6,22},{7,3},{8,24},{9,13},... | collective-permute-start | bytes 589832 | tf_op jit(solution)/shard_map/ppermute | solution.py:30
  62.2 6.9 %collective-permute-done.15 = f32[384,128]{1,0:T(8,128)S(1)} collective-permute-done((f32[384,128]{1,0:T(8,128)S(1)}, f32[384,128]{1,0:T(8,128)S(1)}, u32[]{:S(2)}, u32[]{:S(2)}) %collective-permute-start.15) | collective-permute-done | bytes 196640 | tf_op jit(solution)/shard_map/ppermute | solution.py:30
  69.1 0.1 collective-permute-start.16
  69.2 1.4 %collective-permute-done.16.other_ref = f32[384,128]{1,0:T(8,128)S(1)} collective-permute-done((f32[384,128]{1,0:T(8,128)S(1)}, f32[384,128]{1,0:T(8,128)S(1)}, u32[]{:S(2)}, u32[]{:S(2)}) %collective-permute-start.16) | collective-permute-done | bytes 196640 | tf_op jit(solution)/shard_map/ppermute | solution.py:30
  70.6 1.3 %shard_map.54 = (f32[384,384]{1,0:T(8,128)}, f32[64,384]{1,0:T(8,128)}) custom-call(f32[384,128]{1,0:T(8,128)S(1)} %add.29.keep_ref, f32[384,128]{1,0:T(8,128)S(1)} %collective-permute-done.16.other_ref, f32[64,384]{1,0:T(8,128)S(1)} %copy-done.1), custom_call_target="tpu_custom_call" | custom-call | flops 113246208 | bytes 1179648 | tf_op jit(solution)/shard_map/pallas_call | solution.py:37
  (7 shorter events, 0.2 us)
Async XLA Ops:
  0.6 0.7 copy-start.2
  0.6 21.8 %copy-start = (f32[384,384]{1,0:T(8,128)S(1)}, f32[384,384]{1,0:T(8,128)}, u32[]{:S(2)}) copy-start(f32[384,384]{1,0:T(8,128)} %metric_ref.1) | copy-start | bytes 1769476
  2.3 10.9 %copy-start.1 = (f32[64,384]{1,0:T(8,128)S(1)}, f32[64,384]{1,0:T(8,128)}, u32[]{:S(2)}) copy-start(f32[64,384]{1,0:T(8,128)} %points_ref.1) | copy-start | bytes 294916
  2.3 9.6 %collective-permute-start.1 = (f32[72,384]{1,0:T(8,128)S(1)}, f32[72,384]{1,0:T(8,128)S(1)}, u32[]{:S(2)}, u32[]{:S(2)}) collective-permute-start(f32[72,384]{1,0:T(8,128)S(1)} %pad_maximum_fusion.1), channel_id=1, source_target_pairs={{0,16},{1,17},{2,18},{3,19},{4,20},{5,21},{6,22},{7,23},{8,24},{9,... | collective-permute-start | bytes 331784 | tf_op jit(solution)/shard_map/ppermute | solution.py:30
  6.4 5.8 %collective-permute-start.6 = (f32[72,384]{1,0:T(8,128)S(1)}, f32[72,384]{1,0:T(8,128)S(1)}, u32[]{:S(2)}, u32[]{:S(2)}) collective-permute-start(f32[72,384]{1,0:T(8,128)S(1)} %pad_maximum_fusion.1), channel_id=1, source_target_pairs={{0,8},{1,9},{2,10},{3,11},{4,12},{5,13},{6,14},{7,15},{8,0},{9,1},... | collective-permute-start | bytes 331784 | tf_op jit(solution)/shard_map/ppermute | solution.py:30
  13.1 9.4 %collective-permute-start.7 = (f32[216,384]{1,0:T(8,128)S(1)}, f32[216,384]{1,0:T(8,128)S(1)}, u32[]{:S(2)}, u32[]{:S(2)}) collective-permute-start(f32[216,384]{1,0:T(8,128)S(1)} %pad_maximum_fusion.refs_4_), channel_id=1, source_target_pairs={{0,1},{1,0},{2,3},{3,2},{4,5},{5,4},{6,7},{7,6},{8,9},{9,8},{10,11... | collective-permute-start | bytes 995336 | tf_op jit(solution)/shard_map/ppermute | solution.py:30
  13.2 4.7 %collective-permute-start.4 = (f32[64,384]{1,0:T(8,128)S(1)}, f32[64,384]{1,0:T(8,128)S(1)}, u32[]{:S(2)}, u32[]{:S(2)}) collective-permute-start(f32[64,384]{1,0:T(8,128)S(1)} %copy-done.1), channel_id=1, source_target_pairs={{0,2},{1,5},{2,0},{3,7},{4,6},{5,1},{6,4},{7,3},{8,10},{9,13},{10,... | collective-permute-start | bytes 294920 | tf_op jit(solution)/shard_map/ppermute | solution.py:30
  14.8 5.1 %collective-permute-start.2 = (f32[72,384]{1,0:T(8,128)S(1)}, f32[72,384]{1,0:T(8,128)S(1)}, u32[]{:S(2)}, u32[]{:S(2)}) collective-permute-start(f32[72,384]{1,0:T(8,128)S(1)} %collective-permute-done.1), channel_id=1, source_target_pairs={{0,8},{1,9},{2,10},{3,11},{4,12},{5,13},{6,14},{7,15},{8,0},{9,1},... | collective-permute-start | bytes 331784 | tf_op jit(solution)/shard_map/ppermute | solution.py:30
  16.1 4.6 %collective-permute-start = (f32[64,384]{1,0:T(8,128)S(1)}, f32[64,384]{1,0:T(8,128)S(1)}, u32[]{:S(2)}, u32[]{:S(2)}) collective-permute-start(f32[64,384]{1,0:T(8,128)S(1)} %copy-done.1), channel_id=1, source_target_pairs={{0,4},{1,3},{2,6},{3,1},{4,0},{5,7},{6,2},{7,5},{8,12},{9,11},{10,... | collective-permute-start | bytes 294920 | tf_op jit(solution)/shard_map/ppermute | solution.py:30
  17.8 4.6 %collective-permute-start.5 = (f32[64,384]{1,0:T(8,128)S(1)}, f32[64,384]{1,0:T(8,128)S(1)}, u32[]{:S(2)}, u32[]{:S(2)}) collective-permute-start(f32[64,384]{1,0:T(8,128)S(1)} %collective-permute-done.4.refs_1_), channel_id=1, source_target_pairs={{0,4},{1,3},{2,6},{3,1},{4,0},{5,7},{6,2},{7,5},{8,12},{9,11},{10,... | collective-permute-start | bytes 294920 | tf_op jit(solution)/shard_map/ppermute | solution.py:30
  19.9 6.6 %collective-permute-start.3 = (f32[72,384]{1,0:T(8,128)S(1)}, f32[72,384]{1,0:T(8,128)S(1)}, u32[]{:S(2)}, u32[]{:S(2)}) collective-permute-start(f32[72,384]{1,0:T(8,128)S(1)} %collective-permute-done.2.refs_2_), channel_id=1, source_target_pairs={{0,1},{1,0},{2,3},{3,2},{4,5},{5,4},{6,7},{7,6},{8,9},{9,8},{10,11... | collective-permute-start | bytes 331784 | tf_op jit(solution)/shard_map/ppermute | solution.py:30
  27.9 5.7 %collective-permute-start.9 = (f32[128,384]{1,0:T(8,128)S(1)}, f32[128,384]{1,0:T(8,128)S(1)}, u32[]{:S(2)}, u32[]{:S(2)}) collective-permute-start(f32[128,384]{1,0:T(8,128)S(1)} %get-tuple-element.15), channel_id=1, source_target_pairs={{0,2},{1,5},{2,0},{3,7},{4,6},{5,1},{6,4},{7,3},{8,10},{9,13},{10,... | collective-permute-start | bytes 589832 | tf_op jit(solution)/shard_map/ppermute | solution.py:30
  29.5 8.3 %collective-permute-start.8 = (f32[128,384]{1,0:T(8,128)S(1)}, f32[128,384]{1,0:T(8,128)S(1)}, u32[]{:S(2)}, u32[]{:S(2)}) collective-permute-start(f32[128,384]{1,0:T(8,128)S(1)} %get-tuple-element.13), channel_id=1, source_target_pairs={{0,2},{1,5},{2,0},{3,7},{4,6},{5,1},{6,4},{7,3},{8,10},{9,13},{10,... | collective-permute-start | bytes 589832 | tf_op jit(solution)/shard_map/ppermute | solution.py:30
  33.6 5.9 %collective-permute-start.10 = (f32[128,384]{1,0:T(8,128)S(1)}, f32[128,384]{1,0:T(8,128)S(1)}, u32[]{:S(2)}, u32[]{:S(2)}) collective-permute-start(f32[128,384]{1,0:T(8,128)S(1)} %add.24), channel_id=1, source_target_pairs={{0,4},{1,3},{2,6},{3,1},{4,0},{5,7},{6,2},{7,5},{8,12},{9,11},{10,... | collective-permute-start | bytes 589832 | tf_op jit(solution)/shard_map/ppermute | solution.py:30
  40.7 1.5 %collective-permute-start.11 = (f32[384,128]{1,0:T(8,128)S(1)}, f32[384,128]{1,0:T(8,128)S(1)}, u32[]{:S(2)}, u32[]{:S(2)}) collective-permute-start(f32[384,128]{1,0:T(8,128)S(1)} %get-tuple-element.17), channel_id=1, source_target_pairs={{0,1},{1,0},{2,3},{3,2},{4,5},{5,4},{6,7},{7,6},{8,9},{9,8},{10,11... | collective-permute-start | bytes 589832 | tf_op jit(solution)/shard_map/ppermute | solution.py:30
  42.3 5.7 %collective-permute-start.12 = (f32[384,128]{1,0:T(8,128)S(1)}, f32[384,128]{1,0:T(8,128)S(1)}, u32[]{:S(2)}, u32[]{:S(2)}) collective-permute-start(f32[384,128]{1,0:T(8,128)S(1)} %add.25), channel_id=1, source_target_pairs={{0,2},{1,9},{2,0},{3,11},{4,6},{5,13},{6,4},{7,15},{8,10},{9,1},{1... | collective-permute-start | bytes 589832 | tf_op jit(solution)/shard_map/ppermute | solution.py:30
  48.0 5.7 %collective-permute-start.13 = (f32[384,128]{1,0:T(8,128)S(1)}, f32[384,128]{1,0:T(8,128)S(1)}, u32[]{:S(2)}, u32[]{:S(2)}) collective-permute-start(f32[384,128]{1,0:T(8,128)S(1)} %add.26), channel_id=1, source_target_pairs={{0,4},{1,17},{2,6},{3,19},{4,0},{5,21},{6,2},{7,23},{8,12},{9,25},... | collective-permute-start | bytes 589832 | tf_op jit(solution)/shard_map/ppermute | solution.py:30
  53.8 6.6 %collective-permute-start.14 = (f32[384,128]{1,0:T(8,128)S(1)}, f32[384,128]{1,0:T(8,128)S(1)}, u32[]{:S(2)}, u32[]{:S(2)}) collective-permute-start(f32[384,128]{1,0:T(8,128)S(1)} %add.27), channel_id=1, source_target_pairs={{0,8},{1,3},{2,10},{3,1},{4,12},{5,7},{6,14},{7,5},{8,0},{9,11},{1... | collective-permute-start | bytes 589832 | tf_op jit(solution)/shard_map/ppermute | solution.py:30
  60.4 8.7 %collective-permute-start.15 = (f32[384,128]{1,0:T(8,128)S(1)}, f32[384,128]{1,0:T(8,128)S(1)}, u32[]{:S(2)}, u32[]{:S(2)}) collective-permute-start(f32[384,128]{1,0:T(8,128)S(1)} %add.28), channel_id=1, source_target_pairs={{0,16},{1,5},{2,18},{3,7},{4,20},{5,1},{6,22},{7,3},{8,24},{9,13},... | collective-permute-start | bytes 589832 | tf_op jit(solution)/shard_map/ppermute | solution.py:30
  69.1 1.5 %collective-permute-start.16 = (f32[384,128]{1,0:T(8,128)S(1)}, f32[384,128]{1,0:T(8,128)S(1)}, u32[]{:S(2)}, u32[]{:S(2)}) collective-permute-start(f32[384,128]{1,0:T(8,128)S(1)} %add.29.keep_ref), channel_id=1, source_target_pairs={{0,1},{1,0},{2,3},{3,2},{4,5},{5,4},{6,7},{7,6},{8,9},{9,8},{10,11... | collective-permute-start | bytes 589832 | tf_op jit(solution)/shard_map/ppermute | solution.py:30

commit v3 on v2

v3 whole, which is shorter than its diff:
```python
import jax
import jax.numpy as jnp
from jax import lax
from jax.experimental import pallas as pl
from jax.experimental.pallas import tpu as pltpu
from jax.sharding import PartitionSpec as P

AXES = ("row", "col")
F32, BF16 = jnp.float32, jnp.bfloat16


def halves(x):
    high = x.astype(BF16)
    return high, (x - high.astype(F32)).astype(BF16)


def left(x, axis=1):
    high, low = halves(x)
    return jnp.concatenate([high, high, low], axis=axis)


def right(x, axis=1):
    high, low = halves(x)
    return jnp.concatenate([high, low, high], axis=axis)


def mul(a, b, da=1, db=0):
    return lax.dot_general(a, b, (((da,), (db,)), ((), ())), preferred_element_type=F32)


def round_up(count, step):
    return -(-count // step) * step


def bits_of(count):
    assert count & (count - 1) == 0
    return [1 << b for b in range(count.bit_length() - 1)]


def make_hop(rows, cols):
    def hop(value, even, odd=None):
        odd = even if odd is None else odd
        pairs = []
        for r in range(rows):
            for c in range(cols):
                dr, dc = odd if c & 1 else even
                pairs.append((r * cols + c, (r ^ dr) * cols + (c ^ dc)))
        return lax.ppermute(value, AXES, pairs)

    return hop


def call(body, out_shape, args, flops):
    moved = sum(4 * a.size for a in args) + sum(4 * s.size for s in jax.tree.leaves(out_shape))
    return pl.pallas_call(
        body,
        out_shape=out_shape,
        in_specs=[pl.BlockSpec(memory_space=pltpu.VMEM)] * len(args),
        out_specs=jax.tree.map(lambda _: pl.BlockSpec(memory_space=pltpu.VMEM), out_shape),
        compiler_params=pltpu.CompilerParams(vmem_limit_bytes=40 * 1024 * 1024),
        cost_estimate=pl.CostEstimate(flops=flops, bytes_accessed=moved, transcendentals=0),
    )(*args)


def shape(*dims):
    return jax.ShapeDtypeStruct(dims, F32)


def pack_own(points, coeffs):
    rows, width = points.shape
    outs_n = coeffs.shape[1]
    extra = round_up(outs_n + 1, 8)

    def body(points_ref, cols_ref, out_ref):
        out_ref[0:rows, :] = points_ref[...]
        out_ref[rows:, :] = jnp.zeros((extra, width), F32)
        cols = cols_ref[...]
        out_ref[rows : rows + outs_n, 0 : 2 * rows] = jnp.concatenate([cols, cols], axis=1)

    return call(body, shape(rows + extra, width), [points, coeffs.T], 1)


def norm_rows(centers, metric3, own):
    column = jnp.sum(centers * mul(left(centers), metric3), axis=1, keepdims=True)
    pair = 2 * own
    return [
        jnp.broadcast_to(column[k : k + pair], (pair, round_up(pair, 128))).T[0:1]
        for k in range(0, centers.shape[0], pair)
    ]


def join_blocks(packed, queries, metric, own, outs_n):
    height, width = packed[0].shape
    blocks, count = len(packed), len(queries)

    def body(*refs):
        packed_refs, query_refs = refs[:blocks], refs[blocks : blocks + count]
        metric_ref, joined_ref, mapped_ref, metric3_ref = refs[blocks + count :]
        metric3 = right(metric_ref[...], axis=0)
        metric3_ref[...] = metric3
        query_x = jnp.concatenate([ref[...] for ref in query_refs], axis=0)
        mapped_ref[...] = mul(left(query_x), metric3)
        doubled = []
        for k, ref in enumerate(packed_refs):
            joined_ref[k * height : (k + 1) * height, :] = ref[...]
            doubled += [ref[0:own, :], ref[0:own, :]]
        norms = norm_rows(jnp.concatenate(doubled, axis=0), metric3, own)
        for k, norm in enumerate(norms):
            row = k * height + own + outs_n
            joined_ref[row : row + 1, 0 : 2 * own] = norm

    out = (shape(blocks * height, width), shape(count * own, width), jax.ShapeDtypeStruct((3 * width, width), BF16))
    flops = 6 * (2 * blocks + count) * own * width * width
    return call(body, out, list(packed) + list(queries) + [metric], flops)


def center_terms(refs, own, outs_n, metric3=None):
    pieces, extras = [], []
    height = own + round_up(outs_n + 1, 8)
    for ref in refs:
        for first in range(0, ref.shape[0], height):
            pieces.append(ref[first : first + own, :])
            extras.append(ref[first + own : first + height, 0 : 2 * own])
    centers = jnp.concatenate(pieces, axis=0)
    lane = lax.broadcasted_iota(jnp.int32, extras[0].shape, 1)
    merged = [jnp.where(lane < own, extras[k], extras[k + 1]) for k in range(0, len(extras), 2)]
    rows = jnp.concatenate(merged, axis=1)
    if metric3 is None:
        norm = rows[outs_n : outs_n + 1]
    else:
        norm = jnp.concatenate(norm_rows(centers, metric3, own), axis=1)
    return centers, norm, [rows[c : c + 1] for c in range(outs_n)]


def query_sums(query_x, query_y, centers, norm, coefs):
    query_n = jnp.sum(query_x * query_y, axis=1, keepdims=True)
    cross = mul(left(query_y), right(centers), 1, 1)
    distance = jnp.sqrt(jnp.maximum(query_n + norm - 2.0 * cross, 0.0))
    weights = jnp.exp(-distance) / jnp.maximum(distance, 0.5)
    low = centers.astype(BF16)
    parts = []
    for coef in coefs:
        scaled = weights * coef
        sums = jnp.sum(scaled, axis=1, keepdims=True)
        parts.append(sums * query_x - mul(scaled.astype(BF16), low))
    return parts


def early_sums(queries, mapped, metric3, blocks, outs_n):
    own, width = queries[0].shape
    count = len(queries)

    def body(*refs):
        query_refs, block_refs = refs[:count], refs[count : count + len(blocks)]
        mapped_ref, metric3_ref, total_ref, first_ref = refs[count + len(blocks) :]
        query_x = jnp.concatenate([ref[...] for ref in query_refs], axis=0)
        first_y = mul(left(query_refs[0][...]), metric3_ref[...])
        first_ref[...] = first_y
        query_y = jnp.concatenate([first_y, mapped_ref[...]], axis=0)
        for k in range(0, len(blocks), 2):
            parts = query_sums(query_x, query_y, *center_terms(block_refs[k : k + 2], own, outs_n))
            for c in range(outs_n):
                if k == 0:
                    total_ref[c] = parts[c]
                else:
                    total_ref[c] = total_ref[c] + parts[c]

    args = list(queries) + list(blocks) + [mapped, metric3]
    centers = sum(b.shape[0] for b in blocks)
    flops = 6 * own * width * width + 10 * count * own * centers * width
    return call(body, (shape(outs_n, count * own, width), shape(own, width)), args, flops)


def late_sums(queries, mapped, spans, first, total, metric3, blocks, outs_n):
    own, width = queries[0].shape
    count, maps = len(queries), len(mapped)

    def body(*refs):
        query_refs, block_refs = refs[:count], refs[count : count + len(blocks)]
        mapped_refs = refs[count + len(blocks) : count + len(blocks) + maps]
        total_ref, metric3_ref = refs[count + len(blocks) + maps : count + len(blocks) + maps + 2]
        out_refs = refs[count + len(blocks) + maps + 2 :]
        rows = slice(first * own, (first + count) * own)
        query_x = jnp.concatenate([ref[...] for ref in query_refs], axis=0)
        query_y = [ref[a * own : b * own, :] for ref, (a, b) in zip(mapped_refs, spans)]
        query_y = query_y[0] if maps == 1 else jnp.concatenate(query_y, axis=0)
        sums = [total_ref[c, rows, :] for c in range(outs_n)]
        for k in range(0, len(blocks), 2):
            terms = center_terms(block_refs[k : k + 2], own, outs_n, metric3_ref[...])
            sums = [a + b for a, b in zip(sums, query_sums(query_x, query_y, *terms))]
        for q in range(count):
            for c in range(outs_n):
                out_refs[q][c * own : (c + 1) * own, :] = sums[c][q * own : (q + 1) * own, :]

    args = list(queries) + list(blocks) + list(mapped) + [total, metric3]
    centers = sum(b.shape[0] for b in blocks)
    flops = 6 * centers * width * width + 10 * count * own * centers * width
    return call(body, tuple(shape(outs_n * own, width) for _ in queries), args, flops)


def upper_tiles(width):
    tile = 128 if width % 128 == 0 else width
    span = width // tile
    return tile, span, [(i, j) for i in range(span) for j in range(i, span)]


def outer_halves(part, arrived, metric3):
    width = part.shape[1]
    tile, span, upper = upper_tiles(width)
    half = (len(upper) + 1) // 2

    def body(part_ref, arrived_ref, metric3_ref, keep_ref, send_ref):
        odd = (lax.axis_index("col") & 1) == 1
        grads = mul(left(part_ref[...] + arrived_ref[...]), metric3_ref[...])
        grads_left, grads_right = left(grads, 0), right(grads, 0)
        tiles = [[] for _ in upper]
        for i in range(span):
            slab = mul(grads_left[:, i * tile : (i + 1) * tile], grads_right[:, i * tile :], 0, 0)
            for j in range(i, span):
                tiles[upper.index((i, j))] = slab[:, (j - i) * tile : (j - i + 1) * tile]
        while len(tiles) < 2 * half:
            tiles.append(jnp.zeros((tile, tile), F32))
        for k in range(half):
            keep_ref[k * tile : (k + 1) * tile, :] = jnp.where(odd, tiles[half + k], tiles[k])
            send_ref[k * tile : (k + 1) * tile, :] = jnp.where(odd, tiles[k], tiles[half + k])

    out = shape(half * tile, tile)
    return call(body, (out, out), [part, arrived, metric3], 12 * part.shape[0] * width * width)


def finish(keep, other, points):
    rows, width = points.shape
    tile, span, upper = upper_tiles(width)
    half = (len(upper) + 1) // 2

    def body(keep_ref, other_ref, points_ref, next_ref, mapped_ref):
        odd = (lax.axis_index("col") & 1) == 1
        kept = [keep_ref[k * tile : (k + 1) * tile, :] for k in range(half)]
        came = [other_ref[k * tile : (k + 1) * tile, :] for k in range(half)]
        tiles = [jnp.where(odd, b, a) for a, b in zip(kept, came)]
        tiles += [jnp.where(odd, a, b) for a, b in zip(kept, came)]
        final = dict(zip(upper, tiles))
        diag = final[0, 0]
        for i in range(1, span):
            diag = diag + final[i, i]
        eye = lax.broadcasted_iota(jnp.int32, diag.shape, 0) == lax.broadcasted_iota(jnp.int32, diag.shape, 1)
        trace = jnp.sum(jnp.where(eye, diag, 0.0), keepdims=True)
        scale = width / trace
        for i, j in upper:
            value = final[i, j] * scale
            next_ref[i * tile : (i + 1) * tile, j * tile : (j + 1) * tile] = value
            if i != j:
                next_ref[j * tile : (j + 1) * tile, i * tile : (i + 1) * tile] = value.T
        mapped_ref[...] = mul(left(points_ref[...]), right(next_ref[...], axis=0))

    return call(body, (shape(width, width), shape(rows, width)), [keep, other, points], 6 * rows * width * width)


def make_local(rows_all, cols_all):
    hop = make_hop(rows_all, cols_all)
    row_bits = bits_of(rows_all)
    col_bits = bits_of(cols_all)
    bit_a, bit_b = row_bits[0], row_bits[1]
    line_bits = row_bits[2:]

    def to_a(value):
        return hop(value, (bit_a, 0), (bit_b, 0))

    def to_b(value):
        return hop(value, (bit_b, 0), (bit_a, 0))

    def over_cols(block):
        have = [block]
        for bit in col_bits:
            have = have + [hop(piece, (0, bit)) for piece in have]
        return have

    def local(points, coeffs, metric):
        own, width = points.shape
        outs_n = coeffs.shape[1]
        have = [pack_own(points, coeffs)]
        for bit in reversed(line_bits):
            have = have + [hop(piece, (bit, 0)) for piece in have]
        from_a = to_a(points)
        from_b = to_b(points)
        from_ab = to_b(from_a)
        queries = [from_ab, from_a, from_b, points]
        joined, mapped, metric3 = join_blocks(have[:-1], queries[1:], metric, own, outs_n)
        early, late = over_cols(joined), over_cols(have[-1])
        total, mapped_ab = early_sums(queries, mapped, metric3, early, outs_n)
        part_ab, part_a = late_sums(
            queries[:2], [mapped_ab, mapped], [(0, 1), (0, 1)], 0, total, metric3, late, outs_n
        )
        sent_ab, sent_a = to_a(part_ab), to_a(part_a)
        part_b, part_own = late_sums(queries[2:], [mapped], [(1, 3)], 2, total, metric3, late, outs_n)
        sent_b = to_b(part_b + sent_ab)

        keep, send = outer_halves(part_own + sent_a, sent_b, metric3)
        keep = keep + hop(send, (0, 1))
        rest = [(bit, 0) for bit in row_bits]
        turn = len(rest) // 2
        for even_hop, odd_hop in zip(rest, rest[turn:] + rest[:turn]):
            keep = keep + hop(keep, even_hop, odd_hop)
        for bit in col_bits[1:]:
            keep = keep + hop(keep, (0, bit))
        return finish(keep, hop(keep, (0, 1)), points)

    return local


def solution(mesh):
    return jax.shard_map(
        make_local(mesh.shape["row"], mesh.shape["col"]),
        mesh=mesh,
        in_specs=(P(AXES, None), P(AXES, None), P()),
        out_specs=(P(), P(AXES, None)),
        check_vma=False,
    )
```

time: 72.1 us -> 66.3 us (0.920)
  starting transfers between devices: 25 us -> 19.2 us
  Pallas kernels: 9.26 us -> 5.66 us
  waiting for transfers between devices: 34.2 us -> 37.7 us
  local copies, waits for them, and re-layouts: 0.67 us -> 2.63 us
  other arithmetic: 2.06 us -> 0.15 us
    ppermute x17, starting transfers between devices: 25 us -> 19.2 us  [hop(): return lax.ppermute(value, AXES, pairs)]
    pallas_call x5 -> x7, Pallas kernels: 9.26 us -> 5.66 us  [call(): pl.pallas_call(body, out_shape=out_shape, in_specs=[pl.BlockSpec(memory_s...]
    ppermute x17, waiting for transfers between devices: 34.2 us -> 37.7 us  [hop(): return lax.ppermute(value, AXES, pairs)]
    unnamed x6 -> x8, local copies, waits for them, and re-layouts: 0.67 us -> 2.63 us
    concatenate x3 -> x0, other arithmetic: 1.89 us -> none  [the longest x1 0.92 us: local(): early = over_cols(jnp.concatenate(have[:-1], axis=0))]
  transfers between devices with their start and end apart: 17 -> 17, of which waited for: 15 -> 12; matrix products, arithmetic and copies ran while one was open for 0% -> 0% of each run, Pallas kernels for 7% -> 3%
where the time goes in v3:
time: 66.3 us; the launch traced here: 66.1 us
  waiting for transfers between devices  37.7 us (57%)
  starting transfers between devices  19.2 us (29%)
  Pallas kernels  5.66 us (9%)
  local copies, waits for them, and re-layouts  2.63 us (4%)
  between operations  0.76 us (1%)
    ppermute x17, waiting for transfers between devices, hop(): return lax.ppermute(value, AXES, pairs)  37.7 us
    ppermute x17, starting transfers between devices, hop(): return lax.ppermute(value, AXES, pairs)  19.2 us
    pallas_call x7, Pallas kernels, call(): pl.pallas_call(body, out_shape=out_shape, in_specs=[pl.BlockSpec(memory_s...  5.66 us
    unnamed x8, local copies, waits for them, and re-layouts  2.63 us
  transfers between devices with their start and end apart: 17, of which 12 were waited for; matrix products, arithmetic and copies ran while one was open for 0% of the time, Pallas kernels for 3%

profile of v3, /device:TPU:0, one launch (start us, length us, event | category | flops | bytes accessed | tf_op | source)
XLA Modules:
  0.0 66.1 jit_solution(8526324270275898230)
XLA Ops:
  0.6 0.0 copy-start.2
  0.6 0.7 %copy-done.2 = f32[64,2]{0,1:T(2,128)S(1)} copy-done((f32[64,2]{0,1:T(2,128)S(1)}, f32[64,2]{0,1:T(2,128)}, u32[]{:S(2)}) %copy-start.2) | copy-done | bytes 536
  1.3 0.0 copy-start
  1.3 0.9 %copy-done = f32[64,384]{1,0:T(8,128)S(1)} copy-done((f32[64,384]{1,0:T(8,128)S(1)}, f32[64,384]{1,0:T(8,128)}, u32[]{:S(2)}) %copy-start) | copy-done | bytes 98328
  2.2 0.1 shard_map.50.refs_0_
  2.3 4.0 %collective-permute-start.1 = (f32[72,384]{1,0:T(8,128)S(1)}, f32[72,384]{1,0:T(8,128)S(1)}, u32[]{:S(2)}, u32[]{:S(2)}) collective-permute-start(f32[72,384]{1,0:T(8,128)S(1)} %shard_map.50.refs_0_), channel_id=1, source_target_pairs={{0,16},{1,17},{2,18},{3,19},{4,20},{5,21},{6,22},{7,23},{8,24},{9,... | collective-permute-start | bytes 331784 | tf_op jit(solution)/shard_map/ppermute | solution.py:48
  6.3 1.6 %collective-permute-start.4 = (f32[72,384]{1,0:T(8,128)S(1)}, f32[72,384]{1,0:T(8,128)S(1)}, u32[]{:S(2)}, u32[]{:S(2)}) collective-permute-start(f32[72,384]{1,0:T(8,128)S(1)} %shard_map.50.refs_0_), channel_id=1, source_target_pairs={{0,8},{1,9},{2,10},{3,11},{4,12},{5,13},{6,14},{7,15},{8,0},{9,1},... | collective-permute-start | bytes 331784 | tf_op jit(solution)/shard_map/ppermute | solution.py:48
  7.9 1.5 %collective-permute-start.5 = (f32[64,384]{1,0:T(8,128)S(1)}, f32[64,384]{1,0:T(8,128)S(1)}, u32[]{:S(2)}, u32[]{:S(2)}) collective-permute-start(f32[64,384]{1,0:T(8,128)S(1)} %copy-done), channel_id=1, source_target_pairs={{0,2},{1,5},{2,0},{3,7},{4,6},{5,1},{6,4},{7,3},{8,10},{9,13},{10,... | collective-permute-start | bytes 294920 | tf_op jit(solution)/shard_map/ppermute | solution.py:48
  9.4 1.5 %collective-permute-start = (f32[64,384]{1,0:T(8,128)S(1)}, f32[64,384]{1,0:T(8,128)S(1)}, u32[]{:S(2)}, u32[]{:S(2)}) collective-permute-start(f32[64,384]{1,0:T(8,128)S(1)} %copy-done), channel_id=1, source_target_pairs={{0,4},{1,3},{2,6},{3,1},{4,0},{5,7},{6,2},{7,5},{8,12},{9,11},{10,... | collective-permute-start | bytes 294920 | tf_op jit(solution)/shard_map/ppermute | solution.py:48
  10.9 2.2 %collective-permute-done.5.refs_3_.refs_1_ = f32[64,384]{1,0:T(8,128)S(1)} collective-permute-done((f32[64,384]{1,0:T(8,128)S(1)}, f32[64,384]{1,0:T(8,128)S(1)}, u32[]{:S(2)}, u32[]{:S(2)}) %collective-permute-start.5) | collective-permute-done | bytes 98336 | tf_op jit(solution)/shard_map/ppermute | solution.py:48
  13.1 0.9 %collective-permute-done.refs_4_.refs_2_.refs_0_ = f32[64,384]{1,0:T(8,128)S(1)} collective-permute-done((f32[64,384]{1,0:T(8,128)S(1)}, f32[64,384]{1,0:T(8,128)S(1)}, u32[]{:S(2)}, u32[]{:S(2)}) %collective-permute-start) | collective-permute-done | bytes 98336 | tf_op jit(solution)/shard_map/ppermute | solution.py:48
  14.0 0.0 collective-permute-done.1.refs_1_
  14.0 0.0 collective-permute-done.4.refs_2_
  14.0 0.0 copy-start.3
  14.0 1.1 %copy-done.3 = f32[384,384]{1,0:T(8,128)S(1)} copy-done((f32[384,384]{1,0:T(8,128)S(1)}, f32[384,384]{1,0:T(8,128)}, u32[]{:S(2)}) %copy-start.3) | copy-done | bytes 589848
  15.1 1.0 %shard_map.51 = (f32[216,384]{1,0:T(8,128)S(1)}, f32[192,384]{1,0:T(8,128)S(1)}, bf16[1152,384]{1,0:T(8,128)(2,1)S(1)}) custom-call(f32[72,384]{1,0:T(8,128)S(1)} %shard_map.50.refs_0_, f32[72,384]{1,0:T(8,128)S(1)} %collective-permute-done.1.refs_1_, f32[72,384]{1,0:T(8,128)S(1)} %collective-permute-done.4.refs_2_, ...), custom_call_target="tpu_custom_call" | custom-call | flops 509607936 | bytes 3612672 | tf_op jit(solution)/shard_map/pallas_call | solution.py:55
  16.1 0.1 collective-permute-start.7
  16.2 0.5 collective-permute-start.2
  16.7 1.5 %collective-permute-start.6 = (f32[64,384]{1,0:T(8,128)S(1)}, f32[64,384]{1,0:T(8,128)S(1)}, u32[]{:S(2)}, u32[]{:S(2)}) collective-permute-start(f32[64,384]{1,0:T(8,128)S(1)} %collective-permute-done.5.refs_3_.refs_1_), channel_id=1, source_target_pairs={{0,4},{1,3},{2,6},{3,1},{4,0},{5,7},{6,2},{7,5},{8,12},{9,11},{10,... | collective-permute-start | bytes 294920 | tf_op jit(solution)/shard_map/ppermute | solution.py:48
  18.2 3.4 %collective-permute-done.2.refs_2_ = f32[72,384]{1,0:T(8,128)S(1)} collective-permute-done((f32[72,384]{1,0:T(8,128)S(1)}, f32[72,384]{1,0:T(8,128)S(1)}, u32[]{:S(2)}, u32[]{:S(2)}) %collective-permute-start.2) | collective-permute-done | bytes 110624 | tf_op jit(solution)/shard_map/ppermute | solution.py:48
  21.7 0.0 collective-permute-start.3
  21.7 0.0 collective-permute-done.6.refs_0_
  21.7 0.0 collective-permute-done.7.refs_5_
  21.7 1.3 %shard_map.52 = (f32[2,256,384]{2,1,0:T(8,128)S(1)}, f32[64,384]{1,0:T(8,128)S(1)}) custom-call(f32[64,384]{1,0:T(8,128)S(1)} %collective-permute-done.6.refs_0_, f32[64,384]{1,0:T(8,128)S(1)} %collective-permute-done.5.refs_3_.refs_1_, f32[64,384]{1,0:T(8,128)S(1)} %collective-permute-done.refs_4_.refs_2_.refs_0_, f32[64,384]{1,0:T(8,128)S(1)} %copy-done, ...), custom_call_target="tpu_custom_call" | custom-call | flops 481296384 | bytes 4005888 | tf_op jit(solution)/shard_map/pallas_call | solution.py:55
  23.0 0.0 collective-permute-done.3.refs_3_
  23.0 0.0 copy-start.1
  23.0 0.7 %shard_map.54 = (f32[128,384]{1,0:T(8,128)S(1)}, f32[128,384]{1,0:T(8,128)S(1)}) custom-call(f32[64,384]{1,0:T(8,128)S(1)} %collective-permute-done.6.refs_0_, f32[64,384]{1,0:T(8,128)S(1)} %collective-permute-done.5.refs_3_.refs_1_, f32[72,384]{1,0:T(8,128)S(1)} %collective-permute-done.2.refs_2_, f32[72,384]{1,0:T(8,128)S(1)} %collective-permute-done.3.refs_3_, ...), custom_call_target="tpu_custom_call" | custom-call | flops 198180864 | bytes 3760128 | tf_op jit(solution)/shard_map/pallas_call | solution.py:55
  23.7 0.7 %collective-permute-start.9 = (f32[128,384]{1,0:T(8,128)S(1)}, f32[128,384]{1,0:T(8,128)S(1)}, u32[]{:S(2)}, u32[]{:S(2)}) collective-permute-start(f32[128,384]{1,0:T(8,128)S(1)} %get-tuple-element.21), channel_id=1, source_target_pairs={{0,2},{1,5},{2,0},{3,7},{4,6},{5,1},{6,4},{7,3},{8,10},{9,13},{10,... | collective-permute-start | bytes 589832 | tf_op jit(solution)/shard_map/ppermute | solution.py:48
  24.4 1.4 %collective-permute-start.8 = (f32[128,384]{1,0:T(8,128)S(1)}, f32[128,384]{1,0:T(8,128)S(1)}, u32[]{:S(2)}, u32[]{:S(2)}) collective-permute-start(f32[128,384]{1,0:T(8,128)S(1)} %get-tuple-element.19), channel_id=1, source_target_pairs={{0,2},{1,5},{2,0},{3,7},{4,6},{5,1},{6,4},{7,3},{8,10},{9,13},{10,... | collective-permute-start | bytes 589832 | tf_op jit(solution)/shard_map/ppermute | solution.py:48
  25.8 0.0 copy-done.1
  25.8 0.7 %shard_map.53 = (f32[128,384]{1,0:T(8,128)S(1)}, f32[128,384]{1,0:T(8,128)S(1)}) custom-call(f32[64,384]{1,0:T(8,128)S(1)} %collective-permute-done.refs_4_.refs_2_.refs_0_, f32[64,384]{1,0:T(8,128)S(1)} %copy-done.1, f32[72,384]{1,0:T(8,128)S(1)} %collective-permute-done.2.refs_2_, f32[72,384]{1,0:T(8,128)S(1)} %collective-permute-done.3.refs_3_, ...), custom_call_target="tpu_custom_call" | custom-call | flops 198180864 | bytes 3661824 | tf_op jit(solution)/shard_map/pallas_call | solution.py:55
  26.5 2.9 %collective-permute-done.9 = f32[128,384]{1,0:T(8,128)S(1)} collective-permute-done((f32[128,384]{1,0:T(8,128)S(1)}, f32[128,384]{1,0:T(8,128)S(1)}, u32[]{:S(2)}, u32[]{:S(2)}) %collective-permute-start.9) | collective-permute-done | bytes 196640 | tf_op jit(solution)/shard_map/ppermute | solution.py:48
  29.5 1.6 %collective-permute-start.10 = (f32[128,384]{1,0:T(8,128)S(1)}, f32[128,384]{1,0:T(8,128)S(1)}, u32[]{:S(2)}, u32[]{:S(2)}) collective-permute-start(f32[128,384]{1,0:T(8,128)S(1)} %add.22), channel_id=1, source_target_pairs={{0,4},{1,3},{2,6},{3,1},{4,0},{5,7},{6,2},{7,5},{8,12},{9,11},{10,... | collective-permute-start | bytes 589832 | tf_op jit(solution)/shard_map/ppermute | solution.py:48
  31.1 0.5 collective-permute-done.8
  31.6 3.6 %collective-permute-done.10.arrived_ref = f32[128,384]{1,0:T(8,128)S(1)} collective-permute-done((f32[128,384]{1,0:T(8,128)S(1)}, f32[128,384]{1,0:T(8,128)S(1)}, u32[]{:S(2)}, u32[]{:S(2)}) %collective-permute-start.10) | collective-permute-done | bytes 196640 | tf_op jit(solution)/shard_map/ppermute | solution.py:48
  35.2 0.6 shard_map.55
  35.9 0.1 collective-permute-start.11
  35.9 1.4 %collective-permute-done.11 = f32[384,128]{1,0:T(8,128)S(1)} collective-permute-done((f32[384,128]{1,0:T(8,128)S(1)}, f32[384,128]{1,0:T(8,128)S(1)}, u32[]{:S(2)}, u32[]{:S(2)}) %collective-permute-start.11) | collective-permute-done | bytes 196640 | tf_op jit(solution)/shard_map/ppermute | solution.py:48
  37.4 0.7 %collective-permute-start.12 = (f32[384,128]{1,0:T(8,128)S(1)}, f32[384,128]{1,0:T(8,128)S(1)}, u32[]{:S(2)}, u32[]{:S(2)}) collective-permute-start(f32[384,128]{1,0:T(8,128)S(1)} %add.23), channel_id=1, source_target_pairs={{0,2},{1,9},{2,0},{3,11},{4,6},{5,13},{6,4},{7,15},{8,10},{9,1},{1... | collective-permute-start | bytes 589832 | tf_op jit(solution)/shard_map/ppermute | solution.py:48
  38.1 5.1 %collective-permute-done.12 = f32[384,128]{1,0:T(8,128)S(1)} collective-permute-done((f32[384,128]{1,0:T(8,128)S(1)}, f32[384,128]{1,0:T(8,128)S(1)}, u32[]{:S(2)}, u32[]{:S(2)}) %collective-permute-start.12) | collective-permute-done | bytes 196640 | tf_op jit(solution)/shard_map/ppermute | solution.py:48
  43.2 1.6 %collective-permute-start.13 = (f32[384,128]{1,0:T(8,128)S(1)}, f32[384,128]{1,0:T(8,128)S(1)}, u32[]{:S(2)}, u32[]{:S(2)}) collective-permute-start(f32[384,128]{1,0:T(8,128)S(1)} %add.24), channel_id=1, source_target_pairs={{0,4},{1,17},{2,6},{3,19},{4,0},{5,21},{6,2},{7,23},{8,12},{9,25},... | collective-permute-start | bytes 589832 | tf_op jit(solution)/shard_map/ppermute | solution.py:48
  44.7 4.1 %collective-permute-done.13 = f32[384,128]{1,0:T(8,128)S(1)} collective-permute-done((f32[384,128]{1,0:T(8,128)S(1)}, f32[384,128]{1,0:T(8,128)S(1)}, u32[]{:S(2)}, u32[]{:S(2)}) %collective-permute-start.13) | collective-permute-done | bytes 196640 | tf_op jit(solution)/shard_map/ppermute | solution.py:48
  48.9 1.3 %collective-permute-start.14 = (f32[384,128]{1,0:T(8,128)S(1)}, f32[384,128]{1,0:T(8,128)S(1)}, u32[]{:S(2)}, u32[]{:S(2)}) collective-permute-start(f32[384,128]{1,0:T(8,128)S(1)} %add.25), channel_id=1, source_target_pairs={{0,8},{1,3},{2,10},{3,1},{4,12},{5,7},{6,14},{7,5},{8,0},{9,11},{1... | collective-permute-start | bytes 589832 | tf_op jit(solution)/shard_map/ppermute | solution.py:48
  50.2 4.4 %collective-permute-done.14 = f32[384,128]{1,0:T(8,128)S(1)} collective-permute-done((f32[384,128]{1,0:T(8,128)S(1)}, f32[384,128]{1,0:T(8,128)S(1)}, u32[]{:S(2)}, u32[]{:S(2)}) %collective-permute-start.14) | collective-permute-done | bytes 196640 | tf_op jit(solution)/shard_map/ppermute | solution.py:48
  54.7 1.1 %collective-permute-start.15 = (f32[384,128]{1,0:T(8,128)S(1)}, f32[384,128]{1,0:T(8,128)S(1)}, u32[]{:S(2)}, u32[]{:S(2)}) collective-permute-start(f32[384,128]{1,0:T(8,128)S(1)} %add.26), channel_id=1, source_target_pairs={{0,16},{1,5},{2,18},{3,7},{4,20},{5,1},{6,22},{7,3},{8,24},{9,13},... | collective-permute-start | bytes 589832 | tf_op jit(solution)/shard_map/ppermute | solution.py:48
  55.8 7.6 %collective-permute-done.15 = f32[384,128]{1,0:T(8,128)S(1)} collective-permute-done((f32[384,128]{1,0:T(8,128)S(1)}, f32[384,128]{1,0:T(8,128)S(1)}, u32[]{:S(2)}, u32[]{:S(2)}) %collective-permute-start.15) | collective-permute-done | bytes 196640 | tf_op jit(solution)/shard_map/ppermute | solution.py:48
  63.4 0.1 collective-permute-start.16
  63.5 1.4 %collective-permute-done.16.other_ref = f32[384,128]{1,0:T(8,128)S(1)} collective-permute-done((f32[384,128]{1,0:T(8,128)S(1)}, f32[384,128]{1,0:T(8,128)S(1)}, u32[]{:S(2)}, u32[]{:S(2)}) %collective-permute-start.16) | collective-permute-done | bytes 196640 | tf_op jit(solution)/shard_map/ppermute | solution.py:48
  64.9 1.2 %shard_map.56 = (f32[384,384]{1,0:T(8,128)}, f32[64,384]{1,0:T(8,128)}) custom-call(f32[384,128]{1,0:T(8,128)S(1)} %add.27.keep_ref, f32[384,128]{1,0:T(8,128)S(1)} %collective-permute-done.16.other_ref, f32[64,384]{1,0:T(8,128)S(1)} %copy-done.1), custom_call_target="tpu_custom_call" | custom-call | flops 56623104 | bytes 1179648 | tf_op jit(solution)/shard_map/pallas_call | solution.py:55
  (7 shorter events, 0.2 us)
Async XLA Ops:
  0.6 0.7 %copy-start.2 = (f32[64,2]{0,1:T(2,128)S(1)}, f32[64,2]{0,1:T(2,128)}, u32[]{:S(2)}) copy-start(f32[64,2]{0,1:T(2,128)} %param.4) | copy-start | bytes 1540
  1.3 0.9 %copy-start = (f32[64,384]{1,0:T(8,128)S(1)}, f32[64,384]{1,0:T(8,128)}, u32[]{:S(2)}) copy-start(f32[64,384]{1,0:T(8,128)} %points_ref.3) | copy-start | bytes 294916
  2.3 11.7 %collective-permute-start.1 = (f32[72,384]{1,0:T(8,128)S(1)}, f32[72,384]{1,0:T(8,128)S(1)}, u32[]{:S(2)}, u32[]{:S(2)}) collective-permute-start(f32[72,384]{1,0:T(8,128)S(1)} %shard_map.50.refs_0_), channel_id=1, source_target_pairs={{0,16},{1,17},{2,18},{3,19},{4,20},{5,21},{6,22},{7,23},{8,24},{9,... | collective-permute-start | bytes 331784 | tf_op jit(solution)/shard_map/ppermute | solution.py:48
  6.3 7.7 %collective-permute-start.4 = (f32[72,384]{1,0:T(8,128)S(1)}, f32[72,384]{1,0:T(8,128)S(1)}, u32[]{:S(2)}, u32[]{:S(2)}) collective-permute-start(f32[72,384]{1,0:T(8,128)S(1)} %shard_map.50.refs_0_), channel_id=1, source_target_pairs={{0,8},{1,9},{2,10},{3,11},{4,12},{5,13},{6,14},{7,15},{8,0},{9,1},... | collective-permute-start | bytes 331784 | tf_op jit(solution)/shard_map/ppermute | solution.py:48
  7.9 5.2 %collective-permute-start.5 = (f32[64,384]{1,0:T(8,128)S(1)}, f32[64,384]{1,0:T(8,128)S(1)}, u32[]{:S(2)}, u32[]{:S(2)}) collective-permute-start(f32[64,384]{1,0:T(8,128)S(1)} %copy-done), channel_id=1, source_target_pairs={{0,2},{1,5},{2,0},{3,7},{4,6},{5,1},{6,4},{7,3},{8,10},{9,13},{10,... | collective-permute-start | bytes 294920 | tf_op jit(solution)/shard_map/ppermute | solution.py:48
  9.4 4.6 %collective-permute-start = (f32[64,384]{1,0:T(8,128)S(1)}, f32[64,384]{1,0:T(8,128)S(1)}, u32[]{:S(2)}, u32[]{:S(2)}) collective-permute-start(f32[64,384]{1,0:T(8,128)S(1)} %copy-done), channel_id=1, source_target_pairs={{0,4},{1,3},{2,6},{3,1},{4,0},{5,7},{6,2},{7,5},{8,12},{9,11},{10,... | collective-permute-start | bytes 294920 | tf_op jit(solution)/shard_map/ppermute | solution.py:48
  14.0 1.1 %copy-start.3 = (f32[384,384]{1,0:T(8,128)S(1)}, f32[384,384]{1,0:T(8,128)}, u32[]{:S(2)}) copy-start(f32[384,384]{1,0:T(8,128)} %refs_6_.1) | copy-start | bytes 1769476
  16.1 5.5 %collective-permute-start.7 = (f32[216,384]{1,0:T(8,128)S(1)}, f32[216,384]{1,0:T(8,128)S(1)}, u32[]{:S(2)}, u32[]{:S(2)}) collective-permute-start(f32[216,384]{1,0:T(8,128)S(1)} %get-tuple-element.14.refs_4_), channel_id=1, source_target_pairs={{0,1},{1,0},{2,3},{3,2},{4,5},{5,4},{6,7},{7,6},{8,9},{9,8},{10,11... | collective-permute-start | bytes 995336 | tf_op jit(solution)/shard_map/ppermute | solution.py:48
  16.2 5.5 %collective-permute-start.2 = (f32[72,384]{1,0:T(8,128)S(1)}, f32[72,384]{1,0:T(8,128)S(1)}, u32[]{:S(2)}, u32[]{:S(2)}) collective-permute-start(f32[72,384]{1,0:T(8,128)S(1)} %collective-permute-done.1.refs_1_), channel_id=1, source_target_pairs={{0,8},{1,9},{2,10},{3,11},{4,12},{5,13},{6,14},{7,15},{8,0},{9,1},... | collective-permute-start | bytes 331784 | tf_op jit(solution)/shard_map/ppermute | solution.py:48
  16.7 5.0 %collective-permute-start.6 = (f32[64,384]{1,0:T(8,128)S(1)}, f32[64,384]{1,0:T(8,128)S(1)}, u32[]{:S(2)}, u32[]{:S(2)}) collective-permute-start(f32[64,384]{1,0:T(8,128)S(1)} %collective-permute-done.5.refs_3_.refs_1_), channel_id=1, source_target_pairs={{0,4},{1,3},{2,6},{3,1},{4,0},{5,7},{6,2},{7,5},{8,12},{9,11},{10,... | collective-permute-start | bytes 294920 | tf_op jit(solution)/shard_map/ppermute | solution.py:48
  21.7 1.3 %collective-permute-start.3 = (f32[72,384]{1,0:T(8,128)S(1)}, f32[72,384]{1,0:T(8,128)S(1)}, u32[]{:S(2)}, u32[]{:S(2)}) collective-permute-start(f32[72,384]{1,0:T(8,128)S(1)} %collective-permute-done.2.refs_2_), channel_id=1, source_target_pairs={{0,1},{1,0},{2,3},{3,2},{4,5},{5,4},{6,7},{7,6},{8,9},{9,8},{10,11... | collective-permute-start | bytes 331784 | tf_op jit(solution)/shard_map/ppermute | solution.py:48
  23.0 2.8 %copy-start.1 = (f32[64,384]{1,0:T(8,128)S(1)}, f32[64,384]{1,0:T(8,128)}, u32[]{:S(2)}) copy-start(f32[64,384]{1,0:T(8,128)} %points_ref.3) | copy-start | bytes 294916
  23.7 5.7 %collective-permute-start.9 = (f32[128,384]{1,0:T(8,128)S(1)}, f32[128,384]{1,0:T(8,128)S(1)}, u32[]{:S(2)}, u32[]{:S(2)}) collective-permute-start(f32[128,384]{1,0:T(8,128)S(1)} %get-tuple-element.21), channel_id=1, source_target_pairs={{0,2},{1,5},{2,0},{3,7},{4,6},{5,1},{6,4},{7,3},{8,10},{9,13},{10,... | collective-permute-start | bytes 589832 | tf_op jit(solution)/shard_map/ppermute | solution.py:48
  24.4 7.2 %collective-permute-start.8 = (f32[128,384]{1,0:T(8,128)S(1)}, f32[128,384]{1,0:T(8,128)S(1)}, u32[]{:S(2)}, u32[]{:S(2)}) collective-permute-start(f32[128,384]{1,0:T(8,128)S(1)} %get-tuple-element.19), channel_id=1, source_target_pairs={{0,2},{1,5},{2,0},{3,7},{4,6},{5,1},{6,4},{7,3},{8,10},{9,13},{10,... | collective-permute-start | bytes 589832 | tf_op jit(solution)/shard_map/ppermute | solution.py:48
  29.5 5.7 %collective-permute-start.10 = (f32[128,384]{1,0:T(8,128)S(1)}, f32[128,384]{1,0:T(8,128)S(1)}, u32[]{:S(2)}, u32[]{:S(2)}) collective-permute-start(f32[128,384]{1,0:T(8,128)S(1)} %add.22), channel_id=1, source_target_pairs={{0,4},{1,3},{2,6},{3,1},{4,0},{5,7},{6,2},{7,5},{8,12},{9,11},{10,... | collective-permute-start | bytes 589832 | tf_op jit(solution)/shard_map/ppermute | solution.py:48
  35.9 1.5 %collective-permute-start.11 = (f32[384,128]{1,0:T(8,128)S(1)}, f32[384,128]{1,0:T(8,128)S(1)}, u32[]{:S(2)}, u32[]{:S(2)}) collective-permute-start(f32[384,128]{1,0:T(8,128)S(1)} %get-tuple-element.23), channel_id=1, source_target_pairs={{0,1},{1,0},{2,3},{3,2},{4,5},{5,4},{6,7},{7,6},{8,9},{9,8},{10,11... | collective-permute-start | bytes 589832 | tf_op jit(solution)/shard_map/ppermute | solution.py:48
  37.4 5.7 %collective-permute-start.12 = (f32[384,128]{1,0:T(8,128)S(1)}, f32[384,128]{1,0:T(8,128)S(1)}, u32[]{:S(2)}, u32[]{:S(2)}) collective-permute-start(f32[384,128]{1,0:T(8,128)S(1)} %add.23), channel_id=1, source_target_pairs={{0,2},{1,9},{2,0},{3,11},{4,6},{5,13},{6,4},{7,15},{8,10},{9,1},{1... | collective-permute-start | bytes 589832 | tf_op jit(solution)/shard_map/ppermute | solution.py:48
  43.2 5.7 %collective-permute-start.13 = (f32[384,128]{1,0:T(8,128)S(1)}, f32[384,128]{1,0:T(8,128)S(1)}, u32[]{:S(2)}, u32[]{:S(2)}) collective-permute-start(f32[384,128]{1,0:T(8,128)S(1)} %add.24), channel_id=1, source_target_pairs={{0,4},{1,17},{2,6},{3,19},{4,0},{5,21},{6,2},{7,23},{8,12},{9,25},... | collective-permute-start | bytes 589832 | tf_op jit(solution)/shard_map/ppermute | solution.py:48
  48.9 5.7 %collective-permute-start.14 = (f32[384,128]{1,0:T(8,128)S(1)}, f32[384,128]{1,0:T(8,128)S(1)}, u32[]{:S(2)}, u32[]{:S(2)}) collective-permute-start(f32[384,128]{1,0:T(8,128)S(1)} %add.25), channel_id=1, source_target_pairs={{0,8},{1,3},{2,10},{3,1},{4,12},{5,7},{6,14},{7,5},{8,0},{9,11},{1... | collective-permute-start | bytes 589832 | tf_op jit(solution)/shard_map/ppermute | solution.py:48
  54.7 8.7 %collective-permute-start.15 = (f32[384,128]{1,0:T(8,128)S(1)}, f32[384,128]{1,0:T(8,128)S(1)}, u32[]{:S(2)}, u32[]{:S(2)}) collective-permute-start(f32[384,128]{1,0:T(8,128)S(1)} %add.26), channel_id=1, source_target_pairs={{0,16},{1,5},{2,18},{3,7},{4,20},{5,1},{6,22},{7,3},{8,24},{9,13},... | collective-permute-start | bytes 589832 | tf_op jit(solution)/shard_map/ppermute | solution.py:48
  63.4 1.5 %collective-permute-start.16 = (f32[384,128]{1,0:T(8,128)S(1)}, f32[384,128]{1,0:T(8,128)S(1)}, u32[]{:S(2)}, u32[]{:S(2)}) collective-permute-start(f32[384,128]{1,0:T(8,128)S(1)} %add.27.keep_ref), channel_id=1, source_target_pairs={{0,1},{1,0},{2,3},{3,2},{4,5},{5,4},{6,7},{7,6},{8,9},{9,8},{10,11... | collective-permute-start | bytes 589832 | tf_op jit(solution)/shard_map/ppermute | solution.py:48

commit v4 on v3

--- a/solution.py
+++ b/solution.py
@@ -71,13 +71,36 @@
     outs_n = coeffs.shape[1]
     extra = round_up(outs_n + 1, 8)
 
-    def body(points_ref, cols_ref, out_ref):
-        out_ref[0:rows, :] = points_ref[...]
-        out_ref[rows:, :] = jnp.zeros((extra, width), F32)
-        cols = cols_ref[...]
-        out_ref[rows : rows + outs_n, 0 : 2 * rows] = jnp.concatenate([cols, cols], axis=1)
-
-    return call(body, shape(rows + extra, width), [points, coeffs.T], 1)
+    def body(points_ref, cols_ref, plain_ref, packed_ref, cols_held, sems):
+        copies = [
+            pltpu.make_async_copy(points_ref, plain_ref, sems.at[0]),
+            pltpu.make_async_copy(cols_ref, cols_held, sems.at[1]),
+        ]
+        for copy in copies:
+            copy.start()
+        packed_ref[rows:, :] = jnp.zeros((extra, width), F32)
+        copies[1].wait()
+        cols = cols_held[...]
+        packed_ref[rows : rows + outs_n, 0 : 2 * rows] = jnp.concatenate([cols, cols], axis=1)
+        copies[0].wait()
+        packed_ref[0:rows, :] = plain_ref[...]
+
+    return pl.pallas_call(
+        body,
+        out_shape=(shape(rows, width), shape(rows + extra, width)),
+        in_specs=[pl.BlockSpec(memory_space=pl.ANY)] * 2,
+        out_specs=(pl.BlockSpec(memory_space=pltpu.VMEM),) * 2,
+        scratch_shapes=[pltpu.VMEM((outs_n, rows), F32), pltpu.SemaphoreType.DMA((2,))],
+    )(points, coeffs.T)
+
+
+def metric_halves(metric):
+    width = metric.shape[0]
+
+    def body(metric_ref, out_ref):
+        out_ref[...] = right(metric_ref[...], axis=0)
+
+    return call(body, jax.ShapeDtypeStruct((3 * width, width), BF16), [metric], 1)
 
 
 def norm_rows(centers, metric3, own):
@@ -89,15 +112,14 @@
     ]
 
 
-def join_blocks(packed, queries, metric, own, outs_n):
+def join_blocks(packed, queries, metric3, own, outs_n):
     height, width = packed[0].shape
     blocks, count = len(packed), len(queries)
 
     def body(*refs):
         packed_refs, query_refs = refs[:blocks], refs[blocks : blocks + count]
-        metric_ref, joined_ref, mapped_ref, metric3_ref = refs[blocks + count :]
-        metric3 = right(metric_ref[...], axis=0)
-        metric3_ref[...] = metric3
+        metric3_ref, joined_ref, mapped_ref = refs[blocks + count :]
+        metric3 = metric3_ref[...]
         query_x = jnp.concatenate([ref[...] for ref in query_refs], axis=0)
         mapped_ref[...] = mul(left(query_x), metric3)
         doubled = []
@@ -109,9 +131,9 @@
             row = k * height + own + outs_n
             joined_ref[row : row + 1, 0 : 2 * own] = norm
 
-    out = (shape(blocks * height, width), shape(count * own, width), jax.ShapeDtypeStruct((3 * width, width), BF16))
+    out = (shape(blocks * height, width), shape(count * own, width))
     flops = 6 * (2 * blocks + count) * own * width * width
-    return call(body, out, list(packed) + list(queries) + [metric], flops)
+    return call(body, out, list(packed) + list(queries) + [metric3], flops)
 
 
 def center_terms(refs, own, outs_n, metric3=None):
@@ -226,6 +248,50 @@
 
     out = shape(half * tile, tile)
     return call(body, (out, out), [part, arrived, metric3], 12 * part.shape[0] * width * width)
+
+
+def plane_place(k):
+    row, odd = lax.axis_index("row") & 3, lax.axis_index("col") & 1
+    if k in (1, 2):
+        return row ^ jnp.where(odd == 1, 3 - k, k)
+    return row ^ k
+
+
+def quarter(ref, k):
+    rows = ref.shape[0] // 4
+    return pl.ds(pl.multiple_of(plane_place(k) * rows, rows), rows)
+
+
+def split_quarters(kept, arrived):
+    rows, width = kept.shape
+
+    def body(kept_ref, arrived_ref, *out_refs):
+        for k in range(4):
+            place = quarter(kept_ref, k)
+            out_refs[k][...] = kept_ref[place, :] + arrived_ref[place, :]
+
+    return call(body, (shape(rows // 4, width),) * 4, [kept, arrived], 1)
+
+
+def join_quarters(parts):
+    rows, width = parts[0].shape
+
+    def body(*refs):
+        out_ref = refs[-1]
+        for k in range(4):
+            out_ref[quarter(out_ref, k), :] = refs[k][...]
+
+    return call(body, shape(4 * rows, width), parts, 1)
+
+
+def add_all(parts):
+    def body(*refs):
+        values = [ref[...] for ref in refs[:-1]]
+        while len(values) > 1:
+            values = [a + b for a, b in zip(values[::2], values[1::2])]
+        refs[-1][...] = values[0]
+
+    return call(body, shape(*parts[0].shape), parts, 1)
 
 
 def finish(keep, other, points):
@@ -269,6 +335,15 @@
     def to_b(value):
         return hop(value, (bit_b, 0), (bit_a, 0))
 
+    def in_plane(parts):
+        return [to_a(parts[0]), to_b(parts[1]), hop(parts[2], (bit_a | bit_b, 0))]
+
+    def among(value, shifts):
+        steps = [(0, 0)]
+        for dr, dc in shifts:
+            steps = steps + [(r | dr, c | dc) for r, c in steps]
+        return [value] + [hop(value, step) for step in steps[1:]]
+
     def over_cols(block):
         have = [block]
         for bit in col_bits:
@@ -278,14 +353,16 @@
     def local(points, coeffs, metric):
         own, width = points.shape
         outs_n = coeffs.shape[1]
-        have = [pack_own(points, coeffs)]
+        points, packed = pack_own(points, coeffs)
+        metric3 = metric_halves(metric)
+        have = [packed]
         for bit in reversed(line_bits):
             have = have + [hop(piece, (bit, 0)) for piece in have]
         from_a = to_a(points)
         from_b = to_b(points)
         from_ab = to_b(from_a)
         queries = [from_ab, from_a, from_b, points]
-        joined, mapped, metric3 = join_blocks(have[:-1], queries[1:], metric, own, outs_n)
+        joined, mapped = join_blocks(have[:-1], queries[1:], metric3, own, outs_n)
         early, late = over_cols(joined), over_cols(have[-1])
         total, mapped_ab = early_sums(queries, mapped, metric3, early, outs_n)
         part_ab, part_a = late_sums(
@@ -296,13 +373,13 @@
         sent_b = to_b(part_b + sent_ab)
 
         keep, send = outer_halves(part_own + sent_a, sent_b, metric3)
-        keep = keep + hop(send, (0, 1))
-        rest = [(bit, 0) for bit in row_bits]
-        turn = len(rest) // 2
-        for even_hop, odd_hop in zip(rest, rest[turn:] + rest[:turn]):
-            keep = keep + hop(keep, even_hop, odd_hop)
+        parts = split_quarters(keep, hop(send, (0, 1)))
+        total = add_all([parts[0]] + in_plane(parts[1:]))
+        for k in range(0, len(line_bits), 2):
+            total = add_all(among(total, [(bit, 0) for bit in line_bits[k : k + 2]]))
         for bit in col_bits[1:]:
-            keep = keep + hop(keep, (0, bit))
+            total = add_all(among(total, [(0, bit)]))
+        keep = join_quarters([total] + in_plane([total] * 3))
         return finish(keep, hop(keep, (0, 1)), points)
 
     return local

time: 66.3 us -> 61.5 us (0.928)
  waiting for transfers between devices: 37.7 us -> 25.9 us
  starting transfers between devices: 19.2 us -> 26.2 us
  Pallas kernels: 5.66 us -> 7.35 us
  local copies, waits for them, and re-layouts: 2.63 us -> 1.07 us
    ppermute x17 -> x22, waiting for transfers between devices: 37.7 us -> 25.9 us  [hop(): return lax.ppermute(value, AXES, pairs)]
    ppermute x17 -> x22, starting transfers between devices: 19.2 us -> 26.2 us  [hop(): return lax.ppermute(value, AXES, pairs)]
    pallas_call x0 -> x1, Pallas kernels: none -> 1.59 us  [pack_own(): pl.pallas_call(body, out_shape=(shape(rows, width), shape(rows + extra, w...]
    unnamed x8 -> x6, local copies, waits for them, and re-layouts: 2.63 us -> 1.07 us
    pallas_call x7 -> x11, Pallas kernels: 5.66 us -> 5.76 us  [call(): pl.pallas_call(body, out_shape=out_shape, in_specs=[pl.BlockSpec(memory_s...]
  transfers between devices with their start and end apart: 17 -> 22, of which waited for: 12 -> 16; matrix products, arithmetic and copies ran while one was open for 0% -> 0% of each run, Pallas kernels for 3% -> 3%
where the time goes in v4:
time: 61.5 us; the launch traced here: 61.3 us
  starting transfers between devices  26.2 us (43%)
  waiting for transfers between devices  25.9 us (42%)
  Pallas kernels  7.35 us (12%)
  local copies, waits for them, and re-layouts  1.07 us (2%)
  between operations  0.76 us (1%)
    ppermute x22, starting transfers between devices, hop(): return lax.ppermute(value, AXES, pairs)  26.2 us
    ppermute x22, waiting for transfers between devices, hop(): return lax.ppermute(value, AXES, pairs)  25.9 us
    pallas_call x11, Pallas kernels, call(): pl.pallas_call(body, out_shape=out_shape, in_specs=[pl.BlockSpec(memory_s...  5.76 us
    pallas_call x1, Pallas kernels, pack_own(): pl.pallas_call(body, out_shape=(shape(rows, width), shape(rows + extra, w...  1.59 us
  transfers between devices with their start and end apart: 22, of which 16 were waited for; matrix products, arithmetic and copies ran while one was open for 0% of the time, Pallas kernels for 3%

profile of v4, /device:TPU:0, one launch (start us, length us, event | category | flops | bytes accessed | tf_op | source)
XLA Modules:
  0.0 61.3 jit_solution(4012798669841976700)
XLA Ops:
  0.6 1.6 %shard_map.50 = (f32[64,384]{1,0:T(8,128)}, f32[72,384]{1,0:T(8,128)}) custom-call(f32[64,384]{1,0:T(8,128)} %points_ref.1, f32[2,64]{1,0:T(2,128)} %bitcast.1), custom_call_target="tpu_custom_call" | custom-call | tf_op jit(solution)/shard_map/pallas_call | solution.py:88
  2.2 4.1 %collective-permute-start.1 = (f32[72,384]{1,0:T(8,128)}, f32[72,384]{1,0:T(8,128)S(1)}, u32[]{:S(2)}, u32[]{:S(2)}) collective-permute-start(f32[72,384]{1,0:T(8,128)} %get-tuple-element.19.refs_0_), channel_id=1, source_target_pairs={{0,16},{1,17},{2,18},{3,19},{4,20},{5,21},{6,22},{7,23},{8,24},{9,... | collective-permute-start | bytes 331784 | tf_op jit(solution)/shard_map/ppermute | solution.py:48
  6.3 1.6 %collective-permute-start.4 = (f32[72,384]{1,0:T(8,128)}, f32[72,384]{1,0:T(8,128)S(1)}, u32[]{:S(2)}, u32[]{:S(2)}) collective-permute-start(f32[72,384]{1,0:T(8,128)} %get-tuple-element.19.refs_0_), channel_id=1, source_target_pairs={{0,8},{1,9},{2,10},{3,11},{4,12},{5,13},{6,14},{7,15},{8,0},{9,1},... | collective-permute-start | bytes 331784 | tf_op jit(solution)/shard_map/ppermute | solution.py:48
  7.9 0.0 copy-start
  7.9 1.5 %collective-permute-start.5 = (f32[64,384]{1,0:T(8,128)}, f32[64,384]{1,0:T(8,128)S(1)}, u32[]{:S(2)}, u32[]{:S(2)}) collective-permute-start(f32[64,384]{1,0:T(8,128)} %get-tuple-element.18.refs_5_.refs_3_.refs_1_.points_ref), channel_id=1, source_target_pairs={{0,2},{1,5},{2,0},{3,7},{4,6},{5,1},{6,4},{7,3},{8,10},{9,13},{10,... | collective-permute-start | bytes 294920 | tf_op jit(solution)/shard_map/ppermute | solution.py:48
  9.4 1.5 %collective-permute-start = (f32[64,384]{1,0:T(8,128)}, f32[64,384]{1,0:T(8,128)S(1)}, u32[]{:S(2)}, u32[]{:S(2)}) collective-permute-start(f32[64,384]{1,0:T(8,128)} %get-tuple-element.18.refs_5_.refs_3_.refs_1_.points_ref), channel_id=1, source_target_pairs={{0,4},{1,3},{2,6},{3,1},{4,0},{5,7},{6,2},{7,5},{8,12},{9,11},{10,... | collective-permute-start | bytes 294920 | tf_op jit(solution)/shard_map/ppermute | solution.py:48
  10.9 0.0 copy-start.1
  10.9 1.1 %copy-done.1 = f32[384,384]{1,0:T(8,128)S(1)} copy-done((f32[384,384]{1,0:T(8,128)S(1)}, f32[384,384]{1,0:T(8,128)}, u32[]{:S(2)}) %copy-start.1) | copy-done | bytes 589848
  12.0 0.0 copy-start.2
  12.0 0.1 shard_map.51.refs_6_.refs_7_.metric3_ref
  12.1 1.2 %collective-permute-done.5.refs_3_.refs_1_ = f32[64,384]{1,0:T(8,128)S(1)} collective-permute-done((f32[64,384]{1,0:T(8,128)}, f32[64,384]{1,0:T(8,128)S(1)}, u32[]{:S(2)}, u32[]{:S(2)}) %collective-permute-start.5) | collective-permute-done | bytes 98336 | tf_op jit(solution)/shard_map/ppermute | solution.py:48
  13.3 0.9 %collective-permute-done.refs_4_.refs_2_.refs_0_ = f32[64,384]{1,0:T(8,128)S(1)} collective-permute-done((f32[64,384]{1,0:T(8,128)}, f32[64,384]{1,0:T(8,128)S(1)}, u32[]{:S(2)}, u32[]{:S(2)}) %collective-permute-start) | collective-permute-done | bytes 98336 | tf_op jit(solution)/shard_map/ppermute | solution.py:48
  14.2 0.0 collective-permute-done.1.refs_1_
  14.2 0.0 collective-permute-done.4.refs_2_
  14.2 0.0 copy-done
  14.2 0.0 copy-done.2
  14.2 1.0 %shard_map.52 = (f32[216,384]{1,0:T(8,128)S(1)}, f32[192,384]{1,0:T(8,128)S(1)}) custom-call(f32[72,384]{1,0:T(8,128)S(1)} %copy-done.2, f32[72,384]{1,0:T(8,128)S(1)} %collective-permute-done.1.refs_1_, f32[72,384]{1,0:T(8,128)S(1)} %collective-permute-done.4.refs_2_, f32[64,384]{1,0:T(8,128)S(1)} %collective-permute-done.5.refs_3_.refs_1_, ...), custom_call_target="tpu_custom_call" | custom-call | flops 509607936 | bytes 3022848 | tf_op jit(solution)/shard_map/pallas_call | solution.py:55
  15.3 0.1 collective-permute-start.7
  15.3 0.5 collective-permute-start.2
  15.8 1.5 %collective-permute-start.6 = (f32[64,384]{1,0:T(8,128)S(1)}, f32[64,384]{1,0:T(8,128)S(1)}, u32[]{:S(2)}, u32[]{:S(2)}) collective-permute-start(f32[64,384]{1,0:T(8,128)S(1)} %collective-permute-done.5.refs_3_.refs_1_), channel_id=1, source_target_pairs={{0,4},{1,3},{2,6},{3,1},{4,0},{5,7},{6,2},{7,5},{8,12},{9,11},{10,... | collective-permute-start | bytes 294920 | tf_op jit(solution)/shard_map/ppermute | solution.py:48
  17.4 3.4 %collective-permute-done.2.refs_2_ = f32[72,384]{1,0:T(8,128)S(1)} collective-permute-done((f32[72,384]{1,0:T(8,128)S(1)}, f32[72,384]{1,0:T(8,128)S(1)}, u32[]{:S(2)}, u32[]{:S(2)}) %collective-permute-start.2) | collective-permute-done | bytes 110624 | tf_op jit(solution)/shard_map/ppermute | solution.py:48
  20.8 0.0 collective-permute-start.3
  20.8 0.0 collective-permute-done.6.refs_0_
  20.8 0.0 collective-permute-done.7.refs_5_
  20.8 1.3 %shard_map.53 = (f32[2,256,384]{2,1,0:T(8,128)S(1)}, f32[64,384]{1,0:T(8,128)S(1)}) custom-call(f32[64,384]{1,0:T(8,128)S(1)} %collective-permute-done.6.refs_0_, f32[64,384]{1,0:T(8,128)S(1)} %collective-permute-done.5.refs_3_.refs_1_, f32[64,384]{1,0:T(8,128)S(1)} %collective-permute-done.refs_4_.refs_2_.refs_0_, f32[64,384]{1,0:T(8,128)S(1)} %copy-done, ...), custom_call_target="tpu_custom_call" | custom-call | flops 481296384 | bytes 4005888 | tf_op jit(solution)/shard_map/pallas_call | solution.py:55
  22.1 0.0 collective-permute-done.3.refs_3_
  22.1 0.7 %shard_map.55 = (f32[128,384]{1,0:T(8,128)S(1)}, f32[128,384]{1,0:T(8,128)S(1)}) custom-call(f32[64,384]{1,0:T(8,128)S(1)} %collective-permute-done.6.refs_0_, f32[64,384]{1,0:T(8,128)S(1)} %collective-permute-done.5.refs_3_.refs_1_, f32[72,384]{1,0:T(8,128)S(1)} %collective-permute-done.2.refs_2_, f32[72,384]{1,0:T(8,128)S(1)} %collective-permute-done.3.refs_3_, ...), custom_call_target="tpu_custom_call" | custom-call | flops 198180864 | bytes 3760128 | tf_op jit(solution)/shard_map/pallas_call | solution.py:55
  22.8 0.7 %collective-permute-start.9 = (f32[128,384]{1,0:T(8,128)S(1)}, f32[128,384]{1,0:T(8,128)S(1)}, u32[]{:S(2)}, u32[]{:S(2)}) collective-permute-start(f32[128,384]{1,0:T(8,128)S(1)} %get-tuple-element.27), channel_id=1, source_target_pairs={{0,2},{1,5},{2,0},{3,7},{4,6},{5,1},{6,4},{7,3},{8,10},{9,13},{10,... | collective-permute-start | bytes 589832 | tf_op jit(solution)/shard_map/ppermute | solution.py:48
  23.5 1.4 %collective-permute-start.8 = (f32[128,384]{1,0:T(8,128)S(1)}, f32[128,384]{1,0:T(8,128)S(1)}, u32[]{:S(2)}, u32[]{:S(2)}) collective-permute-start(f32[128,384]{1,0:T(8,128)S(1)} %get-tuple-element.25), channel_id=1, source_target_pairs={{0,2},{1,5},{2,0},{3,7},{4,6},{5,1},{6,4},{7,3},{8,10},{9,13},{10,... | collective-permute-start | bytes 589832 | tf_op jit(solution)/shard_map/ppermute | solution.py:48
  24.9 0.7 %shard_map.54 = (f32[128,384]{1,0:T(8,128)S(1)}, f32[128,384]{1,0:T(8,128)S(1)}) custom-call(f32[64,384]{1,0:T(8,128)S(1)} %collective-permute-done.refs_4_.refs_2_.refs_0_, f32[64,384]{1,0:T(8,128)S(1)} %copy-done, f32[72,384]{1,0:T(8,128)S(1)} %collective-permute-done.2.refs_2_, f32[72,384]{1,0:T(8,128)S(1)} %collective-permute-done.3.refs_3_, ...), custom_call_target="tpu_custom_call" | custom-call | flops 198180864 | bytes 3661824 | tf_op jit(solution)/shard_map/pallas_call | solution.py:55
  25.6 2.9 %collective-permute-done.9 = f32[128,384]{1,0:T(8,128)S(1)} collective-permute-done((f32[128,384]{1,0:T(8,128)S(1)}, f32[128,384]{1,0:T(8,128)S(1)}, u32[]{:S(2)}, u32[]{:S(2)}) %collective-permute-start.9) | collective-permute-done | bytes 196640 | tf_op jit(solution)/shard_map/ppermute | solution.py:48
  28.6 1.6 %collective-permute-start.10 = (f32[128,384]{1,0:T(8,128)S(1)}, f32[128,384]{1,0:T(8,128)S(1)}, u32[]{:S(2)}, u32[]{:S(2)}) collective-permute-start(f32[128,384]{1,0:T(8,128)S(1)} %add.7), channel_id=1, source_target_pairs={{0,4},{1,3},{2,6},{3,1},{4,0},{5,7},{6,2},{7,5},{8,12},{9,11},{10,... | collective-permute-start | bytes 589832 | tf_op jit(solution)/shard_map/ppermute | solution.py:48
  30.2 0.5 collective-permute-done.8
  30.7 3.6 %collective-permute-done.10.arrived_ref = f32[128,384]{1,0:T(8,128)S(1)} collective-permute-done((f32[128,384]{1,0:T(8,128)S(1)}, f32[128,384]{1,0:T(8,128)S(1)}, u32[]{:S(2)}, u32[]{:S(2)}) %collective-permute-start.10) | collective-permute-done | bytes 196640 | tf_op jit(solution)/shard_map/ppermute | solution.py:48
  34.3 0.6 %shard_map.56 = (f32[384,128]{1,0:T(8,128)S(1)}, f32[384,128]{1,0:T(8,128)S(1)}) custom-call(f32[128,384]{1,0:T(8,128)S(1)} %add.6.part_ref, f32[128,384]{1,0:T(8,128)S(1)} %collective-permute-done.10.arrived_ref, bf16[1152,384]{1,0:T(8,128)(2,1)S(1)} %shard_map.51.refs_6_.refs_7_.metric3_ref), custom_call_target="tpu_custom_call" | custom-call | flops 226492416 | bytes 2555904 | tf_op jit(solution)/shard_map/pallas_call | solution.py:55
  35.0 0.1 collective-permute-start.11
  35.1 1.4 %collective-permute-done.11.arrived_ref = f32[384,128]{1,0:T(8,128)S(1)} collective-permute-done((f32[384,128]{1,0:T(8,128)S(1)}, f32[384,128]{1,0:T(8,128)S(1)}, u32[]{:S(2)}, u32[]{:S(2)}) %collective-permute-start.11) | collective-permute-done | bytes 196640 | tf_op jit(solution)/shard_map/ppermute | solution.py:48
  36.5 0.7 %collective-permute-start.12 = (f32[96,128]{1,0:T(8,128)S(1)}, f32[96,128]{1,0:T(8,128)S(1)}, u32[]{:S(2)}, u32[]{:S(2)}) collective-permute-start(f32[96,128]{1,0:T(8,128)S(1)} %get-tuple-element.31), channel_id=1, source_target_pairs={{0,2},{1,5},{2,0},{3,7},{4,6},{5,1},{6,4},{7,3},{8,10},{9,13},{10,... | collective-permute-start | bytes 147464 | tf_op jit(solution)/shard_map/ppermute | solution.py:48
  37.2 1.5 %collective-permute-start.13 = (f32[96,128]{1,0:T(8,128)S(1)}, f32[96,128]{1,0:T(8,128)S(1)}, u32[]{:S(2)}, u32[]{:S(2)}) collective-permute-start(f32[96,128]{1,0:T(8,128)S(1)} %get-tuple-element.32), channel_id=1, source_target_pairs={{0,4},{1,3},{2,6},{3,1},{4,0},{5,7},{6,2},{7,5},{8,12},{9,11},{10,... | collective-permute-start | bytes 147464 | tf_op jit(solution)/shard_map/ppermute | solution.py:48
  38.7 1.4 %collective-permute-start.14 = (f32[96,128]{1,0:T(8,128)S(1)}, f32[96,128]{1,0:T(8,128)S(1)}, u32[]{:S(2)}, u32[]{:S(2)}) collective-permute-start(f32[96,128]{1,0:T(8,128)S(1)} %get-tuple-element.33), channel_id=1, source_target_pairs={{0,6},{1,7},{2,4},{3,5},{4,2},{5,3},{6,0},{7,1},{8,14},{9,15},{10,... | collective-permute-start | bytes 147464 | tf_op jit(solution)/shard_map/ppermute | solution.py:48
  40.1 0.8 %collective-permute-done.12.refs_1_ = f32[96,128]{1,0:T(8,128)S(1)} collective-permute-done((f32[96,128]{1,0:T(8,128)S(1)}, f32[96,128]{1,0:T(8,128)S(1)}, u32[]{:S(2)}, u32[]{:S(2)}) %collective-permute-start.12) | collective-permute-done | bytes 49184 | tf_op jit(solution)/shard_map/ppermute | solution.py:48
  40.9 0.4 collective-permute-done.13.refs_2_
  41.3 2.4 %collective-permute-done.14.refs_3_ = f32[96,128]{1,0:T(8,128)S(1)} collective-permute-done((f32[96,128]{1,0:T(8,128)S(1)}, f32[96,128]{1,0:T(8,128)S(1)}, u32[]{:S(2)}, u32[]{:S(2)}) %collective-permute-start.14) | collective-permute-done | bytes 49184 | tf_op jit(solution)/shard_map/ppermute | solution.py:48
  43.7 1.3 %collective-permute-start.15 = (f32[96,128]{1,0:T(8,128)S(1)}, f32[96,128]{1,0:T(8,128)S(1)}, u32[]{:S(2)}, u32[]{:S(2)}) collective-permute-start(f32[96,128]{1,0:T(8,128)S(1)} %shard_map.58.refs_0_), channel_id=1, source_target_pairs={{0,8},{1,9},{2,10},{3,11},{4,12},{5,13},{6,14},{7,15},{8,0},{9,1},... | collective-permute-start | bytes 147464 | tf_op jit(solution)/shard_map/ppermute | solution.py:48
  44.9 1.6 %collective-permute-start.16 = (f32[96,128]{1,0:T(8,128)S(1)}, f32[96,128]{1,0:T(8,128)S(1)}, u32[]{:S(2)}, u32[]{:S(2)}) collective-permute-start(f32[96,128]{1,0:T(8,128)S(1)} %shard_map.58.refs_0_), channel_id=1, source_target_pairs={{0,16},{1,17},{2,18},{3,19},{4,20},{5,21},{6,22},{7,23},{8,24},{9,... | collective-permute-start | bytes 147464 | tf_op jit(solution)/shard_map/ppermute | solution.py:48
  46.5 1.6 %collective-permute-start.17 = (f32[96,128]{1,0:T(8,128)S(1)}, f32[96,128]{1,0:T(8,128)S(1)}, u32[]{:S(2)}, u32[]{:S(2)}) collective-permute-start(f32[96,128]{1,0:T(8,128)S(1)} %shard_map.58.refs_0_), channel_id=1, source_target_pairs={{0,24},{1,25},{2,26},{3,27},{4,28},{5,29},{6,30},{7,31},{8,16},{9,... | collective-permute-start | bytes 147464 | tf_op jit(solution)/shard_map/ppermute | solution.py:48
  48.1 0.0 collective-permute-done.15.refs_1_
  48.1 2.5 %collective-permute-done.16.refs_2_ = f32[96,128]{1,0:T(8,128)S(1)} collective-permute-done((f32[96,128]{1,0:T(8,128)S(1)}, f32[96,128]{1,0:T(8,128)S(1)}, u32[]{:S(2)}, u32[]{:S(2)}) %collective-permute-start.16) | collective-permute-done | bytes 49184 | tf_op jit(solution)/shard_map/ppermute | solution.py:48
  50.7 1.7 %collective-permute-done.17.refs_3_ = f32[96,128]{1,0:T(8,128)S(1)} collective-permute-done((f32[96,128]{1,0:T(8,128)S(1)}, f32[96,128]{1,0:T(8,128)S(1)}, u32[]{:S(2)}, u32[]{:S(2)}) %collective-permute-start.17) | collective-permute-done | bytes 49184 | tf_op jit(solution)/shard_map/ppermute | solution.py:48
  52.4 0.7 %collective-permute-start.18 = (f32[96,128]{1,0:T(8,128)S(1)}, f32[96,128]{1,0:T(8,128)S(1)}, u32[]{:S(2)}, u32[]{:S(2)}) collective-permute-start(f32[96,128]{1,0:T(8,128)S(1)} %shard_map.59.refs_0_), channel_id=1, source_target_pairs={{0,2},{1,5},{2,0},{3,7},{4,6},{5,1},{6,4},{7,3},{8,10},{9,13},{10,... | collective-permute-start | bytes 147464 | tf_op jit(solution)/shard_map/ppermute | solution.py:48
  53.1 0.5 collective-permute-start.19
  53.6 2.4 %collective-permute-start.20 = (f32[96,128]{1,0:T(8,128)S(1)}, f32[96,128]{1,0:T(8,128)S(1)}, u32[]{:S(2)}, u32[]{:S(2)}) collective-permute-start(f32[96,128]{1,0:T(8,128)S(1)} %shard_map.59.refs_0_), channel_id=1, source_target_pairs={{0,6},{1,7},{2,4},{3,5},{4,2},{5,3},{6,0},{7,1},{8,14},{9,15},{10,... | collective-permute-start | bytes 147464 | tf_op jit(solution)/shard_map/ppermute | solution.py:48
  56.0 0.6 collective-permute-done.18.refs_1_
  56.6 0.6 collective-permute-done.19.refs_2_
  57.2 1.4 %collective-permute-done.20.refs_3_ = f32[96,128]{1,0:T(8,128)S(1)} collective-permute-done((f32[96,128]{1,0:T(8,128)S(1)}, f32[96,128]{1,0:T(8,128)S(1)}, u32[]{:S(2)}, u32[]{:S(2)}) %collective-permute-start.20) | collective-permute-done | bytes 49184 | tf_op jit(solution)/shard_map/ppermute | solution.py:48
  58.6 0.1 collective-permute-start.21
  58.7 1.4 %collective-permute-done.21.other_ref = f32[384,128]{1,0:T(8,128)S(1)} collective-permute-done((f32[384,128]{1,0:T(8,128)S(1)}, f32[384,128]{1,0:T(8,128)S(1)}, u32[]{:S(2)}, u32[]{:S(2)}) %collective-permute-start.21) | collective-permute-done | bytes 196640 | tf_op jit(solution)/shard_map/ppermute | solution.py:48
  60.1 1.2 %shard_map.61 = (f32[384,384]{1,0:T(8,128)}, f32[64,384]{1,0:T(8,128)}) custom-call(f32[384,128]{1,0:T(8,128)S(1)} %shard_map.60.keep_ref, f32[384,128]{1,0:T(8,128)S(1)} %collective-permute-done.21.other_ref, f32[64,384]{1,0:T(8,128)S(1)} %copy-done), custom_call_target="tpu_custom_call" | custom-call | flops 56623104 | bytes 1179648 | tf_op jit(solution)/shard_map/pallas_call | solution.py:55
  (6 shorter events, 0.1 us)
Async XLA Ops:
  2.2 12.0 %collective-permute-start.1 = (f32[72,384]{1,0:T(8,128)}, f32[72,384]{1,0:T(8,128)S(1)}, u32[]{:S(2)}, u32[]{:S(2)}) collective-permute-start(f32[72,384]{1,0:T(8,128)} %get-tuple-element.19.refs_0_), channel_id=1, source_target_pairs={{0,16},{1,17},{2,18},{3,19},{4,20},{5,21},{6,22},{7,23},{8,24},{9,... | collective-permute-start | bytes 331784 | tf_op jit(solution)/shard_map/ppermute | solution.py:48
  6.3 7.9 %collective-permute-start.4 = (f32[72,384]{1,0:T(8,128)}, f32[72,384]{1,0:T(8,128)S(1)}, u32[]{:S(2)}, u32[]{:S(2)}) collective-permute-start(f32[72,384]{1,0:T(8,128)} %get-tuple-element.19.refs_0_), channel_id=1, source_target_pairs={{0,8},{1,9},{2,10},{3,11},{4,12},{5,13},{6,14},{7,15},{8,0},{9,1},... | collective-permute-start | bytes 331784 | tf_op jit(solution)/shard_map/ppermute | solution.py:48
  7.9 6.3 %copy-start = (f32[64,384]{1,0:T(8,128)S(1)}, f32[64,384]{1,0:T(8,128)}, u32[]{:S(2)}) copy-start(f32[64,384]{1,0:T(8,128)} %get-tuple-element.18.refs_5_.refs_3_.refs_1_.points_ref) | copy-start | bytes 294916
  7.9 5.4 %collective-permute-start.5 = (f32[64,384]{1,0:T(8,128)}, f32[64,384]{1,0:T(8,128)S(1)}, u32[]{:S(2)}, u32[]{:S(2)}) collective-permute-start(f32[64,384]{1,0:T(8,128)} %get-tuple-element.18.refs_5_.refs_3_.refs_1_.points_ref), channel_id=1, source_target_pairs={{0,2},{1,5},{2,0},{3,7},{4,6},{5,1},{6,4},{7,3},{8,10},{9,13},{10,... | collective-permute-start | bytes 294920 | tf_op jit(solution)/shard_map/ppermute | solution.py:48
  9.4 4.8 %collective-permute-start = (f32[64,384]{1,0:T(8,128)}, f32[64,384]{1,0:T(8,128)S(1)}, u32[]{:S(2)}, u32[]{:S(2)}) collective-permute-start(f32[64,384]{1,0:T(8,128)} %get-tuple-element.18.refs_5_.refs_3_.refs_1_.points_ref), channel_id=1, source_target_pairs={{0,4},{1,3},{2,6},{3,1},{4,0},{5,7},{6,2},{7,5},{8,12},{9,11},{10,... | collective-permute-start | bytes 294920 | tf_op jit(solution)/shard_map/ppermute | solution.py:48
  10.9 1.1 %copy-start.1 = (f32[384,384]{1,0:T(8,128)S(1)}, f32[384,384]{1,0:T(8,128)}, u32[]{:S(2)}) copy-start(f32[384,384]{1,0:T(8,128)} %metric_ref.1) | copy-start | bytes 1769476
  12.0 2.3 %copy-start.2 = (f32[72,384]{1,0:T(8,128)S(1)}, f32[72,384]{1,0:T(8,128)}, u32[]{:S(2)}) copy-start(f32[72,384]{1,0:T(8,128)} %get-tuple-element.19.refs_0_) | copy-start | bytes 331780
  15.3 5.5 %collective-permute-start.7 = (f32[216,384]{1,0:T(8,128)S(1)}, f32[216,384]{1,0:T(8,128)S(1)}, u32[]{:S(2)}, u32[]{:S(2)}) collective-permute-start(f32[216,384]{1,0:T(8,128)S(1)} %get-tuple-element.21.refs_4_), channel_id=1, source_target_pairs={{0,1},{1,0},{2,3},{3,2},{4,5},{5,4},{6,7},{7,6},{8,9},{9,8},{10,11... | collective-permute-start | bytes 995336 | tf_op jit(solution)/shard_map/ppermute | solution.py:48
  15.3 5.5 %collective-permute-start.2 = (f32[72,384]{1,0:T(8,128)S(1)}, f32[72,384]{1,0:T(8,128)S(1)}, u32[]{:S(2)}, u32[]{:S(2)}) collective-permute-start(f32[72,384]{1,0:T(8,128)S(1)} %collective-permute-done.1.refs_1_), channel_id=1, source_target_pairs={{0,8},{1,9},{2,10},{3,11},{4,12},{5,13},{6,14},{7,15},{8,0},{9,1},... | collective-permute-start | bytes 331784 | tf_op jit(solution)/shard_map/ppermute | solution.py:48
  15.8 5.0 %collective-permute-start.6 = (f32[64,384]{1,0:T(8,128)S(1)}, f32[64,384]{1,0:T(8,128)S(1)}, u32[]{:S(2)}, u32[]{:S(2)}) collective-permute-start(f32[64,384]{1,0:T(8,128)S(1)} %collective-permute-done.5.refs_3_.refs_1_), channel_id=1, source_target_pairs={{0,4},{1,3},{2,6},{3,1},{4,0},{5,7},{6,2},{7,5},{8,12},{9,11},{10,... | collective-permute-start | bytes 294920 | tf_op jit(solution)/shard_map/ppermute | solution.py:48
  20.8 1.3 %collective-permute-start.3 = (f32[72,384]{1,0:T(8,128)S(1)}, f32[72,384]{1,0:T(8,128)S(1)}, u32[]{:S(2)}, u32[]{:S(2)}) collective-permute-start(f32[72,384]{1,0:T(8,128)S(1)} %collective-permute-done.2.refs_2_), channel_id=1, source_target_pairs={{0,1},{1,0},{2,3},{3,2},{4,5},{5,4},{6,7},{7,6},{8,9},{9,8},{10,11... | collective-permute-start | bytes 331784 | tf_op jit(solution)/shard_map/ppermute | solution.py:48
  22.8 5.7 %collective-permute-start.9 = (f32[128,384]{1,0:T(8,128)S(1)}, f32[128,384]{1,0:T(8,128)S(1)}, u32[]{:S(2)}, u32[]{:S(2)}) collective-permute-start(f32[128,384]{1,0:T(8,128)S(1)} %get-tuple-element.27), channel_id=1, source_target_pairs={{0,2},{1,5},{2,0},{3,7},{4,6},{5,1},{6,4},{7,3},{8,10},{9,13},{10,... | collective-permute-start | bytes 589832 | tf_op jit(solution)/shard_map/ppermute | solution.py:48
  23.5 7.2 %collective-permute-start.8 = (f32[128,384]{1,0:T(8,128)S(1)}, f32[128,384]{1,0:T(8,128)S(1)}, u32[]{:S(2)}, u32[]{:S(2)}) collective-permute-start(f32[128,384]{1,0:T(8,128)S(1)} %get-tuple-element.25), channel_id=1, source_target_pairs={{0,2},{1,5},{2,0},{3,7},{4,6},{5,1},{6,4},{7,3},{8,10},{9,13},{10,... | collective-permute-start | bytes 589832 | tf_op jit(solution)/shard_map/ppermute | solution.py:48
  28.6 5.7 %collective-permute-start.10 = (f32[128,384]{1,0:T(8,128)S(1)}, f32[128,384]{1,0:T(8,128)S(1)}, u32[]{:S(2)}, u32[]{:S(2)}) collective-permute-start(f32[128,384]{1,0:T(8,128)S(1)} %add.7), channel_id=1, source_target_pairs={{0,4},{1,3},{2,6},{3,1},{4,0},{5,7},{6,2},{7,5},{8,12},{9,11},{10,... | collective-permute-start | bytes 589832 | tf_op jit(solution)/shard_map/ppermute | solution.py:48
  35.0 1.5 %collective-permute-start.11 = (f32[384,128]{1,0:T(8,128)S(1)}, f32[384,128]{1,0:T(8,128)S(1)}, u32[]{:S(2)}, u32[]{:S(2)}) collective-permute-start(f32[384,128]{1,0:T(8,128)S(1)} %get-tuple-element.29), channel_id=1, source_target_pairs={{0,1},{1,0},{2,3},{3,2},{4,5},{5,4},{6,7},{7,6},{8,9},{9,8},{10,11... | collective-permute-start | bytes 589832 | tf_op jit(solution)/shard_map/ppermute | solution.py:48
  36.5 4.4 %collective-permute-start.12 = (f32[96,128]{1,0:T(8,128)S(1)}, f32[96,128]{1,0:T(8,128)S(1)}, u32[]{:S(2)}, u32[]{:S(2)}) collective-permute-start(f32[96,128]{1,0:T(8,128)S(1)} %get-tuple-element.31), channel_id=1, source_target_pairs={{0,2},{1,5},{2,0},{3,7},{4,6},{5,1},{6,4},{7,3},{8,10},{9,13},{10,... | collective-permute-start | bytes 147464 | tf_op jit(solution)/shard_map/ppermute | solution.py:48
  37.2 4.1 %collective-permute-start.13 = (f32[96,128]{1,0:T(8,128)S(1)}, f32[96,128]{1,0:T(8,128)S(1)}, u32[]{:S(2)}, u32[]{:S(2)}) collective-permute-start(f32[96,128]{1,0:T(8,128)S(1)} %get-tuple-element.32), channel_id=1, source_target_pairs={{0,4},{1,3},{2,6},{3,1},{4,0},{5,7},{6,2},{7,5},{8,12},{9,11},{10,... | collective-permute-start | bytes 147464 | tf_op jit(solution)/shard_map/ppermute | solution.py:48
  38.7 5.0 %collective-permute-start.14 = (f32[96,128]{1,0:T(8,128)S(1)}, f32[96,128]{1,0:T(8,128)S(1)}, u32[]{:S(2)}, u32[]{:S(2)}) collective-permute-start(f32[96,128]{1,0:T(8,128)S(1)} %get-tuple-element.33), channel_id=1, source_target_pairs={{0,6},{1,7},{2,4},{3,5},{4,2},{5,3},{6,0},{7,1},{8,14},{9,15},{10,... | collective-permute-start | bytes 147464 | tf_op jit(solution)/shard_map/ppermute | solution.py:48
  43.7 4.5 %collective-permute-start.15 = (f32[96,128]{1,0:T(8,128)S(1)}, f32[96,128]{1,0:T(8,128)S(1)}, u32[]{:S(2)}, u32[]{:S(2)}) collective-permute-start(f32[96,128]{1,0:T(8,128)S(1)} %shard_map.58.refs_0_), channel_id=1, source_target_pairs={{0,8},{1,9},{2,10},{3,11},{4,12},{5,13},{6,14},{7,15},{8,0},{9,1},... | collective-permute-start | bytes 147464 | tf_op jit(solution)/shard_map/ppermute | solution.py:48
  44.9 5.7 %collective-permute-start.16 = (f32[96,128]{1,0:T(8,128)S(1)}, f32[96,128]{1,0:T(8,128)S(1)}, u32[]{:S(2)}, u32[]{:S(2)}) collective-permute-start(f32[96,128]{1,0:T(8,128)S(1)} %shard_map.58.refs_0_), channel_id=1, source_target_pairs={{0,16},{1,17},{2,18},{3,19},{4,20},{5,21},{6,22},{7,23},{8,24},{9,... | collective-permute-start | bytes 147464 | tf_op jit(solution)/shard_map/ppermute | solution.py:48
  46.5 5.9 %collective-permute-start.17 = (f32[96,128]{1,0:T(8,128)S(1)}, f32[96,128]{1,0:T(8,128)S(1)}, u32[]{:S(2)}, u32[]{:S(2)}) collective-permute-start(f32[96,128]{1,0:T(8,128)S(1)} %shard_map.58.refs_0_), channel_id=1, source_target_pairs={{0,24},{1,25},{2,26},{3,27},{4,28},{5,29},{6,30},{7,31},{8,16},{9,... | collective-permute-start | bytes 147464 | tf_op jit(solution)/shard_map/ppermute | solution.py:48
  52.4 4.2 %collective-permute-start.18 = (f32[96,128]{1,0:T(8,128)S(1)}, f32[96,128]{1,0:T(8,128)S(1)}, u32[]{:S(2)}, u32[]{:S(2)}) collective-permute-start(f32[96,128]{1,0:T(8,128)S(1)} %shard_map.59.refs_0_), channel_id=1, source_target_pairs={{0,2},{1,5},{2,0},{3,7},{4,6},{5,1},{6,4},{7,3},{8,10},{9,13},{10,... | collective-permute-start | bytes 147464 | tf_op jit(solution)/shard_map/ppermute | solution.py:48
  53.1 4.1 %collective-permute-start.19 = (f32[96,128]{1,0:T(8,128)S(1)}, f32[96,128]{1,0:T(8,128)S(1)}, u32[]{:S(2)}, u32[]{:S(2)}) collective-permute-start(f32[96,128]{1,0:T(8,128)S(1)} %shard_map.59.refs_0_), channel_id=1, source_target_pairs={{0,4},{1,3},{2,6},{3,1},{4,0},{5,7},{6,2},{7,5},{8,12},{9,11},{10,... | collective-permute-start | bytes 147464 | tf_op jit(solution)/shard_map/ppermute | solution.py:48
  53.6 5.0 %collective-permute-start.20 = (f32[96,128]{1,0:T(8,128)S(1)}, f32[96,128]{1,0:T(8,128)S(1)}, u32[]{:S(2)}, u32[]{:S(2)}) collective-permute-start(f32[96,128]{1,0:T(8,128)S(1)} %shard_map.59.refs_0_), channel_id=1, source_target_pairs={{0,6},{1,7},{2,4},{3,5},{4,2},{5,3},{6,0},{7,1},{8,14},{9,15},{10,... | collective-permute-start | bytes 147464 | tf_op jit(solution)/shard_map/ppermute | solution.py:48
  58.6 1.5 %collective-permute-start.21 = (f32[384,128]{1,0:T(8,128)S(1)}, f32[384,128]{1,0:T(8,128)S(1)}, u32[]{:S(2)}, u32[]{:S(2)}) collective-permute-start(f32[384,128]{1,0:T(8,128)S(1)} %shard_map.60.keep_ref), channel_id=1, source_target_pairs={{0,1},{1,0},{2,3},{3,2},{4,5},{5,4},{6,7},{7,6},{8,9},{9,8},{10,11... | collective-permute-start | bytes 589832 | tf_op jit(solution)/shard_map/ppermute | solution.py:48

commit v5 on v4

v5 whole, which is shorter than its diff:
```python
import jax
import jax.numpy as jnp
from jax import lax
from jax.experimental import pallas as pl
from jax.experimental.pallas import tpu as pltpu
from jax.sharding import PartitionSpec as P

AXES = ("row", "col")
F32, BF16 = jnp.float32, jnp.bfloat16


def halves(x):
    high = x.astype(BF16)
    return high, (x - high.astype(F32)).astype(BF16)


def left(x, axis=1):
    high, low = halves(x)
    return jnp.concatenate([high, high, low], axis=axis)


def right(x, axis=1):
    high, low = halves(x)
    return jnp.concatenate([high, low, high], axis=axis)


def mul(a, b, da=1, db=0):
    return lax.dot_general(a, b, (((da,), (db,)), ((), ())), preferred_element_type=F32)


def round_up(count, step):
    return -(-count // step) * step


def bits_of(count):
    assert count & (count - 1) == 0
    return [1 << b for b in range(count.bit_length() - 1)]


def parity(x):
    return bin(x).count("1") & 1


def make_hop(rows, cols):
    def hop(value, even, odd=None):
        odd = even if odd is None else odd
        pairs = []
        for r in range(rows):
            for c in range(cols):
                dr, dc = odd if parity(r) ^ (c & 1) else even
                pairs.append((r * cols + c, (r ^ dr) * cols + (c ^ dc ^ parity(dr))))
        return lax.ppermute(value, AXES, pairs)

    return hop


def my_kind(rows):
    row, kind = lax.axis_index("row"), lax.axis_index("col")
    for bit in range(len(bits_of(rows))):
        kind = kind ^ (row >> bit)
    return kind & 1


def call(body, out_shape, args, flops):
    moved = sum(4 * a.size for a in args) + sum(4 * s.size for s in jax.tree.leaves(out_shape))
    return pl.pallas_call(
        body,
        out_shape=out_shape,
        in_specs=[pl.BlockSpec(memory_space=pltpu.VMEM)] * len(args),
        out_specs=jax.tree.map(lambda _: pl.BlockSpec(memory_space=pltpu.VMEM), out_shape),
        compiler_params=pltpu.CompilerParams(vmem_limit_bytes=40 * 1024 * 1024),
        cost_estimate=pl.CostEstimate(flops=flops, bytes_accessed=moved, transcendentals=0),
    )(*args)


def shape(*dims):
    return jax.ShapeDtypeStruct(dims, F32)


def pack_own(points, coeffs):
    rows, width = points.shape
    outs_n = coeffs.shape[1]
    extra = round_up(outs_n + 1, 8)

    def body(points_ref, cols_ref, plain_ref, packed_ref, cols_held, sems):
        copies = [
            pltpu.make_async_copy(points_ref, plain_ref, sems.at[0]),
            pltpu.make_async_copy(cols_ref, cols_held, sems.at[1]),
        ]
        for copy in copies:
            copy.start()
        packed_ref[rows:, :] = jnp.zeros((extra, width), F32)
        copies[1].wait()
        cols = cols_held[...]
        packed_ref[rows : rows + outs_n, 0 : 2 * rows] = jnp.concatenate([cols, cols], axis=1)
        copies[0].wait()
        packed_ref[0:rows, :] = plain_ref[...]

    return pl.pallas_call(
        body,
        out_shape=(pltpu.VMEM((rows, width), F32), pltpu.VMEM((rows + extra, width), F32)),
        in_specs=[pl.BlockSpec(memory_space=pl.ANY)] * 2,
        out_specs=(pl.BlockSpec(memory_space=pltpu.VMEM),) * 2,
        scratch_shapes=[pltpu.VMEM((outs_n, rows), F32), pltpu.SemaphoreType.DMA((2,))],
    )(points, coeffs.T)


def metric_halves(metric):
    width = metric.shape[0]

    def body(metric_ref, out_ref):
        out_ref[...] = right(metric_ref[...], axis=0)

    return call(body, jax.ShapeDtypeStruct((3 * width, width), BF16), [metric], 1)


def norm_rows(centers, metric3, own):
    column = jnp.sum(centers * mul(left(centers), metric3), axis=1, keepdims=True)
    pair = 2 * own
    rows = [
        jnp.broadcast_to(column[k : k + pair], (pair, round_up(pair, 128))).T[0:1]
        for k in range(0, centers.shape[0], pair)
    ]
    return jnp.concatenate(rows, axis=1)


def center_terms(refs, own, outs_n, metric3):
    pieces, extras = [], []
    height = own + round_up(outs_n + 1, 8)
    for ref in refs:
        for first in range(0, ref.shape[0], height):
            pieces.append(ref[first : first + own, :])
            extras.append(ref[first + own : first + height, 0 : 2 * own])
    centers = jnp.concatenate(pieces, axis=0)
    lane = lax.broadcasted_iota(jnp.int32, extras[0].shape, 1)
    merged = [jnp.where(lane < own, extras[k], extras[k + 1]) for k in range(0, len(extras), 2)]
    rows = jnp.concatenate(merged, axis=1)
    return centers, norm_rows(centers, metric3, own), [rows[c : c + 1] for c in range(outs_n)]


def query_sums(query_x, query_y, centers, norm, coefs):
    query_n = jnp.sum(query_x * query_y, axis=1, keepdims=True)
    cross = mul(left(query_y), right(centers), 1, 1)
    distance = jnp.sqrt(jnp.maximum(query_n + norm - 2.0 * cross, 0.0))
    weights = jnp.exp(-distance) / jnp.maximum(distance, 0.5)
    low = centers.astype(BF16)
    parts = []
    for coef in coefs:
        scaled = weights * coef
        sums = jnp.sum(scaled, axis=1, keepdims=True)
        parts.append(sums * query_x - mul(scaled.astype(BF16), low))
    return parts


def chunks(refs):
    return [refs[k : k + 8] for k in range(0, len(refs), 8)]


def early_sums(queries, blocks, metric3, outs_n):
    own, width = queries[0].shape
    count = len(queries)

    def body(*refs):
        query_refs, block_refs = refs[:count], refs[count : count + len(blocks)]
        metric3_ref, total_ref, mapped_ref = refs[count + len(blocks) :]
        query_x = jnp.concatenate([ref[...] for ref in query_refs], axis=0)
        query_y = mul(left(query_x), metric3_ref[...])
        mapped_ref[...] = query_y
        for k, run in enumerate(chunks(block_refs)):
            parts = query_sums(query_x, query_y, *center_terms(run, own, outs_n, metric3_ref[...]))
            for c in range(outs_n):
                total_ref[c] = parts[c] if k == 0 else total_ref[c] + parts[c]

    args = list(queries) + list(blocks) + [metric3]
    centers = sum(b.shape[0] for b in blocks)
    flops = 6 * (count * own + centers) * width * width + 10 * count * own * centers * width
    return call(body, (shape(outs_n, count * own, width), shape(count * own, width)), args, flops)


def late_sums(queries, first, total, mapped, metric3, blocks, outs_n):
    own, width = queries[0].shape
    count = len(queries)

    def body(*refs):
        query_refs, block_refs = refs[:count], refs[count : count + len(blocks)]
        total_ref, mapped_ref, metric3_ref = refs[count + len(blocks) : count + len(blocks) + 3]
        out_refs = refs[count + len(blocks) + 3 :]
        rows = slice(first * own, (first + count) * own)
        query_x = jnp.concatenate([ref[...] for ref in query_refs], axis=0)
        query_y = mapped_ref[rows, :]
        sums = [total_ref[c, rows, :] for c in range(outs_n)]
        for run in chunks(block_refs):
            terms = center_terms(run, own, outs_n, metric3_ref[...])
            sums = [a + b for a, b in zip(sums, query_sums(query_x, query_y, *terms))]
        for q in range(count):
            for c in range(outs_n):
                out_refs[q][c * own : (c + 1) * own, :] = sums[c][q * own : (q + 1) * own, :]

    args = list(queries) + list(blocks) + [total, mapped, metric3]
    centers = sum(b.shape[0] for b in blocks)
    flops = 6 * centers * width * width + 10 * count * own * centers * width
    return call(body, tuple(shape(outs_n * own, width) for _ in queries), args, flops)


def upper_tiles(width):
    tile = 128 if width % 128 == 0 else width
    span = width // tile
    return tile, span, [(i, j) for i in range(span) for j in range(i, span)]


def outer_halves(part, arrived, metric3, rows_all):
    width = part.shape[1]
    tile, span, upper = upper_tiles(width)
    half = (len(upper) + 1) // 2

    def body(part_ref, arrived_ref, metric3_ref, keep_ref, send_ref):
        odd = my_kind(rows_all) == 1
        grads = mul(left(part_ref[...] + arrived_ref[...]), metric3_ref[...])
        grads_left, grads_right = left(grads, 0), right(grads, 0)
        tiles = [[] for _ in upper]
        for i in range(span):
            slab = mul(grads_left[:, i * tile : (i + 1) * tile], grads_right[:, i * tile :], 0, 0)
            for j in range(i, span):
                tiles[upper.index((i, j))] = slab[:, (j - i) * tile : (j - i + 1) * tile]
        while len(tiles) < 2 * half:
            tiles.append(jnp.zeros((tile, tile), F32))
        for k in range(half):
            keep_ref[k * tile : (k + 1) * tile, :] = jnp.where(odd, tiles[half + k], tiles[k])
            send_ref[k * tile : (k + 1) * tile, :] = jnp.where(odd, tiles[k], tiles[half + k])

    out = shape(half * tile, tile)
    return call(body, (out, out), [part, arrived, metric3], 12 * part.shape[0] * width * width)


def plane_place(k, rows_all):
    row = lax.axis_index("row") & 3
    if k in (1, 2):
        return row ^ jnp.where(my_kind(rows_all) == 1, 3 - k, k)
    return row ^ k


def quarter(ref, k, rows_all):
    rows = ref.shape[0] // 4
    return pl.ds(pl.multiple_of(plane_place(k, rows_all) * rows, rows), rows)


def split_quarters(kept, arrived, rows_all):
    rows, width = kept.shape

    def body(kept_ref, arrived_ref, *out_refs):
        for k in range(4):
            place = quarter(kept_ref, k, rows_all)
            out_refs[k][...] = kept_ref[place, :] + arrived_ref[place, :]

    return call(body, (shape(rows // 4, width),) * 4, [kept, arrived], 1)


def join_quarters(parts, rows_all):
    rows, width = parts[0].shape

    def body(*refs):
        out_ref = refs[-1]
        for k in range(4):
            out_ref[quarter(out_ref, k, rows_all), :] = refs[k][...]

    return call(body, shape(4 * rows, width), parts, 1)


def add_all(parts):
    def body(*refs):
        values = [ref[...] for ref in refs[:-1]]
        while len(values) > 1:
            values = [a + b for a, b in zip(values[::2], values[1::2])]
        refs[-1][...] = values[0]

    return call(body, shape(*parts[0].shape), parts, 1)


def finish(keep, other, points, rows_all):
    rows, width = points.shape
    tile, span, upper = upper_tiles(width)
    half = (len(upper) + 1) // 2

    def body(keep_ref, other_ref, points_ref, next_ref, mapped_ref, next_held, mapped_held, sems):
        odd = my_kind(rows_all) == 1
        kept = [keep_ref[k * tile : (k + 1) * tile, :] for k in range(half)]
        came = [other_ref[k * tile : (k + 1) * tile, :] for k in range(half)]
        tiles = [jnp.where(odd, b, a) for a, b in zip(kept, came)]
        tiles += [jnp.where(odd, a, b) for a, b in zip(kept, came)]
        final = dict(zip(upper, tiles))
        diag = final[0, 0]
        for i in range(1, span):
            diag = diag + final[i, i]
        eye = lax.broadcasted_iota(jnp.int32, diag.shape, 0) == lax.broadcasted_iota(jnp.int32, diag.shape, 1)
        trace = jnp.sum(jnp.where(eye, diag, 0.0), keepdims=True)
        scale = width / trace
        for i, j in upper:
            value = final[i, j] * scale
            next_held[i * tile : (i + 1) * tile, j * tile : (j + 1) * tile] = value
            if i != j:
                next_held[j * tile : (j + 1) * tile, i * tile : (i + 1) * tile] = value.T
        next_copy = pltpu.make_async_copy(next_held, next_ref, sems.at[0])
        next_copy.start()
        mapped_held[...] = mul(left(points_ref[...]), right(next_held[...], axis=0))
        mapped_copy = pltpu.make_async_copy(mapped_held, mapped_ref, sems.at[1])
        mapped_copy.start()
        next_copy.wait()
        mapped_copy.wait()

    return pl.pallas_call(
        body,
        out_shape=(shape(width, width), shape(rows, width)),
        in_specs=[pl.BlockSpec(memory_space=pltpu.VMEM)] * 3,
        out_specs=(pl.BlockSpec(memory_space=pl.ANY),) * 2,
        scratch_shapes=[
            pltpu.VMEM((width, width), F32),
            pltpu.VMEM((rows, width), F32),
            pltpu.SemaphoreType.DMA((2,)),
        ],
        compiler_params=pltpu.CompilerParams(vmem_limit_bytes=40 * 1024 * 1024),
    )(keep, other, points)


def make_local(rows_all, cols_all):
    hop = make_hop(rows_all, cols_all)
    row_bits = bits_of(rows_all)
    col_bits = bits_of(cols_all)
    bit_a, bit_b = row_bits[0], row_bits[1]
    line_bits = row_bits[2:]

    def to_a(value):
        return hop(value, (bit_a, 0), (bit_b, 0))

    def to_b(value):
        return hop(value, (bit_b, 0), (bit_a, 0))

    def in_plane(parts):
        return [to_a(parts[0]), to_b(parts[1]), hop(parts[2], (bit_a | bit_b, 0))]

    def among(value, shifts):
        steps = [(0, 0)]
        for dr, dc in shifts:
            steps = steps + [(r | dr, c | dc) for r, c in steps]
        return [value] + [hop(value, step) for step in steps[1:]]

    def local(points, coeffs, metric):
        own, width = points.shape
        outs_n = coeffs.shape[1]
        points, packed = pack_own(points, coeffs)
        metric3 = metric_halves(metric)
        near = among(packed, [(bit, 0) for bit in reversed(line_bits)])
        from_a = to_a(points)
        from_b = to_b(points)
        queries = [to_b(from_a), from_a, from_b, points]
        total, mapped = early_sums(queries, near, metric3, outs_n)
        late = [other for block in near for other in among(block, [(0, bit) for bit in col_bits])[1:]]
        part_ab, part_a = late_sums(queries[:2], 0, total, mapped, metric3, late, outs_n)
        sent_ab, sent_a = to_a(part_ab), to_a(part_a)
        part_b, part_own = late_sums(queries[2:], 2, total, mapped, metric3, late, outs_n)
        sent_b = to_b(part_b + sent_ab)

        keep, send = outer_halves(part_own + sent_a, sent_b, metric3, rows_all)
        parts = split_quarters(keep, hop(send, (0, 1)), rows_all)
        total = add_all([parts[0]] + in_plane(parts[1:]))
        for k in range(0, len(line_bits), 2):
            total = add_all(among(total, [(bit, 0) for bit in line_bits[k : k + 2]]))
        for bit in col_bits[1:]:
            total = add_all(among(total, [(0, bit)]))
        keep = join_quarters([total] + in_plane([total] * 3), rows_all)
        return finish(keep, hop(keep, (0, 1)), points, rows_all)

    return local


def solution(mesh):
    return jax.shard_map(
        make_local(mesh.shape["row"], mesh.shape["col"]),
        mesh=mesh,
        in_specs=(P(AXES, None), P(AXES, None), P()),
        out_specs=(P(), P(AXES, None)),
        check_vma=False,
    )
```

time: 61.5 us -> 57.6 us (0.937)
  starting transfers between devices: 26.2 us -> 23.8 us
  Pallas kernels: 7.35 us -> 6.57 us
  waiting for transfers between devices: 25.9 us -> 25.2 us
    ppermute x22 -> x24, starting transfers between devices: 26.2 us -> 23.8 us  [hop(): return lax.ppermute(value, AXES, pairs)]
    pallas_call x11 -> x9, Pallas kernels: 5.76 us -> 4.44 us  [call(): pl.pallas_call(body, out_shape=out_shape, in_specs=[pl.BlockSpec(memory_s...]
    ppermute x22 -> x24, waiting for transfers between devices: 25.9 us -> 25.2 us  [hop(): return lax.ppermute(value, AXES, pairs)]
    pallas_call x1 -> x2, Pallas kernels: 1.59 us -> 2.13 us  [the longest x1 1.21 us: finish(): pl.pallas_call(body, out_shape=(shape(width, width), shape(rows, width)),...]
  transfers between devices with their start and end apart: 22 -> 24, of which waited for: 16 -> 15; matrix products, arithmetic and copies ran while one was open for 0% -> 0% of each run, Pallas kernels for 3% -> 5%
where the time goes in v5:
time: 57.6 us; the launch traced here: 57.4 us
  waiting for transfers between devices  25.2 us (44%)
  starting transfers between devices  23.8 us (41%)
  Pallas kernels  6.57 us (11%)
  local copies, waits for them, and re-layouts  1.06 us (2%)
  between operations  0.74 us (1%)
    ppermute x24, waiting for transfers between devices, hop(): return lax.ppermute(value, AXES, pairs)  25.2 us
    ppermute x24, starting transfers between devices, hop(): return lax.ppermute(value, AXES, pairs)  23.8 us
    pallas_call x9, Pallas kernels, call(): pl.pallas_call(body, out_shape=out_shape, in_specs=[pl.BlockSpec(memory_s...  4.44 us
    pallas_call x1, Pallas kernels, finish(): pl.pallas_call(body, out_shape=(shape(width, width), shape(rows, width)),...  1.21 us
  transfers between devices with their start and end apart: 24, of which 15 were waited for; matrix products, arithmetic and copies ran while one was open for 0% of the time, Pallas kernels for 5%

profile of v5, /device:TPU:0, one launch (start us, length us, event | category | flops | bytes accessed | tf_op | source)
XLA Modules:
  0.0 57.4 jit_solution(8417407481666399189)
XLA Ops:
  0.6 0.9 %shard_map.50 = (f32[64,384]{1,0:T(8,128)S(1)}, f32[72,384]{1,0:T(8,128)S(1)}) custom-call(f32[64,384]{1,0:T(8,128)} %points_ref.1, f32[2,64]{1,0:T(2,128)} %bitcast.1), custom_call_target="tpu_custom_call" | custom-call | tf_op jit(solution)/shard_map/pallas_call | solution.py:99
  1.6 2.4 %collective-permute-start.8 = (f32[64,384]{1,0:T(8,128)S(1)}, f32[64,384]{1,0:T(8,128)S(1)}, u32[]{:S(2)}, u32[]{:S(2)}) collective-permute-start(f32[64,384]{1,0:T(8,128)S(1)} %get-tuple-element.16.refs_3_.refs_1_.points_ref), channel_id=1, source_target_pairs={{0,3},{1,4},{2,7},{3,0},{4,1},{5,6},{6,5},{7,2},{8,13},{9,10},{10,... | collective-permute-start | bytes 294920 | tf_op jit(solution)/shard_map/ppermute | solution.py:52
  4.0 3.6 %collective-permute-start.6 = (f32[72,384]{1,0:T(8,128)S(1)}, f32[72,384]{1,0:T(8,128)S(1)}, u32[]{:S(2)}, u32[]{:S(2)}) collective-permute-start(f32[72,384]{1,0:T(8,128)S(1)} %get-tuple-element.17.refs_4_), channel_id=1, source_target_pairs={{0,24},{1,25},{2,26},{3,27},{4,28},{5,29},{6,30},{7,31},{8,16},{9,... | collective-permute-start | bytes 331784 | tf_op jit(solution)/shard_map/ppermute | solution.py:52
  7.6 0.0 collective-permute-start.4
  7.6 0.5 collective-permute-start.2
  8.1 1.6 %collective-permute-start = (f32[64,384]{1,0:T(8,128)S(1)}, f32[64,384]{1,0:T(8,128)S(1)}, u32[]{:S(2)}, u32[]{:S(2)}) collective-permute-start(f32[64,384]{1,0:T(8,128)S(1)} %get-tuple-element.16.refs_3_.refs_1_.points_ref), channel_id=1, source_target_pairs={{0,5},{1,2},{2,1},{3,6},{4,7},{5,0},{6,3},{7,4},{8,11},{9,12},{10,... | collective-permute-start | bytes 294920 | tf_op jit(solution)/shard_map/ppermute | solution.py:52
  9.7 0.0 collective-permute-done.8.refs_1_
  9.7 0.2 collective-permute-start.9
  9.9 2.3 %collective-permute-done.refs_2_.refs_0_ = f32[64,384]{1,0:T(8,128)S(1)} collective-permute-done((f32[64,384]{1,0:T(8,128)S(1)}, f32[64,384]{1,0:T(8,128)S(1)}, u32[]{:S(2)}, u32[]{:S(2)}) %collective-permute-start) | collective-permute-done | bytes 98336 | tf_op jit(solution)/shard_map/ppermute | solution.py:52
  12.1 0.8 %collective-permute-start.1 = (f32[72,384]{1,0:T(8,128)S(1)}, f32[72,384]{1,0:T(8,128)S(1)}, u32[]{:S(2)}, u32[]{:S(2)}) collective-permute-start(f32[72,384]{1,0:T(8,128)S(1)} %get-tuple-element.17.refs_4_), channel_id=1, source_target_pairs={{0,1},{1,0},{2,3},{3,2},{4,5},{5,4},{6,7},{7,6},{8,9},{9,8},{10,11... | collective-permute-start | bytes 331784 | tf_op jit(solution)/shard_map/ppermute | solution.py:52
  12.9 0.0 collective-permute-done.6.refs_7_
  12.9 0.0 collective-permute-start.7
  12.9 2.0 %collective-permute-done.4.refs_6_ = f32[72,384]{1,0:T(8,128)S(1)} collective-permute-done((f32[72,384]{1,0:T(8,128)S(1)}, f32[72,384]{1,0:T(8,128)S(1)}, u32[]{:S(2)}, u32[]{:S(2)}) %collective-permute-start.4) | collective-permute-done | bytes 110624 | tf_op jit(solution)/shard_map/ppermute | solution.py:52
  15.0 0.2 collective-permute-start.5
  15.1 2.3 %collective-permute-done.2.refs_5_ = f32[72,384]{1,0:T(8,128)S(1)} collective-permute-done((f32[72,384]{1,0:T(8,128)S(1)}, f32[72,384]{1,0:T(8,128)S(1)}, u32[]{:S(2)}, u32[]{:S(2)}) %collective-permute-start.2) | collective-permute-done | bytes 110624 | tf_op jit(solution)/shard_map/ppermute | solution.py:52
  17.4 0.1 collective-permute-start.3
  17.6 0.0 copy-start
  17.6 1.1 %copy-done = f32[384,384]{1,0:T(8,128)S(1)} copy-done((f32[384,384]{1,0:T(8,128)S(1)}, f32[384,384]{1,0:T(8,128)}, u32[]{:S(2)}) %copy-start) | copy-done | bytes 589848
  18.6 0.1 shard_map.51.refs_8_.metric3_ref
  18.8 0.0 collective-permute-done.9.refs_0_
  18.8 1.6 %shard_map.52 = (f32[2,256,384]{2,1,0:T(8,128)S(1)}, f32[256,384]{1,0:T(8,128)S(1)}) custom-call(f32[64,384]{1,0:T(8,128)S(1)} %collective-permute-done.9.refs_0_, f32[64,384]{1,0:T(8,128)S(1)} %collective-permute-done.8.refs_1_, f32[64,384]{1,0:T(8,128)S(1)} %collective-permute-done.refs_2_.refs_0_, ...), custom_call_target="tpu_custom_call" | custom-call | flops 764411904 | bytes 3784704 | tf_op jit(solution)/shard_map/pallas_call | solution.py:66
  20.4 0.0 collective-permute-done.1.refs_2_
  20.4 0.0 collective-permute-done.7.refs_5_
  20.4 0.0 collective-permute-done.5.refs_4_
  20.4 0.0 collective-permute-done.3.refs_3_
  20.4 1.0 %shard_map.54 = (f32[128,384]{1,0:T(8,128)S(1)}, f32[128,384]{1,0:T(8,128)S(1)}) custom-call(f32[64,384]{1,0:T(8,128)S(1)} %collective-permute-done.9.refs_0_, f32[64,384]{1,0:T(8,128)S(1)} %collective-permute-done.8.refs_1_, f32[72,384]{1,0:T(8,128)S(1)} %collective-permute-done.1.refs_2_, f32[72,384]{1,0:T(8,128)S(1)} %collective-permute-done.3.refs_3_, ...), custom_call_target="tpu_custom_call" | custom-call | flops 396361728 | bytes 3981312 | tf_op jit(solution)/shard_map/pallas_call | solution.py:66
  21.4 1.3 %collective-permute-start.11 = (f32[128,384]{1,0:T(8,128)S(1)}, f32[128,384]{1,0:T(8,128)S(1)}, u32[]{:S(2)}, u32[]{:S(2)}) collective-permute-start(f32[128,384]{1,0:T(8,128)S(1)} %get-tuple-element.23), channel_id=1, source_target_pairs={{0,3},{1,4},{2,7},{3,0},{4,1},{5,6},{6,5},{7,2},{8,13},{9,10},{10,... | collective-permute-start | bytes 589832 | tf_op jit(solution)/shard_map/ppermute | solution.py:52
  22.7 0.5 collective-permute-start.10
  23.2 1.0 %shard_map.53 = (f32[128,384]{1,0:T(8,128)S(1)}, f32[128,384]{1,0:T(8,128)S(1)}) custom-call(f32[64,384]{1,0:T(8,128)S(1)} %collective-permute-done.refs_2_.refs_0_, f32[64,384]{1,0:T(8,128)S(1)} %get-tuple-element.16.refs_3_.refs_1_.points_ref, f32[72,384]{1,0:T(8,128)S(1)} %collective-permute-done.1.refs_2_, f32[72,384]{1,0:T(8,128)S(1)} %collective-permute-done.3.refs_3_, ...), custom_call_target="tpu_custom_call" | custom-call | flops 396361728 | bytes 3981312 | tf_op jit(solution)/shard_map/pallas_call | solution.py:66
  24.3 2.3 %collective-permute-done.11 = f32[128,384]{1,0:T(8,128)S(1)} collective-permute-done((f32[128,384]{1,0:T(8,128)S(1)}, f32[128,384]{1,0:T(8,128)S(1)}, u32[]{:S(2)}, u32[]{:S(2)}) %collective-permute-start.11) | collective-permute-done | bytes 196640 | tf_op jit(solution)/shard_map/ppermute | solution.py:52
  26.6 0.5 collective-permute-start.12
  27.2 1.5 %collective-permute-done.10 = f32[128,384]{1,0:T(8,128)S(1)} collective-permute-done((f32[128,384]{1,0:T(8,128)S(1)}, f32[128,384]{1,0:T(8,128)S(1)}, u32[]{:S(2)}, u32[]{:S(2)}) %collective-permute-start.10) | collective-permute-done | bytes 196640 | tf_op jit(solution)/shard_map/ppermute | solution.py:52
  28.7 3.1 %collective-permute-done.12.arrived_ref = f32[128,384]{1,0:T(8,128)S(1)} collective-permute-done((f32[128,384]{1,0:T(8,128)S(1)}, f32[128,384]{1,0:T(8,128)S(1)}, u32[]{:S(2)}, u32[]{:S(2)}) %collective-permute-start.12) | collective-permute-done | bytes 196640 | tf_op jit(solution)/shard_map/ppermute | solution.py:52
  31.8 0.6 %shard_map.55 = (f32[384,128]{1,0:T(8,128)S(1)}, f32[384,128]{1,0:T(8,128)S(1)}) custom-call(f32[128,384]{1,0:T(8,128)S(1)} %add.6.part_ref, f32[128,384]{1,0:T(8,128)S(1)} %collective-permute-done.12.arrived_ref, bf16[1152,384]{1,0:T(8,128)(2,1)S(1)} %shard_map.51.refs_8_.metric3_ref), custom_call_target="tpu_custom_call" | custom-call | flops 226492416 | bytes 2555904 | tf_op jit(solution)/shard_map/pallas_call | solution.py:66
  32.4 0.7 %collective-permute-start.13 = (f32[384,128]{1,0:T(8,128)S(1)}, f32[384,128]{1,0:T(8,128)S(1)}, u32[]{:S(2)}, u32[]{:S(2)}) collective-permute-start(f32[384,128]{1,0:T(8,128)S(1)} %get-tuple-element.25), channel_id=1, source_target_pairs={{0,1},{1,0},{2,3},{3,2},{4,5},{5,4},{6,7},{7,6},{8,9},{9,8},{10,11... | collective-permute-start | bytes 589832 | tf_op jit(solution)/shard_map/ppermute | solution.py:52
  33.2 1.1 %collective-permute-done.13.arrived_ref = f32[384,128]{1,0:T(8,128)S(1)} collective-permute-done((f32[384,128]{1,0:T(8,128)S(1)}, f32[384,128]{1,0:T(8,128)S(1)}, u32[]{:S(2)}, u32[]{:S(2)}) %collective-permute-start.13) | collective-permute-done | bytes 196640 | tf_op jit(solution)/shard_map/ppermute | solution.py:52
  34.3 1.3 %collective-permute-start.14 = (f32[96,128]{1,0:T(8,128)S(1)}, f32[96,128]{1,0:T(8,128)S(1)}, u32[]{:S(2)}, u32[]{:S(2)}) collective-permute-start(f32[96,128]{1,0:T(8,128)S(1)} %get-tuple-element.27), channel_id=1, source_target_pairs={{0,3},{1,4},{2,7},{3,0},{4,1},{5,6},{6,5},{7,2},{8,13},{9,10},{10,... | collective-permute-start | bytes 147464 | tf_op jit(solution)/shard_map/ppermute | solution.py:52
  35.6 0.5 collective-permute-start.15
  36.1 1.4 %collective-permute-start.16 = (f32[96,128]{1,0:T(8,128)S(1)}, f32[96,128]{1,0:T(8,128)S(1)}, u32[]{:S(2)}, u32[]{:S(2)}) collective-permute-start(f32[96,128]{1,0:T(8,128)S(1)} %get-tuple-element.29), channel_id=1, source_target_pairs={{0,6},{1,7},{2,4},{3,5},{4,2},{5,3},{6,0},{7,1},{8,14},{9,15},{10,... | collective-permute-start | bytes 147464 | tf_op jit(solution)/shard_map/ppermute | solution.py:52
  37.5 0.3 collective-permute-done.14.refs_1_
  37.8 1.2 %collective-permute-done.15.refs_2_ = f32[96,128]{1,0:T(8,128)S(1)} collective-permute-done((f32[96,128]{1,0:T(8,128)S(1)}, f32[96,128]{1,0:T(8,128)S(1)}, u32[]{:S(2)}, u32[]{:S(2)}) %collective-permute-start.15) | collective-permute-done | bytes 49184 | tf_op jit(solution)/shard_map/ppermute | solution.py:52
  39.1 2.0 %collective-permute-done.16.refs_3_ = f32[96,128]{1,0:T(8,128)S(1)} collective-permute-done((f32[96,128]{1,0:T(8,128)S(1)}, f32[96,128]{1,0:T(8,128)S(1)}, u32[]{:S(2)}, u32[]{:S(2)}) %collective-permute-start.16) | collective-permute-done | bytes 49184 | tf_op jit(solution)/shard_map/ppermute | solution.py:52
  41.1 2.5 %collective-permute-start.19 = (f32[96,128]{1,0:T(8,128)S(1)}, f32[96,128]{1,0:T(8,128)S(1)}, u32[]{:S(2)}, u32[]{:S(2)}) collective-permute-start(f32[96,128]{1,0:T(8,128)S(1)} %shard_map.57.refs_0_), channel_id=1, source_target_pairs={{0,24},{1,25},{2,26},{3,27},{4,28},{5,29},{6,30},{7,31},{8,16},{9,... | collective-permute-start | bytes 147464 | tf_op jit(solution)/shard_map/ppermute | solution.py:52
  43.7 0.0 collective-permute-start.18
  43.7 1.6 %collective-permute-start.17 = (f32[96,128]{1,0:T(8,128)S(1)}, f32[96,128]{1,0:T(8,128)S(1)}, u32[]{:S(2)}, u32[]{:S(2)}) collective-permute-start(f32[96,128]{1,0:T(8,128)S(1)} %shard_map.57.refs_0_), channel_id=1, source_target_pairs={{0,9},{1,8},{2,11},{3,10},{4,13},{5,12},{6,15},{7,14},{8,1},{9,0},... | collective-permute-start | bytes 147464 | tf_op jit(solution)/shard_map/ppermute | solution.py:52
  45.3 2.1 %collective-permute-done.19.refs_3_ = f32[96,128]{1,0:T(8,128)S(1)} collective-permute-done((f32[96,128]{1,0:T(8,128)S(1)}, f32[96,128]{1,0:T(8,128)S(1)}, u32[]{:S(2)}, u32[]{:S(2)}) %collective-permute-start.19) | collective-permute-done | bytes 49184 | tf_op jit(solution)/shard_map/ppermute | solution.py:52
  47.4 1.5 %collective-permute-done.18.refs_2_ = f32[96,128]{1,0:T(8,128)S(1)} collective-permute-done((f32[96,128]{1,0:T(8,128)S(1)}, f32[96,128]{1,0:T(8,128)S(1)}, u32[]{:S(2)}, u32[]{:S(2)}) %collective-permute-start.18) | collective-permute-done | bytes 49184 | tf_op jit(solution)/shard_map/ppermute | solution.py:52
  48.9 0.0 collective-permute-done.17.refs_1_
  48.9 1.5 %collective-permute-start.22 = (f32[96,128]{1,0:T(8,128)S(1)}, f32[96,128]{1,0:T(8,128)S(1)}, u32[]{:S(2)}, u32[]{:S(2)}) collective-permute-start(f32[96,128]{1,0:T(8,128)S(1)} %shard_map.58.refs_0_), channel_id=1, source_target_pairs={{0,6},{1,7},{2,4},{3,5},{4,2},{5,3},{6,0},{7,1},{8,14},{9,15},{10,... | collective-permute-start | bytes 147464 | tf_op jit(solution)/shard_map/ppermute | solution.py:52
  50.5 0.0 collective-permute-start.21
  50.5 1.7 %collective-permute-start.20 = (f32[96,128]{1,0:T(8,128)S(1)}, f32[96,128]{1,0:T(8,128)S(1)}, u32[]{:S(2)}, u32[]{:S(2)}) collective-permute-start(f32[96,128]{1,0:T(8,128)S(1)} %shard_map.58.refs_0_), channel_id=1, source_target_pairs={{0,3},{1,4},{2,7},{3,0},{4,1},{5,6},{6,5},{7,2},{8,13},{9,10},{10,... | collective-permute-start | bytes 147464 | tf_op jit(solution)/shard_map/ppermute | solution.py:52
  52.2 2.1 %collective-permute-done.22.refs_3_ = f32[96,128]{1,0:T(8,128)S(1)} collective-permute-done((f32[96,128]{1,0:T(8,128)S(1)}, f32[96,128]{1,0:T(8,128)S(1)}, u32[]{:S(2)}, u32[]{:S(2)}) %collective-permute-start.22) | collective-permute-done | bytes 49184 | tf_op jit(solution)/shard_map/ppermute | solution.py:52
  54.3 0.2 collective-permute-done.21.refs_2_
  54.5 0.0 collective-permute-done.20.refs_1_
  54.6 0.6 %collective-permute-start.23 = (f32[384,128]{1,0:T(8,128)S(1)}, f32[384,128]{1,0:T(8,128)S(1)}, u32[]{:S(2)}, u32[]{:S(2)}) collective-permute-start(f32[384,128]{1,0:T(8,128)S(1)} %shard_map.59.keep_ref), channel_id=1, source_target_pairs={{0,1},{1,0},{2,3},{3,2},{4,5},{5,4},{6,7},{7,6},{8,9},{9,8},{10,11... | collective-permute-start | bytes 589832 | tf_op jit(solution)/shard_map/ppermute | solution.py:52
  55.2 1.1 %collective-permute-done.23.other_ref = f32[384,128]{1,0:T(8,128)S(1)} collective-permute-done((f32[384,128]{1,0:T(8,128)S(1)}, f32[384,128]{1,0:T(8,128)S(1)}, u32[]{:S(2)}, u32[]{:S(2)}) %collective-permute-start.23) | collective-permute-done | bytes 196640 | tf_op jit(solution)/shard_map/ppermute | solution.py:52
  56.2 1.2 %shard_map.60 = (f32[384,384]{1,0:T(8,128)}, f32[64,384]{1,0:T(8,128)}) custom-call(f32[384,128]{1,0:T(8,128)S(1)} %shard_map.59.keep_ref, f32[384,128]{1,0:T(8,128)S(1)} %collective-permute-done.23.other_ref, f32[64,384]{1,0:T(8,128)S(1)} %get-tuple-element.16.refs_3_.refs_1_.points_ref), custom_call_target="tpu_custom_call" | custom-call | tf_op jit(solution)/shard_map/pallas_call | solution.py:310
  (6 shorter events, 0.1 us)
Async XLA Ops:
  1.6 8.1 %collective-permute-start.8 = (f32[64,384]{1,0:T(8,128)S(1)}, f32[64,384]{1,0:T(8,128)S(1)}, u32[]{:S(2)}, u32[]{:S(2)}) collective-permute-start(f32[64,384]{1,0:T(8,128)S(1)} %get-tuple-element.16.refs_3_.refs_1_.points_ref), channel_id=1, source_target_pairs={{0,3},{1,4},{2,7},{3,0},{4,1},{5,6},{6,5},{7,2},{8,13},{9,10},{10,... | collective-permute-start | bytes 294920 | tf_op jit(solution)/shard_map/ppermute | solution.py:52
  4.0 8.9 %collective-permute-start.6 = (f32[72,384]{1,0:T(8,128)S(1)}, f32[72,384]{1,0:T(8,128)S(1)}, u32[]{:S(2)}, u32[]{:S(2)}) collective-permute-start(f32[72,384]{1,0:T(8,128)S(1)} %get-tuple-element.17.refs_4_), channel_id=1, source_target_pairs={{0,24},{1,25},{2,26},{3,27},{4,28},{5,29},{6,30},{7,31},{8,16},{9,... | collective-permute-start | bytes 331784 | tf_op jit(solution)/shard_map/ppermute | solution.py:52
  7.6 7.4 %collective-permute-start.4 = (f32[72,384]{1,0:T(8,128)S(1)}, f32[72,384]{1,0:T(8,128)S(1)}, u32[]{:S(2)}, u32[]{:S(2)}) collective-permute-start(f32[72,384]{1,0:T(8,128)S(1)} %get-tuple-element.17.refs_4_), channel_id=1, source_target_pairs={{0,9},{1,8},{2,11},{3,10},{4,13},{5,12},{6,15},{7,14},{8,1},{9,0},... | collective-permute-start | bytes 331784 | tf_op jit(solution)/shard_map/ppermute | solution.py:52
  7.6 9.8 %collective-permute-start.2 = (f32[72,384]{1,0:T(8,128)S(1)}, f32[72,384]{1,0:T(8,128)S(1)}, u32[]{:S(2)}, u32[]{:S(2)}) collective-permute-start(f32[72,384]{1,0:T(8,128)S(1)} %get-tuple-element.17.refs_4_), channel_id=1, source_target_pairs={{0,17},{1,16},{2,19},{3,18},{4,21},{5,20},{6,23},{7,22},{8,25},{9,... | collective-permute-start | bytes 331784 | tf_op jit(solution)/shard_map/ppermute | solution.py:52
  8.1 4.0 %collective-permute-start = (f32[64,384]{1,0:T(8,128)S(1)}, f32[64,384]{1,0:T(8,128)S(1)}, u32[]{:S(2)}, u32[]{:S(2)}) collective-permute-start(f32[64,384]{1,0:T(8,128)S(1)} %get-tuple-element.16.refs_3_.refs_1_.points_ref), channel_id=1, source_target_pairs={{0,5},{1,2},{2,1},{3,6},{4,7},{5,0},{6,3},{7,4},{8,11},{9,12},{10,... | collective-permute-start | bytes 294920 | tf_op jit(solution)/shard_map/ppermute | solution.py:52
  9.7 9.1 %collective-permute-start.9 = (f32[64,384]{1,0:T(8,128)S(1)}, f32[64,384]{1,0:T(8,128)S(1)}, u32[]{:S(2)}, u32[]{:S(2)}) collective-permute-start(f32[64,384]{1,0:T(8,128)S(1)} %collective-permute-done.8.refs_1_), channel_id=1, source_target_pairs={{0,5},{1,2},{2,1},{3,6},{4,7},{5,0},{6,3},{7,4},{8,11},{9,12},{10,... | collective-permute-start | bytes 294920 | tf_op jit(solution)/shard_map/ppermute | solution.py:52
  12.1 8.2 %collective-permute-start.1 = (f32[72,384]{1,0:T(8,128)S(1)}, f32[72,384]{1,0:T(8,128)S(1)}, u32[]{:S(2)}, u32[]{:S(2)}) collective-permute-start(f32[72,384]{1,0:T(8,128)S(1)} %get-tuple-element.17.refs_4_), channel_id=1, source_target_pairs={{0,1},{1,0},{2,3},{3,2},{4,5},{5,4},{6,7},{7,6},{8,9},{9,8},{10,11... | collective-permute-start | bytes 331784 | tf_op jit(solution)/shard_map/ppermute | solution.py:52
  12.9 7.4 %collective-permute-start.7 = (f32[72,384]{1,0:T(8,128)S(1)}, f32[72,384]{1,0:T(8,128)S(1)}, u32[]{:S(2)}, u32[]{:S(2)}) collective-permute-start(f32[72,384]{1,0:T(8,128)S(1)} %collective-permute-done.6.refs_7_), channel_id=1, source_target_pairs={{0,1},{1,0},{2,3},{3,2},{4,5},{5,4},{6,7},{7,6},{8,9},{9,8},{10,11... | collective-permute-start | bytes 331784 | tf_op jit(solution)/shard_map/ppermute | solution.py:52
  15.0 5.4 %collective-permute-start.5 = (f32[72,384]{1,0:T(8,128)S(1)}, f32[72,384]{1,0:T(8,128)S(1)}, u32[]{:S(2)}, u32[]{:S(2)}) collective-permute-start(f32[72,384]{1,0:T(8,128)S(1)} %collective-permute-done.4.refs_6_), channel_id=1, source_target_pairs={{0,1},{1,0},{2,3},{3,2},{4,5},{5,4},{6,7},{7,6},{8,9},{9,8},{10,11... | collective-permute-start | bytes 331784 | tf_op jit(solution)/shard_map/ppermute | solution.py:52
  17.4 3.0 %collective-permute-start.3 = (f32[72,384]{1,0:T(8,128)S(1)}, f32[72,384]{1,0:T(8,128)S(1)}, u32[]{:S(2)}, u32[]{:S(2)}) collective-permute-start(f32[72,384]{1,0:T(8,128)S(1)} %collective-permute-done.2.refs_5_), channel_id=1, source_target_pairs={{0,1},{1,0},{2,3},{3,2},{4,5},{5,4},{6,7},{7,6},{8,9},{9,8},{10,11... | collective-permute-start | bytes 331784 | tf_op jit(solution)/shard_map/ppermute | solution.py:52
  17.6 1.1 %copy-start = (f32[384,384]{1,0:T(8,128)S(1)}, f32[384,384]{1,0:T(8,128)}, u32[]{:S(2)}) copy-start(f32[384,384]{1,0:T(8,128)} %metric_ref.1) | copy-start | bytes 1769476
  21.4 5.2 %collective-permute-start.11 = (f32[128,384]{1,0:T(8,128)S(1)}, f32[128,384]{1,0:T(8,128)S(1)}, u32[]{:S(2)}, u32[]{:S(2)}) collective-permute-start(f32[128,384]{1,0:T(8,128)S(1)} %get-tuple-element.23), channel_id=1, source_target_pairs={{0,3},{1,4},{2,7},{3,0},{4,1},{5,6},{6,5},{7,2},{8,13},{9,10},{10,... | collective-permute-start | bytes 589832 | tf_op jit(solution)/shard_map/ppermute | solution.py:52
  22.7 6.0 %collective-permute-start.10 = (f32[128,384]{1,0:T(8,128)S(1)}, f32[128,384]{1,0:T(8,128)S(1)}, u32[]{:S(2)}, u32[]{:S(2)}) collective-permute-start(f32[128,384]{1,0:T(8,128)S(1)} %get-tuple-element.21), channel_id=1, source_target_pairs={{0,3},{1,4},{2,7},{3,0},{4,1},{5,6},{6,5},{7,2},{8,13},{9,10},{10,... | collective-permute-start | bytes 589832 | tf_op jit(solution)/shard_map/ppermute | solution.py:52
  26.6 5.2 %collective-permute-start.12 = (f32[128,384]{1,0:T(8,128)S(1)}, f32[128,384]{1,0:T(8,128)S(1)}, u32[]{:S(2)}, u32[]{:S(2)}) collective-permute-start(f32[128,384]{1,0:T(8,128)S(1)} %add.7), channel_id=1, source_target_pairs={{0,5},{1,2},{2,1},{3,6},{4,7},{5,0},{6,3},{7,4},{8,11},{9,12},{10,... | collective-permute-start | bytes 589832 | tf_op jit(solution)/shard_map/ppermute | solution.py:52
  32.4 1.8 %collective-permute-start.13 = (f32[384,128]{1,0:T(8,128)S(1)}, f32[384,128]{1,0:T(8,128)S(1)}, u32[]{:S(2)}, u32[]{:S(2)}) collective-permute-start(f32[384,128]{1,0:T(8,128)S(1)} %get-tuple-element.25), channel_id=1, source_target_pairs={{0,1},{1,0},{2,3},{3,2},{4,5},{5,4},{6,7},{7,6},{8,9},{9,8},{10,11... | collective-permute-start | bytes 589832 | tf_op jit(solution)/shard_map/ppermute | solution.py:52
  34.3 3.6 %collective-permute-start.14 = (f32[96,128]{1,0:T(8,128)S(1)}, f32[96,128]{1,0:T(8,128)S(1)}, u32[]{:S(2)}, u32[]{:S(2)}) collective-permute-start(f32[96,128]{1,0:T(8,128)S(1)} %get-tuple-element.27), channel_id=1, source_target_pairs={{0,3},{1,4},{2,7},{3,0},{4,1},{5,6},{6,5},{7,2},{8,13},{9,10},{10,... | collective-permute-start | bytes 147464 | tf_op jit(solution)/shard_map/ppermute | solution.py:52
  35.6 3.5 %collective-permute-start.15 = (f32[96,128]{1,0:T(8,128)S(1)}, f32[96,128]{1,0:T(8,128)S(1)}, u32[]{:S(2)}, u32[]{:S(2)}) collective-permute-start(f32[96,128]{1,0:T(8,128)S(1)} %get-tuple-element.28), channel_id=1, source_target_pairs={{0,5},{1,2},{2,1},{3,6},{4,7},{5,0},{6,3},{7,4},{8,11},{9,12},{10,... | collective-permute-start | bytes 147464 | tf_op jit(solution)/shard_map/ppermute | solution.py:52
  36.1 5.0 %collective-permute-start.16 = (f32[96,128]{1,0:T(8,128)S(1)}, f32[96,128]{1,0:T(8,128)S(1)}, u32[]{:S(2)}, u32[]{:S(2)}) collective-permute-start(f32[96,128]{1,0:T(8,128)S(1)} %get-tuple-element.29), channel_id=1, source_target_pairs={{0,6},{1,7},{2,4},{3,5},{4,2},{5,3},{6,0},{7,1},{8,14},{9,15},{10,... | collective-permute-start | bytes 147464 | tf_op jit(solution)/shard_map/ppermute | solution.py:52
  41.1 6.3 %collective-permute-start.19 = (f32[96,128]{1,0:T(8,128)S(1)}, f32[96,128]{1,0:T(8,128)S(1)}, u32[]{:S(2)}, u32[]{:S(2)}) collective-permute-start(f32[96,128]{1,0:T(8,128)S(1)} %shard_map.57.refs_0_), channel_id=1, source_target_pairs={{0,24},{1,25},{2,26},{3,27},{4,28},{5,29},{6,30},{7,31},{8,16},{9,... | collective-permute-start | bytes 147464 | tf_op jit(solution)/shard_map/ppermute | solution.py:52
  43.7 5.2 %collective-permute-start.18 = (f32[96,128]{1,0:T(8,128)S(1)}, f32[96,128]{1,0:T(8,128)S(1)}, u32[]{:S(2)}, u32[]{:S(2)}) collective-permute-start(f32[96,128]{1,0:T(8,128)S(1)} %shard_map.57.refs_0_), channel_id=1, source_target_pairs={{0,17},{1,16},{2,19},{3,18},{4,21},{5,20},{6,23},{7,22},{8,25},{9,... | collective-permute-start | bytes 147464 | tf_op jit(solution)/shard_map/ppermute | solution.py:52
  43.7 5.2 %collective-permute-start.17 = (f32[96,128]{1,0:T(8,128)S(1)}, f32[96,128]{1,0:T(8,128)S(1)}, u32[]{:S(2)}, u32[]{:S(2)}) collective-permute-start(f32[96,128]{1,0:T(8,128)S(1)} %shard_map.57.refs_0_), channel_id=1, source_target_pairs={{0,9},{1,8},{2,11},{3,10},{4,13},{5,12},{6,15},{7,14},{8,1},{9,0},... | collective-permute-start | bytes 147464 | tf_op jit(solution)/shard_map/ppermute | solution.py:52
  48.9 5.4 %collective-permute-start.22 = (f32[96,128]{1,0:T(8,128)S(1)}, f32[96,128]{1,0:T(8,128)S(1)}, u32[]{:S(2)}, u32[]{:S(2)}) collective-permute-start(f32[96,128]{1,0:T(8,128)S(1)} %shard_map.58.refs_0_), channel_id=1, source_target_pairs={{0,6},{1,7},{2,4},{3,5},{4,2},{5,3},{6,0},{7,1},{8,14},{9,15},{10,... | collective-permute-start | bytes 147464 | tf_op jit(solution)/shard_map/ppermute | solution.py:52
  50.5 4.0 %collective-permute-start.21 = (f32[96,128]{1,0:T(8,128)S(1)}, f32[96,128]{1,0:T(8,128)S(1)}, u32[]{:S(2)}, u32[]{:S(2)}) collective-permute-start(f32[96,128]{1,0:T(8,128)S(1)} %shard_map.58.refs_0_), channel_id=1, source_target_pairs={{0,5},{1,2},{2,1},{3,6},{4,7},{5,0},{6,3},{7,4},{8,11},{9,12},{10,... | collective-permute-start | bytes 147464 | tf_op jit(solution)/shard_map/ppermute | solution.py:52
  50.5 4.0 %collective-permute-start.20 = (f32[96,128]{1,0:T(8,128)S(1)}, f32[96,128]{1,0:T(8,128)S(1)}, u32[]{:S(2)}, u32[]{:S(2)}) collective-permute-start(f32[96,128]{1,0:T(8,128)S(1)} %shard_map.58.refs_0_), channel_id=1, source_target_pairs={{0,3},{1,4},{2,7},{3,0},{4,1},{5,6},{6,5},{7,2},{8,13},{9,10},{10,... | collective-permute-start | bytes 147464 | tf_op jit(solution)/shard_map/ppermute | solution.py:52
  54.6 1.7 %collective-permute-start.23 = (f32[384,128]{1,0:T(8,128)S(1)}, f32[384,128]{1,0:T(8,128)S(1)}, u32[]{:S(2)}, u32[]{:S(2)}) collective-permute-start(f32[384,128]{1,0:T(8,128)S(1)} %shard_map.59.keep_ref), channel_id=1, source_target_pairs={{0,1},{1,0},{2,3},{3,2},{4,5},{5,4},{6,7},{7,6},{8,9},{9,8},{10,11... | collective-permute-start | bytes 589832 | tf_op jit(solution)/shard_map/ppermute | solution.py:52

commit v6 on v5

--- a/solution.py
+++ b/solution.py
@@ -105,13 +105,17 @@
     )(points, coeffs.T)
 
 
+def copy_after(value, wanted):
+    def body(value_ref, wanted_ref, out_ref):
+        out_ref[...] = value_ref[...]
+
+    return call(body, shape(*value.shape), [value, wanted], 1)
+
+
 def metric_halves(metric):
-    width = metric.shape[0]
-
-    def body(metric_ref, out_ref):
-        out_ref[...] = right(metric_ref[...], axis=0)
-
-    return call(body, jax.ShapeDtypeStruct((3 * width, width), BF16), [metric], 1)
+    high = lax.reduce_precision(metric, 8, 7)
+    low = (metric - high).astype(BF16)
+    return jnp.concatenate([high.astype(BF16), low, high.astype(BF16)], axis=0)
 
 
 def norm_rows(centers, metric3, own):
@@ -349,13 +353,14 @@
         points, packed = pack_own(points, coeffs)
         metric3 = metric_halves(metric)
         near = among(packed, [(bit, 0) for bit in reversed(line_bits)])
-        from_a = to_a(points)
-        from_b = to_b(points)
-        queries = [to_b(from_a), from_a, from_b, points]
+        late = [other for block in near for other in among(block, [(0, bit) for bit in col_bits])[1:]]
+        source = copy_after(points, late[0])
+        queries = [hop(source, (bit_a | bit_b, 0)), to_a(source), to_b(source), points]
         total, mapped = early_sums(queries, near, metric3, outs_n)
-        late = [other for block in near for other in among(block, [(0, bit) for bit in col_bits])[1:]]
-        part_ab, part_a = late_sums(queries[:2], 0, total, mapped, metric3, late, outs_n)
-        sent_ab, sent_a = to_a(part_ab), to_a(part_a)
+        (part_ab,) = late_sums(queries[:1], 0, total, mapped, metric3, late, outs_n)
+        sent_ab = to_a(part_ab)
+        (part_a,) = late_sums(queries[1:2], 1, total, mapped, metric3, late, outs_n)
+        sent_a = to_a(part_a)
         part_b, part_own = late_sums(queries[2:], 2, total, mapped, metric3, late, outs_n)
         sent_b = to_b(part_b + sent_ab)
 

time: 57.6 us -> 56.3 us (0.977)
  waiting for transfers between devices: 25.2 us -> 21.9 us
  other arithmetic: 0.05 us -> 1.28 us
  starting transfers between devices: 23.8 us -> 24.9 us
  local copies, waits for them, and re-layouts: 1.06 us -> 0 us
  Pallas kernels: 6.57 us -> 7.29 us
    ppermute x24, waiting for transfers between devices: 25.2 us -> 21.9 us  [hop(): return lax.ppermute(value, AXES, pairs)]
    convert_element_type x0 -> x1, other arithmetic: none -> 1.14 us  [metric_halves(): low = (metric - high).astype(BF16)]
    unnamed x2 -> x0, local copies, waits for them, and re-layouts: 1.06 us -> none
    ppermute x24, starting transfers between devices: 23.8 us -> 24.9 us  [hop(): return lax.ppermute(value, AXES, pairs)]
    pallas_call x9 -> x10, Pallas kernels: 4.44 us -> 5.16 us  [call(): pl.pallas_call(body, out_shape=out_shape, in_specs=[pl.BlockSpec(memory_s...]
  transfers between devices with their start and end apart: 24 -> 24, of which waited for: 15 -> 13; matrix products, arithmetic and copies ran while one was open for 0% -> 2% of each run, Pallas kernels for 5% -> 6%
where the time goes in v6:
time: 56.3 us; the launch traced here: 56.1 us
  starting transfers between devices  24.9 us (44%)
  waiting for transfers between devices  21.9 us (39%)
  Pallas kernels  7.29 us (13%)
  other arithmetic  1.28 us (2%)
  between operations  0.75 us (1%)
    ppermute x24, starting transfers between devices, hop(): return lax.ppermute(value, AXES, pairs)  24.9 us
    ppermute x24, waiting for transfers between devices, hop(): return lax.ppermute(value, AXES, pairs)  21.9 us
    pallas_call x10, Pallas kernels, call(): pl.pallas_call(body, out_shape=out_shape, in_specs=[pl.BlockSpec(memory_s...  5.16 us
    pallas_call x1, Pallas kernels, finish(): pl.pallas_call(body, out_shape=(shape(width, width), shape(rows, width)),...  1.21 us
    convert_element_type x1, other arithmetic, metric_halves(): low = (metric - high).astype(BF16)  1.14 us
  transfers between devices with their start and end apart: 24, of which 13 were waited for; matrix products, arithmetic and copies ran while one was open for 2% of the time, Pallas kernels for 6%

profile of v6, /device:TPU:0, one launch (start us, length us, event | category | flops | bytes accessed | tf_op | source)
XLA Modules:
  0.0 56.1 jit_solution(17820267448451854163)
XLA Ops:
  0.6 0.9 %shard_map.50 = (f32[64,384]{1,0:T(8,128)S(1)}, f32[72,384]{1,0:T(8,128)S(1)}) custom-call(f32[64,384]{1,0:T(8,128)} %points_ref.1, f32[2,64]{1,0:T(2,128)} %bitcast.1), custom_call_target="tpu_custom_call" | custom-call | tf_op jit(solution)/shard_map/pallas_call | solution.py:99
  1.6 0.5 collective-permute-start
  2.1 4.7 %collective-permute-start.6 = (f32[72,384]{1,0:T(8,128)S(1)}, f32[72,384]{1,0:T(8,128)S(1)}, u32[]{:S(2)}, u32[]{:S(2)}) collective-permute-start(f32[72,384]{1,0:T(8,128)S(1)} %get-tuple-element.15.refs_4_), channel_id=1, source_target_pairs={{0,24},{1,25},{2,26},{3,27},{4,28},{5,29},{6,30},{7,31},{8,16},{9,... | collective-permute-start | bytes 331784 | tf_op jit(solution)/shard_map/ppermute | solution.py:52
  6.7 0.0 collective-permute-start.4
  6.8 0.4 collective-permute-start.2
  7.1 0.0 collective-permute-done.wanted_ref.refs_2_.refs_1_
  7.1 1.5 %collective-permute-start.9 = (f32[64,384]{1,0:T(8,128)S(1)}, f32[64,384]{1,0:T(8,128)S(1)}, u32[]{:S(2)}, u32[]{:S(2)}) collective-permute-start(f32[64,384]{1,0:T(8,128)S(1)} %shard_map.51), channel_id=1, source_target_pairs={{0,3},{1,4},{2,7},{3,0},{4,1},{5,6},{6,5},{7,2},{8,13},{9,10},{10,... | collective-permute-start | bytes 294920 | tf_op jit(solution)/shard_map/ppermute | solution.py:52
  8.6 1.1 %fusion = (bf16[384,384]{1,0:T(8,128)(2,1)S(1)}, bf16[384,384]{1,0:T(8,128)(2,1)S(1)}) fusion(f32[384,384]{1,0:T(8,128)} %param.5), kind=kLoop, calls=%fused_computation.3 | loop fusion | flops 589824 | bytes 1179648 | tf_op jit(solution)/shard_map/convert_element_type | solution.py:117
  9.8 1.6 %collective-permute-start.8 = (f32[64,384]{1,0:T(8,128)S(1)}, f32[64,384]{1,0:T(8,128)S(1)}, u32[]{:S(2)}, u32[]{:S(2)}) collective-permute-start(f32[64,384]{1,0:T(8,128)S(1)} %shard_map.51), channel_id=1, source_target_pairs={{0,6},{1,7},{2,4},{3,5},{4,2},{5,3},{6,0},{7,1},{8,14},{9,15},{10,... | collective-permute-start | bytes 294920 | tf_op jit(solution)/shard_map/ppermute | solution.py:52
  11.3 0.0 collective-permute-done.6.refs_7_
  11.3 0.0 collective-permute-start.1
  11.4 2.4 %collective-permute-done.4.refs_6_ = f32[72,384]{1,0:T(8,128)S(1)} collective-permute-done((f32[72,384]{1,0:T(8,128)S(1)}, f32[72,384]{1,0:T(8,128)S(1)}, u32[]{:S(2)}, u32[]{:S(2)}) %collective-permute-start.4) | collective-permute-done | bytes 110624 | tf_op jit(solution)/shard_map/ppermute | solution.py:52
  13.8 0.1 collective-permute-start.7
  14.0 2.3 %collective-permute-done.2.refs_5_ = f32[72,384]{1,0:T(8,128)S(1)} collective-permute-done((f32[72,384]{1,0:T(8,128)S(1)}, f32[72,384]{1,0:T(8,128)S(1)}, u32[]{:S(2)}, u32[]{:S(2)}) %collective-permute-start.2) | collective-permute-done | bytes 110624 | tf_op jit(solution)/shard_map/ppermute | solution.py:52
  16.2 0.3 collective-permute-start.5
  16.5 0.0 collective-permute-done.9.refs_1_.refs_0_
  16.5 0.2 collective-permute-start.3
  16.7 0.1 pad_maximum_fusion.refs_8_.refs_7_.metric3_ref
  16.8 0.0 collective-permute-done.8.refs_0_
  16.8 0.0 collective-permute-done.1.refs_2_.refs_0_
  16.8 1.6 %shard_map.52 = (f32[2,256,384]{2,1,0:T(8,128)S(1)}, f32[256,384]{1,0:T(8,128)S(1)}) custom-call(f32[64,384]{1,0:T(8,128)S(1)} %collective-permute-done.8.refs_0_, f32[64,384]{1,0:T(8,128)S(1)} %collective-permute-done.9.refs_1_.refs_0_, f32[64,384]{1,0:T(8,128)S(1)} %collective-permute-done.1.refs_2_.refs_0_, ...), custom_call_target="tpu_custom_call" | custom-call | flops 764411904 | bytes 3784704 | tf_op jit(solution)/shard_map/pallas_call | solution.py:66
  18.4 0.0 collective-permute-done.7.refs_5_.refs_4_
  18.4 0.0 collective-permute-done.5.refs_4_.refs_3_
  18.4 0.0 collective-permute-done.3.refs_3_.refs_2_
  18.4 0.9 %shard_map.55 = f32[128,384]{1,0:T(8,128)S(1)} custom-call(f32[64,384]{1,0:T(8,128)S(1)} %collective-permute-done.8.refs_0_, f32[72,384]{1,0:T(8,128)S(1)} %collective-permute-done.wanted_ref.refs_2_.refs_1_, f32[72,384]{1,0:T(8,128)S(1)} %collective-permute-done.3.refs_3_.refs_2_, f32[72,384]{1,0:T(8,128)S(1)} %collective-permute-done.5.refs_4_.refs_3_, ...), custom_call_target="tpu_custom_call" | custom-call | flops 325582848 | bytes 3686400 | tf_op jit(solution)/shard_map/pallas_call | solution.py:66
  19.4 1.4 %collective-permute-start.11 = (f32[128,384]{1,0:T(8,128)S(1)}, f32[128,384]{1,0:T(8,128)S(1)}, u32[]{:S(2)}, u32[]{:S(2)}) collective-permute-start(f32[128,384]{1,0:T(8,128)S(1)} %shard_map.55), channel_id=1, source_target_pairs={{0,3},{1,4},{2,7},{3,0},{4,1},{5,6},{6,5},{7,2},{8,13},{9,10},{10,... | collective-permute-start | bytes 589832 | tf_op jit(solution)/shard_map/ppermute | solution.py:52
  20.8 0.9 %shard_map.54 = f32[128,384]{1,0:T(8,128)S(1)} custom-call(f32[64,384]{1,0:T(8,128)S(1)} %collective-permute-done.9.refs_1_.refs_0_, f32[72,384]{1,0:T(8,128)S(1)} %collective-permute-done.wanted_ref.refs_2_.refs_1_, f32[72,384]{1,0:T(8,128)S(1)} %collective-permute-done.3.refs_3_.refs_2_, f32[72,384]{1,0:T(8,128)S(1)} %collective-permute-done.5.refs_4_.refs_3_, ...), custom_call_target="tpu_custom_call" | custom-call | flops 325582848 | bytes 3686400 | tf_op jit(solution)/shard_map/pallas_call | solution.py:66
  21.8 0.5 collective-permute-start.10
  22.2 1.0 %shard_map.53 = (f32[128,384]{1,0:T(8,128)S(1)}, f32[128,384]{1,0:T(8,128)S(1)}) custom-call(f32[64,384]{1,0:T(8,128)S(1)} %collective-permute-done.1.refs_2_.refs_0_, f32[64,384]{1,0:T(8,128)S(1)} %get-tuple-element.14.value_ref.refs_3_.refs_1_.points_ref, f32[72,384]{1,0:T(8,128)S(1)} %collective-permute-done.wanted_ref.refs_2_.refs_1_, ...), custom_call_target="tpu_custom_call" | custom-call | flops 396361728 | bytes 3981312 | tf_op jit(solution)/shard_map/pallas_call | solution.py:66
  23.2 1.3 %collective-permute-done.11 = f32[128,384]{1,0:T(8,128)S(1)} collective-permute-done((f32[128,384]{1,0:T(8,128)S(1)}, f32[128,384]{1,0:T(8,128)S(1)}, u32[]{:S(2)}, u32[]{:S(2)}) %collective-permute-start.11) | collective-permute-done | bytes 196640 | tf_op jit(solution)/shard_map/ppermute | solution.py:52
  24.6 1.8 %collective-permute-start.12 = (f32[128,384]{1,0:T(8,128)S(1)}, f32[128,384]{1,0:T(8,128)S(1)}, u32[]{:S(2)}, u32[]{:S(2)}) collective-permute-start(f32[128,384]{1,0:T(8,128)S(1)} %add.7), channel_id=1, source_target_pairs={{0,5},{1,2},{2,1},{3,6},{4,7},{5,0},{6,3},{7,4},{8,11},{9,12},{10,... | collective-permute-start | bytes 589832 | tf_op jit(solution)/shard_map/ppermute | solution.py:52
  26.3 0.6 %collective-permute-done.10 = f32[128,384]{1,0:T(8,128)S(1)} collective-permute-done((f32[128,384]{1,0:T(8,128)S(1)}, f32[128,384]{1,0:T(8,128)S(1)}, u32[]{:S(2)}, u32[]{:S(2)}) %collective-permute-start.10) | collective-permute-done | bytes 196640 | tf_op jit(solution)/shard_map/ppermute | solution.py:52
  27.0 2.8 %collective-permute-done.12.arrived_ref = f32[128,384]{1,0:T(8,128)S(1)} collective-permute-done((f32[128,384]{1,0:T(8,128)S(1)}, f32[128,384]{1,0:T(8,128)S(1)}, u32[]{:S(2)}, u32[]{:S(2)}) %collective-permute-start.12) | collective-permute-done | bytes 196640 | tf_op jit(solution)/shard_map/ppermute | solution.py:52
  29.7 0.6 %shard_map.56 = (f32[384,128]{1,0:T(8,128)S(1)}, f32[384,128]{1,0:T(8,128)S(1)}) custom-call(f32[128,384]{1,0:T(8,128)S(1)} %add.6.part_ref, f32[128,384]{1,0:T(8,128)S(1)} %collective-permute-done.12.arrived_ref, bf16[1152,384]{1,0:T(8,128)(2,1)S(1)} %pad_maximum_fusion.refs_8_.refs_7_.metric3_ref), custom_call_target="tpu_custom_call" | custom-call | flops 226492416 | bytes 2555904 | tf_op jit(solution)/shard_map/pallas_call | solution.py:66
  30.4 0.6 %collective-permute-start.13 = (f32[384,128]{1,0:T(8,128)S(1)}, f32[384,128]{1,0:T(8,128)S(1)}, u32[]{:S(2)}, u32[]{:S(2)}) collective-permute-start(f32[384,128]{1,0:T(8,128)S(1)} %get-tuple-element.21), channel_id=1, source_target_pairs={{0,1},{1,0},{2,3},{3,2},{4,5},{5,4},{6,7},{7,6},{8,9},{9,8},{10,11... | collective-permute-start | bytes 589832 | tf_op jit(solution)/shard_map/ppermute | solution.py:52
  31.0 1.1 %collective-permute-done.13.arrived_ref = f32[384,128]{1,0:T(8,128)S(1)} collective-permute-done((f32[384,128]{1,0:T(8,128)S(1)}, f32[384,128]{1,0:T(8,128)S(1)}, u32[]{:S(2)}, u32[]{:S(2)}) %collective-permute-start.13) | collective-permute-done | bytes 196640 | tf_op jit(solution)/shard_map/ppermute | solution.py:52
  32.1 1.5 %collective-permute-start.14 = (f32[96,128]{1,0:T(8,128)S(1)}, f32[96,128]{1,0:T(8,128)S(1)}, u32[]{:S(2)}, u32[]{:S(2)}) collective-permute-start(f32[96,128]{1,0:T(8,128)S(1)} %get-tuple-element.23), channel_id=1, source_target_pairs={{0,3},{1,4},{2,7},{3,0},{4,1},{5,6},{6,5},{7,2},{8,13},{9,10},{10,... | collective-permute-start | bytes 147464 | tf_op jit(solution)/shard_map/ppermute | solution.py:52
  33.6 1.3 %collective-permute-start.15 = (f32[96,128]{1,0:T(8,128)S(1)}, f32[96,128]{1,0:T(8,128)S(1)}, u32[]{:S(2)}, u32[]{:S(2)}) collective-permute-start(f32[96,128]{1,0:T(8,128)S(1)} %get-tuple-element.24), channel_id=1, source_target_pairs={{0,5},{1,2},{2,1},{3,6},{4,7},{5,0},{6,3},{7,4},{8,11},{9,12},{10,... | collective-permute-start | bytes 147464 | tf_op jit(solution)/shard_map/ppermute | solution.py:52
  34.9 0.5 collective-permute-start.16
  35.4 0.3 collective-permute-done.14.refs_1_
  35.7 1.5 %collective-permute-done.15.refs_2_ = f32[96,128]{1,0:T(8,128)S(1)} collective-permute-done((f32[96,128]{1,0:T(8,128)S(1)}, f32[96,128]{1,0:T(8,128)S(1)}, u32[]{:S(2)}, u32[]{:S(2)}) %collective-permute-start.15) | collective-permute-done | bytes 49184 | tf_op jit(solution)/shard_map/ppermute | solution.py:52
  37.2 2.8 %collective-permute-done.16.refs_3_ = f32[96,128]{1,0:T(8,128)S(1)} collective-permute-done((f32[96,128]{1,0:T(8,128)S(1)}, f32[96,128]{1,0:T(8,128)S(1)}, u32[]{:S(2)}, u32[]{:S(2)}) %collective-permute-start.16) | collective-permute-done | bytes 49184 | tf_op jit(solution)/shard_map/ppermute | solution.py:52
  39.9 2.6 %collective-permute-start.19 = (f32[96,128]{1,0:T(8,128)S(1)}, f32[96,128]{1,0:T(8,128)S(1)}, u32[]{:S(2)}, u32[]{:S(2)}) collective-permute-start(f32[96,128]{1,0:T(8,128)S(1)} %shard_map.58.refs_0_), channel_id=1, source_target_pairs={{0,24},{1,25},{2,26},{3,27},{4,28},{5,29},{6,30},{7,31},{8,16},{9,... | collective-permute-start | bytes 147464 | tf_op jit(solution)/shard_map/ppermute | solution.py:52
  42.6 0.0 collective-permute-start.18
  42.6 1.5 %collective-permute-start.17 = (f32[96,128]{1,0:T(8,128)S(1)}, f32[96,128]{1,0:T(8,128)S(1)}, u32[]{:S(2)}, u32[]{:S(2)}) collective-permute-start(f32[96,128]{1,0:T(8,128)S(1)} %shard_map.58.refs_0_), channel_id=1, source_target_pairs={{0,9},{1,8},{2,11},{3,10},{4,13},{5,12},{6,15},{7,14},{8,1},{9,0},... | collective-permute-start | bytes 147464 | tf_op jit(solution)/shard_map/ppermute | solution.py:52
  44.1 2.2 %collective-permute-done.19.refs_3_ = f32[96,128]{1,0:T(8,128)S(1)} collective-permute-done((f32[96,128]{1,0:T(8,128)S(1)}, f32[96,128]{1,0:T(8,128)S(1)}, u32[]{:S(2)}, u32[]{:S(2)}) %collective-permute-start.19) | collective-permute-done | bytes 49184 | tf_op jit(solution)/shard_map/ppermute | solution.py:52
  46.3 1.5 %collective-permute-done.18.refs_2_ = f32[96,128]{1,0:T(8,128)S(1)} collective-permute-done((f32[96,128]{1,0:T(8,128)S(1)}, f32[96,128]{1,0:T(8,128)S(1)}, u32[]{:S(2)}, u32[]{:S(2)}) %collective-permute-start.18) | collective-permute-done | bytes 49184 | tf_op jit(solution)/shard_map/ppermute | solution.py:52
  47.8 0.0 collective-permute-done.17.refs_1_
  47.8 1.0 %collective-permute-start.22 = (f32[96,128]{1,0:T(8,128)S(1)}, f32[96,128]{1,0:T(8,128)S(1)}, u32[]{:S(2)}, u32[]{:S(2)}) collective-permute-start(f32[96,128]{1,0:T(8,128)S(1)} %shard_map.59.refs_0_), channel_id=1, source_target_pairs={{0,6},{1,7},{2,4},{3,5},{4,2},{5,3},{6,0},{7,1},{8,14},{9,15},{10,... | collective-permute-start | bytes 147464 | tf_op jit(solution)/shard_map/ppermute | solution.py:52
  48.8 0.6 %collective-permute-start.21 = (f32[96,128]{1,0:T(8,128)S(1)}, f32[96,128]{1,0:T(8,128)S(1)}, u32[]{:S(2)}, u32[]{:S(2)}) collective-permute-start(f32[96,128]{1,0:T(8,128)S(1)} %shard_map.59.refs_0_), channel_id=1, source_target_pairs={{0,5},{1,2},{2,1},{3,6},{4,7},{5,0},{6,3},{7,4},{8,11},{9,12},{10,... | collective-permute-start | bytes 147464 | tf_op jit(solution)/shard_map/ppermute | solution.py:52
  49.4 1.6 %collective-permute-start.20 = (f32[96,128]{1,0:T(8,128)S(1)}, f32[96,128]{1,0:T(8,128)S(1)}, u32[]{:S(2)}, u32[]{:S(2)}) collective-permute-start(f32[96,128]{1,0:T(8,128)S(1)} %shard_map.59.refs_0_), channel_id=1, source_target_pairs={{0,3},{1,4},{2,7},{3,0},{4,1},{5,6},{6,5},{7,2},{8,13},{9,10},{10,... | collective-permute-start | bytes 147464 | tf_op jit(solution)/shard_map/ppermute | solution.py:52
  51.1 2.1 %collective-permute-done.22.refs_3_ = f32[96,128]{1,0:T(8,128)S(1)} collective-permute-done((f32[96,128]{1,0:T(8,128)S(1)}, f32[96,128]{1,0:T(8,128)S(1)}, u32[]{:S(2)}, u32[]{:S(2)}) %collective-permute-start.22) | collective-permute-done | bytes 49184 | tf_op jit(solution)/shard_map/ppermute | solution.py:52
  53.2 0.0 collective-permute-done.21.refs_2_
  53.2 0.0 collective-permute-done.20.refs_1_
  53.2 0.5 collective-permute-start.23
  53.8 1.1 %collective-permute-done.23.other_ref = f32[384,128]{1,0:T(8,128)S(1)} collective-permute-done((f32[384,128]{1,0:T(8,128)S(1)}, f32[384,128]{1,0:T(8,128)S(1)}, u32[]{:S(2)}, u32[]{:S(2)}) %collective-permute-start.23) | collective-permute-done | bytes 196640 | tf_op jit(solution)/shard_map/ppermute | solution.py:52
  54.8 1.2 %shard_map.61 = (f32[384,384]{1,0:T(8,128)}, f32[64,384]{1,0:T(8,128)}) custom-call(f32[384,128]{1,0:T(8,128)S(1)} %shard_map.60.keep_ref, f32[384,128]{1,0:T(8,128)S(1)} %collective-permute-done.23.other_ref, f32[64,384]{1,0:T(8,128)S(1)} %get-tuple-element.14.value_ref.refs_3_.refs_1_.points_ref), custom_call_target="tpu_custom_call" | custom-call | tf_op jit(solution)/shard_map/pallas_call | solution.py:314
  (7 shorter events, 0.1 us)
Async XLA Ops:
  1.6 5.6 %collective-permute-start = (f32[72,384]{1,0:T(8,128)S(1)}, f32[72,384]{1,0:T(8,128)S(1)}, u32[]{:S(2)}, u32[]{:S(2)}) collective-permute-start(f32[72,384]{1,0:T(8,128)S(1)} %get-tuple-element.15.refs_4_), channel_id=1, source_target_pairs={{0,1},{1,0},{2,3},{3,2},{4,5},{5,4},{6,7},{7,6},{8,9},{9,8},{10,11... | collective-permute-start | bytes 331784 | tf_op jit(solution)/shard_map/ppermute | solution.py:52
  2.1 9.3 %collective-permute-start.6 = (f32[72,384]{1,0:T(8,128)S(1)}, f32[72,384]{1,0:T(8,128)S(1)}, u32[]{:S(2)}, u32[]{:S(2)}) collective-permute-start(f32[72,384]{1,0:T(8,128)S(1)} %get-tuple-element.15.refs_4_), channel_id=1, source_target_pairs={{0,24},{1,25},{2,26},{3,27},{4,28},{5,29},{6,30},{7,31},{8,16},{9,... | collective-permute-start | bytes 331784 | tf_op jit(solution)/shard_map/ppermute | solution.py:52
  6.7 7.1 %collective-permute-start.4 = (f32[72,384]{1,0:T(8,128)S(1)}, f32[72,384]{1,0:T(8,128)S(1)}, u32[]{:S(2)}, u32[]{:S(2)}) collective-permute-start(f32[72,384]{1,0:T(8,128)S(1)} %get-tuple-element.15.refs_4_), channel_id=1, source_target_pairs={{0,9},{1,8},{2,11},{3,10},{4,13},{5,12},{6,15},{7,14},{8,1},{9,0},... | collective-permute-start | bytes 331784 | tf_op jit(solution)/shard_map/ppermute | solution.py:52
  6.8 9.5 %collective-permute-start.2 = (f32[72,384]{1,0:T(8,128)S(1)}, f32[72,384]{1,0:T(8,128)S(1)}, u32[]{:S(2)}, u32[]{:S(2)}) collective-permute-start(f32[72,384]{1,0:T(8,128)S(1)} %get-tuple-element.15.refs_4_), channel_id=1, source_target_pairs={{0,17},{1,16},{2,19},{3,18},{4,21},{5,20},{6,23},{7,22},{8,25},{9,... | collective-permute-start | bytes 331784 | tf_op jit(solution)/shard_map/ppermute | solution.py:52
  7.1 9.4 %collective-permute-start.9 = (f32[64,384]{1,0:T(8,128)S(1)}, f32[64,384]{1,0:T(8,128)S(1)}, u32[]{:S(2)}, u32[]{:S(2)}) collective-permute-start(f32[64,384]{1,0:T(8,128)S(1)} %shard_map.51), channel_id=1, source_target_pairs={{0,3},{1,4},{2,7},{3,0},{4,1},{5,6},{6,5},{7,2},{8,13},{9,10},{10,... | collective-permute-start | bytes 294920 | tf_op jit(solution)/shard_map/ppermute | solution.py:52
  9.8 7.0 %collective-permute-start.8 = (f32[64,384]{1,0:T(8,128)S(1)}, f32[64,384]{1,0:T(8,128)S(1)}, u32[]{:S(2)}, u32[]{:S(2)}) collective-permute-start(f32[64,384]{1,0:T(8,128)S(1)} %shard_map.51), channel_id=1, source_target_pairs={{0,6},{1,7},{2,4},{3,5},{4,2},{5,3},{6,0},{7,1},{8,14},{9,15},{10,... | collective-permute-start | bytes 294920 | tf_op jit(solution)/shard_map/ppermute | solution.py:52
  11.3 5.5 %collective-permute-start.1 = (f32[64,384]{1,0:T(8,128)S(1)}, f32[64,384]{1,0:T(8,128)S(1)}, u32[]{:S(2)}, u32[]{:S(2)}) collective-permute-start(f32[64,384]{1,0:T(8,128)S(1)} %shard_map.51), channel_id=1, source_target_pairs={{0,5},{1,2},{2,1},{3,6},{4,7},{5,0},{6,3},{7,4},{8,11},{9,12},{10,... | collective-permute-start | bytes 294920 | tf_op jit(solution)/shard_map/ppermute | solution.py:52
  13.8 4.6 %collective-permute-start.7 = (f32[72,384]{1,0:T(8,128)S(1)}, f32[72,384]{1,0:T(8,128)S(1)}, u32[]{:S(2)}, u32[]{:S(2)}) collective-permute-start(f32[72,384]{1,0:T(8,128)S(1)} %collective-permute-done.6.refs_7_), channel_id=1, source_target_pairs={{0,1},{1,0},{2,3},{3,2},{4,5},{5,4},{6,7},{7,6},{8,9},{9,8},{10,11... | collective-permute-start | bytes 331784 | tf_op jit(solution)/shard_map/ppermute | solution.py:52
  16.2 2.2 %collective-permute-start.5 = (f32[72,384]{1,0:T(8,128)S(1)}, f32[72,384]{1,0:T(8,128)S(1)}, u32[]{:S(2)}, u32[]{:S(2)}) collective-permute-start(f32[72,384]{1,0:T(8,128)S(1)} %collective-permute-done.4.refs_6_), channel_id=1, source_target_pairs={{0,1},{1,0},{2,3},{3,2},{4,5},{5,4},{6,7},{7,6},{8,9},{9,8},{10,11... | collective-permute-start | bytes 331784 | tf_op jit(solution)/shard_map/ppermute | solution.py:52
  16.5 1.9 %collective-permute-start.3 = (f32[72,384]{1,0:T(8,128)S(1)}, f32[72,384]{1,0:T(8,128)S(1)}, u32[]{:S(2)}, u32[]{:S(2)}) collective-permute-start(f32[72,384]{1,0:T(8,128)S(1)} %collective-permute-done.2.refs_5_), channel_id=1, source_target_pairs={{0,1},{1,0},{2,3},{3,2},{4,5},{5,4},{6,7},{7,6},{8,9},{9,8},{10,11... | collective-permute-start | bytes 331784 | tf_op jit(solution)/shard_map/ppermute | solution.py:52
  19.4 5.2 %collective-permute-start.11 = (f32[128,384]{1,0:T(8,128)S(1)}, f32[128,384]{1,0:T(8,128)S(1)}, u32[]{:S(2)}, u32[]{:S(2)}) collective-permute-start(f32[128,384]{1,0:T(8,128)S(1)} %shard_map.55), channel_id=1, source_target_pairs={{0,3},{1,4},{2,7},{3,0},{4,1},{5,6},{6,5},{7,2},{8,13},{9,10},{10,... | collective-permute-start | bytes 589832 | tf_op jit(solution)/shard_map/ppermute | solution.py:52
  21.8 5.2 %collective-permute-start.10 = (f32[128,384]{1,0:T(8,128)S(1)}, f32[128,384]{1,0:T(8,128)S(1)}, u32[]{:S(2)}, u32[]{:S(2)}) collective-permute-start(f32[128,384]{1,0:T(8,128)S(1)} %shard_map.54), channel_id=1, source_target_pairs={{0,3},{1,4},{2,7},{3,0},{4,1},{5,6},{6,5},{7,2},{8,13},{9,10},{10,... | collective-permute-start | bytes 589832 | tf_op jit(solution)/shard_map/ppermute | solution.py:52
  24.6 5.2 %collective-permute-start.12 = (f32[128,384]{1,0:T(8,128)S(1)}, f32[128,384]{1,0:T(8,128)S(1)}, u32[]{:S(2)}, u32[]{:S(2)}) collective-permute-start(f32[128,384]{1,0:T(8,128)S(1)} %add.7), channel_id=1, source_target_pairs={{0,5},{1,2},{2,1},{3,6},{4,7},{5,0},{6,3},{7,4},{8,11},{9,12},{10,... | collective-permute-start | bytes 589832 | tf_op jit(solution)/shard_map/ppermute | solution.py:52
  30.4 1.7 %collective-permute-start.13 = (f32[384,128]{1,0:T(8,128)S(1)}, f32[384,128]{1,0:T(8,128)S(1)}, u32[]{:S(2)}, u32[]{:S(2)}) collective-permute-start(f32[384,128]{1,0:T(8,128)S(1)} %get-tuple-element.21), channel_id=1, source_target_pairs={{0,1},{1,0},{2,3},{3,2},{4,5},{5,4},{6,7},{7,6},{8,9},{9,8},{10,11... | collective-permute-start | bytes 589832 | tf_op jit(solution)/shard_map/ppermute | solution.py:52
  32.1 3.6 %collective-permute-start.14 = (f32[96,128]{1,0:T(8,128)S(1)}, f32[96,128]{1,0:T(8,128)S(1)}, u32[]{:S(2)}, u32[]{:S(2)}) collective-permute-start(f32[96,128]{1,0:T(8,128)S(1)} %get-tuple-element.23), channel_id=1, source_target_pairs={{0,3},{1,4},{2,7},{3,0},{4,1},{5,6},{6,5},{7,2},{8,13},{9,10},{10,... | collective-permute-start | bytes 147464 | tf_op jit(solution)/shard_map/ppermute | solution.py:52
  33.6 3.5 %collective-permute-start.15 = (f32[96,128]{1,0:T(8,128)S(1)}, f32[96,128]{1,0:T(8,128)S(1)}, u32[]{:S(2)}, u32[]{:S(2)}) collective-permute-start(f32[96,128]{1,0:T(8,128)S(1)} %get-tuple-element.24), channel_id=1, source_target_pairs={{0,5},{1,2},{2,1},{3,6},{4,7},{5,0},{6,3},{7,4},{8,11},{9,12},{10,... | collective-permute-start | bytes 147464 | tf_op jit(solution)/shard_map/ppermute | solution.py:52
  34.9 5.0 %collective-permute-start.16 = (f32[96,128]{1,0:T(8,128)S(1)}, f32[96,128]{1,0:T(8,128)S(1)}, u32[]{:S(2)}, u32[]{:S(2)}) collective-permute-start(f32[96,128]{1,0:T(8,128)S(1)} %get-tuple-element.25), channel_id=1, source_target_pairs={{0,6},{1,7},{2,4},{3,5},{4,2},{5,3},{6,0},{7,1},{8,14},{9,15},{10,... | collective-permute-start | bytes 147464 | tf_op jit(solution)/shard_map/ppermute | solution.py:52
  39.9 6.4 %collective-permute-start.19 = (f32[96,128]{1,0:T(8,128)S(1)}, f32[96,128]{1,0:T(8,128)S(1)}, u32[]{:S(2)}, u32[]{:S(2)}) collective-permute-start(f32[96,128]{1,0:T(8,128)S(1)} %shard_map.58.refs_0_), channel_id=1, source_target_pairs={{0,24},{1,25},{2,26},{3,27},{4,28},{5,29},{6,30},{7,31},{8,16},{9,... | collective-permute-start | bytes 147464 | tf_op jit(solution)/shard_map/ppermute | solution.py:52
  42.6 5.2 %collective-permute-start.18 = (f32[96,128]{1,0:T(8,128)S(1)}, f32[96,128]{1,0:T(8,128)S(1)}, u32[]{:S(2)}, u32[]{:S(2)}) collective-permute-start(f32[96,128]{1,0:T(8,128)S(1)} %shard_map.58.refs_0_), channel_id=1, source_target_pairs={{0,17},{1,16},{2,19},{3,18},{4,21},{5,20},{6,23},{7,22},{8,25},{9,... | collective-permute-start | bytes 147464 | tf_op jit(solution)/shard_map/ppermute | solution.py:52
  42.6 5.2 %collective-permute-start.17 = (f32[96,128]{1,0:T(8,128)S(1)}, f32[96,128]{1,0:T(8,128)S(1)}, u32[]{:S(2)}, u32[]{:S(2)}) collective-permute-start(f32[96,128]{1,0:T(8,128)S(1)} %shard_map.58.refs_0_), channel_id=1, source_target_pairs={{0,9},{1,8},{2,11},{3,10},{4,13},{5,12},{6,15},{7,14},{8,1},{9,0},... | collective-permute-start | bytes 147464 | tf_op jit(solution)/shard_map/ppermute | solution.py:52
  47.8 5.4 %collective-permute-start.22 = (f32[96,128]{1,0:T(8,128)S(1)}, f32[96,128]{1,0:T(8,128)S(1)}, u32[]{:S(2)}, u32[]{:S(2)}) collective-permute-start(f32[96,128]{1,0:T(8,128)S(1)} %shard_map.59.refs_0_), channel_id=1, source_target_pairs={{0,6},{1,7},{2,4},{3,5},{4,2},{5,3},{6,0},{7,1},{8,14},{9,15},{10,... | collective-permute-start | bytes 147464 | tf_op jit(solution)/shard_map/ppermute | solution.py:52
  48.8 4.4 %collective-permute-start.21 = (f32[96,128]{1,0:T(8,128)S(1)}, f32[96,128]{1,0:T(8,128)S(1)}, u32[]{:S(2)}, u32[]{:S(2)}) collective-permute-start(f32[96,128]{1,0:T(8,128)S(1)} %shard_map.59.refs_0_), channel_id=1, source_target_pairs={{0,5},{1,2},{2,1},{3,6},{4,7},{5,0},{6,3},{7,4},{8,11},{9,12},{10,... | collective-permute-start | bytes 147464 | tf_op jit(solution)/shard_map/ppermute | solution.py:52
  49.4 3.8 %collective-permute-start.20 = (f32[96,128]{1,0:T(8,128)S(1)}, f32[96,128]{1,0:T(8,128)S(1)}, u32[]{:S(2)}, u32[]{:S(2)}) collective-permute-start(f32[96,128]{1,0:T(8,128)S(1)} %shard_map.59.refs_0_), channel_id=1, source_target_pairs={{0,3},{1,4},{2,7},{3,0},{4,1},{5,6},{6,5},{7,2},{8,13},{9,10},{10,... | collective-permute-start | bytes 147464 | tf_op jit(solution)/shard_map/ppermute | solution.py:52
  53.2 1.6 %collective-permute-start.23 = (f32[384,128]{1,0:T(8,128)S(1)}, f32[384,128]{1,0:T(8,128)S(1)}, u32[]{:S(2)}, u32[]{:S(2)}) collective-permute-start(f32[384,128]{1,0:T(8,128)S(1)} %shard_map.60.keep_ref), channel_id=1, source_target_pairs={{0,1},{1,0},{2,3},{3,2},{4,5},{5,4},{6,7},{7,6},{8,9},{9,8},{10,11... | collective-permute-start | bytes 589832 | tf_op jit(solution)/shard_map/ppermute | solution.py:52

commit v7 on v6

--- a/solution.py
+++ b/solution.py
@@ -212,28 +212,36 @@
     return tile, span, [(i, j) for i in range(span) for j in range(i, span)]
 
 
-def outer_halves(part, arrived, metric3, rows_all):
-    width = part.shape[1]
+def outer_quarters(sums, metric3, rows_all):
+    width = metric3.shape[1]
     tile, span, upper = upper_tiles(width)
-    half = (len(upper) + 1) // 2
-
-    def body(part_ref, arrived_ref, metric3_ref, keep_ref, send_ref):
-        odd = my_kind(rows_all) == 1
-        grads = mul(left(part_ref[...] + arrived_ref[...]), metric3_ref[...])
+    count = round_up(len(upper), 2)
+    rows = count * tile // 4
+
+    def body(*refs):
+        metric3_ref, mine_ref, away_ref, full_ref = refs[len(sums) :]
+        pairs = [refs[k][...] + refs[k + 1][...] for k in range(0, len(sums), 2)]
+        grads = mul(left(jnp.concatenate(pairs, axis=0)), metric3_ref[...])
         grads_left, grads_right = left(grads, 0), right(grads, 0)
-        tiles = [[] for _ in upper]
         for i in range(span):
             slab = mul(grads_left[:, i * tile : (i + 1) * tile], grads_right[:, i * tile :], 0, 0)
             for j in range(i, span):
-                tiles[upper.index((i, j))] = slab[:, (j - i) * tile : (j - i + 1) * tile]
-        while len(tiles) < 2 * half:
-            tiles.append(jnp.zeros((tile, tile), F32))
-        for k in range(half):
-            keep_ref[k * tile : (k + 1) * tile, :] = jnp.where(odd, tiles[half + k], tiles[k])
-            send_ref[k * tile : (k + 1) * tile, :] = jnp.where(odd, tiles[k], tiles[half + k])
-
-    out = shape(half * tile, tile)
-    return call(body, (out, out), [part, arrived, metric3], 12 * part.shape[0] * width * width)
+                row = upper.index((i, j)) * tile
+                full_ref[row : row + tile, :] = slab[:, (j - i) * tile : (j - i + 1) * tile]
+        if count > len(upper):
+            full_ref[len(upper) * tile :, :] = jnp.zeros(((count - len(upper)) * tile, tile), F32)
+        for k, out_ref in enumerate([mine_ref, away_ref]):
+            out_ref[...] = full_ref[quarter(full_ref, k, rows_all), :]
+
+    out = shape(rows, tile)
+    return pl.pallas_call(
+        body,
+        out_shape=(out, out),
+        in_specs=[pl.BlockSpec(memory_space=pltpu.VMEM)] * (len(sums) + 1),
+        out_specs=(pl.BlockSpec(memory_space=pltpu.VMEM),) * 2,
+        scratch_shapes=[pltpu.VMEM((count * tile, tile), F32)],
+        compiler_params=pltpu.CompilerParams(vmem_limit_bytes=40 * 1024 * 1024),
+    )(*sums, metric3)
 
 
 def plane_place(k, rows_all):
@@ -248,15 +256,17 @@
     return pl.ds(pl.multiple_of(plane_place(k, rows_all) * rows, rows), rows)
 
 
-def split_quarters(kept, arrived, rows_all):
-    rows, width = kept.shape
-
-    def body(kept_ref, arrived_ref, *out_refs):
-        for k in range(4):
-            place = quarter(kept_ref, k, rows_all)
-            out_refs[k][...] = kept_ref[place, :] + arrived_ref[place, :]
-
-    return call(body, (shape(rows // 4, width),) * 4, [kept, arrived], 1)
+def split_halves(mine, arrived, rows_all):
+    rows, width = mine.shape
+    half = rows // 2
+
+    def body(mine_ref, arrived_ref, keep_ref, send_ref):
+        kind = my_kind(rows_all)
+        for place, out_ref in ((kind, keep_ref), (1 - kind, send_ref)):
+            here = pl.ds(pl.multiple_of(place * half, half), half)
+            out_ref[...] = mine_ref[here, :] + arrived_ref[here, :]
+
+    return call(body, (shape(half, width),) * 2, [mine, arrived], 1)
 
 
 def join_quarters(parts, rows_all):
@@ -283,14 +293,16 @@
 def finish(keep, other, points, rows_all):
     rows, width = points.shape
     tile, span, upper = upper_tiles(width)
-    half = (len(upper) + 1) // 2
 
     def body(keep_ref, other_ref, points_ref, next_ref, mapped_ref, next_held, mapped_held, sems):
         odd = my_kind(rows_all) == 1
-        kept = [keep_ref[k * tile : (k + 1) * tile, :] for k in range(half)]
-        came = [other_ref[k * tile : (k + 1) * tile, :] for k in range(half)]
-        tiles = [jnp.where(odd, b, a) for a, b in zip(kept, came)]
-        tiles += [jnp.where(odd, a, b) for a, b in zip(kept, came)]
+        piece = keep_ref.shape[0] // 4
+        rows_of = []
+        for k in range(4):
+            kept, came = (ref[k * piece : (k + 1) * piece, :] for ref in (keep_ref, other_ref))
+            rows_of += [jnp.where(odd, came, kept), jnp.where(odd, kept, came)]
+        full = jnp.concatenate(rows_of, axis=0)
+        tiles = [full[k * tile : (k + 1) * tile] for k in range(len(upper))]
         final = dict(zip(upper, tiles))
         diag = final[0, 0]
         for i in range(1, span):
@@ -362,11 +374,14 @@
         (part_a,) = late_sums(queries[1:2], 1, total, mapped, metric3, late, outs_n)
         sent_a = to_a(part_a)
         part_b, part_own = late_sums(queries[2:], 2, total, mapped, metric3, late, outs_n)
-        sent_b = to_b(part_b + sent_ab)
-
-        keep, send = outer_halves(part_own + sent_a, sent_b, metric3, rows_all)
-        parts = split_quarters(keep, hop(send, (0, 1)), rows_all)
-        total = add_all([parts[0]] + in_plane(parts[1:]))
+        half_b = part_b + sent_ab
+        rest_own = to_b(half_b)
+        half_own = part_own + sent_a
+        rest_b = to_b(half_own)
+
+        mine, away = outer_quarters([half_own, rest_own, half_b, rest_b], metric3, rows_all)
+        keep, send = split_halves(mine, to_a(away), rows_all)
+        total = add_all([keep, hop(send, (0, 1))])
         for k in range(0, len(line_bits), 2):
             total = add_all(among(total, [(bit, 0) for bit in line_bits[k : k + 2]]))
         for bit in col_bits[1:]:

time: 56.3 us -> 56 us (level)
  starting transfers between devices: 24.9 us -> 23.8 us
    ppermute x24 -> x23, starting transfers between devices: 24.9 us -> 23.8 us  [hop(): return lax.ppermute(value, AXES, pairs)]
    pallas_call x0 -> x1, Pallas kernels: none -> 0.93 us  [outer_quarters(): pl.pallas_call(body, out_shape=(out, out), in_specs=[pl.BlockSpec(memory_...]
    pallas_call x10 -> x9, Pallas kernels: 5.16 us -> 4.51 us  [call(): pl.pallas_call(body, out_shape=out_shape, in_specs=[pl.BlockSpec(memory_s...]
    ppermute x24 -> x23, waiting for transfers between devices: 21.9 us -> 22.4 us  [hop(): return lax.ppermute(value, AXES, pairs)]
  transfers between devices with their start and end apart: 24 -> 23, of which waited for: 13 -> 15; matrix products, arithmetic and copies ran while one was open for 2% -> 2% of each run, Pallas kernels for 6% -> 6%
where the time goes in v7:
time: 56 us; the launch traced here: 55.8 us
  starting transfers between devices  23.8 us (42%)
  waiting for transfers between devices  22.4 us (40%)
  Pallas kernels  7.58 us (14%)
  other arithmetic  1.27 us (2%)
  between operations  0.75 us (1%)
    ppermute x23, starting transfers between devices, hop(): return lax.ppermute(value, AXES, pairs)  23.8 us
    ppermute x23, waiting for transfers between devices, hop(): return lax.ppermute(value, AXES, pairs)  22.4 us
    pallas_call x9, Pallas kernels, call(): pl.pallas_call(body, out_shape=out_shape, in_specs=[pl.BlockSpec(memory_s...  4.51 us
    pallas_call x1, Pallas kernels, finish(): pl.pallas_call(body, out_shape=(shape(width, width), shape(rows, width)),...  1.22 us
    convert_element_type x1, other arithmetic, metric_halves(): low = (metric - high).astype(BF16)  1.14 us
  transfers between devices with their start and end apart: 23, of which 15 were waited for; matrix products, arithmetic and copies ran while one was open for 2% of the time, Pallas kernels for 6%

profile of v7, /device:TPU:0, one launch (start us, length us, event | category | flops | bytes accessed | tf_op | source)
XLA Modules:
  0.0 55.8 jit_solution(7160594320226039568)
XLA Ops:
  0.6 0.9 %shard_map.50 = (f32[64,384]{1,0:T(8,128)S(1)}, f32[72,384]{1,0:T(8,128)S(1)}) custom-call(f32[64,384]{1,0:T(8,128)} %points_ref.1, f32[2,64]{1,0:T(2,128)} %bitcast.1), custom_call_target="tpu_custom_call" | custom-call | tf_op jit(solution)/shard_map/pallas_call | solution.py:99
  1.6 0.5 collective-permute-start
  2.1 4.7 %collective-permute-start.6 = (f32[72,384]{1,0:T(8,128)S(1)}, f32[72,384]{1,0:T(8,128)S(1)}, u32[]{:S(2)}, u32[]{:S(2)}) collective-permute-start(f32[72,384]{1,0:T(8,128)S(1)} %get-tuple-element.13.refs_4_), channel_id=1, source_target_pairs={{0,24},{1,25},{2,26},{3,27},{4,28},{5,29},{6,30},{7,31},{8,16},{9,... | collective-permute-start | bytes 331784 | tf_op jit(solution)/shard_map/ppermute | solution.py:52
  6.7 0.0 collective-permute-start.4
  6.8 0.4 collective-permute-start.2
  7.1 0.0 collective-permute-done.wanted_ref.refs_2_.refs_1_
  7.1 1.5 %collective-permute-start.9 = (f32[64,384]{1,0:T(8,128)S(1)}, f32[64,384]{1,0:T(8,128)S(1)}, u32[]{:S(2)}, u32[]{:S(2)}) collective-permute-start(f32[64,384]{1,0:T(8,128)S(1)} %shard_map.51), channel_id=1, source_target_pairs={{0,3},{1,4},{2,7},{3,0},{4,1},{5,6},{6,5},{7,2},{8,13},{9,10},{10,... | collective-permute-start | bytes 294920 | tf_op jit(solution)/shard_map/ppermute | solution.py:52
  8.6 1.1 %fusion = (bf16[384,384]{1,0:T(8,128)(2,1)S(1)}, bf16[384,384]{1,0:T(8,128)(2,1)S(1)}) fusion(f32[384,384]{1,0:T(8,128)} %param.5), kind=kLoop, calls=%fused_computation.3 | loop fusion | flops 589824 | bytes 1179648 | tf_op jit(solution)/shard_map/convert_element_type | solution.py:117
  9.8 1.6 %collective-permute-start.8 = (f32[64,384]{1,0:T(8,128)S(1)}, f32[64,384]{1,0:T(8,128)S(1)}, u32[]{:S(2)}, u32[]{:S(2)}) collective-permute-start(f32[64,384]{1,0:T(8,128)S(1)} %shard_map.51), channel_id=1, source_target_pairs={{0,6},{1,7},{2,4},{3,5},{4,2},{5,3},{6,0},{7,1},{8,14},{9,15},{10,... | collective-permute-start | bytes 294920 | tf_op jit(solution)/shard_map/ppermute | solution.py:52
  11.3 0.0 collective-permute-done.6.refs_7_
  11.3 0.0 collective-permute-start.1
  11.4 2.4 %collective-permute-done.4.refs_6_ = f32[72,384]{1,0:T(8,128)S(1)} collective-permute-done((f32[72,384]{1,0:T(8,128)S(1)}, f32[72,384]{1,0:T(8,128)S(1)}, u32[]{:S(2)}, u32[]{:S(2)}) %collective-permute-start.4) | collective-permute-done | bytes 110624 | tf_op jit(solution)/shard_map/ppermute | solution.py:52
  13.8 0.1 collective-permute-start.7
  14.0 2.3 %collective-permute-done.2.refs_5_ = f32[72,384]{1,0:T(8,128)S(1)} collective-permute-done((f32[72,384]{1,0:T(8,128)S(1)}, f32[72,384]{1,0:T(8,128)S(1)}, u32[]{:S(2)}, u32[]{:S(2)}) %collective-permute-start.2) | collective-permute-done | bytes 110624 | tf_op jit(solution)/shard_map/ppermute | solution.py:52
  16.2 0.3 collective-permute-start.5
  16.5 0.0 collective-permute-done.9.refs_1_.refs_0_
  16.5 0.2 collective-permute-start.3
  16.7 0.1 pad_maximum_fusion.refs_8_.refs_7_.refs_4_
  16.8 0.0 collective-permute-done.8.refs_0_
  16.8 0.0 collective-permute-done.1.refs_2_.refs_0_
  16.8 1.6 %shard_map.52 = (f32[2,256,384]{2,1,0:T(8,128)S(1)}, f32[256,384]{1,0:T(8,128)S(1)}) custom-call(f32[64,384]{1,0:T(8,128)S(1)} %collective-permute-done.8.refs_0_, f32[64,384]{1,0:T(8,128)S(1)} %collective-permute-done.9.refs_1_.refs_0_, f32[64,384]{1,0:T(8,128)S(1)} %collective-permute-done.1.refs_2_.refs_0_, ...), custom_call_target="tpu_custom_call" | custom-call | flops 764411904 | bytes 3784704 | tf_op jit(solution)/shard_map/pallas_call | solution.py:66
  18.4 0.0 collective-permute-done.7.refs_5_.refs_4_
  18.4 0.0 collective-permute-done.5.refs_4_.refs_3_
  18.4 0.0 collective-permute-done.3.refs_3_.refs_2_
  18.4 0.9 %shard_map.54 = f32[128,384]{1,0:T(8,128)S(1)} custom-call(f32[64,384]{1,0:T(8,128)S(1)} %collective-permute-done.9.refs_1_.refs_0_, f32[72,384]{1,0:T(8,128)S(1)} %collective-permute-done.wanted_ref.refs_2_.refs_1_, f32[72,384]{1,0:T(8,128)S(1)} %collective-permute-done.3.refs_3_.refs_2_, f32[72,384]{1,0:T(8,128)S(1)} %collective-permute-done.5.refs_4_.refs_3_, ...), custom_call_target="tpu_custom_call" | custom-call | flops 325582848 | bytes 3686400 | tf_op jit(solution)/shard_map/pallas_call | solution.py:66
  19.4 1.4 %collective-permute-start.10 = (f32[128,384]{1,0:T(8,128)S(1)}, f32[128,384]{1,0:T(8,128)S(1)}, u32[]{:S(2)}, u32[]{:S(2)}) collective-permute-start(f32[128,384]{1,0:T(8,128)S(1)} %shard_map.54), channel_id=1, source_target_pairs={{0,3},{1,4},{2,7},{3,0},{4,1},{5,6},{6,5},{7,2},{8,13},{9,10},{10,... | collective-permute-start | bytes 589832 | tf_op jit(solution)/shard_map/ppermute | solution.py:52
  20.8 0.9 %shard_map.55 = f32[128,384]{1,0:T(8,128)S(1)} custom-call(f32[64,384]{1,0:T(8,128)S(1)} %collective-permute-done.8.refs_0_, f32[72,384]{1,0:T(8,128)S(1)} %collective-permute-done.wanted_ref.refs_2_.refs_1_, f32[72,384]{1,0:T(8,128)S(1)} %collective-permute-done.3.refs_3_.refs_2_, f32[72,384]{1,0:T(8,128)S(1)} %collective-permute-done.5.refs_4_.refs_3_, ...), custom_call_target="tpu_custom_call" | custom-call | flops 325582848 | bytes 3686400 | tf_op jit(solution)/shard_map/pallas_call | solution.py:66
  21.8 0.4 collective-permute-start.11
  22.2 1.0 %shard_map.53 = (f32[128,384]{1,0:T(8,128)S(1)}, f32[128,384]{1,0:T(8,128)S(1)}) custom-call(f32[64,384]{1,0:T(8,128)S(1)} %collective-permute-done.1.refs_2_.refs_0_, f32[64,384]{1,0:T(8,128)S(1)} %get-tuple-element.12.value_ref.refs_3_.refs_1_.points_ref, f32[72,384]{1,0:T(8,128)S(1)} %collective-permute-done.wanted_ref.refs_2_.refs_1_, ...), custom_call_target="tpu_custom_call" | custom-call | flops 396361728 | bytes 3981312 | tf_op jit(solution)/shard_map/pallas_call | solution.py:66
  23.2 1.3 %collective-permute-done.10 = f32[128,384]{1,0:T(8,128)S(1)} collective-permute-done((f32[128,384]{1,0:T(8,128)S(1)}, f32[128,384]{1,0:T(8,128)S(1)}, u32[]{:S(2)}, u32[]{:S(2)}) %collective-permute-start.10) | collective-permute-done | bytes 196640 | tf_op jit(solution)/shard_map/ppermute | solution.py:52
  24.6 1.8 %collective-permute-start.13 = (f32[128,384]{1,0:T(8,128)S(1)}, f32[128,384]{1,0:T(8,128)S(1)}, u32[]{:S(2)}, u32[]{:S(2)}) collective-permute-start(f32[128,384]{1,0:T(8,128)S(1)} %add.6.refs_0_), channel_id=1, source_target_pairs={{0,5},{1,2},{2,1},{3,6},{4,7},{5,0},{6,3},{7,4},{8,11},{9,12},{10,... | collective-permute-start | bytes 589832 | tf_op jit(solution)/shard_map/ppermute | solution.py:52
  26.3 0.6 %collective-permute-done.11 = f32[128,384]{1,0:T(8,128)S(1)} collective-permute-done((f32[128,384]{1,0:T(8,128)S(1)}, f32[128,384]{1,0:T(8,128)S(1)}, u32[]{:S(2)}, u32[]{:S(2)}) %collective-permute-start.11) | collective-permute-done | bytes 196640 | tf_op jit(solution)/shard_map/ppermute | solution.py:52
  27.0 1.4 %collective-permute-start.12 = (f32[128,384]{1,0:T(8,128)S(1)}, f32[128,384]{1,0:T(8,128)S(1)}, u32[]{:S(2)}, u32[]{:S(2)}) collective-permute-start(f32[128,384]{1,0:T(8,128)S(1)} %add.7.refs_2_), channel_id=1, source_target_pairs={{0,5},{1,2},{2,1},{3,6},{4,7},{5,0},{6,3},{7,4},{8,11},{9,12},{10,... | collective-permute-start | bytes 589832 | tf_op jit(solution)/shard_map/ppermute | solution.py:52
  28.4 1.3 %collective-permute-done.13.refs_3_ = f32[128,384]{1,0:T(8,128)S(1)} collective-permute-done((f32[128,384]{1,0:T(8,128)S(1)}, f32[128,384]{1,0:T(8,128)S(1)}, u32[]{:S(2)}, u32[]{:S(2)}) %collective-permute-start.13) | collective-permute-done | bytes 196640 | tf_op jit(solution)/shard_map/ppermute | solution.py:52
  29.7 2.4 %collective-permute-done.12.refs_1_ = f32[128,384]{1,0:T(8,128)S(1)} collective-permute-done((f32[128,384]{1,0:T(8,128)S(1)}, f32[128,384]{1,0:T(8,128)S(1)}, u32[]{:S(2)}, u32[]{:S(2)}) %collective-permute-start.12) | collective-permute-done | bytes 196640 | tf_op jit(solution)/shard_map/ppermute | solution.py:52
  32.1 0.9 %shard_map.56 = (f32[192,128]{1,0:T(8,128)S(1)}, f32[192,128]{1,0:T(8,128)S(1)}) custom-call(f32[128,384]{1,0:T(8,128)S(1)} %add.6.refs_0_, f32[128,384]{1,0:T(8,128)S(1)} %collective-permute-done.12.refs_1_, f32[128,384]{1,0:T(8,128)S(1)} %add.7.refs_2_, f32[128,384]{1,0:T(8,128)S(1)} %collective-permute-done.13.refs_3_, ...), custom_call_target="tpu_custom_call" | custom-call | tf_op jit(solution)/shard_map/pallas_call | solution.py:237
  33.0 1.5 %collective-permute-start.14 = (f32[192,128]{1,0:T(8,128)S(1)}, f32[192,128]{1,0:T(8,128)S(1)}, u32[]{:S(2)}, u32[]{:S(2)}) collective-permute-start(f32[192,128]{1,0:T(8,128)S(1)} %get-tuple-element.19), channel_id=1, source_target_pairs={{0,3},{1,4},{2,7},{3,0},{4,1},{5,6},{6,5},{7,2},{8,13},{9,10},{10,... | collective-permute-start | bytes 294920 | tf_op jit(solution)/shard_map/ppermute | solution.py:52
  34.5 2.7 %collective-permute-done.14.arrived_ref = f32[192,128]{1,0:T(8,128)S(1)} collective-permute-done((f32[192,128]{1,0:T(8,128)S(1)}, f32[192,128]{1,0:T(8,128)S(1)}, u32[]{:S(2)}, u32[]{:S(2)}) %collective-permute-start.14) | collective-permute-done | bytes 98336 | tf_op jit(solution)/shard_map/ppermute | solution.py:52
  37.2 0.4 collective-permute-start.15
  37.5 0.9 %collective-permute-done.15.refs_1_ = f32[96,128]{1,0:T(8,128)S(1)} collective-permute-done((f32[96,128]{1,0:T(8,128)S(1)}, f32[96,128]{1,0:T(8,128)S(1)}, u32[]{:S(2)}, u32[]{:S(2)}) %collective-permute-start.15) | collective-permute-done | bytes 49184 | tf_op jit(solution)/shard_map/ppermute | solution.py:52
  38.5 3.4 %collective-permute-start.18 = (f32[96,128]{1,0:T(8,128)S(1)}, f32[96,128]{1,0:T(8,128)S(1)}, u32[]{:S(2)}, u32[]{:S(2)}) collective-permute-start(f32[96,128]{1,0:T(8,128)S(1)} %shard_map.58.refs_0_), channel_id=1, source_target_pairs={{0,24},{1,25},{2,26},{3,27},{4,28},{5,29},{6,30},{7,31},{8,16},{9,... | collective-permute-start | bytes 147464 | tf_op jit(solution)/shard_map/ppermute | solution.py:52
  41.9 0.0 collective-permute-start.17
  41.9 0.8 %collective-permute-start.16 = (f32[96,128]{1,0:T(8,128)S(1)}, f32[96,128]{1,0:T(8,128)S(1)}, u32[]{:S(2)}, u32[]{:S(2)}) collective-permute-start(f32[96,128]{1,0:T(8,128)S(1)} %shard_map.58.refs_0_), channel_id=1, source_target_pairs={{0,9},{1,8},{2,11},{3,10},{4,13},{5,12},{6,15},{7,14},{8,1},{9,0},... | collective-permute-start | bytes 147464 | tf_op jit(solution)/shard_map/ppermute | solution.py:52
  42.6 2.0 %collective-permute-done.18.refs_3_ = f32[96,128]{1,0:T(8,128)S(1)} collective-permute-done((f32[96,128]{1,0:T(8,128)S(1)}, f32[96,128]{1,0:T(8,128)S(1)}, u32[]{:S(2)}, u32[]{:S(2)}) %collective-permute-start.18) | collective-permute-done | bytes 49184 | tf_op jit(solution)/shard_map/ppermute | solution.py:52
  44.7 2.2 %collective-permute-done.17.refs_2_ = f32[96,128]{1,0:T(8,128)S(1)} collective-permute-done((f32[96,128]{1,0:T(8,128)S(1)}, f32[96,128]{1,0:T(8,128)S(1)}, u32[]{:S(2)}, u32[]{:S(2)}) %collective-permute-start.17) | collective-permute-done | bytes 49184 | tf_op jit(solution)/shard_map/ppermute | solution.py:52
  46.9 0.1 collective-permute-done.16.refs_1_
  46.9 2.1 %collective-permute-start.21 = (f32[96,128]{1,0:T(8,128)S(1)}, f32[96,128]{1,0:T(8,128)S(1)}, u32[]{:S(2)}, u32[]{:S(2)}) collective-permute-start(f32[96,128]{1,0:T(8,128)S(1)} %shard_map.59.refs_0_), channel_id=1, source_target_pairs={{0,6},{1,7},{2,4},{3,5},{4,2},{5,3},{6,0},{7,1},{8,14},{9,15},{10,... | collective-permute-start | bytes 147464 | tf_op jit(solution)/shard_map/ppermute | solution.py:52
  49.0 0.0 collective-permute-start.20
  49.0 1.2 %collective-permute-start.19 = (f32[96,128]{1,0:T(8,128)S(1)}, f32[96,128]{1,0:T(8,128)S(1)}, u32[]{:S(2)}, u32[]{:S(2)}) collective-permute-start(f32[96,128]{1,0:T(8,128)S(1)} %shard_map.59.refs_0_), channel_id=1, source_target_pairs={{0,3},{1,4},{2,7},{3,0},{4,1},{5,6},{6,5},{7,2},{8,13},{9,10},{10,... | collective-permute-start | bytes 147464 | tf_op jit(solution)/shard_map/ppermute | solution.py:52
  50.2 1.8 %collective-permute-done.21.refs_3_ = f32[96,128]{1,0:T(8,128)S(1)} collective-permute-done((f32[96,128]{1,0:T(8,128)S(1)}, f32[96,128]{1,0:T(8,128)S(1)}, u32[]{:S(2)}, u32[]{:S(2)}) %collective-permute-start.21) | collective-permute-done | bytes 49184 | tf_op jit(solution)/shard_map/ppermute | solution.py:52
  52.0 0.5 collective-permute-done.20.refs_2_
  52.5 0.5 collective-permute-done.19.refs_1_
  53.0 0.2 collective-permute-start.22
  53.2 1.3 %collective-permute-done.22.other_ref = f32[384,128]{1,0:T(8,128)S(1)} collective-permute-done((f32[384,128]{1,0:T(8,128)S(1)}, f32[384,128]{1,0:T(8,128)S(1)}, u32[]{:S(2)}, u32[]{:S(2)}) %collective-permute-start.22) | collective-permute-done | bytes 196640 | tf_op jit(solution)/shard_map/ppermute | solution.py:52
  54.6 1.2 %shard_map.61 = (f32[384,384]{1,0:T(8,128)}, f32[64,384]{1,0:T(8,128)}) custom-call(f32[384,128]{1,0:T(8,128)S(1)} %shard_map.60.keep_ref, f32[384,128]{1,0:T(8,128)S(1)} %collective-permute-done.22.other_ref, f32[64,384]{1,0:T(8,128)S(1)} %get-tuple-element.12.value_ref.refs_3_.refs_1_.points_ref), custom_call_target="tpu_custom_call" | custom-call | tf_op jit(solution)/shard_map/pallas_call | solution.py:326
  (7 shorter events, 0.1 us)
Async XLA Ops:
  1.6 5.6 %collective-permute-start = (f32[72,384]{1,0:T(8,128)S(1)}, f32[72,384]{1,0:T(8,128)S(1)}, u32[]{:S(2)}, u32[]{:S(2)}) collective-permute-start(f32[72,384]{1,0:T(8,128)S(1)} %get-tuple-element.13.refs_4_), channel_id=1, source_target_pairs={{0,1},{1,0},{2,3},{3,2},{4,5},{5,4},{6,7},{7,6},{8,9},{9,8},{10,11... | collective-permute-start | bytes 331784 | tf_op jit(solution)/shard_map/ppermute | solution.py:52
  2.1 9.3 %collective-permute-start.6 = (f32[72,384]{1,0:T(8,128)S(1)}, f32[72,384]{1,0:T(8,128)S(1)}, u32[]{:S(2)}, u32[]{:S(2)}) collective-permute-start(f32[72,384]{1,0:T(8,128)S(1)} %get-tuple-element.13.refs_4_), channel_id=1, source_target_pairs={{0,24},{1,25},{2,26},{3,27},{4,28},{5,29},{6,30},{7,31},{8,16},{9,... | collective-permute-start | bytes 331784 | tf_op jit(solution)/shard_map/ppermute | solution.py:52
  6.7 7.1 %collective-permute-start.4 = (f32[72,384]{1,0:T(8,128)S(1)}, f32[72,384]{1,0:T(8,128)S(1)}, u32[]{:S(2)}, u32[]{:S(2)}) collective-permute-start(f32[72,384]{1,0:T(8,128)S(1)} %get-tuple-element.13.refs_4_), channel_id=1, source_target_pairs={{0,9},{1,8},{2,11},{3,10},{4,13},{5,12},{6,15},{7,14},{8,1},{9,0},... | collective-permute-start | bytes 331784 | tf_op jit(solution)/shard_map/ppermute | solution.py:52
  6.8 9.5 %collective-permute-start.2 = (f32[72,384]{1,0:T(8,128)S(1)}, f32[72,384]{1,0:T(8,128)S(1)}, u32[]{:S(2)}, u32[]{:S(2)}) collective-permute-start(f32[72,384]{1,0:T(8,128)S(1)} %get-tuple-element.13.refs_4_), channel_id=1, source_target_pairs={{0,17},{1,16},{2,19},{3,18},{4,21},{5,20},{6,23},{7,22},{8,25},{9,... | collective-permute-start | bytes 331784 | tf_op jit(solution)/shard_map/ppermute | solution.py:52
  7.1 9.4 %collective-permute-start.9 = (f32[64,384]{1,0:T(8,128)S(1)}, f32[64,384]{1,0:T(8,128)S(1)}, u32[]{:S(2)}, u32[]{:S(2)}) collective-permute-start(f32[64,384]{1,0:T(8,128)S(1)} %shard_map.51), channel_id=1, source_target_pairs={{0,3},{1,4},{2,7},{3,0},{4,1},{5,6},{6,5},{7,2},{8,13},{9,10},{10,... | collective-permute-start | bytes 294920 | tf_op jit(solution)/shard_map/ppermute | solution.py:52
  9.8 7.0 %collective-permute-start.8 = (f32[64,384]{1,0:T(8,128)S(1)}, f32[64,384]{1,0:T(8,128)S(1)}, u32[]{:S(2)}, u32[]{:S(2)}) collective-permute-start(f32[64,384]{1,0:T(8,128)S(1)} %shard_map.51), channel_id=1, source_target_pairs={{0,6},{1,7},{2,4},{3,5},{4,2},{5,3},{6,0},{7,1},{8,14},{9,15},{10,... | collective-permute-start | bytes 294920 | tf_op jit(solution)/shard_map/ppermute | solution.py:52
  11.3 5.5 %collective-permute-start.1 = (f32[64,384]{1,0:T(8,128)S(1)}, f32[64,384]{1,0:T(8,128)S(1)}, u32[]{:S(2)}, u32[]{:S(2)}) collective-permute-start(f32[64,384]{1,0:T(8,128)S(1)} %shard_map.51), channel_id=1, source_target_pairs={{0,5},{1,2},{2,1},{3,6},{4,7},{5,0},{6,3},{7,4},{8,11},{9,12},{10,... | collective-permute-start | bytes 294920 | tf_op jit(solution)/shard_map/ppermute | solution.py:52
  13.8 4.6 %collective-permute-start.7 = (f32[72,384]{1,0:T(8,128)S(1)}, f32[72,384]{1,0:T(8,128)S(1)}, u32[]{:S(2)}, u32[]{:S(2)}) collective-permute-start(f32[72,384]{1,0:T(8,128)S(1)} %collective-permute-done.6.refs_7_), channel_id=1, source_target_pairs={{0,1},{1,0},{2,3},{3,2},{4,5},{5,4},{6,7},{7,6},{8,9},{9,8},{10,11... | collective-permute-start | bytes 331784 | tf_op jit(solution)/shard_map/ppermute | solution.py:52
  16.2 2.2 %collective-permute-start.5 = (f32[72,384]{1,0:T(8,128)S(1)}, f32[72,384]{1,0:T(8,128)S(1)}, u32[]{:S(2)}, u32[]{:S(2)}) collective-permute-start(f32[72,384]{1,0:T(8,128)S(1)} %collective-permute-done.4.refs_6_), channel_id=1, source_target_pairs={{0,1},{1,0},{2,3},{3,2},{4,5},{5,4},{6,7},{7,6},{8,9},{9,8},{10,11... | collective-permute-start | bytes 331784 | tf_op jit(solution)/shard_map/ppermute | solution.py:52
  16.5 1.9 %collective-permute-start.3 = (f32[72,384]{1,0:T(8,128)S(1)}, f32[72,384]{1,0:T(8,128)S(1)}, u32[]{:S(2)}, u32[]{:S(2)}) collective-permute-start(f32[72,384]{1,0:T(8,128)S(1)} %collective-permute-done.2.refs_5_), channel_id=1, source_target_pairs={{0,1},{1,0},{2,3},{3,2},{4,5},{5,4},{6,7},{7,6},{8,9},{9,8},{10,11... | collective-permute-start | bytes 331784 | tf_op jit(solution)/shard_map/ppermute | solution.py:52
  19.4 5.2 %collective-permute-start.10 = (f32[128,384]{1,0:T(8,128)S(1)}, f32[128,384]{1,0:T(8,128)S(1)}, u32[]{:S(2)}, u32[]{:S(2)}) collective-permute-start(f32[128,384]{1,0:T(8,128)S(1)} %shard_map.54), channel_id=1, source_target_pairs={{0,3},{1,4},{2,7},{3,0},{4,1},{5,6},{6,5},{7,2},{8,13},{9,10},{10,... | collective-permute-start | bytes 589832 | tf_op jit(solution)/shard_map/ppermute | solution.py:52
  21.8 5.2 %collective-permute-start.11 = (f32[128,384]{1,0:T(8,128)S(1)}, f32[128,384]{1,0:T(8,128)S(1)}, u32[]{:S(2)}, u32[]{:S(2)}) collective-permute-start(f32[128,384]{1,0:T(8,128)S(1)} %shard_map.55), channel_id=1, source_target_pairs={{0,3},{1,4},{2,7},{3,0},{4,1},{5,6},{6,5},{7,2},{8,13},{9,10},{10,... | collective-permute-start | bytes 589832 | tf_op jit(solution)/shard_map/ppermute | solution.py:52
  24.6 5.2 %collective-permute-start.13 = (f32[128,384]{1,0:T(8,128)S(1)}, f32[128,384]{1,0:T(8,128)S(1)}, u32[]{:S(2)}, u32[]{:S(2)}) collective-permute-start(f32[128,384]{1,0:T(8,128)S(1)} %add.6.refs_0_), channel_id=1, source_target_pairs={{0,5},{1,2},{2,1},{3,6},{4,7},{5,0},{6,3},{7,4},{8,11},{9,12},{10,... | collective-permute-start | bytes 589832 | tf_op jit(solution)/shard_map/ppermute | solution.py:52
  27.0 5.2 %collective-permute-start.12 = (f32[128,384]{1,0:T(8,128)S(1)}, f32[128,384]{1,0:T(8,128)S(1)}, u32[]{:S(2)}, u32[]{:S(2)}) collective-permute-start(f32[128,384]{1,0:T(8,128)S(1)} %add.7.refs_2_), channel_id=1, source_target_pairs={{0,5},{1,2},{2,1},{3,6},{4,7},{5,0},{6,3},{7,4},{8,11},{9,12},{10,... | collective-permute-start | bytes 589832 | tf_op jit(solution)/shard_map/ppermute | solution.py:52
  33.0 4.1 %collective-permute-start.14 = (f32[192,128]{1,0:T(8,128)S(1)}, f32[192,128]{1,0:T(8,128)S(1)}, u32[]{:S(2)}, u32[]{:S(2)}) collective-permute-start(f32[192,128]{1,0:T(8,128)S(1)} %get-tuple-element.19), channel_id=1, source_target_pairs={{0,3},{1,4},{2,7},{3,0},{4,1},{5,6},{6,5},{7,2},{8,13},{9,10},{10,... | collective-permute-start | bytes 294920 | tf_op jit(solution)/shard_map/ppermute | solution.py:52
  37.2 1.3 %collective-permute-start.15 = (f32[96,128]{1,0:T(8,128)S(1)}, f32[96,128]{1,0:T(8,128)S(1)}, u32[]{:S(2)}, u32[]{:S(2)}) collective-permute-start(f32[96,128]{1,0:T(8,128)S(1)} %get-tuple-element.21), channel_id=1, source_target_pairs={{0,1},{1,0},{2,3},{3,2},{4,5},{5,4},{6,7},{7,6},{8,9},{9,8},{10,11... | collective-permute-start | bytes 147464 | tf_op jit(solution)/shard_map/ppermute | solution.py:52
  38.5 6.2 %collective-permute-start.18 = (f32[96,128]{1,0:T(8,128)S(1)}, f32[96,128]{1,0:T(8,128)S(1)}, u32[]{:S(2)}, u32[]{:S(2)}) collective-permute-start(f32[96,128]{1,0:T(8,128)S(1)} %shard_map.58.refs_0_), channel_id=1, source_target_pairs={{0,24},{1,25},{2,26},{3,27},{4,28},{5,29},{6,30},{7,31},{8,16},{9,... | collective-permute-start | bytes 147464 | tf_op jit(solution)/shard_map/ppermute | solution.py:52
  41.9 5.0 %collective-permute-start.17 = (f32[96,128]{1,0:T(8,128)S(1)}, f32[96,128]{1,0:T(8,128)S(1)}, u32[]{:S(2)}, u32[]{:S(2)}) collective-permute-start(f32[96,128]{1,0:T(8,128)S(1)} %shard_map.58.refs_0_), channel_id=1, source_target_pairs={{0,17},{1,16},{2,19},{3,18},{4,21},{5,20},{6,23},{7,22},{8,25},{9,... | collective-permute-start | bytes 147464 | tf_op jit(solution)/shard_map/ppermute | solution.py:52
  41.9 5.1 %collective-permute-start.16 = (f32[96,128]{1,0:T(8,128)S(1)}, f32[96,128]{1,0:T(8,128)S(1)}, u32[]{:S(2)}, u32[]{:S(2)}) collective-permute-start(f32[96,128]{1,0:T(8,128)S(1)} %shard_map.58.refs_0_), channel_id=1, source_target_pairs={{0,9},{1,8},{2,11},{3,10},{4,13},{5,12},{6,15},{7,14},{8,1},{9,0},... | collective-permute-start | bytes 147464 | tf_op jit(solution)/shard_map/ppermute | solution.py:52
  46.9 5.1 %collective-permute-start.21 = (f32[96,128]{1,0:T(8,128)S(1)}, f32[96,128]{1,0:T(8,128)S(1)}, u32[]{:S(2)}, u32[]{:S(2)}) collective-permute-start(f32[96,128]{1,0:T(8,128)S(1)} %shard_map.59.refs_0_), channel_id=1, source_target_pairs={{0,6},{1,7},{2,4},{3,5},{4,2},{5,3},{6,0},{7,1},{8,14},{9,15},{10,... | collective-permute-start | bytes 147464 | tf_op jit(solution)/shard_map/ppermute | solution.py:52
  49.0 3.5 %collective-permute-start.20 = (f32[96,128]{1,0:T(8,128)S(1)}, f32[96,128]{1,0:T(8,128)S(1)}, u32[]{:S(2)}, u32[]{:S(2)}) collective-permute-start(f32[96,128]{1,0:T(8,128)S(1)} %shard_map.59.refs_0_), channel_id=1, source_target_pairs={{0,5},{1,2},{2,1},{3,6},{4,7},{5,0},{6,3},{7,4},{8,11},{9,12},{10,... | collective-permute-start | bytes 147464 | tf_op jit(solution)/shard_map/ppermute | solution.py:52
  49.0 4.0 %collective-permute-start.19 = (f32[96,128]{1,0:T(8,128)S(1)}, f32[96,128]{1,0:T(8,128)S(1)}, u32[]{:S(2)}, u32[]{:S(2)}) collective-permute-start(f32[96,128]{1,0:T(8,128)S(1)} %shard_map.59.refs_0_), channel_id=1, source_target_pairs={{0,3},{1,4},{2,7},{3,0},{4,1},{5,6},{6,5},{7,2},{8,13},{9,10},{10,... | collective-permute-start | bytes 147464 | tf_op jit(solution)/shard_map/ppermute | solution.py:52
  53.0 1.5 %collective-permute-start.22 = (f32[384,128]{1,0:T(8,128)S(1)}, f32[384,128]{1,0:T(8,128)S(1)}, u32[]{:S(2)}, u32[]{:S(2)}) collective-permute-start(f32[384,128]{1,0:T(8,128)S(1)} %shard_map.60.keep_ref), channel_id=1, source_target_pairs={{0,1},{1,0},{2,3},{3,2},{4,5},{5,4},{6,7},{7,6},{8,9},{9,8},{10,11... | collective-permute-start | bytes 589832 | tf_op jit(solution)/shard_map/ppermute | solution.py:52

commit v8 on v7

--- a/solution.py
+++ b/solution.py
@@ -181,14 +181,14 @@
     return call(body, (shape(outs_n, count * own, width), shape(count * own, width)), args, flops)
 
 
-def late_sums(queries, first, total, mapped, metric3, blocks, outs_n):
+def late_sums(queries, first, total, mapped, metric3, blocks, outs_n, wanted=()):
     own, width = queries[0].shape
     count = len(queries)
 
     def body(*refs):
         query_refs, block_refs = refs[:count], refs[count : count + len(blocks)]
         total_ref, mapped_ref, metric3_ref = refs[count + len(blocks) : count + len(blocks) + 3]
-        out_refs = refs[count + len(blocks) + 3 :]
+        out_refs = refs[count + len(blocks) + 3 + len(wanted) :]
         rows = slice(first * own, (first + count) * own)
         query_x = jnp.concatenate([ref[...] for ref in query_refs], axis=0)
         query_y = mapped_ref[rows, :]
@@ -200,9 +200,32 @@
             for c in range(outs_n):
                 out_refs[q][c * own : (c + 1) * own, :] = sums[c][q * own : (q + 1) * own, :]
 
-    args = list(queries) + list(blocks) + [total, mapped, metric3]
+    args = list(queries) + list(blocks) + [total, mapped, metric3] + list(wanted)
     centers = sum(b.shape[0] for b in blocks)
     flops = 6 * centers * width * width + 10 * count * own * centers * width
+    return call(body, tuple(shape(outs_n * own, width) for _ in queries), args, flops)
+
+
+def whole_sums(queries, blocks, metric3, outs_n):
+    own, width = queries[0].shape
+    count = len(queries)
+
+    def body(*refs):
+        query_refs, block_refs = refs[:count], refs[count : count + len(blocks)]
+        metric3_ref, out_refs = refs[count + len(blocks)], refs[count + len(blocks) + 1 :]
+        query_x = jnp.concatenate([ref[...] for ref in query_refs], axis=0)
+        query_y = mul(left(query_x), metric3_ref[...])
+        sums = None
+        for run in chunks(block_refs):
+            parts = query_sums(query_x, query_y, *center_terms(run, own, outs_n, metric3_ref[...]))
+            sums = parts if sums is None else [a + b for a, b in zip(sums, parts)]
+        for q in range(count):
+            for c in range(outs_n):
+                out_refs[q][c * own : (c + 1) * own, :] = sums[c][q * own : (q + 1) * own, :]
+
+    args = list(queries) + list(blocks) + [metric3]
+    centers = sum(b.shape[0] for b in blocks)
+    flops = 6 * (count * own + centers) * width * width + 10 * count * own * centers * width
     return call(body, tuple(shape(outs_n * own, width) for _ in queries), args, flops)
 
 
@@ -368,12 +391,12 @@
         late = [other for block in near for other in among(block, [(0, bit) for bit in col_bits])[1:]]
         source = copy_after(points, late[0])
         queries = [hop(source, (bit_a | bit_b, 0)), to_a(source), to_b(source), points]
-        total, mapped = early_sums(queries, near, metric3, outs_n)
-        (part_ab,) = late_sums(queries[:1], 0, total, mapped, metric3, late, outs_n)
+        total, mapped = early_sums(queries[:2], near, metric3, outs_n)
+        (part_ab,) = late_sums(queries[:1], 0, total, mapped, metric3, late, outs_n, queries[2:3])
         sent_ab = to_a(part_ab)
         (part_a,) = late_sums(queries[1:2], 1, total, mapped, metric3, late, outs_n)
         sent_a = to_a(part_a)
-        part_b, part_own = late_sums(queries[2:], 2, total, mapped, metric3, late, outs_n)
+        part_b, part_own = whole_sums(queries[2:], near + late, metric3, outs_n)
         half_b = part_b + sent_ab
         rest_own = to_b(half_b)
         half_own = part_own + sent_a

time: 56 us -> 55.6 us (level)
  waiting for transfers between devices: 22.4 us -> 21.4 us
    ppermute x23, waiting for transfers between devices: 22.4 us -> 21.4 us  [hop(): return lax.ppermute(value, AXES, pairs)]
  transfers between devices with their start and end apart: 23 -> 23, of which waited for: 15 -> 15; matrix products, arithmetic and copies ran while one was open for 2% -> 2% of each run, Pallas kernels for 6% -> 8%
where the time goes in v8:
time: 55.6 us; the launch traced here: 55.4 us
  starting transfers between devices  24.1 us (43%)
  waiting for transfers between devices  21.4 us (38%)
  Pallas kernels  7.83 us (14%)
  other arithmetic  1.28 us (2%)
  between operations  0.75 us (1%)
    ppermute x23, starting transfers between devices, hop(): return lax.ppermute(value, AXES, pairs)  24.1 us
    ppermute x23, waiting for transfers between devices, hop(): return lax.ppermute(value, AXES, pairs)  21.4 us
    pallas_call x9, Pallas kernels, call(): pl.pallas_call(body, out_shape=out_shape, in_specs=[pl.BlockSpec(memory_s...  4.76 us
    pallas_call x1, Pallas kernels, finish(): pl.pallas_call(body, out_shape=(shape(width, width), shape(rows, width)),...  1.22 us
    convert_element_type x1, other arithmetic, metric_halves(): low = (metric - high).astype(BF16)  1.14 us
  transfers between devices with their start and end apart: 23, of which 15 were waited for; matrix products, arithmetic and copies ran while one was open for 2% of the time, Pallas kernels for 8%

profile of v8, /device:TPU:0, one launch (start us, length us, event | category | flops | bytes accessed | tf_op | source)
XLA Modules:
  0.0 55.4 jit_solution(13454691620722208953)
XLA Ops:
  0.6 0.9 %shard_map.50 = (f32[64,384]{1,0:T(8,128)S(1)}, f32[72,384]{1,0:T(8,128)S(1)}) custom-call(f32[64,384]{1,0:T(8,128)} %points_ref.1, f32[2,64]{1,0:T(2,128)} %bitcast.1), custom_call_target="tpu_custom_call" | custom-call | tf_op jit(solution)/shard_map/pallas_call | solution.py:99
  1.6 0.5 collective-permute-start
  2.1 4.7 %collective-permute-start.4 = (f32[72,384]{1,0:T(8,128)S(1)}, f32[72,384]{1,0:T(8,128)S(1)}, u32[]{:S(2)}, u32[]{:S(2)}) collective-permute-start(f32[72,384]{1,0:T(8,128)S(1)} %get-tuple-element.13.refs_2_), channel_id=1, source_target_pairs={{0,24},{1,25},{2,26},{3,27},{4,28},{5,29},{6,30},{7,31},{8,16},{9,... | collective-permute-start | bytes 331784 | tf_op jit(solution)/shard_map/ppermute | solution.py:52
  6.7 0.0 collective-permute-start.3
  6.8 0.4 collective-permute-start.2
  7.1 0.0 collective-permute-done.wanted_ref.refs_6_.refs_1_
  7.1 2.7 %collective-permute-start.9 = (f32[64,384]{1,0:T(8,128)S(1)}, f32[64,384]{1,0:T(8,128)S(1)}, u32[]{:S(2)}, u32[]{:S(2)}) collective-permute-start(f32[64,384]{1,0:T(8,128)S(1)} %shard_map.51), channel_id=1, source_target_pairs={{0,6},{1,7},{2,4},{3,5},{4,2},{5,3},{6,0},{7,1},{8,14},{9,15},{10,... | collective-permute-start | bytes 294920 | tf_op jit(solution)/shard_map/ppermute | solution.py:52
  9.8 1.1 %fusion = (bf16[384,384]{1,0:T(8,128)(2,1)S(1)}, bf16[384,384]{1,0:T(8,128)(2,1)S(1)}) fusion(f32[384,384]{1,0:T(8,128)} %param.5), kind=kLoop, calls=%fused_computation.3 | loop fusion | flops 589824 | bytes 1179648 | tf_op jit(solution)/shard_map/convert_element_type | solution.py:117
  10.9 0.1 collective-permute-start.8
  11.1 0.0 collective-permute-done.4.refs_5_
  11.1 0.5 collective-permute-start.1
  11.6 2.2 %collective-permute-done.3.refs_4_ = f32[72,384]{1,0:T(8,128)S(1)} collective-permute-done((f32[72,384]{1,0:T(8,128)S(1)}, f32[72,384]{1,0:T(8,128)S(1)}, u32[]{:S(2)}, u32[]{:S(2)}) %collective-permute-start.3) | collective-permute-done | bytes 110624 | tf_op jit(solution)/shard_map/ppermute | solution.py:52
  13.8 0.1 collective-permute-start.7
  14.0 2.3 %collective-permute-done.2.refs_3_ = f32[72,384]{1,0:T(8,128)S(1)} collective-permute-done((f32[72,384]{1,0:T(8,128)S(1)}, f32[72,384]{1,0:T(8,128)S(1)}, u32[]{:S(2)}, u32[]{:S(2)}) %collective-permute-start.2) | collective-permute-done | bytes 110624 | tf_op jit(solution)/shard_map/ppermute | solution.py:52
  16.2 0.3 collective-permute-start.6
  16.5 0.0 collective-permute-done.9.refs_0_
  16.5 0.2 collective-permute-start.5
  16.7 0.1 pad_maximum_fusion.refs_10_.refs_6_.refs_7_.refs_4_
  16.8 0.0 collective-permute-done.8.refs_1_.refs_0_
  16.8 1.2 %shard_map.53 = (f32[2,128,384]{2,1,0:T(8,128)S(1)}, f32[128,384]{1,0:T(8,128)S(1)}) custom-call(f32[64,384]{1,0:T(8,128)S(1)} %collective-permute-done.9.refs_0_, f32[64,384]{1,0:T(8,128)S(1)} %collective-permute-done.8.refs_1_.refs_0_, f32[72,384]{1,0:T(8,128)S(1)} %get-tuple-element.13.refs_2_, f32[72,384]{1,0:T(8,128)S(1)} %collective-permute-done.2.refs_3_, ...), custom_call_target="tpu_custom_call" | custom-call | flops 509607936 | bytes 2998272 | tf_op jit(solution)/shard_map/pallas_call | solution.py:66
  18.0 0.0 collective-permute-done.7.refs_9_.refs_4_
  18.0 0.0 collective-permute-done.6.refs_8_.refs_3_
  18.0 0.0 collective-permute-done.5.refs_7_.refs_2_
  18.1 0.9 %shard_map.54 = f32[128,384]{1,0:T(8,128)S(1)} custom-call(f32[64,384]{1,0:T(8,128)S(1)} %collective-permute-done.8.refs_1_.refs_0_, f32[72,384]{1,0:T(8,128)S(1)} %collective-permute-done.wanted_ref.refs_6_.refs_1_, f32[72,384]{1,0:T(8,128)S(1)} %collective-permute-done.5.refs_7_.refs_2_, f32[72,384]{1,0:T(8,128)S(1)} %collective-permute-done.6.refs_8_.refs_3_, ...), custom_call_target="tpu_custom_call" | custom-call | flops 325582848 | bytes 3096576 | tf_op jit(solution)/shard_map/pallas_call | solution.py:66
  19.0 1.4 %collective-permute-start.10 = (f32[128,384]{1,0:T(8,128)S(1)}, f32[128,384]{1,0:T(8,128)S(1)}, u32[]{:S(2)}, u32[]{:S(2)}) collective-permute-start(f32[128,384]{1,0:T(8,128)S(1)} %shard_map.54), channel_id=1, source_target_pairs={{0,3},{1,4},{2,7},{3,0},{4,1},{5,6},{6,5},{7,2},{8,13},{9,10},{10,... | collective-permute-start | bytes 589832 | tf_op jit(solution)/shard_map/ppermute | solution.py:52
  20.4 0.0 collective-permute-done.1.refs_0_.refs_8_
  20.4 0.9 %shard_map.55 = f32[128,384]{1,0:T(8,128)S(1)} custom-call(f32[64,384]{1,0:T(8,128)S(1)} %collective-permute-done.9.refs_0_, f32[72,384]{1,0:T(8,128)S(1)} %collective-permute-done.wanted_ref.refs_6_.refs_1_, f32[72,384]{1,0:T(8,128)S(1)} %collective-permute-done.5.refs_7_.refs_2_, f32[72,384]{1,0:T(8,128)S(1)} %collective-permute-done.6.refs_8_.refs_3_, ...), custom_call_target="tpu_custom_call" | custom-call | flops 325582848 | bytes 3194880 | tf_op jit(solution)/shard_map/pallas_call | solution.py:66
  21.4 0.4 collective-permute-start.11
  21.8 1.6 %shard_map.52 = (f32[128,384]{1,0:T(8,128)S(1)}, f32[128,384]{1,0:T(8,128)S(1)}) custom-call(f32[64,384]{1,0:T(8,128)S(1)} %collective-permute-done.1.refs_0_.refs_8_, f32[64,384]{1,0:T(8,128)S(1)} %get-tuple-element.12.value_ref.refs_1_.points_ref, f32[72,384]{1,0:T(8,128)S(1)} %get-tuple-element.13.refs_2_, f32[72,384]{1,0:T(8,128)S(1)} %collective-permute-done.2.refs_3_, ...), custom_call_target="tpu_custom_call" | custom-call | flops 905969664 | bytes 3244032 | tf_op jit(solution)/shard_map/pallas_call | solution.py:66
  23.5 0.7 %collective-permute-done.10 = f32[128,384]{1,0:T(8,128)S(1)} collective-permute-done((f32[128,384]{1,0:T(8,128)S(1)}, f32[128,384]{1,0:T(8,128)S(1)}, u32[]{:S(2)}, u32[]{:S(2)}) %collective-permute-start.10) | collective-permute-done | bytes 196640 | tf_op jit(solution)/shard_map/ppermute | solution.py:52
  24.2 1.8 %collective-permute-start.13 = (f32[128,384]{1,0:T(8,128)S(1)}, f32[128,384]{1,0:T(8,128)S(1)}, u32[]{:S(2)}, u32[]{:S(2)}) collective-permute-start(f32[128,384]{1,0:T(8,128)S(1)} %add.6.refs_0_), channel_id=1, source_target_pairs={{0,5},{1,2},{2,1},{3,6},{4,7},{5,0},{6,3},{7,4},{8,11},{9,12},{10,... | collective-permute-start | bytes 589832 | tf_op jit(solution)/shard_map/ppermute | solution.py:52
  25.9 0.6 %collective-permute-done.11 = f32[128,384]{1,0:T(8,128)S(1)} collective-permute-done((f32[128,384]{1,0:T(8,128)S(1)}, f32[128,384]{1,0:T(8,128)S(1)}, u32[]{:S(2)}, u32[]{:S(2)}) %collective-permute-start.11) | collective-permute-done | bytes 196640 | tf_op jit(solution)/shard_map/ppermute | solution.py:52
  26.6 1.4 %collective-permute-start.12 = (f32[128,384]{1,0:T(8,128)S(1)}, f32[128,384]{1,0:T(8,128)S(1)}, u32[]{:S(2)}, u32[]{:S(2)}) collective-permute-start(f32[128,384]{1,0:T(8,128)S(1)} %add.7.refs_2_), channel_id=1, source_target_pairs={{0,5},{1,2},{2,1},{3,6},{4,7},{5,0},{6,3},{7,4},{8,11},{9,12},{10,... | collective-permute-start | bytes 589832 | tf_op jit(solution)/shard_map/ppermute | solution.py:52
  28.0 1.4 %collective-permute-done.13.refs_3_ = f32[128,384]{1,0:T(8,128)S(1)} collective-permute-done((f32[128,384]{1,0:T(8,128)S(1)}, f32[128,384]{1,0:T(8,128)S(1)}, u32[]{:S(2)}, u32[]{:S(2)}) %collective-permute-start.13) | collective-permute-done | bytes 196640 | tf_op jit(solution)/shard_map/ppermute | solution.py:52
  29.3 2.4 %collective-permute-done.12.refs_1_ = f32[128,384]{1,0:T(8,128)S(1)} collective-permute-done((f32[128,384]{1,0:T(8,128)S(1)}, f32[128,384]{1,0:T(8,128)S(1)}, u32[]{:S(2)}, u32[]{:S(2)}) %collective-permute-start.12) | collective-permute-done | bytes 196640 | tf_op jit(solution)/shard_map/ppermute | solution.py:52
  31.7 0.9 %shard_map.56 = (f32[192,128]{1,0:T(8,128)S(1)}, f32[192,128]{1,0:T(8,128)S(1)}) custom-call(f32[128,384]{1,0:T(8,128)S(1)} %add.6.refs_0_, f32[128,384]{1,0:T(8,128)S(1)} %collective-permute-done.12.refs_1_, f32[128,384]{1,0:T(8,128)S(1)} %add.7.refs_2_, f32[128,384]{1,0:T(8,128)S(1)} %collective-permute-done.13.refs_3_, ...), custom_call_target="tpu_custom_call" | custom-call | tf_op jit(solution)/shard_map/pallas_call | solution.py:260
  32.7 1.5 %collective-permute-start.14 = (f32[192,128]{1,0:T(8,128)S(1)}, f32[192,128]{1,0:T(8,128)S(1)}, u32[]{:S(2)}, u32[]{:S(2)}) collective-permute-start(f32[192,128]{1,0:T(8,128)S(1)} %get-tuple-element.19), channel_id=1, source_target_pairs={{0,3},{1,4},{2,7},{3,0},{4,1},{5,6},{6,5},{7,2},{8,13},{9,10},{10,... | collective-permute-start | bytes 294920 | tf_op jit(solution)/shard_map/ppermute | solution.py:52
  34.1 2.6 %collective-permute-done.14.arrived_ref = f32[192,128]{1,0:T(8,128)S(1)} collective-permute-done((f32[192,128]{1,0:T(8,128)S(1)}, f32[192,128]{1,0:T(8,128)S(1)}, u32[]{:S(2)}, u32[]{:S(2)}) %collective-permute-start.14) | collective-permute-done | bytes 98336 | tf_op jit(solution)/shard_map/ppermute | solution.py:52
  36.8 0.4 collective-permute-start.15
  37.1 0.9 %collective-permute-done.15.refs_1_ = f32[96,128]{1,0:T(8,128)S(1)} collective-permute-done((f32[96,128]{1,0:T(8,128)S(1)}, f32[96,128]{1,0:T(8,128)S(1)}, u32[]{:S(2)}, u32[]{:S(2)}) %collective-permute-start.15) | collective-permute-done | bytes 49184 | tf_op jit(solution)/shard_map/ppermute | solution.py:52
  38.1 2.7 %collective-permute-start.18 = (f32[96,128]{1,0:T(8,128)S(1)}, f32[96,128]{1,0:T(8,128)S(1)}, u32[]{:S(2)}, u32[]{:S(2)}) collective-permute-start(f32[96,128]{1,0:T(8,128)S(1)} %shard_map.58.refs_0_), channel_id=1, source_target_pairs={{0,24},{1,25},{2,26},{3,27},{4,28},{5,29},{6,30},{7,31},{8,16},{9,... | collective-permute-start | bytes 147464 | tf_op jit(solution)/shard_map/ppermute | solution.py:52
  40.8 0.0 collective-permute-start.17
  40.8 1.5 %collective-permute-start.16 = (f32[96,128]{1,0:T(8,128)S(1)}, f32[96,128]{1,0:T(8,128)S(1)}, u32[]{:S(2)}, u32[]{:S(2)}) collective-permute-start(f32[96,128]{1,0:T(8,128)S(1)} %shard_map.58.refs_0_), channel_id=1, source_target_pairs={{0,9},{1,8},{2,11},{3,10},{4,13},{5,12},{6,15},{7,14},{8,1},{9,0},... | collective-permute-start | bytes 147464 | tf_op jit(solution)/shard_map/ppermute | solution.py:52
  42.3 2.3 %collective-permute-done.18.refs_3_ = f32[96,128]{1,0:T(8,128)S(1)} collective-permute-done((f32[96,128]{1,0:T(8,128)S(1)}, f32[96,128]{1,0:T(8,128)S(1)}, u32[]{:S(2)}, u32[]{:S(2)}) %collective-permute-start.18) | collective-permute-done | bytes 49184 | tf_op jit(solution)/shard_map/ppermute | solution.py:52
  44.5 1.5 %collective-permute-done.17.refs_2_ = f32[96,128]{1,0:T(8,128)S(1)} collective-permute-done((f32[96,128]{1,0:T(8,128)S(1)}, f32[96,128]{1,0:T(8,128)S(1)}, u32[]{:S(2)}, u32[]{:S(2)}) %collective-permute-start.17) | collective-permute-done | bytes 49184 | tf_op jit(solution)/shard_map/ppermute | solution.py:52
  46.0 0.1 collective-permute-done.16.refs_1_
  46.1 2.5 %collective-permute-start.21 = (f32[96,128]{1,0:T(8,128)S(1)}, f32[96,128]{1,0:T(8,128)S(1)}, u32[]{:S(2)}, u32[]{:S(2)}) collective-permute-start(f32[96,128]{1,0:T(8,128)S(1)} %shard_map.59.refs_0_), channel_id=1, source_target_pairs={{0,6},{1,7},{2,4},{3,5},{4,2},{5,3},{6,0},{7,1},{8,14},{9,15},{10,... | collective-permute-start | bytes 147464 | tf_op jit(solution)/shard_map/ppermute | solution.py:52
  48.6 0.0 collective-permute-start.20
  48.6 0.8 %collective-permute-start.19 = (f32[96,128]{1,0:T(8,128)S(1)}, f32[96,128]{1,0:T(8,128)S(1)}, u32[]{:S(2)}, u32[]{:S(2)}) collective-permute-start(f32[96,128]{1,0:T(8,128)S(1)} %shard_map.59.refs_0_), channel_id=1, source_target_pairs={{0,3},{1,4},{2,7},{3,0},{4,1},{5,6},{6,5},{7,2},{8,13},{9,10},{10,... | collective-permute-start | bytes 147464 | tf_op jit(solution)/shard_map/ppermute | solution.py:52
  49.4 1.8 %collective-permute-done.21.refs_3_ = f32[96,128]{1,0:T(8,128)S(1)} collective-permute-done((f32[96,128]{1,0:T(8,128)S(1)}, f32[96,128]{1,0:T(8,128)S(1)}, u32[]{:S(2)}, u32[]{:S(2)}) %collective-permute-start.21) | collective-permute-done | bytes 49184 | tf_op jit(solution)/shard_map/ppermute | solution.py:52
  51.1 1.0 %collective-permute-done.20.refs_2_ = f32[96,128]{1,0:T(8,128)S(1)} collective-permute-done((f32[96,128]{1,0:T(8,128)S(1)}, f32[96,128]{1,0:T(8,128)S(1)}, u32[]{:S(2)}, u32[]{:S(2)}) %collective-permute-start.20) | collective-permute-done | bytes 49184 | tf_op jit(solution)/shard_map/ppermute | solution.py:52
  52.1 0.5 collective-permute-done.19.refs_1_
  52.6 0.2 collective-permute-start.22
  52.9 1.3 %collective-permute-done.22.other_ref = f32[384,128]{1,0:T(8,128)S(1)} collective-permute-done((f32[384,128]{1,0:T(8,128)S(1)}, f32[384,128]{1,0:T(8,128)S(1)}, u32[]{:S(2)}, u32[]{:S(2)}) %collective-permute-start.22) | collective-permute-done | bytes 196640 | tf_op jit(solution)/shard_map/ppermute | solution.py:52
  54.1 1.2 %shard_map.61 = (f32[384,384]{1,0:T(8,128)}, f32[64,384]{1,0:T(8,128)}) custom-call(f32[384,128]{1,0:T(8,128)S(1)} %shard_map.60.keep_ref, f32[384,128]{1,0:T(8,128)S(1)} %collective-permute-done.22.other_ref, f32[64,384]{1,0:T(8,128)S(1)} %get-tuple-element.12.value_ref.refs_1_.points_ref), custom_call_target="tpu_custom_call" | custom-call | tf_op jit(solution)/shard_map/pallas_call | solution.py:349
  (7 shorter events, 0.1 us)
Async XLA Ops:
  1.6 5.6 %collective-permute-start = (f32[72,384]{1,0:T(8,128)S(1)}, f32[72,384]{1,0:T(8,128)S(1)}, u32[]{:S(2)}, u32[]{:S(2)}) collective-permute-start(f32[72,384]{1,0:T(8,128)S(1)} %get-tuple-element.13.refs_2_), channel_id=1, source_target_pairs={{0,1},{1,0},{2,3},{3,2},{4,5},{5,4},{6,7},{7,6},{8,9},{9,8},{10,11... | collective-permute-start | bytes 331784 | tf_op jit(solution)/shard_map/ppermute | solution.py:52
  2.1 9.0 %collective-permute-start.4 = (f32[72,384]{1,0:T(8,128)S(1)}, f32[72,384]{1,0:T(8,128)S(1)}, u32[]{:S(2)}, u32[]{:S(2)}) collective-permute-start(f32[72,384]{1,0:T(8,128)S(1)} %get-tuple-element.13.refs_2_), channel_id=1, source_target_pairs={{0,24},{1,25},{2,26},{3,27},{4,28},{5,29},{6,30},{7,31},{8,16},{9,... | collective-permute-start | bytes 331784 | tf_op jit(solution)/shard_map/ppermute | solution.py:52
  6.7 7.1 %collective-permute-start.3 = (f32[72,384]{1,0:T(8,128)S(1)}, f32[72,384]{1,0:T(8,128)S(1)}, u32[]{:S(2)}, u32[]{:S(2)}) collective-permute-start(f32[72,384]{1,0:T(8,128)S(1)} %get-tuple-element.13.refs_2_), channel_id=1, source_target_pairs={{0,9},{1,8},{2,11},{3,10},{4,13},{5,12},{6,15},{7,14},{8,1},{9,0},... | collective-permute-start | bytes 331784 | tf_op jit(solution)/shard_map/ppermute | solution.py:52
  6.8 9.5 %collective-permute-start.2 = (f32[72,384]{1,0:T(8,128)S(1)}, f32[72,384]{1,0:T(8,128)S(1)}, u32[]{:S(2)}, u32[]{:S(2)}) collective-permute-start(f32[72,384]{1,0:T(8,128)S(1)} %get-tuple-element.13.refs_2_), channel_id=1, source_target_pairs={{0,17},{1,16},{2,19},{3,18},{4,21},{5,20},{6,23},{7,22},{8,25},{9,... | collective-permute-start | bytes 331784 | tf_op jit(solution)/shard_map/ppermute | solution.py:52
  7.1 9.4 %collective-permute-start.9 = (f32[64,384]{1,0:T(8,128)S(1)}, f32[64,384]{1,0:T(8,128)S(1)}, u32[]{:S(2)}, u32[]{:S(2)}) collective-permute-start(f32[64,384]{1,0:T(8,128)S(1)} %shard_map.51), channel_id=1, source_target_pairs={{0,6},{1,7},{2,4},{3,5},{4,2},{5,3},{6,0},{7,1},{8,14},{9,15},{10,... | collective-permute-start | bytes 294920 | tf_op jit(solution)/shard_map/ppermute | solution.py:52
  10.9 5.9 %collective-permute-start.8 = (f32[64,384]{1,0:T(8,128)S(1)}, f32[64,384]{1,0:T(8,128)S(1)}, u32[]{:S(2)}, u32[]{:S(2)}) collective-permute-start(f32[64,384]{1,0:T(8,128)S(1)} %shard_map.51), channel_id=1, source_target_pairs={{0,3},{1,4},{2,7},{3,0},{4,1},{5,6},{6,5},{7,2},{8,13},{9,10},{10,... | collective-permute-start | bytes 294920 | tf_op jit(solution)/shard_map/ppermute | solution.py:52
  11.1 9.4 %collective-permute-start.1 = (f32[64,384]{1,0:T(8,128)S(1)}, f32[64,384]{1,0:T(8,128)S(1)}, u32[]{:S(2)}, u32[]{:S(2)}) collective-permute-start(f32[64,384]{1,0:T(8,128)S(1)} %shard_map.51), channel_id=1, source_target_pairs={{0,5},{1,2},{2,1},{3,6},{4,7},{5,0},{6,3},{7,4},{8,11},{9,12},{10,... | collective-permute-start | bytes 294920 | tf_op jit(solution)/shard_map/ppermute | solution.py:52
  13.8 4.2 %collective-permute-start.7 = (f32[72,384]{1,0:T(8,128)S(1)}, f32[72,384]{1,0:T(8,128)S(1)}, u32[]{:S(2)}, u32[]{:S(2)}) collective-permute-start(f32[72,384]{1,0:T(8,128)S(1)} %collective-permute-done.4.refs_5_), channel_id=1, source_target_pairs={{0,1},{1,0},{2,3},{3,2},{4,5},{5,4},{6,7},{7,6},{8,9},{9,8},{10,11... | collective-permute-start | bytes 331784 | tf_op jit(solution)/shard_map/ppermute | solution.py:52
  16.2 1.8 %collective-permute-start.6 = (f32[72,384]{1,0:T(8,128)S(1)}, f32[72,384]{1,0:T(8,128)S(1)}, u32[]{:S(2)}, u32[]{:S(2)}) collective-permute-start(f32[72,384]{1,0:T(8,128)S(1)} %collective-permute-done.3.refs_4_), channel_id=1, source_target_pairs={{0,1},{1,0},{2,3},{3,2},{4,5},{5,4},{6,7},{7,6},{8,9},{9,8},{10,11... | collective-permute-start | bytes 331784 | tf_op jit(solution)/shard_map/ppermute | solution.py:52
  16.5 1.5 %collective-permute-start.5 = (f32[72,384]{1,0:T(8,128)S(1)}, f32[72,384]{1,0:T(8,128)S(1)}, u32[]{:S(2)}, u32[]{:S(2)}) collective-permute-start(f32[72,384]{1,0:T(8,128)S(1)} %collective-permute-done.2.refs_3_), channel_id=1, source_target_pairs={{0,1},{1,0},{2,3},{3,2},{4,5},{5,4},{6,7},{7,6},{8,9},{9,8},{10,11... | collective-permute-start | bytes 331784 | tf_op jit(solution)/shard_map/ppermute | solution.py:52
  19.0 5.2 %collective-permute-start.10 = (f32[128,384]{1,0:T(8,128)S(1)}, f32[128,384]{1,0:T(8,128)S(1)}, u32[]{:S(2)}, u32[]{:S(2)}) collective-permute-start(f32[128,384]{1,0:T(8,128)S(1)} %shard_map.54), channel_id=1, source_target_pairs={{0,3},{1,4},{2,7},{3,0},{4,1},{5,6},{6,5},{7,2},{8,13},{9,10},{10,... | collective-permute-start | bytes 589832 | tf_op jit(solution)/shard_map/ppermute | solution.py:52
  21.4 5.2 %collective-permute-start.11 = (f32[128,384]{1,0:T(8,128)S(1)}, f32[128,384]{1,0:T(8,128)S(1)}, u32[]{:S(2)}, u32[]{:S(2)}) collective-permute-start(f32[128,384]{1,0:T(8,128)S(1)} %shard_map.55), channel_id=1, source_target_pairs={{0,3},{1,4},{2,7},{3,0},{4,1},{5,6},{6,5},{7,2},{8,13},{9,10},{10,... | collective-permute-start | bytes 589832 | tf_op jit(solution)/shard_map/ppermute | solution.py:52
  24.2 5.2 %collective-permute-start.13 = (f32[128,384]{1,0:T(8,128)S(1)}, f32[128,384]{1,0:T(8,128)S(1)}, u32[]{:S(2)}, u32[]{:S(2)}) collective-permute-start(f32[128,384]{1,0:T(8,128)S(1)} %add.6.refs_0_), channel_id=1, source_target_pairs={{0,5},{1,2},{2,1},{3,6},{4,7},{5,0},{6,3},{7,4},{8,11},{9,12},{10,... | collective-permute-start | bytes 589832 | tf_op jit(solution)/shard_map/ppermute | solution.py:52
  26.6 5.2 %collective-permute-start.12 = (f32[128,384]{1,0:T(8,128)S(1)}, f32[128,384]{1,0:T(8,128)S(1)}, u32[]{:S(2)}, u32[]{:S(2)}) collective-permute-start(f32[128,384]{1,0:T(8,128)S(1)} %add.7.refs_2_), channel_id=1, source_target_pairs={{0,5},{1,2},{2,1},{3,6},{4,7},{5,0},{6,3},{7,4},{8,11},{9,12},{10,... | collective-permute-start | bytes 589832 | tf_op jit(solution)/shard_map/ppermute | solution.py:52
  32.7 4.1 %collective-permute-start.14 = (f32[192,128]{1,0:T(8,128)S(1)}, f32[192,128]{1,0:T(8,128)S(1)}, u32[]{:S(2)}, u32[]{:S(2)}) collective-permute-start(f32[192,128]{1,0:T(8,128)S(1)} %get-tuple-element.19), channel_id=1, source_target_pairs={{0,3},{1,4},{2,7},{3,0},{4,1},{5,6},{6,5},{7,2},{8,13},{9,10},{10,... | collective-permute-start | bytes 294920 | tf_op jit(solution)/shard_map/ppermute | solution.py:52
  36.8 1.3 %collective-permute-start.15 = (f32[96,128]{1,0:T(8,128)S(1)}, f32[96,128]{1,0:T(8,128)S(1)}, u32[]{:S(2)}, u32[]{:S(2)}) collective-permute-start(f32[96,128]{1,0:T(8,128)S(1)} %get-tuple-element.21), channel_id=1, source_target_pairs={{0,1},{1,0},{2,3},{3,2},{4,5},{5,4},{6,7},{7,6},{8,9},{9,8},{10,11... | collective-permute-start | bytes 147464 | tf_op jit(solution)/shard_map/ppermute | solution.py:52
  38.1 6.4 %collective-permute-start.18 = (f32[96,128]{1,0:T(8,128)S(1)}, f32[96,128]{1,0:T(8,128)S(1)}, u32[]{:S(2)}, u32[]{:S(2)}) collective-permute-start(f32[96,128]{1,0:T(8,128)S(1)} %shard_map.58.refs_0_), channel_id=1, source_target_pairs={{0,24},{1,25},{2,26},{3,27},{4,28},{5,29},{6,30},{7,31},{8,16},{9,... | collective-permute-start | bytes 147464 | tf_op jit(solution)/shard_map/ppermute | solution.py:52
  40.8 5.2 %collective-permute-start.17 = (f32[96,128]{1,0:T(8,128)S(1)}, f32[96,128]{1,0:T(8,128)S(1)}, u32[]{:S(2)}, u32[]{:S(2)}) collective-permute-start(f32[96,128]{1,0:T(8,128)S(1)} %shard_map.58.refs_0_), channel_id=1, source_target_pairs={{0,17},{1,16},{2,19},{3,18},{4,21},{5,20},{6,23},{7,22},{8,25},{9,... | collective-permute-start | bytes 147464 | tf_op jit(solution)/shard_map/ppermute | solution.py:52
  40.8 5.3 %collective-permute-start.16 = (f32[96,128]{1,0:T(8,128)S(1)}, f32[96,128]{1,0:T(8,128)S(1)}, u32[]{:S(2)}, u32[]{:S(2)}) collective-permute-start(f32[96,128]{1,0:T(8,128)S(1)} %shard_map.58.refs_0_), channel_id=1, source_target_pairs={{0,9},{1,8},{2,11},{3,10},{4,13},{5,12},{6,15},{7,14},{8,1},{9,0},... | collective-permute-start | bytes 147464 | tf_op jit(solution)/shard_map/ppermute | solution.py:52
  46.1 5.1 %collective-permute-start.21 = (f32[96,128]{1,0:T(8,128)S(1)}, f32[96,128]{1,0:T(8,128)S(1)}, u32[]{:S(2)}, u32[]{:S(2)}) collective-permute-start(f32[96,128]{1,0:T(8,128)S(1)} %shard_map.59.refs_0_), channel_id=1, source_target_pairs={{0,6},{1,7},{2,4},{3,5},{4,2},{5,3},{6,0},{7,1},{8,14},{9,15},{10,... | collective-permute-start | bytes 147464 | tf_op jit(solution)/shard_map/ppermute | solution.py:52
  48.6 3.5 %collective-permute-start.20 = (f32[96,128]{1,0:T(8,128)S(1)}, f32[96,128]{1,0:T(8,128)S(1)}, u32[]{:S(2)}, u32[]{:S(2)}) collective-permute-start(f32[96,128]{1,0:T(8,128)S(1)} %shard_map.59.refs_0_), channel_id=1, source_target_pairs={{0,5},{1,2},{2,1},{3,6},{4,7},{5,0},{6,3},{7,4},{8,11},{9,12},{10,... | collective-permute-start | bytes 147464 | tf_op jit(solution)/shard_map/ppermute | solution.py:52
  48.6 4.0 %collective-permute-start.19 = (f32[96,128]{1,0:T(8,128)S(1)}, f32[96,128]{1,0:T(8,128)S(1)}, u32[]{:S(2)}, u32[]{:S(2)}) collective-permute-start(f32[96,128]{1,0:T(8,128)S(1)} %shard_map.59.refs_0_), channel_id=1, source_target_pairs={{0,3},{1,4},{2,7},{3,0},{4,1},{5,6},{6,5},{7,2},{8,13},{9,10},{10,... | collective-permute-start | bytes 147464 | tf_op jit(solution)/shard_map/ppermute | solution.py:52
  52.6 1.5 %collective-permute-start.22 = (f32[384,128]{1,0:T(8,128)S(1)}, f32[384,128]{1,0:T(8,128)S(1)}, u32[]{:S(2)}, u32[]{:S(2)}) collective-permute-start(f32[384,128]{1,0:T(8,128)S(1)} %shard_map.60.keep_ref), channel_id=1, source_target_pairs={{0,1},{1,0},{2,3},{3,2},{4,5},{5,4},{6,7},{7,6},{8,9},{9,8},{10,11... | collective-permute-start | bytes 589832 | tf_op jit(solution)/shard_map/ppermute | solution.py:52

commit v9 on v8

--- a/solution.py
+++ b/solution.py
@@ -388,6 +388,7 @@
         points, packed = pack_own(points, coeffs)
         metric3 = metric_halves(metric)
         near = among(packed, [(bit, 0) for bit in reversed(line_bits)])
+        near = near[:1] + near[:0:-1]
         late = [other for block in near for other in among(block, [(0, bit) for bit in col_bits])[1:]]
         source = copy_after(points, late[0])
         queries = [hop(source, (bit_a | bit_b, 0)), to_a(source), to_b(source), points]

time: 55.6 us -> 55.3 us (level)
  waiting for transfers between devices: 21.4 us -> 19.3 us
  starting transfers between devices: 24.1 us -> 26 us
    ppermute x23, waiting for transfers between devices: 21.4 us -> 19.3 us  [hop(): return lax.ppermute(value, AXES, pairs)]
    ppermute x23, starting transfers between devices: 24.1 us -> 26 us  [hop(): return lax.ppermute(value, AXES, pairs)]
  transfers between devices with their start and end apart: 23 -> 23, of which waited for: 15 -> 14; matrix products, arithmetic and copies ran while one was open for 2% -> 2% of each run, Pallas kernels for 8% -> 9%
where the time goes in v9:
time: 55.3 us; the launch traced here: 55.1 us
  starting transfers between devices  26 us (47%)
  waiting for transfers between devices  19.3 us (35%)
  Pallas kernels  7.82 us (14%)
  other arithmetic  1.28 us (2%)
  between operations  0.75 us (1%)
    ppermute x23, starting transfers between devices, hop(): return lax.ppermute(value, AXES, pairs)  26 us
    ppermute x23, waiting for transfers between devices, hop(): return lax.ppermute(value, AXES, pairs)  19.3 us
    pallas_call x9, Pallas kernels, call(): pl.pallas_call(body, out_shape=out_shape, in_specs=[pl.BlockSpec(memory_s...  4.76 us
    pallas_call x1, Pallas kernels, finish(): pl.pallas_call(body, out_shape=(shape(width, width), shape(rows, width)),...  1.22 us
    convert_element_type x1, other arithmetic, metric_halves(): low = (metric - high).astype(BF16)  1.14 us
  transfers between devices with their start and end apart: 23, of which 14 were waited for; matrix products, arithmetic and copies ran while one was open for 2% of the time, Pallas kernels for 9%

profile of v9, /device:TPU:0, one launch (start us, length us, event | category | flops | bytes accessed | tf_op | source)
XLA Modules:
  0.0 55.1 jit_solution(10119414734727077718)
XLA Ops:
  0.6 0.9 %shard_map.50 = (f32[64,384]{1,0:T(8,128)S(1)}, f32[72,384]{1,0:T(8,128)S(1)}) custom-call(f32[64,384]{1,0:T(8,128)} %points_ref.1, f32[2,64]{1,0:T(2,128)} %bitcast.1), custom_call_target="tpu_custom_call" | custom-call | tf_op jit(solution)/shard_map/pallas_call | solution.py:99
  1.6 0.5 collective-permute-start
  2.1 3.7 %collective-permute-start.4 = (f32[72,384]{1,0:T(8,128)S(1)}, f32[72,384]{1,0:T(8,128)S(1)}, u32[]{:S(2)}, u32[]{:S(2)}) collective-permute-start(f32[72,384]{1,0:T(8,128)S(1)} %get-tuple-element.13.refs_2_), channel_id=1, source_target_pairs={{0,17},{1,16},{2,19},{3,18},{4,21},{5,20},{6,23},{7,22},{8,25},{9,... | collective-permute-start | bytes 331784 | tf_op jit(solution)/shard_map/ppermute | solution.py:52
  5.8 1.2 %collective-permute-start.3 = (f32[72,384]{1,0:T(8,128)S(1)}, f32[72,384]{1,0:T(8,128)S(1)}, u32[]{:S(2)}, u32[]{:S(2)}) collective-permute-start(f32[72,384]{1,0:T(8,128)S(1)} %get-tuple-element.13.refs_2_), channel_id=1, source_target_pairs={{0,9},{1,8},{2,11},{3,10},{4,13},{5,12},{6,15},{7,14},{8,1},{9,0},... | collective-permute-start | bytes 331784 | tf_op jit(solution)/shard_map/ppermute | solution.py:52
  7.0 0.2 collective-permute-start.2
  7.2 0.0 collective-permute-done.wanted_ref.refs_6_.refs_1_
  7.3 2.5 %collective-permute-start.9 = (f32[64,384]{1,0:T(8,128)S(1)}, f32[64,384]{1,0:T(8,128)S(1)}, u32[]{:S(2)}, u32[]{:S(2)}) collective-permute-start(f32[64,384]{1,0:T(8,128)S(1)} %shard_map.51), channel_id=1, source_target_pairs={{0,6},{1,7},{2,4},{3,5},{4,2},{5,3},{6,0},{7,1},{8,14},{9,15},{10,... | collective-permute-start | bytes 294920 | tf_op jit(solution)/shard_map/ppermute | solution.py:52
  9.8 1.1 %fusion = (bf16[384,384]{1,0:T(8,128)(2,1)S(1)}, bf16[384,384]{1,0:T(8,128)(2,1)S(1)}) fusion(f32[384,384]{1,0:T(8,128)} %param.5), kind=kLoop, calls=%fused_computation.3 | loop fusion | flops 589824 | bytes 1179648 | tf_op jit(solution)/shard_map/convert_element_type | solution.py:117
  10.9 0.2 collective-permute-start.8
  11.1 0.5 collective-permute-done.4.refs_5_
  11.6 2.1 %collective-permute-start.1 = (f32[64,384]{1,0:T(8,128)S(1)}, f32[64,384]{1,0:T(8,128)S(1)}, u32[]{:S(2)}, u32[]{:S(2)}) collective-permute-start(f32[64,384]{1,0:T(8,128)S(1)} %shard_map.51), channel_id=1, source_target_pairs={{0,5},{1,2},{2,1},{3,6},{4,7},{5,0},{6,3},{7,4},{8,11},{9,12},{10,... | collective-permute-start | bytes 294920 | tf_op jit(solution)/shard_map/ppermute | solution.py:52
  13.7 0.0 collective-permute-done.3.refs_4_
  13.7 0.0 collective-permute-start.7
  13.7 1.6 %collective-permute-done.2.refs_3_ = f32[72,384]{1,0:T(8,128)S(1)} collective-permute-done((f32[72,384]{1,0:T(8,128)S(1)}, f32[72,384]{1,0:T(8,128)S(1)}, u32[]{:S(2)}, u32[]{:S(2)}) %collective-permute-start.2) | collective-permute-done | bytes 110624 | tf_op jit(solution)/shard_map/ppermute | solution.py:52
  15.3 0.0 collective-permute-start.6
  15.3 0.0 collective-permute-done.9.refs_0_
  15.3 0.5 collective-permute-start.5
  15.8 0.1 pad_maximum_fusion.refs_10_.refs_6_.refs_7_.refs_4_
  15.9 0.0 collective-permute-done.8.refs_1_.refs_0_
  15.9 1.2 %shard_map.53 = (f32[2,128,384]{2,1,0:T(8,128)S(1)}, f32[128,384]{1,0:T(8,128)S(1)}) custom-call(f32[64,384]{1,0:T(8,128)S(1)} %collective-permute-done.9.refs_0_, f32[64,384]{1,0:T(8,128)S(1)} %collective-permute-done.8.refs_1_.refs_0_, f32[72,384]{1,0:T(8,128)S(1)} %get-tuple-element.13.refs_2_, f32[72,384]{1,0:T(8,128)S(1)} %collective-permute-done.2.refs_3_, ...), custom_call_target="tpu_custom_call" | custom-call | flops 509607936 | bytes 2998272 | tf_op jit(solution)/shard_map/pallas_call | solution.py:66
  17.1 0.0 collective-permute-done.7.refs_9_.refs_4_
  17.1 0.0 collective-permute-done.6.refs_8_.refs_3_
  17.1 0.0 collective-permute-done.5.refs_7_.refs_2_
  17.1 0.9 %shard_map.54 = f32[128,384]{1,0:T(8,128)S(1)} custom-call(f32[64,384]{1,0:T(8,128)S(1)} %collective-permute-done.8.refs_1_.refs_0_, f32[72,384]{1,0:T(8,128)S(1)} %collective-permute-done.wanted_ref.refs_6_.refs_1_, f32[72,384]{1,0:T(8,128)S(1)} %collective-permute-done.5.refs_7_.refs_2_, f32[72,384]{1,0:T(8,128)S(1)} %collective-permute-done.6.refs_8_.refs_3_, ...), custom_call_target="tpu_custom_call" | custom-call | flops 325582848 | bytes 3096576 | tf_op jit(solution)/shard_map/pallas_call | solution.py:66
  18.1 1.2 %collective-permute-start.10 = (f32[128,384]{1,0:T(8,128)S(1)}, f32[128,384]{1,0:T(8,128)S(1)}, u32[]{:S(2)}, u32[]{:S(2)}) collective-permute-start(f32[128,384]{1,0:T(8,128)S(1)} %shard_map.54), channel_id=1, source_target_pairs={{0,3},{1,4},{2,7},{3,0},{4,1},{5,6},{6,5},{7,2},{8,13},{9,10},{10,... | collective-permute-start | bytes 589832 | tf_op jit(solution)/shard_map/ppermute | solution.py:52
  19.2 0.0 collective-permute-done.1.refs_0_.refs_8_
  19.2 0.9 %shard_map.55 = f32[128,384]{1,0:T(8,128)S(1)} custom-call(f32[64,384]{1,0:T(8,128)S(1)} %collective-permute-done.9.refs_0_, f32[72,384]{1,0:T(8,128)S(1)} %collective-permute-done.wanted_ref.refs_6_.refs_1_, f32[72,384]{1,0:T(8,128)S(1)} %collective-permute-done.5.refs_7_.refs_2_, f32[72,384]{1,0:T(8,128)S(1)} %collective-permute-done.6.refs_8_.refs_3_, ...), custom_call_target="tpu_custom_call" | custom-call | flops 325582848 | bytes 3194880 | tf_op jit(solution)/shard_map/pallas_call | solution.py:66
  20.2 0.7 %collective-permute-start.11 = (f32[128,384]{1,0:T(8,128)S(1)}, f32[128,384]{1,0:T(8,128)S(1)}, u32[]{:S(2)}, u32[]{:S(2)}) collective-permute-start(f32[128,384]{1,0:T(8,128)S(1)} %shard_map.55), channel_id=1, source_target_pairs={{0,3},{1,4},{2,7},{3,0},{4,1},{5,6},{6,5},{7,2},{8,13},{9,10},{10,... | collective-permute-start | bytes 589832 | tf_op jit(solution)/shard_map/ppermute | solution.py:52
  20.9 1.6 %shard_map.52 = (f32[128,384]{1,0:T(8,128)S(1)}, f32[128,384]{1,0:T(8,128)S(1)}) custom-call(f32[64,384]{1,0:T(8,128)S(1)} %collective-permute-done.1.refs_0_.refs_8_, f32[64,384]{1,0:T(8,128)S(1)} %get-tuple-element.12.value_ref.refs_1_.points_ref, f32[72,384]{1,0:T(8,128)S(1)} %get-tuple-element.13.refs_2_, f32[72,384]{1,0:T(8,128)S(1)} %collective-permute-done.2.refs_3_, ...), custom_call_target="tpu_custom_call" | custom-call | flops 905969664 | bytes 3244032 | tf_op jit(solution)/shard_map/pallas_call | solution.py:66
  22.5 0.7 %collective-permute-done.10 = f32[128,384]{1,0:T(8,128)S(1)} collective-permute-done((f32[128,384]{1,0:T(8,128)S(1)}, f32[128,384]{1,0:T(8,128)S(1)}, u32[]{:S(2)}, u32[]{:S(2)}) %collective-permute-start.10) | collective-permute-done | bytes 196640 | tf_op jit(solution)/shard_map/ppermute | solution.py:52
  23.3 1.5 %collective-permute-start.13 = (f32[128,384]{1,0:T(8,128)S(1)}, f32[128,384]{1,0:T(8,128)S(1)}, u32[]{:S(2)}, u32[]{:S(2)}) collective-permute-start(f32[128,384]{1,0:T(8,128)S(1)} %add.6.refs_0_), channel_id=1, source_target_pairs={{0,5},{1,2},{2,1},{3,6},{4,7},{5,0},{6,3},{7,4},{8,11},{9,12},{10,... | collective-permute-start | bytes 589832 | tf_op jit(solution)/shard_map/ppermute | solution.py:52
  24.8 0.6 %collective-permute-done.11 = f32[128,384]{1,0:T(8,128)S(1)} collective-permute-done((f32[128,384]{1,0:T(8,128)S(1)}, f32[128,384]{1,0:T(8,128)S(1)}, u32[]{:S(2)}, u32[]{:S(2)}) %collective-permute-start.11) | collective-permute-done | bytes 196640 | tf_op jit(solution)/shard_map/ppermute | solution.py:52
  25.4 1.7 %collective-permute-start.12 = (f32[128,384]{1,0:T(8,128)S(1)}, f32[128,384]{1,0:T(8,128)S(1)}, u32[]{:S(2)}, u32[]{:S(2)}) collective-permute-start(f32[128,384]{1,0:T(8,128)S(1)} %add.7.refs_2_), channel_id=1, source_target_pairs={{0,5},{1,2},{2,1},{3,6},{4,7},{5,0},{6,3},{7,4},{8,11},{9,12},{10,... | collective-permute-start | bytes 589832 | tf_op jit(solution)/shard_map/ppermute | solution.py:52
  27.1 1.4 %collective-permute-done.13.refs_3_ = f32[128,384]{1,0:T(8,128)S(1)} collective-permute-done((f32[128,384]{1,0:T(8,128)S(1)}, f32[128,384]{1,0:T(8,128)S(1)}, u32[]{:S(2)}, u32[]{:S(2)}) %collective-permute-start.13) | collective-permute-done | bytes 196640 | tf_op jit(solution)/shard_map/ppermute | solution.py:52
  28.4 2.1 %collective-permute-done.12.refs_1_ = f32[128,384]{1,0:T(8,128)S(1)} collective-permute-done((f32[128,384]{1,0:T(8,128)S(1)}, f32[128,384]{1,0:T(8,128)S(1)}, u32[]{:S(2)}, u32[]{:S(2)}) %collective-permute-start.12) | collective-permute-done | bytes 196640 | tf_op jit(solution)/shard_map/ppermute | solution.py:52
  30.5 0.9 %shard_map.56 = (f32[192,128]{1,0:T(8,128)S(1)}, f32[192,128]{1,0:T(8,128)S(1)}) custom-call(f32[128,384]{1,0:T(8,128)S(1)} %add.6.refs_0_, f32[128,384]{1,0:T(8,128)S(1)} %collective-permute-done.12.refs_1_, f32[128,384]{1,0:T(8,128)S(1)} %add.7.refs_2_, f32[128,384]{1,0:T(8,128)S(1)} %collective-permute-done.13.refs_3_, ...), custom_call_target="tpu_custom_call" | custom-call | tf_op jit(solution)/shard_map/pallas_call | solution.py:260
  31.5 1.5 %collective-permute-start.14 = (f32[192,128]{1,0:T(8,128)S(1)}, f32[192,128]{1,0:T(8,128)S(1)}, u32[]{:S(2)}, u32[]{:S(2)}) collective-permute-start(f32[192,128]{1,0:T(8,128)S(1)} %get-tuple-element.19), channel_id=1, source_target_pairs={{0,3},{1,4},{2,7},{3,0},{4,1},{5,6},{6,5},{7,2},{8,13},{9,10},{10,... | collective-permute-start | bytes 294920 | tf_op jit(solution)/shard_map/ppermute | solution.py:52
  32.9 2.6 %collective-permute-done.14.arrived_ref = f32[192,128]{1,0:T(8,128)S(1)} collective-permute-done((f32[192,128]{1,0:T(8,128)S(1)}, f32[192,128]{1,0:T(8,128)S(1)}, u32[]{:S(2)}, u32[]{:S(2)}) %collective-permute-start.14) | collective-permute-done | bytes 98336 | tf_op jit(solution)/shard_map/ppermute | solution.py:52
  35.6 0.6 %collective-permute-start.15 = (f32[96,128]{1,0:T(8,128)S(1)}, f32[96,128]{1,0:T(8,128)S(1)}, u32[]{:S(2)}, u32[]{:S(2)}) collective-permute-start(f32[96,128]{1,0:T(8,128)S(1)} %get-tuple-element.21), channel_id=1, source_target_pairs={{0,1},{1,0},{2,3},{3,2},{4,5},{5,4},{6,7},{7,6},{8,9},{9,8},{10,11... | collective-permute-start | bytes 147464 | tf_op jit(solution)/shard_map/ppermute | solution.py:52
  36.2 0.9 %collective-permute-done.15.refs_1_ = f32[96,128]{1,0:T(8,128)S(1)} collective-permute-done((f32[96,128]{1,0:T(8,128)S(1)}, f32[96,128]{1,0:T(8,128)S(1)}, u32[]{:S(2)}, u32[]{:S(2)}) %collective-permute-start.15) | collective-permute-done | bytes 49184 | tf_op jit(solution)/shard_map/ppermute | solution.py:52
  37.1 2.7 %collective-permute-start.18 = (f32[96,128]{1,0:T(8,128)S(1)}, f32[96,128]{1,0:T(8,128)S(1)}, u32[]{:S(2)}, u32[]{:S(2)}) collective-permute-start(f32[96,128]{1,0:T(8,128)S(1)} %shard_map.58.refs_0_), channel_id=1, source_target_pairs={{0,24},{1,25},{2,26},{3,27},{4,28},{5,29},{6,30},{7,31},{8,16},{9,... | collective-permute-start | bytes 147464 | tf_op jit(solution)/shard_map/ppermute | solution.py:52
  39.8 1.2 %collective-permute-start.17 = (f32[96,128]{1,0:T(8,128)S(1)}, f32[96,128]{1,0:T(8,128)S(1)}, u32[]{:S(2)}, u32[]{:S(2)}) collective-permute-start(f32[96,128]{1,0:T(8,128)S(1)} %shard_map.58.refs_0_), channel_id=1, source_target_pairs={{0,17},{1,16},{2,19},{3,18},{4,21},{5,20},{6,23},{7,22},{8,25},{9,... | collective-permute-start | bytes 147464 | tf_op jit(solution)/shard_map/ppermute | solution.py:52
  40.9 0.3 collective-permute-start.16
  41.2 1.9 %collective-permute-done.18.refs_3_ = f32[96,128]{1,0:T(8,128)S(1)} collective-permute-done((f32[96,128]{1,0:T(8,128)S(1)}, f32[96,128]{1,0:T(8,128)S(1)}, u32[]{:S(2)}, u32[]{:S(2)}) %collective-permute-start.18) | collective-permute-done | bytes 49184 | tf_op jit(solution)/shard_map/ppermute | solution.py:52
  43.0 3.0 %collective-permute-done.17.refs_2_ = f32[96,128]{1,0:T(8,128)S(1)} collective-permute-done((f32[96,128]{1,0:T(8,128)S(1)}, f32[96,128]{1,0:T(8,128)S(1)}, u32[]{:S(2)}, u32[]{:S(2)}) %collective-permute-start.17) | collective-permute-done | bytes 49184 | tf_op jit(solution)/shard_map/ppermute | solution.py:52
  46.1 0.0 collective-permute-done.16.refs_1_
  46.1 2.0 %collective-permute-start.21 = (f32[96,128]{1,0:T(8,128)S(1)}, f32[96,128]{1,0:T(8,128)S(1)}, u32[]{:S(2)}, u32[]{:S(2)}) collective-permute-start(f32[96,128]{1,0:T(8,128)S(1)} %shard_map.59.refs_0_), channel_id=1, source_target_pairs={{0,6},{1,7},{2,4},{3,5},{4,2},{5,3},{6,0},{7,1},{8,14},{9,15},{10,... | collective-permute-start | bytes 147464 | tf_op jit(solution)/shard_map/ppermute | solution.py:52
  48.1 0.2 collective-permute-start.20
  48.3 1.1 %collective-permute-start.19 = (f32[96,128]{1,0:T(8,128)S(1)}, f32[96,128]{1,0:T(8,128)S(1)}, u32[]{:S(2)}, u32[]{:S(2)}) collective-permute-start(f32[96,128]{1,0:T(8,128)S(1)} %shard_map.59.refs_0_), channel_id=1, source_target_pairs={{0,3},{1,4},{2,7},{3,0},{4,1},{5,6},{6,5},{7,2},{8,13},{9,10},{10,... | collective-permute-start | bytes 147464 | tf_op jit(solution)/shard_map/ppermute | solution.py:52
  49.4 1.8 %collective-permute-done.21.refs_3_ = f32[96,128]{1,0:T(8,128)S(1)} collective-permute-done((f32[96,128]{1,0:T(8,128)S(1)}, f32[96,128]{1,0:T(8,128)S(1)}, u32[]{:S(2)}, u32[]{:S(2)}) %collective-permute-start.21) | collective-permute-done | bytes 49184 | tf_op jit(solution)/shard_map/ppermute | solution.py:52
  51.2 0.5 collective-permute-done.20.refs_2_
  51.7 0.6 %collective-permute-done.19.refs_1_ = f32[96,128]{1,0:T(8,128)S(1)} collective-permute-done((f32[96,128]{1,0:T(8,128)S(1)}, f32[96,128]{1,0:T(8,128)S(1)}, u32[]{:S(2)}, u32[]{:S(2)}) %collective-permute-start.19) | collective-permute-done | bytes 49184 | tf_op jit(solution)/shard_map/ppermute | solution.py:52
  52.3 0.6 %collective-permute-start.22 = (f32[384,128]{1,0:T(8,128)S(1)}, f32[384,128]{1,0:T(8,128)S(1)}, u32[]{:S(2)}, u32[]{:S(2)}) collective-permute-start(f32[384,128]{1,0:T(8,128)S(1)} %shard_map.60.keep_ref), channel_id=1, source_target_pairs={{0,1},{1,0},{2,3},{3,2},{4,5},{5,4},{6,7},{7,6},{8,9},{9,8},{10,11... | collective-permute-start | bytes 589832 | tf_op jit(solution)/shard_map/ppermute | solution.py:52
  52.8 1.1 %collective-permute-done.22.other_ref = f32[384,128]{1,0:T(8,128)S(1)} collective-permute-done((f32[384,128]{1,0:T(8,128)S(1)}, f32[384,128]{1,0:T(8,128)S(1)}, u32[]{:S(2)}, u32[]{:S(2)}) %collective-permute-start.22) | collective-permute-done | bytes 196640 | tf_op jit(solution)/shard_map/ppermute | solution.py:52
  53.9 1.2 %shard_map.61 = (f32[384,384]{1,0:T(8,128)}, f32[64,384]{1,0:T(8,128)}) custom-call(f32[384,128]{1,0:T(8,128)S(1)} %shard_map.60.keep_ref, f32[384,128]{1,0:T(8,128)S(1)} %collective-permute-done.22.other_ref, f32[64,384]{1,0:T(8,128)S(1)} %get-tuple-element.12.value_ref.refs_1_.points_ref), custom_call_target="tpu_custom_call" | custom-call | tf_op jit(solution)/shard_map/pallas_call | solution.py:349
  (7 shorter events, 0.1 us)
Async XLA Ops:
  1.6 5.7 %collective-permute-start = (f32[72,384]{1,0:T(8,128)S(1)}, f32[72,384]{1,0:T(8,128)S(1)}, u32[]{:S(2)}, u32[]{:S(2)}) collective-permute-start(f32[72,384]{1,0:T(8,128)S(1)} %get-tuple-element.13.refs_2_), channel_id=1, source_target_pairs={{0,1},{1,0},{2,3},{3,2},{4,5},{5,4},{6,7},{7,6},{8,9},{9,8},{10,11... | collective-permute-start | bytes 331784 | tf_op jit(solution)/shard_map/ppermute | solution.py:52
  2.1 9.5 %collective-permute-start.4 = (f32[72,384]{1,0:T(8,128)S(1)}, f32[72,384]{1,0:T(8,128)S(1)}, u32[]{:S(2)}, u32[]{:S(2)}) collective-permute-start(f32[72,384]{1,0:T(8,128)S(1)} %get-tuple-element.13.refs_2_), channel_id=1, source_target_pairs={{0,17},{1,16},{2,19},{3,18},{4,21},{5,20},{6,23},{7,22},{8,25},{9,... | collective-permute-start | bytes 331784 | tf_op jit(solution)/shard_map/ppermute | solution.py:52
  5.8 7.9 %collective-permute-start.3 = (f32[72,384]{1,0:T(8,128)S(1)}, f32[72,384]{1,0:T(8,128)S(1)}, u32[]{:S(2)}, u32[]{:S(2)}) collective-permute-start(f32[72,384]{1,0:T(8,128)S(1)} %get-tuple-element.13.refs_2_), channel_id=1, source_target_pairs={{0,9},{1,8},{2,11},{3,10},{4,13},{5,12},{6,15},{7,14},{8,1},{9,0},... | collective-permute-start | bytes 331784 | tf_op jit(solution)/shard_map/ppermute | solution.py:52
  7.0 8.3 %collective-permute-start.2 = (f32[72,384]{1,0:T(8,128)S(1)}, f32[72,384]{1,0:T(8,128)S(1)}, u32[]{:S(2)}, u32[]{:S(2)}) collective-permute-start(f32[72,384]{1,0:T(8,128)S(1)} %get-tuple-element.13.refs_2_), channel_id=1, source_target_pairs={{0,24},{1,25},{2,26},{3,27},{4,28},{5,29},{6,30},{7,31},{8,16},{9,... | collective-permute-start | bytes 331784 | tf_op jit(solution)/shard_map/ppermute | solution.py:52
  7.3 8.1 %collective-permute-start.9 = (f32[64,384]{1,0:T(8,128)S(1)}, f32[64,384]{1,0:T(8,128)S(1)}, u32[]{:S(2)}, u32[]{:S(2)}) collective-permute-start(f32[64,384]{1,0:T(8,128)S(1)} %shard_map.51), channel_id=1, source_target_pairs={{0,6},{1,7},{2,4},{3,5},{4,2},{5,3},{6,0},{7,1},{8,14},{9,15},{10,... | collective-permute-start | bytes 294920 | tf_op jit(solution)/shard_map/ppermute | solution.py:52
  10.9 5.0 %collective-permute-start.8 = (f32[64,384]{1,0:T(8,128)S(1)}, f32[64,384]{1,0:T(8,128)S(1)}, u32[]{:S(2)}, u32[]{:S(2)}) collective-permute-start(f32[64,384]{1,0:T(8,128)S(1)} %shard_map.51), channel_id=1, source_target_pairs={{0,3},{1,4},{2,7},{3,0},{4,1},{5,6},{6,5},{7,2},{8,13},{9,10},{10,... | collective-permute-start | bytes 294920 | tf_op jit(solution)/shard_map/ppermute | solution.py:52
  11.6 7.6 %collective-permute-start.1 = (f32[64,384]{1,0:T(8,128)S(1)}, f32[64,384]{1,0:T(8,128)S(1)}, u32[]{:S(2)}, u32[]{:S(2)}) collective-permute-start(f32[64,384]{1,0:T(8,128)S(1)} %shard_map.51), channel_id=1, source_target_pairs={{0,5},{1,2},{2,1},{3,6},{4,7},{5,0},{6,3},{7,4},{8,11},{9,12},{10,... | collective-permute-start | bytes 294920 | tf_op jit(solution)/shard_map/ppermute | solution.py:52
  13.7 3.5 %collective-permute-start.7 = (f32[72,384]{1,0:T(8,128)S(1)}, f32[72,384]{1,0:T(8,128)S(1)}, u32[]{:S(2)}, u32[]{:S(2)}) collective-permute-start(f32[72,384]{1,0:T(8,128)S(1)} %collective-permute-done.4.refs_5_), channel_id=1, source_target_pairs={{0,1},{1,0},{2,3},{3,2},{4,5},{5,4},{6,7},{7,6},{8,9},{9,8},{10,11... | collective-permute-start | bytes 331784 | tf_op jit(solution)/shard_map/ppermute | solution.py:52
  15.3 1.8 %collective-permute-start.6 = (f32[72,384]{1,0:T(8,128)S(1)}, f32[72,384]{1,0:T(8,128)S(1)}, u32[]{:S(2)}, u32[]{:S(2)}) collective-permute-start(f32[72,384]{1,0:T(8,128)S(1)} %collective-permute-done.3.refs_4_), channel_id=1, source_target_pairs={{0,1},{1,0},{2,3},{3,2},{4,5},{5,4},{6,7},{7,6},{8,9},{9,8},{10,11... | collective-permute-start | bytes 331784 | tf_op jit(solution)/shard_map/ppermute | solution.py:52
  15.3 1.8 %collective-permute-start.5 = (f32[72,384]{1,0:T(8,128)S(1)}, f32[72,384]{1,0:T(8,128)S(1)}, u32[]{:S(2)}, u32[]{:S(2)}) collective-permute-start(f32[72,384]{1,0:T(8,128)S(1)} %collective-permute-done.2.refs_3_), channel_id=1, source_target_pairs={{0,1},{1,0},{2,3},{3,2},{4,5},{5,4},{6,7},{7,6},{8,9},{9,8},{10,11... | collective-permute-start | bytes 331784 | tf_op jit(solution)/shard_map/ppermute | solution.py:52
  18.1 5.2 %collective-permute-start.10 = (f32[128,384]{1,0:T(8,128)S(1)}, f32[128,384]{1,0:T(8,128)S(1)}, u32[]{:S(2)}, u32[]{:S(2)}) collective-permute-start(f32[128,384]{1,0:T(8,128)S(1)} %shard_map.54), channel_id=1, source_target_pairs={{0,3},{1,4},{2,7},{3,0},{4,1},{5,6},{6,5},{7,2},{8,13},{9,10},{10,... | collective-permute-start | bytes 589832 | tf_op jit(solution)/shard_map/ppermute | solution.py:52
  20.2 5.2 %collective-permute-start.11 = (f32[128,384]{1,0:T(8,128)S(1)}, f32[128,384]{1,0:T(8,128)S(1)}, u32[]{:S(2)}, u32[]{:S(2)}) collective-permute-start(f32[128,384]{1,0:T(8,128)S(1)} %shard_map.55), channel_id=1, source_target_pairs={{0,3},{1,4},{2,7},{3,0},{4,1},{5,6},{6,5},{7,2},{8,13},{9,10},{10,... | collective-permute-start | bytes 589832 | tf_op jit(solution)/shard_map/ppermute | solution.py:52
  23.3 5.2 %collective-permute-start.13 = (f32[128,384]{1,0:T(8,128)S(1)}, f32[128,384]{1,0:T(8,128)S(1)}, u32[]{:S(2)}, u32[]{:S(2)}) collective-permute-start(f32[128,384]{1,0:T(8,128)S(1)} %add.6.refs_0_), channel_id=1, source_target_pairs={{0,5},{1,2},{2,1},{3,6},{4,7},{5,0},{6,3},{7,4},{8,11},{9,12},{10,... | collective-permute-start | bytes 589832 | tf_op jit(solution)/shard_map/ppermute | solution.py:52
  25.4 5.2 %collective-permute-start.12 = (f32[128,384]{1,0:T(8,128)S(1)}, f32[128,384]{1,0:T(8,128)S(1)}, u32[]{:S(2)}, u32[]{:S(2)}) collective-permute-start(f32[128,384]{1,0:T(8,128)S(1)} %add.7.refs_2_), channel_id=1, source_target_pairs={{0,5},{1,2},{2,1},{3,6},{4,7},{5,0},{6,3},{7,4},{8,11},{9,12},{10,... | collective-permute-start | bytes 589832 | tf_op jit(solution)/shard_map/ppermute | solution.py:52
  31.5 4.1 %collective-permute-start.14 = (f32[192,128]{1,0:T(8,128)S(1)}, f32[192,128]{1,0:T(8,128)S(1)}, u32[]{:S(2)}, u32[]{:S(2)}) collective-permute-start(f32[192,128]{1,0:T(8,128)S(1)} %get-tuple-element.19), channel_id=1, source_target_pairs={{0,3},{1,4},{2,7},{3,0},{4,1},{5,6},{6,5},{7,2},{8,13},{9,10},{10,... | collective-permute-start | bytes 294920 | tf_op jit(solution)/shard_map/ppermute | solution.py:52
  35.6 1.5 %collective-permute-start.15 = (f32[96,128]{1,0:T(8,128)S(1)}, f32[96,128]{1,0:T(8,128)S(1)}, u32[]{:S(2)}, u32[]{:S(2)}) collective-permute-start(f32[96,128]{1,0:T(8,128)S(1)} %get-tuple-element.21), channel_id=1, source_target_pairs={{0,1},{1,0},{2,3},{3,2},{4,5},{5,4},{6,7},{7,6},{8,9},{9,8},{10,11... | collective-permute-start | bytes 147464 | tf_op jit(solution)/shard_map/ppermute | solution.py:52
  37.1 6.0 %collective-permute-start.18 = (f32[96,128]{1,0:T(8,128)S(1)}, f32[96,128]{1,0:T(8,128)S(1)}, u32[]{:S(2)}, u32[]{:S(2)}) collective-permute-start(f32[96,128]{1,0:T(8,128)S(1)} %shard_map.58.refs_0_), channel_id=1, source_target_pairs={{0,24},{1,25},{2,26},{3,27},{4,28},{5,29},{6,30},{7,31},{8,16},{9,... | collective-permute-start | bytes 147464 | tf_op jit(solution)/shard_map/ppermute | solution.py:52
  39.8 6.3 %collective-permute-start.17 = (f32[96,128]{1,0:T(8,128)S(1)}, f32[96,128]{1,0:T(8,128)S(1)}, u32[]{:S(2)}, u32[]{:S(2)}) collective-permute-start(f32[96,128]{1,0:T(8,128)S(1)} %shard_map.58.refs_0_), channel_id=1, source_target_pairs={{0,17},{1,16},{2,19},{3,18},{4,21},{5,20},{6,23},{7,22},{8,25},{9,... | collective-permute-start | bytes 147464 | tf_op jit(solution)/shard_map/ppermute | solution.py:52
  40.9 5.1 %collective-permute-start.16 = (f32[96,128]{1,0:T(8,128)S(1)}, f32[96,128]{1,0:T(8,128)S(1)}, u32[]{:S(2)}, u32[]{:S(2)}) collective-permute-start(f32[96,128]{1,0:T(8,128)S(1)} %shard_map.58.refs_0_), channel_id=1, source_target_pairs={{0,9},{1,8},{2,11},{3,10},{4,13},{5,12},{6,15},{7,14},{8,1},{9,0},... | collective-permute-start | bytes 147464 | tf_op jit(solution)/shard_map/ppermute | solution.py:52
  46.1 5.1 %collective-permute-start.21 = (f32[96,128]{1,0:T(8,128)S(1)}, f32[96,128]{1,0:T(8,128)S(1)}, u32[]{:S(2)}, u32[]{:S(2)}) collective-permute-start(f32[96,128]{1,0:T(8,128)S(1)} %shard_map.59.refs_0_), channel_id=1, source_target_pairs={{0,6},{1,7},{2,4},{3,5},{4,2},{5,3},{6,0},{7,1},{8,14},{9,15},{10,... | collective-permute-start | bytes 147464 | tf_op jit(solution)/shard_map/ppermute | solution.py:52
  48.1 3.5 %collective-permute-start.20 = (f32[96,128]{1,0:T(8,128)S(1)}, f32[96,128]{1,0:T(8,128)S(1)}, u32[]{:S(2)}, u32[]{:S(2)}) collective-permute-start(f32[96,128]{1,0:T(8,128)S(1)} %shard_map.59.refs_0_), channel_id=1, source_target_pairs={{0,5},{1,2},{2,1},{3,6},{4,7},{5,0},{6,3},{7,4},{8,11},{9,12},{10,... | collective-permute-start | bytes 147464 | tf_op jit(solution)/shard_map/ppermute | solution.py:52
  48.3 3.9 %collective-permute-start.19 = (f32[96,128]{1,0:T(8,128)S(1)}, f32[96,128]{1,0:T(8,128)S(1)}, u32[]{:S(2)}, u32[]{:S(2)}) collective-permute-start(f32[96,128]{1,0:T(8,128)S(1)} %shard_map.59.refs_0_), channel_id=1, source_target_pairs={{0,3},{1,4},{2,7},{3,0},{4,1},{5,6},{6,5},{7,2},{8,13},{9,10},{10,... | collective-permute-start | bytes 147464 | tf_op jit(solution)/shard_map/ppermute | solution.py:52
  52.3 1.7 %collective-permute-start.22 = (f32[384,128]{1,0:T(8,128)S(1)}, f32[384,128]{1,0:T(8,128)S(1)}, u32[]{:S(2)}, u32[]{:S(2)}) collective-permute-start(f32[384,128]{1,0:T(8,128)S(1)} %shard_map.60.keep_ref), channel_id=1, source_target_pairs={{0,1},{1,0},{2,3},{3,2},{4,5},{5,4},{6,7},{7,6},{8,9},{9,8},{10,11... | collective-permute-start | bytes 589832 | tf_op jit(solution)/shard_map/ppermute | solution.py:52

commit v10 on v9

--- a/solution.py
+++ b/solution.py
@@ -389,15 +389,16 @@
         metric3 = metric_halves(metric)
         near = among(packed, [(bit, 0) for bit in reversed(line_bits)])
         near = near[:1] + near[:0:-1]
-        late = [other for block in near for other in among(block, [(0, bit) for bit in col_bits])[1:]]
-        source = copy_after(points, late[0])
+        across = [among(block, [(0, bit) for bit in col_bits])[1:] for block in near]
+        first, late = across[0] + across[-1], [other for blocks in across[1:-1] for other in blocks]
+        source = copy_after(points, first[0])
         queries = [hop(source, (bit_a | bit_b, 0)), to_a(source), to_b(source), points]
-        total, mapped = early_sums(queries[:2], near, metric3, outs_n)
+        total, mapped = early_sums(queries[:2], near + first, metric3, outs_n)
         (part_ab,) = late_sums(queries[:1], 0, total, mapped, metric3, late, outs_n, queries[2:3])
         sent_ab = to_a(part_ab)
         (part_a,) = late_sums(queries[1:2], 1, total, mapped, metric3, late, outs_n)
         sent_a = to_a(part_a)
-        part_b, part_own = whole_sums(queries[2:], near + late, metric3, outs_n)
+        part_b, part_own = whole_sums(queries[2:], near + first + late, metric3, outs_n)
         half_b = part_b + sent_ab
         rest_own = to_b(half_b)
         half_own = part_own + sent_a

time: 55.3 us -> 55.1 us (level)
  starting transfers between devices: 26 us -> 25.2 us
  waiting for transfers between devices: 19.3 us -> 20.1 us
    ppermute x23, waiting for transfers between devices: 19.3 us -> 20.1 us  [hop(): return lax.ppermute(value, AXES, pairs)]
    ppermute x23, starting transfers between devices: 26 us -> 25.2 us  [hop(): return lax.ppermute(value, AXES, pairs)]
  transfers between devices with their start and end apart: 23 -> 23, of which waited for: 14 -> 15; matrix products, arithmetic and copies ran while one was open for 2% -> 2% of each run, Pallas kernels for 9% -> 8%
where the time goes in v10:
time: 55.1 us; the launch traced here: 54.9 us
  starting transfers between devices  25.2 us (46%)
  waiting for transfers between devices  20.1 us (36%)
  Pallas kernels  7.58 us (14%)
  other arithmetic  1.27 us (2%)
  between operations  0.76 us (1%)
    ppermute x23, starting transfers between devices, hop(): return lax.ppermute(value, AXES, pairs)  25.2 us
    ppermute x23, waiting for transfers between devices, hop(): return lax.ppermute(value, AXES, pairs)  20.1 us
    pallas_call x9, Pallas kernels, call(): pl.pallas_call(body, out_shape=out_shape, in_specs=[pl.BlockSpec(memory_s...  4.51 us
    pallas_call x1, Pallas kernels, finish(): pl.pallas_call(body, out_shape=(shape(width, width), shape(rows, width)),...  1.22 us
    convert_element_type x1, other arithmetic, metric_halves(): low = (metric - high).astype(BF16)  1.14 us
  transfers between devices with their start and end apart: 23, of which 15 were waited for; matrix products, arithmetic and copies ran while one was open for 2% of the time, Pallas kernels for 8%

profile of v10, /device:TPU:0, one launch (start us, length us, event | category | flops | bytes accessed | tf_op | source)
XLA Modules:
  0.0 54.9 jit_solution(6769997236669446654)
XLA Ops:
  0.6 0.9 %shard_map.50 = (f32[64,384]{1,0:T(8,128)S(1)}, f32[72,384]{1,0:T(8,128)S(1)}) custom-call(f32[64,384]{1,0:T(8,128)} %points_ref.1, f32[2,64]{1,0:T(2,128)} %bitcast.1), custom_call_target="tpu_custom_call" | custom-call | tf_op jit(solution)/shard_map/pallas_call | solution.py:99
  1.6 0.5 collective-permute-start
  2.1 3.7 %collective-permute-start.4 = (f32[72,384]{1,0:T(8,128)S(1)}, f32[72,384]{1,0:T(8,128)S(1)}, u32[]{:S(2)}, u32[]{:S(2)}) collective-permute-start(f32[72,384]{1,0:T(8,128)S(1)} %get-tuple-element.13.refs_2_), channel_id=1, source_target_pairs={{0,17},{1,16},{2,19},{3,18},{4,21},{5,20},{6,23},{7,22},{8,25},{9,... | collective-permute-start | bytes 331784 | tf_op jit(solution)/shard_map/ppermute | solution.py:52
  5.8 1.2 %collective-permute-start.3 = (f32[72,384]{1,0:T(8,128)S(1)}, f32[72,384]{1,0:T(8,128)S(1)}, u32[]{:S(2)}, u32[]{:S(2)}) collective-permute-start(f32[72,384]{1,0:T(8,128)S(1)} %get-tuple-element.13.refs_2_), channel_id=1, source_target_pairs={{0,9},{1,8},{2,11},{3,10},{4,13},{5,12},{6,15},{7,14},{8,1},{9,0},... | collective-permute-start | bytes 331784 | tf_op jit(solution)/shard_map/ppermute | solution.py:52
  7.0 0.2 collective-permute-start.2
  7.2 0.0 collective-permute-done.wanted_ref.refs_6_
  7.3 2.5 %collective-permute-start.9 = (f32[64,384]{1,0:T(8,128)S(1)}, f32[64,384]{1,0:T(8,128)S(1)}, u32[]{:S(2)}, u32[]{:S(2)}) collective-permute-start(f32[64,384]{1,0:T(8,128)S(1)} %shard_map.51), channel_id=1, source_target_pairs={{0,6},{1,7},{2,4},{3,5},{4,2},{5,3},{6,0},{7,1},{8,14},{9,15},{10,... | collective-permute-start | bytes 294920 | tf_op jit(solution)/shard_map/ppermute | solution.py:52
  9.8 1.1 %fusion = (bf16[384,384]{1,0:T(8,128)(2,1)S(1)}, bf16[384,384]{1,0:T(8,128)(2,1)S(1)}) fusion(f32[384,384]{1,0:T(8,128)} %param.5), kind=kLoop, calls=%fused_computation.3 | loop fusion | flops 589824 | bytes 1179648 | tf_op jit(solution)/shard_map/convert_element_type | solution.py:117
  10.9 0.2 collective-permute-start.8
  11.1 0.5 collective-permute-done.4.refs_5_
  11.6 2.1 %collective-permute-start.1 = (f32[64,384]{1,0:T(8,128)S(1)}, f32[64,384]{1,0:T(8,128)S(1)}, u32[]{:S(2)}, u32[]{:S(2)}) collective-permute-start(f32[64,384]{1,0:T(8,128)S(1)} %shard_map.51), channel_id=1, source_target_pairs={{0,5},{1,2},{2,1},{3,6},{4,7},{5,0},{6,3},{7,4},{8,11},{9,12},{10,... | collective-permute-start | bytes 294920 | tf_op jit(solution)/shard_map/ppermute | solution.py:52
  13.7 0.0 collective-permute-done.3.refs_4_
  13.7 0.0 collective-permute-start.5
  13.7 1.6 %collective-permute-done.2.refs_3_ = f32[72,384]{1,0:T(8,128)S(1)} collective-permute-done((f32[72,384]{1,0:T(8,128)S(1)}, f32[72,384]{1,0:T(8,128)S(1)}, u32[]{:S(2)}, u32[]{:S(2)}) %collective-permute-start.2) | collective-permute-done | bytes 110624 | tf_op jit(solution)/shard_map/ppermute | solution.py:52
  15.3 0.0 collective-permute-start.7
  15.3 0.0 collective-permute-done.9.refs_0_
  15.3 0.5 collective-permute-start.6
  15.8 0.1 pad_maximum_fusion.refs_10_.refs_8_.refs_5_.refs_4_
  15.9 0.0 collective-permute-done.8.refs_1_.refs_0_
  15.9 0.0 collective-permute-done.5.refs_7_
  15.9 1.5 %shard_map.53 = (f32[2,128,384]{2,1,0:T(8,128)S(1)}, f32[128,384]{1,0:T(8,128)S(1)}) custom-call(f32[64,384]{1,0:T(8,128)S(1)} %collective-permute-done.9.refs_0_, f32[64,384]{1,0:T(8,128)S(1)} %collective-permute-done.8.refs_1_.refs_0_, f32[72,384]{1,0:T(8,128)S(1)} %get-tuple-element.13.refs_2_, f32[72,384]{1,0:T(8,128)S(1)} %collective-permute-done.2.refs_3_, ...), custom_call_target="tpu_custom_call" | custom-call | flops 707788800 | bytes 3219456 | tf_op jit(solution)/shard_map/pallas_call | solution.py:66
  17.4 0.0 collective-permute-done.7.refs_9_.refs_2_
  17.4 0.0 collective-permute-done.6.refs_8_.refs_1_
  17.4 0.7 %shard_map.54 = f32[128,384]{1,0:T(8,128)S(1)} custom-call(f32[64,384]{1,0:T(8,128)S(1)} %collective-permute-done.8.refs_1_.refs_0_, f32[72,384]{1,0:T(8,128)S(1)} %collective-permute-done.6.refs_8_.refs_1_, f32[72,384]{1,0:T(8,128)S(1)} %collective-permute-done.7.refs_9_.refs_2_, f32[2,128,384]{2,1,0:T(8,128)S(1)} %get-tuple-element.15.refs_3_, ...), custom_call_target="tpu_custom_call" | custom-call | flops 162791424 | bytes 2875392 | tf_op jit(solution)/shard_map/pallas_call | solution.py:66
  18.1 1.2 %collective-permute-start.10 = (f32[128,384]{1,0:T(8,128)S(1)}, f32[128,384]{1,0:T(8,128)S(1)}, u32[]{:S(2)}, u32[]{:S(2)}) collective-permute-start(f32[128,384]{1,0:T(8,128)S(1)} %shard_map.54), channel_id=1, source_target_pairs={{0,3},{1,4},{2,7},{3,0},{4,1},{5,6},{6,5},{7,2},{8,13},{9,10},{10,... | collective-permute-start | bytes 589832 | tf_op jit(solution)/shard_map/ppermute | solution.py:52
  19.3 0.0 collective-permute-done.1.refs_0_.refs_6_
  19.3 0.7 %shard_map.55 = f32[128,384]{1,0:T(8,128)S(1)} custom-call(f32[64,384]{1,0:T(8,128)S(1)} %collective-permute-done.9.refs_0_, f32[72,384]{1,0:T(8,128)S(1)} %collective-permute-done.6.refs_8_.refs_1_, f32[72,384]{1,0:T(8,128)S(1)} %collective-permute-done.7.refs_9_.refs_2_, f32[2,128,384]{2,1,0:T(8,128)S(1)} %get-tuple-element.15.refs_3_, ...), custom_call_target="tpu_custom_call" | custom-call | flops 162791424 | bytes 2973696 | tf_op jit(solution)/shard_map/pallas_call | solution.py:66
  19.9 0.7 %collective-permute-start.11 = (f32[128,384]{1,0:T(8,128)S(1)}, f32[128,384]{1,0:T(8,128)S(1)}, u32[]{:S(2)}, u32[]{:S(2)}) collective-permute-start(f32[128,384]{1,0:T(8,128)S(1)} %shard_map.55), channel_id=1, source_target_pairs={{0,3},{1,4},{2,7},{3,0},{4,1},{5,6},{6,5},{7,2},{8,13},{9,10},{10,... | collective-permute-start | bytes 589832 | tf_op jit(solution)/shard_map/ppermute | solution.py:52
  20.6 1.7 %shard_map.52 = (f32[128,384]{1,0:T(8,128)S(1)}, f32[128,384]{1,0:T(8,128)S(1)}) custom-call(f32[64,384]{1,0:T(8,128)S(1)} %collective-permute-done.1.refs_0_.refs_6_, f32[64,384]{1,0:T(8,128)S(1)} %get-tuple-element.12.value_ref.refs_1_.points_ref, f32[72,384]{1,0:T(8,128)S(1)} %get-tuple-element.13.refs_2_, f32[72,384]{1,0:T(8,128)S(1)} %collective-permute-done.2.refs_3_, ...), custom_call_target="tpu_custom_call" | custom-call | flops 905969664 | bytes 3244032 | tf_op jit(solution)/shard_map/pallas_call | solution.py:66
  22.3 0.9 %collective-permute-done.10 = f32[128,384]{1,0:T(8,128)S(1)} collective-permute-done((f32[128,384]{1,0:T(8,128)S(1)}, f32[128,384]{1,0:T(8,128)S(1)}, u32[]{:S(2)}, u32[]{:S(2)}) %collective-permute-start.10) | collective-permute-done | bytes 196640 | tf_op jit(solution)/shard_map/ppermute | solution.py:52
  23.3 1.5 %collective-permute-start.13 = (f32[128,384]{1,0:T(8,128)S(1)}, f32[128,384]{1,0:T(8,128)S(1)}, u32[]{:S(2)}, u32[]{:S(2)}) collective-permute-start(f32[128,384]{1,0:T(8,128)S(1)} %add.6.refs_0_), channel_id=1, source_target_pairs={{0,5},{1,2},{2,1},{3,6},{4,7},{5,0},{6,3},{7,4},{8,11},{9,12},{10,... | collective-permute-start | bytes 589832 | tf_op jit(solution)/shard_map/ppermute | solution.py:52
  24.8 0.6 %collective-permute-done.11 = f32[128,384]{1,0:T(8,128)S(1)} collective-permute-done((f32[128,384]{1,0:T(8,128)S(1)}, f32[128,384]{1,0:T(8,128)S(1)}, u32[]{:S(2)}, u32[]{:S(2)}) %collective-permute-start.11) | collective-permute-done | bytes 196640 | tf_op jit(solution)/shard_map/ppermute | solution.py:52
  25.4 1.4 %collective-permute-start.12 = (f32[128,384]{1,0:T(8,128)S(1)}, f32[128,384]{1,0:T(8,128)S(1)}, u32[]{:S(2)}, u32[]{:S(2)}) collective-permute-start(f32[128,384]{1,0:T(8,128)S(1)} %add.7.refs_2_), channel_id=1, source_target_pairs={{0,5},{1,2},{2,1},{3,6},{4,7},{5,0},{6,3},{7,4},{8,11},{9,12},{10,... | collective-permute-start | bytes 589832 | tf_op jit(solution)/shard_map/ppermute | solution.py:52
  26.8 1.6 %collective-permute-done.13.refs_3_ = f32[128,384]{1,0:T(8,128)S(1)} collective-permute-done((f32[128,384]{1,0:T(8,128)S(1)}, f32[128,384]{1,0:T(8,128)S(1)}, u32[]{:S(2)}, u32[]{:S(2)}) %collective-permute-start.13) | collective-permute-done | bytes 196640 | tf_op jit(solution)/shard_map/ppermute | solution.py:52
  28.4 2.1 %collective-permute-done.12.refs_1_ = f32[128,384]{1,0:T(8,128)S(1)} collective-permute-done((f32[128,384]{1,0:T(8,128)S(1)}, f32[128,384]{1,0:T(8,128)S(1)}, u32[]{:S(2)}, u32[]{:S(2)}) %collective-permute-start.12) | collective-permute-done | bytes 196640 | tf_op jit(solution)/shard_map/ppermute | solution.py:52
  30.5 0.9 %shard_map.56 = (f32[192,128]{1,0:T(8,128)S(1)}, f32[192,128]{1,0:T(8,128)S(1)}) custom-call(f32[128,384]{1,0:T(8,128)S(1)} %add.6.refs_0_, f32[128,384]{1,0:T(8,128)S(1)} %collective-permute-done.12.refs_1_, f32[128,384]{1,0:T(8,128)S(1)} %add.7.refs_2_, f32[128,384]{1,0:T(8,128)S(1)} %collective-permute-done.13.refs_3_, ...), custom_call_target="tpu_custom_call" | custom-call | tf_op jit(solution)/shard_map/pallas_call | solution.py:260
  31.5 1.5 %collective-permute-start.14 = (f32[192,128]{1,0:T(8,128)S(1)}, f32[192,128]{1,0:T(8,128)S(1)}, u32[]{:S(2)}, u32[]{:S(2)}) collective-permute-start(f32[192,128]{1,0:T(8,128)S(1)} %get-tuple-element.19), channel_id=1, source_target_pairs={{0,3},{1,4},{2,7},{3,0},{4,1},{5,6},{6,5},{7,2},{8,13},{9,10},{10,... | collective-permute-start | bytes 294920 | tf_op jit(solution)/shard_map/ppermute | solution.py:52
  33.0 2.6 %collective-permute-done.14.arrived_ref = f32[192,128]{1,0:T(8,128)S(1)} collective-permute-done((f32[192,128]{1,0:T(8,128)S(1)}, f32[192,128]{1,0:T(8,128)S(1)}, u32[]{:S(2)}, u32[]{:S(2)}) %collective-permute-start.14) | collective-permute-done | bytes 98336 | tf_op jit(solution)/shard_map/ppermute | solution.py:52
  35.6 0.4 collective-permute-start.15
  36.0 0.9 %collective-permute-done.15.refs_1_ = f32[96,128]{1,0:T(8,128)S(1)} collective-permute-done((f32[96,128]{1,0:T(8,128)S(1)}, f32[96,128]{1,0:T(8,128)S(1)}, u32[]{:S(2)}, u32[]{:S(2)}) %collective-permute-start.15) | collective-permute-done | bytes 49184 | tf_op jit(solution)/shard_map/ppermute | solution.py:52
  36.9 2.9 %collective-permute-start.18 = (f32[96,128]{1,0:T(8,128)S(1)}, f32[96,128]{1,0:T(8,128)S(1)}, u32[]{:S(2)}, u32[]{:S(2)}) collective-permute-start(f32[96,128]{1,0:T(8,128)S(1)} %shard_map.58.refs_0_), channel_id=1, source_target_pairs={{0,24},{1,25},{2,26},{3,27},{4,28},{5,29},{6,30},{7,31},{8,16},{9,... | collective-permute-start | bytes 147464 | tf_op jit(solution)/shard_map/ppermute | solution.py:52
  39.8 1.0 %collective-permute-start.17 = (f32[96,128]{1,0:T(8,128)S(1)}, f32[96,128]{1,0:T(8,128)S(1)}, u32[]{:S(2)}, u32[]{:S(2)}) collective-permute-start(f32[96,128]{1,0:T(8,128)S(1)} %shard_map.58.refs_0_), channel_id=1, source_target_pairs={{0,17},{1,16},{2,19},{3,18},{4,21},{5,20},{6,23},{7,22},{8,25},{9,... | collective-permute-start | bytes 147464 | tf_op jit(solution)/shard_map/ppermute | solution.py:52
  40.8 0.3 collective-permute-start.16
  41.1 1.8 %collective-permute-done.18.refs_3_ = f32[96,128]{1,0:T(8,128)S(1)} collective-permute-done((f32[96,128]{1,0:T(8,128)S(1)}, f32[96,128]{1,0:T(8,128)S(1)}, u32[]{:S(2)}, u32[]{:S(2)}) %collective-permute-start.18) | collective-permute-done | bytes 49184 | tf_op jit(solution)/shard_map/ppermute | solution.py:52
  42.9 1.8 %collective-permute-done.17.refs_2_ = f32[96,128]{1,0:T(8,128)S(1)} collective-permute-done((f32[96,128]{1,0:T(8,128)S(1)}, f32[96,128]{1,0:T(8,128)S(1)}, u32[]{:S(2)}, u32[]{:S(2)}) %collective-permute-start.17) | collective-permute-done | bytes 49184 | tf_op jit(solution)/shard_map/ppermute | solution.py:52
  44.7 1.0 %collective-permute-done.16.refs_1_ = f32[96,128]{1,0:T(8,128)S(1)} collective-permute-done((f32[96,128]{1,0:T(8,128)S(1)}, f32[96,128]{1,0:T(8,128)S(1)}, u32[]{:S(2)}, u32[]{:S(2)}) %collective-permute-start.16) | collective-permute-done | bytes 49184 | tf_op jit(solution)/shard_map/ppermute | solution.py:52
  45.7 2.4 %collective-permute-start.21 = (f32[96,128]{1,0:T(8,128)S(1)}, f32[96,128]{1,0:T(8,128)S(1)}, u32[]{:S(2)}, u32[]{:S(2)}) collective-permute-start(f32[96,128]{1,0:T(8,128)S(1)} %shard_map.59.refs_0_), channel_id=1, source_target_pairs={{0,6},{1,7},{2,4},{3,5},{4,2},{5,3},{6,0},{7,1},{8,14},{9,15},{10,... | collective-permute-start | bytes 147464 | tf_op jit(solution)/shard_map/ppermute | solution.py:52
  48.2 0.0 collective-permute-start.20
  48.2 0.9 %collective-permute-start.19 = (f32[96,128]{1,0:T(8,128)S(1)}, f32[96,128]{1,0:T(8,128)S(1)}, u32[]{:S(2)}, u32[]{:S(2)}) collective-permute-start(f32[96,128]{1,0:T(8,128)S(1)} %shard_map.59.refs_0_), channel_id=1, source_target_pairs={{0,3},{1,4},{2,7},{3,0},{4,1},{5,6},{6,5},{7,2},{8,13},{9,10},{10,... | collective-permute-start | bytes 147464 | tf_op jit(solution)/shard_map/ppermute | solution.py:52
  49.0 1.8 %collective-permute-done.21.refs_3_ = f32[96,128]{1,0:T(8,128)S(1)} collective-permute-done((f32[96,128]{1,0:T(8,128)S(1)}, f32[96,128]{1,0:T(8,128)S(1)}, u32[]{:S(2)}, u32[]{:S(2)}) %collective-permute-start.21) | collective-permute-done | bytes 49184 | tf_op jit(solution)/shard_map/ppermute | solution.py:52
  50.8 0.9 %collective-permute-done.20.refs_2_ = f32[96,128]{1,0:T(8,128)S(1)} collective-permute-done((f32[96,128]{1,0:T(8,128)S(1)}, f32[96,128]{1,0:T(8,128)S(1)}, u32[]{:S(2)}, u32[]{:S(2)}) %collective-permute-start.20) | collective-permute-done | bytes 49184 | tf_op jit(solution)/shard_map/ppermute | solution.py:52
  51.7 0.5 collective-permute-done.19.refs_1_
  52.2 0.2 collective-permute-start.22
  52.4 1.3 %collective-permute-done.22.other_ref = f32[384,128]{1,0:T(8,128)S(1)} collective-permute-done((f32[384,128]{1,0:T(8,128)S(1)}, f32[384,128]{1,0:T(8,128)S(1)}, u32[]{:S(2)}, u32[]{:S(2)}) %collective-permute-start.22) | collective-permute-done | bytes 196640 | tf_op jit(solution)/shard_map/ppermute | solution.py:52
  53.7 1.2 %shard_map.61 = (f32[384,384]{1,0:T(8,128)}, f32[64,384]{1,0:T(8,128)}) custom-call(f32[384,128]{1,0:T(8,128)S(1)} %shard_map.60.keep_ref, f32[384,128]{1,0:T(8,128)S(1)} %collective-permute-done.22.other_ref, f32[64,384]{1,0:T(8,128)S(1)} %get-tuple-element.12.value_ref.refs_1_.points_ref), custom_call_target="tpu_custom_call" | custom-call | tf_op jit(solution)/shard_map/pallas_call | solution.py:349
  (7 shorter events, 0.1 us)
Async XLA Ops:
  1.6 5.7 %collective-permute-start = (f32[72,384]{1,0:T(8,128)S(1)}, f32[72,384]{1,0:T(8,128)S(1)}, u32[]{:S(2)}, u32[]{:S(2)}) collective-permute-start(f32[72,384]{1,0:T(8,128)S(1)} %get-tuple-element.13.refs_2_), channel_id=1, source_target_pairs={{0,1},{1,0},{2,3},{3,2},{4,5},{5,4},{6,7},{7,6},{8,9},{9,8},{10,11... | collective-permute-start | bytes 331784 | tf_op jit(solution)/shard_map/ppermute | solution.py:52
  2.1 9.5 %collective-permute-start.4 = (f32[72,384]{1,0:T(8,128)S(1)}, f32[72,384]{1,0:T(8,128)S(1)}, u32[]{:S(2)}, u32[]{:S(2)}) collective-permute-start(f32[72,384]{1,0:T(8,128)S(1)} %get-tuple-element.13.refs_2_), channel_id=1, source_target_pairs={{0,17},{1,16},{2,19},{3,18},{4,21},{5,20},{6,23},{7,22},{8,25},{9,... | collective-permute-start | bytes 331784 | tf_op jit(solution)/shard_map/ppermute | solution.py:52
  5.8 7.9 %collective-permute-start.3 = (f32[72,384]{1,0:T(8,128)S(1)}, f32[72,384]{1,0:T(8,128)S(1)}, u32[]{:S(2)}, u32[]{:S(2)}) collective-permute-start(f32[72,384]{1,0:T(8,128)S(1)} %get-tuple-element.13.refs_2_), channel_id=1, source_target_pairs={{0,9},{1,8},{2,11},{3,10},{4,13},{5,12},{6,15},{7,14},{8,1},{9,0},... | collective-permute-start | bytes 331784 | tf_op jit(solution)/shard_map/ppermute | solution.py:52
  7.0 8.3 %collective-permute-start.2 = (f32[72,384]{1,0:T(8,128)S(1)}, f32[72,384]{1,0:T(8,128)S(1)}, u32[]{:S(2)}, u32[]{:S(2)}) collective-permute-start(f32[72,384]{1,0:T(8,128)S(1)} %get-tuple-element.13.refs_2_), channel_id=1, source_target_pairs={{0,24},{1,25},{2,26},{3,27},{4,28},{5,29},{6,30},{7,31},{8,16},{9,... | collective-permute-start | bytes 331784 | tf_op jit(solution)/shard_map/ppermute | solution.py:52
  7.3 8.1 %collective-permute-start.9 = (f32[64,384]{1,0:T(8,128)S(1)}, f32[64,384]{1,0:T(8,128)S(1)}, u32[]{:S(2)}, u32[]{:S(2)}) collective-permute-start(f32[64,384]{1,0:T(8,128)S(1)} %shard_map.51), channel_id=1, source_target_pairs={{0,6},{1,7},{2,4},{3,5},{4,2},{5,3},{6,0},{7,1},{8,14},{9,15},{10,... | collective-permute-start | bytes 294920 | tf_op jit(solution)/shard_map/ppermute | solution.py:52
  10.9 5.0 %collective-permute-start.8 = (f32[64,384]{1,0:T(8,128)S(1)}, f32[64,384]{1,0:T(8,128)S(1)}, u32[]{:S(2)}, u32[]{:S(2)}) collective-permute-start(f32[64,384]{1,0:T(8,128)S(1)} %shard_map.51), channel_id=1, source_target_pairs={{0,3},{1,4},{2,7},{3,0},{4,1},{5,6},{6,5},{7,2},{8,13},{9,10},{10,... | collective-permute-start | bytes 294920 | tf_op jit(solution)/shard_map/ppermute | solution.py:52
  11.6 7.7 %collective-permute-start.1 = (f32[64,384]{1,0:T(8,128)S(1)}, f32[64,384]{1,0:T(8,128)S(1)}, u32[]{:S(2)}, u32[]{:S(2)}) collective-permute-start(f32[64,384]{1,0:T(8,128)S(1)} %shard_map.51), channel_id=1, source_target_pairs={{0,5},{1,2},{2,1},{3,6},{4,7},{5,0},{6,3},{7,4},{8,11},{9,12},{10,... | collective-permute-start | bytes 294920 | tf_op jit(solution)/shard_map/ppermute | solution.py:52
  13.7 2.3 %collective-permute-start.5 = (f32[72,384]{1,0:T(8,128)S(1)}, f32[72,384]{1,0:T(8,128)S(1)}, u32[]{:S(2)}, u32[]{:S(2)}) collective-permute-start(f32[72,384]{1,0:T(8,128)S(1)} %collective-permute-done.4.refs_5_), channel_id=1, source_target_pairs={{0,1},{1,0},{2,3},{3,2},{4,5},{5,4},{6,7},{7,6},{8,9},{9,8},{10,11... | collective-permute-start | bytes 331784 | tf_op jit(solution)/shard_map/ppermute | solution.py:52
  15.3 2.1 %collective-permute-start.7 = (f32[72,384]{1,0:T(8,128)S(1)}, f32[72,384]{1,0:T(8,128)S(1)}, u32[]{:S(2)}, u32[]{:S(2)}) collective-permute-start(f32[72,384]{1,0:T(8,128)S(1)} %collective-permute-done.3.refs_4_), channel_id=1, source_target_pairs={{0,1},{1,0},{2,3},{3,2},{4,5},{5,4},{6,7},{7,6},{8,9},{9,8},{10,11... | collective-permute-start | bytes 331784 | tf_op jit(solution)/shard_map/ppermute | solution.py:52
  15.3 2.1 %collective-permute-start.6 = (f32[72,384]{1,0:T(8,128)S(1)}, f32[72,384]{1,0:T(8,128)S(1)}, u32[]{:S(2)}, u32[]{:S(2)}) collective-permute-start(f32[72,384]{1,0:T(8,128)S(1)} %collective-permute-done.2.refs_3_), channel_id=1, source_target_pairs={{0,1},{1,0},{2,3},{3,2},{4,5},{5,4},{6,7},{7,6},{8,9},{9,8},{10,11... | collective-permute-start | bytes 331784 | tf_op jit(solution)/shard_map/ppermute | solution.py:52
  18.1 5.2 %collective-permute-start.10 = (f32[128,384]{1,0:T(8,128)S(1)}, f32[128,384]{1,0:T(8,128)S(1)}, u32[]{:S(2)}, u32[]{:S(2)}) collective-permute-start(f32[128,384]{1,0:T(8,128)S(1)} %shard_map.54), channel_id=1, source_target_pairs={{0,3},{1,4},{2,7},{3,0},{4,1},{5,6},{6,5},{7,2},{8,13},{9,10},{10,... | collective-permute-start | bytes 589832 | tf_op jit(solution)/shard_map/ppermute | solution.py:52
  19.9 5.4 %collective-permute-start.11 = (f32[128,384]{1,0:T(8,128)S(1)}, f32[128,384]{1,0:T(8,128)S(1)}, u32[]{:S(2)}, u32[]{:S(2)}) collective-permute-start(f32[128,384]{1,0:T(8,128)S(1)} %shard_map.55), channel_id=1, source_target_pairs={{0,3},{1,4},{2,7},{3,0},{4,1},{5,6},{6,5},{7,2},{8,13},{9,10},{10,... | collective-permute-start | bytes 589832 | tf_op jit(solution)/shard_map/ppermute | solution.py:52
  23.3 5.2 %collective-permute-start.13 = (f32[128,384]{1,0:T(8,128)S(1)}, f32[128,384]{1,0:T(8,128)S(1)}, u32[]{:S(2)}, u32[]{:S(2)}) collective-permute-start(f32[128,384]{1,0:T(8,128)S(1)} %add.6.refs_0_), channel_id=1, source_target_pairs={{0,5},{1,2},{2,1},{3,6},{4,7},{5,0},{6,3},{7,4},{8,11},{9,12},{10,... | collective-permute-start | bytes 589832 | tf_op jit(solution)/shard_map/ppermute | solution.py:52
  25.4 5.2 %collective-permute-start.12 = (f32[128,384]{1,0:T(8,128)S(1)}, f32[128,384]{1,0:T(8,128)S(1)}, u32[]{:S(2)}, u32[]{:S(2)}) collective-permute-start(f32[128,384]{1,0:T(8,128)S(1)} %add.7.refs_2_), channel_id=1, source_target_pairs={{0,5},{1,2},{2,1},{3,6},{4,7},{5,0},{6,3},{7,4},{8,11},{9,12},{10,... | collective-permute-start | bytes 589832 | tf_op jit(solution)/shard_map/ppermute | solution.py:52
  31.5 4.1 %collective-permute-start.14 = (f32[192,128]{1,0:T(8,128)S(1)}, f32[192,128]{1,0:T(8,128)S(1)}, u32[]{:S(2)}, u32[]{:S(2)}) collective-permute-start(f32[192,128]{1,0:T(8,128)S(1)} %get-tuple-element.19), channel_id=1, source_target_pairs={{0,3},{1,4},{2,7},{3,0},{4,1},{5,6},{6,5},{7,2},{8,13},{9,10},{10,... | collective-permute-start | bytes 294920 | tf_op jit(solution)/shard_map/ppermute | solution.py:52
  35.6 1.3 %collective-permute-start.15 = (f32[96,128]{1,0:T(8,128)S(1)}, f32[96,128]{1,0:T(8,128)S(1)}, u32[]{:S(2)}, u32[]{:S(2)}) collective-permute-start(f32[96,128]{1,0:T(8,128)S(1)} %get-tuple-element.21), channel_id=1, source_target_pairs={{0,1},{1,0},{2,3},{3,2},{4,5},{5,4},{6,7},{7,6},{8,9},{9,8},{10,11... | collective-permute-start | bytes 147464 | tf_op jit(solution)/shard_map/ppermute | solution.py:52
  36.9 6.0 %collective-permute-start.18 = (f32[96,128]{1,0:T(8,128)S(1)}, f32[96,128]{1,0:T(8,128)S(1)}, u32[]{:S(2)}, u32[]{:S(2)}) collective-permute-start(f32[96,128]{1,0:T(8,128)S(1)} %shard_map.58.refs_0_), channel_id=1, source_target_pairs={{0,24},{1,25},{2,26},{3,27},{4,28},{5,29},{6,30},{7,31},{8,16},{9,... | collective-permute-start | bytes 147464 | tf_op jit(solution)/shard_map/ppermute | solution.py:52
  39.8 4.9 %collective-permute-start.17 = (f32[96,128]{1,0:T(8,128)S(1)}, f32[96,128]{1,0:T(8,128)S(1)}, u32[]{:S(2)}, u32[]{:S(2)}) collective-permute-start(f32[96,128]{1,0:T(8,128)S(1)} %shard_map.58.refs_0_), channel_id=1, source_target_pairs={{0,17},{1,16},{2,19},{3,18},{4,21},{5,20},{6,23},{7,22},{8,25},{9,... | collective-permute-start | bytes 147464 | tf_op jit(solution)/shard_map/ppermute | solution.py:52
  40.8 4.9 %collective-permute-start.16 = (f32[96,128]{1,0:T(8,128)S(1)}, f32[96,128]{1,0:T(8,128)S(1)}, u32[]{:S(2)}, u32[]{:S(2)}) collective-permute-start(f32[96,128]{1,0:T(8,128)S(1)} %shard_map.58.refs_0_), channel_id=1, source_target_pairs={{0,9},{1,8},{2,11},{3,10},{4,13},{5,12},{6,15},{7,14},{8,1},{9,0},... | collective-permute-start | bytes 147464 | tf_op jit(solution)/shard_map/ppermute | solution.py:52
  45.7 5.1 %collective-permute-start.21 = (f32[96,128]{1,0:T(8,128)S(1)}, f32[96,128]{1,0:T(8,128)S(1)}, u32[]{:S(2)}, u32[]{:S(2)}) collective-permute-start(f32[96,128]{1,0:T(8,128)S(1)} %shard_map.59.refs_0_), channel_id=1, source_target_pairs={{0,6},{1,7},{2,4},{3,5},{4,2},{5,3},{6,0},{7,1},{8,14},{9,15},{10,... | collective-permute-start | bytes 147464 | tf_op jit(solution)/shard_map/ppermute | solution.py:52
  48.2 3.5 %collective-permute-start.20 = (f32[96,128]{1,0:T(8,128)S(1)}, f32[96,128]{1,0:T(8,128)S(1)}, u32[]{:S(2)}, u32[]{:S(2)}) collective-permute-start(f32[96,128]{1,0:T(8,128)S(1)} %shard_map.59.refs_0_), channel_id=1, source_target_pairs={{0,5},{1,2},{2,1},{3,6},{4,7},{5,0},{6,3},{7,4},{8,11},{9,12},{10,... | collective-permute-start | bytes 147464 | tf_op jit(solution)/shard_map/ppermute | solution.py:52
  48.2 4.0 %collective-permute-start.19 = (f32[96,128]{1,0:T(8,128)S(1)}, f32[96,128]{1,0:T(8,128)S(1)}, u32[]{:S(2)}, u32[]{:S(2)}) collective-permute-start(f32[96,128]{1,0:T(8,128)S(1)} %shard_map.59.refs_0_), channel_id=1, source_target_pairs={{0,3},{1,4},{2,7},{3,0},{4,1},{5,6},{6,5},{7,2},{8,13},{9,10},{10,... | collective-permute-start | bytes 147464 | tf_op jit(solution)/shard_map/ppermute | solution.py:52
  52.2 1.5 %collective-permute-start.22 = (f32[384,128]{1,0:T(8,128)S(1)}, f32[384,128]{1,0:T(8,128)S(1)}, u32[]{:S(2)}, u32[]{:S(2)}) collective-permute-start(f32[384,128]{1,0:T(8,128)S(1)} %shard_map.60.keep_ref), channel_id=1, source_target_pairs={{0,1},{1,0},{2,3},{3,2},{4,5},{5,4},{6,7},{7,6},{8,9},{9,8},{10,11... | collective-permute-start | bytes 589832 | tf_op jit(solution)/shard_map/ppermute | solution.py:52

commit v11 on v10

--- a/solution.py
+++ b/solution.py
@@ -394,9 +394,9 @@
         source = copy_after(points, first[0])
         queries = [hop(source, (bit_a | bit_b, 0)), to_a(source), to_b(source), points]
         total, mapped = early_sums(queries[:2], near + first, metric3, outs_n)
-        (part_ab,) = late_sums(queries[:1], 0, total, mapped, metric3, late, outs_n, queries[2:3])
+        (part_ab,) = late_sums(queries[:1], 0, total, mapped, metric3, late, outs_n)
         sent_ab = to_a(part_ab)
-        (part_a,) = late_sums(queries[1:2], 1, total, mapped, metric3, late, outs_n)
+        (part_a,) = late_sums(queries[1:2], 1, total, mapped, metric3, late, outs_n, queries[2:3])
         sent_a = to_a(part_a)
         part_b, part_own = whole_sums(queries[2:], near + first + late, metric3, outs_n)
         half_b = part_b + sent_ab

time: 55.1 us -> 55.1 us (level)
  no operation moved by 1% of the time
where the time goes in v11:
time: 55.1 us; the launch traced here: 55 us
  starting transfers between devices  25.2 us (46%)
  waiting for transfers between devices  20.1 us (36%)
  Pallas kernels  7.59 us (14%)
  other arithmetic  1.27 us (2%)
  between operations  0.76 us (1%)
    ppermute x23, starting transfers between devices, hop(): return lax.ppermute(value, AXES, pairs)  25.2 us
    ppermute x23, waiting for transfers between devices, hop(): return lax.ppermute(value, AXES, pairs)  20.1 us
    pallas_call x9, Pallas kernels, call(): pl.pallas_call(body, out_shape=out_shape, in_specs=[pl.BlockSpec(memory_s...  4.52 us
    pallas_call x1, Pallas kernels, finish(): pl.pallas_call(body, out_shape=(shape(width, width), shape(rows, width)),...  1.22 us
    convert_element_type x1, other arithmetic, metric_halves(): low = (metric - high).astype(BF16)  1.14 us
  transfers between devices with their start and end apart: 23, of which 15 were waited for; matrix products, arithmetic and copies ran while one was open for 2% of the time, Pallas kernels for 8%

profile of v11, /device:TPU:0, one launch (start us, length us, event | category | flops | bytes accessed | tf_op | source)
XLA Modules:
  0.0 55.0 jit_solution(15588967451029116979)
XLA Ops:
  0.6 0.9 %shard_map.50 = (f32[64,384]{1,0:T(8,128)S(1)}, f32[72,384]{1,0:T(8,128)S(1)}) custom-call(f32[64,384]{1,0:T(8,128)} %points_ref.1, f32[2,64]{1,0:T(2,128)} %bitcast.1), custom_call_target="tpu_custom_call" | custom-call | tf_op jit(solution)/shard_map/pallas_call | solution.py:99
  1.6 0.5 collective-permute-start
  2.1 3.7 %collective-permute-start.4 = (f32[72,384]{1,0:T(8,128)S(1)}, f32[72,384]{1,0:T(8,128)S(1)}, u32[]{:S(2)}, u32[]{:S(2)}) collective-permute-start(f32[72,384]{1,0:T(8,128)S(1)} %get-tuple-element.13.refs_2_), channel_id=1, source_target_pairs={{0,17},{1,16},{2,19},{3,18},{4,21},{5,20},{6,23},{7,22},{8,25},{9,... | collective-permute-start | bytes 331784 | tf_op jit(solution)/shard_map/ppermute | solution.py:52
  5.8 1.2 %collective-permute-start.3 = (f32[72,384]{1,0:T(8,128)S(1)}, f32[72,384]{1,0:T(8,128)S(1)}, u32[]{:S(2)}, u32[]{:S(2)}) collective-permute-start(f32[72,384]{1,0:T(8,128)S(1)} %get-tuple-element.13.refs_2_), channel_id=1, source_target_pairs={{0,9},{1,8},{2,11},{3,10},{4,13},{5,12},{6,15},{7,14},{8,1},{9,0},... | collective-permute-start | bytes 331784 | tf_op jit(solution)/shard_map/ppermute | solution.py:52
  7.0 0.2 collective-permute-start.2
  7.2 0.0 collective-permute-done.wanted_ref.refs_6_
  7.3 2.5 %collective-permute-start.9 = (f32[64,384]{1,0:T(8,128)S(1)}, f32[64,384]{1,0:T(8,128)S(1)}, u32[]{:S(2)}, u32[]{:S(2)}) collective-permute-start(f32[64,384]{1,0:T(8,128)S(1)} %shard_map.51), channel_id=1, source_target_pairs={{0,6},{1,7},{2,4},{3,5},{4,2},{5,3},{6,0},{7,1},{8,14},{9,15},{10,... | collective-permute-start | bytes 294920 | tf_op jit(solution)/shard_map/ppermute | solution.py:52
  9.8 1.1 %fusion = (bf16[384,384]{1,0:T(8,128)(2,1)S(1)}, bf16[384,384]{1,0:T(8,128)(2,1)S(1)}) fusion(f32[384,384]{1,0:T(8,128)} %param.5), kind=kLoop, calls=%fused_computation.3 | loop fusion | flops 589824 | bytes 1179648 | tf_op jit(solution)/shard_map/convert_element_type | solution.py:117
  10.9 0.2 collective-permute-start.8
  11.1 0.5 collective-permute-done.4.refs_5_
  11.6 2.1 %collective-permute-start.1 = (f32[64,384]{1,0:T(8,128)S(1)}, f32[64,384]{1,0:T(8,128)S(1)}, u32[]{:S(2)}, u32[]{:S(2)}) collective-permute-start(f32[64,384]{1,0:T(8,128)S(1)} %shard_map.51), channel_id=1, source_target_pairs={{0,5},{1,2},{2,1},{3,6},{4,7},{5,0},{6,3},{7,4},{8,11},{9,12},{10,... | collective-permute-start | bytes 294920 | tf_op jit(solution)/shard_map/ppermute | solution.py:52
  13.7 0.0 collective-permute-done.3.refs_4_
  13.7 0.0 collective-permute-start.5
  13.7 1.6 %collective-permute-done.2.refs_3_ = f32[72,384]{1,0:T(8,128)S(1)} collective-permute-done((f32[72,384]{1,0:T(8,128)S(1)}, f32[72,384]{1,0:T(8,128)S(1)}, u32[]{:S(2)}, u32[]{:S(2)}) %collective-permute-start.2) | collective-permute-done | bytes 110624 | tf_op jit(solution)/shard_map/ppermute | solution.py:52
  15.3 0.0 collective-permute-start.7
  15.3 0.0 collective-permute-done.9.refs_0_
  15.3 0.5 collective-permute-start.6
  15.8 0.1 pad_maximum_fusion.refs_10_.refs_8_.refs_5_.refs_4_
  15.9 0.0 collective-permute-done.8.refs_1_.refs_0_
  15.9 0.0 collective-permute-done.5.refs_7_
  15.9 1.5 %shard_map.53 = (f32[2,128,384]{2,1,0:T(8,128)S(1)}, f32[128,384]{1,0:T(8,128)S(1)}) custom-call(f32[64,384]{1,0:T(8,128)S(1)} %collective-permute-done.9.refs_0_, f32[64,384]{1,0:T(8,128)S(1)} %collective-permute-done.8.refs_1_.refs_0_, f32[72,384]{1,0:T(8,128)S(1)} %get-tuple-element.13.refs_2_, f32[72,384]{1,0:T(8,128)S(1)} %collective-permute-done.2.refs_3_, ...), custom_call_target="tpu_custom_call" | custom-call | flops 707788800 | bytes 3219456 | tf_op jit(solution)/shard_map/pallas_call | solution.py:66
  17.4 0.0 collective-permute-done.7.refs_9_.refs_2_
  17.4 0.0 collective-permute-done.6.refs_8_.refs_1_
  17.4 0.7 %shard_map.55 = f32[128,384]{1,0:T(8,128)S(1)} custom-call(f32[64,384]{1,0:T(8,128)S(1)} %collective-permute-done.9.refs_0_, f32[72,384]{1,0:T(8,128)S(1)} %collective-permute-done.6.refs_8_.refs_1_, f32[72,384]{1,0:T(8,128)S(1)} %collective-permute-done.7.refs_9_.refs_2_, f32[2,128,384]{2,1,0:T(8,128)S(1)} %get-tuple-element.15.refs_3_, ...), custom_call_target="tpu_custom_call" | custom-call | flops 162791424 | bytes 2875392 | tf_op jit(solution)/shard_map/pallas_call | solution.py:66
  18.1 1.2 %collective-permute-start.11 = (f32[128,384]{1,0:T(8,128)S(1)}, f32[128,384]{1,0:T(8,128)S(1)}, u32[]{:S(2)}, u32[]{:S(2)}) collective-permute-start(f32[128,384]{1,0:T(8,128)S(1)} %shard_map.55), channel_id=1, source_target_pairs={{0,3},{1,4},{2,7},{3,0},{4,1},{5,6},{6,5},{7,2},{8,13},{9,10},{10,... | collective-permute-start | bytes 589832 | tf_op jit(solution)/shard_map/ppermute | solution.py:52
  19.3 0.0 collective-permute-done.1.refs_0_.refs_6_
  19.3 0.7 %shard_map.54 = f32[128,384]{1,0:T(8,128)S(1)} custom-call(f32[64,384]{1,0:T(8,128)S(1)} %collective-permute-done.8.refs_1_.refs_0_, f32[72,384]{1,0:T(8,128)S(1)} %collective-permute-done.6.refs_8_.refs_1_, f32[72,384]{1,0:T(8,128)S(1)} %collective-permute-done.7.refs_9_.refs_2_, f32[2,128,384]{2,1,0:T(8,128)S(1)} %get-tuple-element.15.refs_3_, ...), custom_call_target="tpu_custom_call" | custom-call | flops 162791424 | bytes 2973696 | tf_op jit(solution)/shard_map/pallas_call | solution.py:66
  19.9 0.7 %collective-permute-start.10 = (f32[128,384]{1,0:T(8,128)S(1)}, f32[128,384]{1,0:T(8,128)S(1)}, u32[]{:S(2)}, u32[]{:S(2)}) collective-permute-start(f32[128,384]{1,0:T(8,128)S(1)} %shard_map.54), channel_id=1, source_target_pairs={{0,3},{1,4},{2,7},{3,0},{4,1},{5,6},{6,5},{7,2},{8,13},{9,10},{10,... | collective-permute-start | bytes 589832 | tf_op jit(solution)/shard_map/ppermute | solution.py:52
  20.7 1.7 %shard_map.52 = (f32[128,384]{1,0:T(8,128)S(1)}, f32[128,384]{1,0:T(8,128)S(1)}) custom-call(f32[64,384]{1,0:T(8,128)S(1)} %collective-permute-done.1.refs_0_.refs_6_, f32[64,384]{1,0:T(8,128)S(1)} %get-tuple-element.12.value_ref.refs_1_.points_ref, f32[72,384]{1,0:T(8,128)S(1)} %get-tuple-element.13.refs_2_, f32[72,384]{1,0:T(8,128)S(1)} %collective-permute-done.2.refs_3_, ...), custom_call_target="tpu_custom_call" | custom-call | flops 905969664 | bytes 3244032 | tf_op jit(solution)/shard_map/pallas_call | solution.py:66
  22.3 0.9 %collective-permute-done.11 = f32[128,384]{1,0:T(8,128)S(1)} collective-permute-done((f32[128,384]{1,0:T(8,128)S(1)}, f32[128,384]{1,0:T(8,128)S(1)}, u32[]{:S(2)}, u32[]{:S(2)}) %collective-permute-start.11) | collective-permute-done | bytes 196640 | tf_op jit(solution)/shard_map/ppermute | solution.py:52
  23.3 1.5 %collective-permute-start.12 = (f32[128,384]{1,0:T(8,128)S(1)}, f32[128,384]{1,0:T(8,128)S(1)}, u32[]{:S(2)}, u32[]{:S(2)}) collective-permute-start(f32[128,384]{1,0:T(8,128)S(1)} %add.7.refs_2_), channel_id=1, source_target_pairs={{0,5},{1,2},{2,1},{3,6},{4,7},{5,0},{6,3},{7,4},{8,11},{9,12},{10,... | collective-permute-start | bytes 589832 | tf_op jit(solution)/shard_map/ppermute | solution.py:52
  24.8 0.6 %collective-permute-done.10 = f32[128,384]{1,0:T(8,128)S(1)} collective-permute-done((f32[128,384]{1,0:T(8,128)S(1)}, f32[128,384]{1,0:T(8,128)S(1)}, u32[]{:S(2)}, u32[]{:S(2)}) %collective-permute-start.10) | collective-permute-done | bytes 196640 | tf_op jit(solution)/shard_map/ppermute | solution.py:52
  25.4 1.4 %collective-permute-start.13 = (f32[128,384]{1,0:T(8,128)S(1)}, f32[128,384]{1,0:T(8,128)S(1)}, u32[]{:S(2)}, u32[]{:S(2)}) collective-permute-start(f32[128,384]{1,0:T(8,128)S(1)} %add.6.refs_0_), channel_id=1, source_target_pairs={{0,5},{1,2},{2,1},{3,6},{4,7},{5,0},{6,3},{7,4},{8,11},{9,12},{10,... | collective-permute-start | bytes 589832 | tf_op jit(solution)/shard_map/ppermute | solution.py:52
  26.8 1.6 %collective-permute-done.12.refs_1_ = f32[128,384]{1,0:T(8,128)S(1)} collective-permute-done((f32[128,384]{1,0:T(8,128)S(1)}, f32[128,384]{1,0:T(8,128)S(1)}, u32[]{:S(2)}, u32[]{:S(2)}) %collective-permute-start.12) | collective-permute-done | bytes 196640 | tf_op jit(solution)/shard_map/ppermute | solution.py:52
  28.4 2.1 %collective-permute-done.13.refs_3_ = f32[128,384]{1,0:T(8,128)S(1)} collective-permute-done((f32[128,384]{1,0:T(8,128)S(1)}, f32[128,384]{1,0:T(8,128)S(1)}, u32[]{:S(2)}, u32[]{:S(2)}) %collective-permute-start.13) | collective-permute-done | bytes 196640 | tf_op jit(solution)/shard_map/ppermute | solution.py:52
  30.6 0.9 %shard_map.56 = (f32[192,128]{1,0:T(8,128)S(1)}, f32[192,128]{1,0:T(8,128)S(1)}) custom-call(f32[128,384]{1,0:T(8,128)S(1)} %add.6.refs_0_, f32[128,384]{1,0:T(8,128)S(1)} %collective-permute-done.12.refs_1_, f32[128,384]{1,0:T(8,128)S(1)} %add.7.refs_2_, f32[128,384]{1,0:T(8,128)S(1)} %collective-permute-done.13.refs_3_, ...), custom_call_target="tpu_custom_call" | custom-call | tf_op jit(solution)/shard_map/pallas_call | solution.py:260
  31.5 1.5 %collective-permute-start.14 = (f32[192,128]{1,0:T(8,128)S(1)}, f32[192,128]{1,0:T(8,128)S(1)}, u32[]{:S(2)}, u32[]{:S(2)}) collective-permute-start(f32[192,128]{1,0:T(8,128)S(1)} %get-tuple-element.19), channel_id=1, source_target_pairs={{0,3},{1,4},{2,7},{3,0},{4,1},{5,6},{6,5},{7,2},{8,13},{9,10},{10,... | collective-permute-start | bytes 294920 | tf_op jit(solution)/shard_map/ppermute | solution.py:52
  33.0 2.6 %collective-permute-done.14.arrived_ref = f32[192,128]{1,0:T(8,128)S(1)} collective-permute-done((f32[192,128]{1,0:T(8,128)S(1)}, f32[192,128]{1,0:T(8,128)S(1)}, u32[]{:S(2)}, u32[]{:S(2)}) %collective-permute-start.14) | collective-permute-done | bytes 98336 | tf_op jit(solution)/shard_map/ppermute | solution.py:52
  35.6 0.4 collective-permute-start.15
  36.0 0.9 %collective-permute-done.15.refs_1_ = f32[96,128]{1,0:T(8,128)S(1)} collective-permute-done((f32[96,128]{1,0:T(8,128)S(1)}, f32[96,128]{1,0:T(8,128)S(1)}, u32[]{:S(2)}, u32[]{:S(2)}) %collective-permute-start.15) | collective-permute-done | bytes 49184 | tf_op jit(solution)/shard_map/ppermute | solution.py:52
  36.9 2.9 %collective-permute-start.18 = (f32[96,128]{1,0:T(8,128)S(1)}, f32[96,128]{1,0:T(8,128)S(1)}, u32[]{:S(2)}, u32[]{:S(2)}) collective-permute-start(f32[96,128]{1,0:T(8,128)S(1)} %shard_map.58.refs_0_), channel_id=1, source_target_pairs={{0,24},{1,25},{2,26},{3,27},{4,28},{5,29},{6,30},{7,31},{8,16},{9,... | collective-permute-start | bytes 147464 | tf_op jit(solution)/shard_map/ppermute | solution.py:52
  39.8 1.0 %collective-permute-start.17 = (f32[96,128]{1,0:T(8,128)S(1)}, f32[96,128]{1,0:T(8,128)S(1)}, u32[]{:S(2)}, u32[]{:S(2)}) collective-permute-start(f32[96,128]{1,0:T(8,128)S(1)} %shard_map.58.refs_0_), channel_id=1, source_target_pairs={{0,17},{1,16},{2,19},{3,18},{4,21},{5,20},{6,23},{7,22},{8,25},{9,... | collective-permute-start | bytes 147464 | tf_op jit(solution)/shard_map/ppermute | solution.py:52
  40.8 0.3 collective-permute-start.16
  41.1 1.8 %collective-permute-done.18.refs_3_ = f32[96,128]{1,0:T(8,128)S(1)} collective-permute-done((f32[96,128]{1,0:T(8,128)S(1)}, f32[96,128]{1,0:T(8,128)S(1)}, u32[]{:S(2)}, u32[]{:S(2)}) %collective-permute-start.18) | collective-permute-done | bytes 49184 | tf_op jit(solution)/shard_map/ppermute | solution.py:52
  42.9 1.8 %collective-permute-done.17.refs_2_ = f32[96,128]{1,0:T(8,128)S(1)} collective-permute-done((f32[96,128]{1,0:T(8,128)S(1)}, f32[96,128]{1,0:T(8,128)S(1)}, u32[]{:S(2)}, u32[]{:S(2)}) %collective-permute-start.17) | collective-permute-done | bytes 49184 | tf_op jit(solution)/shard_map/ppermute | solution.py:52
  44.7 1.0 %collective-permute-done.16.refs_1_ = f32[96,128]{1,0:T(8,128)S(1)} collective-permute-done((f32[96,128]{1,0:T(8,128)S(1)}, f32[96,128]{1,0:T(8,128)S(1)}, u32[]{:S(2)}, u32[]{:S(2)}) %collective-permute-start.16) | collective-permute-done | bytes 49184 | tf_op jit(solution)/shard_map/ppermute | solution.py:52
  45.7 2.4 %collective-permute-start.21 = (f32[96,128]{1,0:T(8,128)S(1)}, f32[96,128]{1,0:T(8,128)S(1)}, u32[]{:S(2)}, u32[]{:S(2)}) collective-permute-start(f32[96,128]{1,0:T(8,128)S(1)} %shard_map.59.refs_0_), channel_id=1, source_target_pairs={{0,6},{1,7},{2,4},{3,5},{4,2},{5,3},{6,0},{7,1},{8,14},{9,15},{10,... | collective-permute-start | bytes 147464 | tf_op jit(solution)/shard_map/ppermute | solution.py:52
  48.2 0.0 collective-permute-start.20
  48.2 0.8 %collective-permute-start.19 = (f32[96,128]{1,0:T(8,128)S(1)}, f32[96,128]{1,0:T(8,128)S(1)}, u32[]{:S(2)}, u32[]{:S(2)}) collective-permute-start(f32[96,128]{1,0:T(8,128)S(1)} %shard_map.59.refs_0_), channel_id=1, source_target_pairs={{0,3},{1,4},{2,7},{3,0},{4,1},{5,6},{6,5},{7,2},{8,13},{9,10},{10,... | collective-permute-start | bytes 147464 | tf_op jit(solution)/shard_map/ppermute | solution.py:52
  49.0 1.8 %collective-permute-done.21.refs_3_ = f32[96,128]{1,0:T(8,128)S(1)} collective-permute-done((f32[96,128]{1,0:T(8,128)S(1)}, f32[96,128]{1,0:T(8,128)S(1)}, u32[]{:S(2)}, u32[]{:S(2)}) %collective-permute-start.21) | collective-permute-done | bytes 49184 | tf_op jit(solution)/shard_map/ppermute | solution.py:52
  50.8 0.9 %collective-permute-done.20.refs_2_ = f32[96,128]{1,0:T(8,128)S(1)} collective-permute-done((f32[96,128]{1,0:T(8,128)S(1)}, f32[96,128]{1,0:T(8,128)S(1)}, u32[]{:S(2)}, u32[]{:S(2)}) %collective-permute-start.20) | collective-permute-done | bytes 49184 | tf_op jit(solution)/shard_map/ppermute | solution.py:52
  51.7 0.5 collective-permute-done.19.refs_1_
  52.2 0.2 collective-permute-start.22
  52.4 1.3 %collective-permute-done.22.other_ref = f32[384,128]{1,0:T(8,128)S(1)} collective-permute-done((f32[384,128]{1,0:T(8,128)S(1)}, f32[384,128]{1,0:T(8,128)S(1)}, u32[]{:S(2)}, u32[]{:S(2)}) %collective-permute-start.22) | collective-permute-done | bytes 196640 | tf_op jit(solution)/shard_map/ppermute | solution.py:52
  53.7 1.2 %shard_map.61 = (f32[384,384]{1,0:T(8,128)}, f32[64,384]{1,0:T(8,128)}) custom-call(f32[384,128]{1,0:T(8,128)S(1)} %shard_map.60.keep_ref, f32[384,128]{1,0:T(8,128)S(1)} %collective-permute-done.22.other_ref, f32[64,384]{1,0:T(8,128)S(1)} %get-tuple-element.12.value_ref.refs_1_.points_ref), custom_call_target="tpu_custom_call" | custom-call | tf_op jit(solution)/shard_map/pallas_call | solution.py:349
  (7 shorter events, 0.1 us)
Async XLA Ops:
  1.6 5.7 %collective-permute-start = (f32[72,384]{1,0:T(8,128)S(1)}, f32[72,384]{1,0:T(8,128)S(1)}, u32[]{:S(2)}, u32[]{:S(2)}) collective-permute-start(f32[72,384]{1,0:T(8,128)S(1)} %get-tuple-element.13.refs_2_), channel_id=1, source_target_pairs={{0,1},{1,0},{2,3},{3,2},{4,5},{5,4},{6,7},{7,6},{8,9},{9,8},{10,11... | collective-permute-start | bytes 331784 | tf_op jit(solution)/shard_map/ppermute | solution.py:52
  2.1 9.5 %collective-permute-start.4 = (f32[72,384]{1,0:T(8,128)S(1)}, f32[72,384]{1,0:T(8,128)S(1)}, u32[]{:S(2)}, u32[]{:S(2)}) collective-permute-start(f32[72,384]{1,0:T(8,128)S(1)} %get-tuple-element.13.refs_2_), channel_id=1, source_target_pairs={{0,17},{1,16},{2,19},{3,18},{4,21},{5,20},{6,23},{7,22},{8,25},{9,... | collective-permute-start | bytes 331784 | tf_op jit(solution)/shard_map/ppermute | solution.py:52
  5.8 7.9 %collective-permute-start.3 = (f32[72,384]{1,0:T(8,128)S(1)}, f32[72,384]{1,0:T(8,128)S(1)}, u32[]{:S(2)}, u32[]{:S(2)}) collective-permute-start(f32[72,384]{1,0:T(8,128)S(1)} %get-tuple-element.13.refs_2_), channel_id=1, source_target_pairs={{0,9},{1,8},{2,11},{3,10},{4,13},{5,12},{6,15},{7,14},{8,1},{9,0},... | collective-permute-start | bytes 331784 | tf_op jit(solution)/shard_map/ppermute | solution.py:52
  7.0 8.3 %collective-permute-start.2 = (f32[72,384]{1,0:T(8,128)S(1)}, f32[72,384]{1,0:T(8,128)S(1)}, u32[]{:S(2)}, u32[]{:S(2)}) collective-permute-start(f32[72,384]{1,0:T(8,128)S(1)} %get-tuple-element.13.refs_2_), channel_id=1, source_target_pairs={{0,24},{1,25},{2,26},{3,27},{4,28},{5,29},{6,30},{7,31},{8,16},{9,... | collective-permute-start | bytes 331784 | tf_op jit(solution)/shard_map/ppermute | solution.py:52
  7.3 8.1 %collective-permute-start.9 = (f32[64,384]{1,0:T(8,128)S(1)}, f32[64,384]{1,0:T(8,128)S(1)}, u32[]{:S(2)}, u32[]{:S(2)}) collective-permute-start(f32[64,384]{1,0:T(8,128)S(1)} %shard_map.51), channel_id=1, source_target_pairs={{0,6},{1,7},{2,4},{3,5},{4,2},{5,3},{6,0},{7,1},{8,14},{9,15},{10,... | collective-permute-start | bytes 294920 | tf_op jit(solution)/shard_map/ppermute | solution.py:52
  10.9 5.0 %collective-permute-start.8 = (f32[64,384]{1,0:T(8,128)S(1)}, f32[64,384]{1,0:T(8,128)S(1)}, u32[]{:S(2)}, u32[]{:S(2)}) collective-permute-start(f32[64,384]{1,0:T(8,128)S(1)} %shard_map.51), channel_id=1, source_target_pairs={{0,3},{1,4},{2,7},{3,0},{4,1},{5,6},{6,5},{7,2},{8,13},{9,10},{10,... | collective-permute-start | bytes 294920 | tf_op jit(solution)/shard_map/ppermute | solution.py:52
  11.6 7.7 %collective-permute-start.1 = (f32[64,384]{1,0:T(8,128)S(1)}, f32[64,384]{1,0:T(8,128)S(1)}, u32[]{:S(2)}, u32[]{:S(2)}) collective-permute-start(f32[64,384]{1,0:T(8,128)S(1)} %shard_map.51), channel_id=1, source_target_pairs={{0,5},{1,2},{2,1},{3,6},{4,7},{5,0},{6,3},{7,4},{8,11},{9,12},{10,... | collective-permute-start | bytes 294920 | tf_op jit(solution)/shard_map/ppermute | solution.py:52
  13.7 2.3 %collective-permute-start.5 = (f32[72,384]{1,0:T(8,128)S(1)}, f32[72,384]{1,0:T(8,128)S(1)}, u32[]{:S(2)}, u32[]{:S(2)}) collective-permute-start(f32[72,384]{1,0:T(8,128)S(1)} %collective-permute-done.4.refs_5_), channel_id=1, source_target_pairs={{0,1},{1,0},{2,3},{3,2},{4,5},{5,4},{6,7},{7,6},{8,9},{9,8},{10,11... | collective-permute-start | bytes 331784 | tf_op jit(solution)/shard_map/ppermute | solution.py:52
  15.3 2.1 %collective-permute-start.7 = (f32[72,384]{1,0:T(8,128)S(1)}, f32[72,384]{1,0:T(8,128)S(1)}, u32[]{:S(2)}, u32[]{:S(2)}) collective-permute-start(f32[72,384]{1,0:T(8,128)S(1)} %collective-permute-done.3.refs_4_), channel_id=1, source_target_pairs={{0,1},{1,0},{2,3},{3,2},{4,5},{5,4},{6,7},{7,6},{8,9},{9,8},{10,11... | collective-permute-start | bytes 331784 | tf_op jit(solution)/shard_map/ppermute | solution.py:52
  15.3 2.1 %collective-permute-start.6 = (f32[72,384]{1,0:T(8,128)S(1)}, f32[72,384]{1,0:T(8,128)S(1)}, u32[]{:S(2)}, u32[]{:S(2)}) collective-permute-start(f32[72,384]{1,0:T(8,128)S(1)} %collective-permute-done.2.refs_3_), channel_id=1, source_target_pairs={{0,1},{1,0},{2,3},{3,2},{4,5},{5,4},{6,7},{7,6},{8,9},{9,8},{10,11... | collective-permute-start | bytes 331784 | tf_op jit(solution)/shard_map/ppermute | solution.py:52
  18.1 5.2 %collective-permute-start.11 = (f32[128,384]{1,0:T(8,128)S(1)}, f32[128,384]{1,0:T(8,128)S(1)}, u32[]{:S(2)}, u32[]{:S(2)}) collective-permute-start(f32[128,384]{1,0:T(8,128)S(1)} %shard_map.55), channel_id=1, source_target_pairs={{0,3},{1,4},{2,7},{3,0},{4,1},{5,6},{6,5},{7,2},{8,13},{9,10},{10,... | collective-permute-start | bytes 589832 | tf_op jit(solution)/shard_map/ppermute | solution.py:52
  19.9 5.4 %collective-permute-start.10 = (f32[128,384]{1,0:T(8,128)S(1)}, f32[128,384]{1,0:T(8,128)S(1)}, u32[]{:S(2)}, u32[]{:S(2)}) collective-permute-start(f32[128,384]{1,0:T(8,128)S(1)} %shard_map.54), channel_id=1, source_target_pairs={{0,3},{1,4},{2,7},{3,0},{4,1},{5,6},{6,5},{7,2},{8,13},{9,10},{10,... | collective-permute-start | bytes 589832 | tf_op jit(solution)/shard_map/ppermute | solution.py:52
  23.3 5.2 %collective-permute-start.12 = (f32[128,384]{1,0:T(8,128)S(1)}, f32[128,384]{1,0:T(8,128)S(1)}, u32[]{:S(2)}, u32[]{:S(2)}) collective-permute-start(f32[128,384]{1,0:T(8,128)S(1)} %add.7.refs_2_), channel_id=1, source_target_pairs={{0,5},{1,2},{2,1},{3,6},{4,7},{5,0},{6,3},{7,4},{8,11},{9,12},{10,... | collective-permute-start | bytes 589832 | tf_op jit(solution)/shard_map/ppermute | solution.py:52
  25.4 5.2 %collective-permute-start.13 = (f32[128,384]{1,0:T(8,128)S(1)}, f32[128,384]{1,0:T(8,128)S(1)}, u32[]{:S(2)}, u32[]{:S(2)}) collective-permute-start(f32[128,384]{1,0:T(8,128)S(1)} %add.6.refs_0_), channel_id=1, source_target_pairs={{0,5},{1,2},{2,1},{3,6},{4,7},{5,0},{6,3},{7,4},{8,11},{9,12},{10,... | collective-permute-start | bytes 589832 | tf_op jit(solution)/shard_map/ppermute | solution.py:52
  31.5 4.1 %collective-permute-start.14 = (f32[192,128]{1,0:T(8,128)S(1)}, f32[192,128]{1,0:T(8,128)S(1)}, u32[]{:S(2)}, u32[]{:S(2)}) collective-permute-start(f32[192,128]{1,0:T(8,128)S(1)} %get-tuple-element.19), channel_id=1, source_target_pairs={{0,3},{1,4},{2,7},{3,0},{4,1},{5,6},{6,5},{7,2},{8,13},{9,10},{10,... | collective-permute-start | bytes 294920 | tf_op jit(solution)/shard_map/ppermute | solution.py:52
  35.6 1.3 %collective-permute-start.15 = (f32[96,128]{1,0:T(8,128)S(1)}, f32[96,128]{1,0:T(8,128)S(1)}, u32[]{:S(2)}, u32[]{:S(2)}) collective-permute-start(f32[96,128]{1,0:T(8,128)S(1)} %get-tuple-element.21), channel_id=1, source_target_pairs={{0,1},{1,0},{2,3},{3,2},{4,5},{5,4},{6,7},{7,6},{8,9},{9,8},{10,11... | collective-permute-start | bytes 147464 | tf_op jit(solution)/shard_map/ppermute | solution.py:52
  36.9 6.0 %collective-permute-start.18 = (f32[96,128]{1,0:T(8,128)S(1)}, f32[96,128]{1,0:T(8,128)S(1)}, u32[]{:S(2)}, u32[]{:S(2)}) collective-permute-start(f32[96,128]{1,0:T(8,128)S(1)} %shard_map.58.refs_0_), channel_id=1, source_target_pairs={{0,24},{1,25},{2,26},{3,27},{4,28},{5,29},{6,30},{7,31},{8,16},{9,... | collective-permute-start | bytes 147464 | tf_op jit(solution)/shard_map/ppermute | solution.py:52
  39.8 4.9 %collective-permute-start.17 = (f32[96,128]{1,0:T(8,128)S(1)}, f32[96,128]{1,0:T(8,128)S(1)}, u32[]{:S(2)}, u32[]{:S(2)}) collective-permute-start(f32[96,128]{1,0:T(8,128)S(1)} %shard_map.58.refs_0_), channel_id=1, source_target_pairs={{0,17},{1,16},{2,19},{3,18},{4,21},{5,20},{6,23},{7,22},{8,25},{9,... | collective-permute-start | bytes 147464 | tf_op jit(solution)/shard_map/ppermute | solution.py:52
  40.8 4.9 %collective-permute-start.16 = (f32[96,128]{1,0:T(8,128)S(1)}, f32[96,128]{1,0:T(8,128)S(1)}, u32[]{:S(2)}, u32[]{:S(2)}) collective-permute-start(f32[96,128]{1,0:T(8,128)S(1)} %shard_map.58.refs_0_), channel_id=1, source_target_pairs={{0,9},{1,8},{2,11},{3,10},{4,13},{5,12},{6,15},{7,14},{8,1},{9,0},... | collective-permute-start | bytes 147464 | tf_op jit(solution)/shard_map/ppermute | solution.py:52
  45.7 5.1 %collective-permute-start.21 = (f32[96,128]{1,0:T(8,128)S(1)}, f32[96,128]{1,0:T(8,128)S(1)}, u32[]{:S(2)}, u32[]{:S(2)}) collective-permute-start(f32[96,128]{1,0:T(8,128)S(1)} %shard_map.59.refs_0_), channel_id=1, source_target_pairs={{0,6},{1,7},{2,4},{3,5},{4,2},{5,3},{6,0},{7,1},{8,14},{9,15},{10,... | collective-permute-start | bytes 147464 | tf_op jit(solution)/shard_map/ppermute | solution.py:52
  48.2 3.5 %collective-permute-start.20 = (f32[96,128]{1,0:T(8,128)S(1)}, f32[96,128]{1,0:T(8,128)S(1)}, u32[]{:S(2)}, u32[]{:S(2)}) collective-permute-start(f32[96,128]{1,0:T(8,128)S(1)} %shard_map.59.refs_0_), channel_id=1, source_target_pairs={{0,5},{1,2},{2,1},{3,6},{4,7},{5,0},{6,3},{7,4},{8,11},{9,12},{10,... | collective-permute-start | bytes 147464 | tf_op jit(solution)/shard_map/ppermute | solution.py:52
  48.2 4.0 %collective-permute-start.19 = (f32[96,128]{1,0:T(8,128)S(1)}, f32[96,128]{1,0:T(8,128)S(1)}, u32[]{:S(2)}, u32[]{:S(2)}) collective-permute-start(f32[96,128]{1,0:T(8,128)S(1)} %shard_map.59.refs_0_), channel_id=1, source_target_pairs={{0,3},{1,4},{2,7},{3,0},{4,1},{5,6},{6,5},{7,2},{8,13},{9,10},{10,... | collective-permute-start | bytes 147464 | tf_op jit(solution)/shard_map/ppermute | solution.py:52
  52.2 1.5 %collective-permute-start.22 = (f32[384,128]{1,0:T(8,128)S(1)}, f32[384,128]{1,0:T(8,128)S(1)}, u32[]{:S(2)}, u32[]{:S(2)}) collective-permute-start(f32[384,128]{1,0:T(8,128)S(1)} %shard_map.60.keep_ref), channel_id=1, source_target_pairs={{0,1},{1,0},{2,3},{3,2},{4,5},{5,4},{6,7},{7,6},{8,9},{9,8},{10,11... | collective-permute-start | bytes 589832 | tf_op jit(solution)/shard_map/ppermute | solution.py:52
